TPU v7x, 32 devices: a whole 2x2x4 slice. The times are simulated.
32 devices in a mesh: dp: 8 (over z, y), tensor: 4 (over x, core).
Axes of the slice: x: 2, y: 2, z: 4, core: 2. Of those that a mesh axis runs over, the one named last changes fastest.
Arguments:
- tokens: bfloat16 [4096, 1024], P(('dp', 'tensor')), may hold values from -6 to 6
- lengths: int32 [8, 4], P('dp'), may hold values from 0 to 512, as said below
- cotangent: bfloat16 [4096, 1024], P(('dp', 'tensor')), may hold values from -6 to 6
- pre_gain: bfloat16 [1024], P(('dp', 'tensor')), may hold values from 0.5 to 1.5
- input_weight: bfloat16 [1024, 2, 2048], P('dp', None, 'tensor'), may hold values from -0.1875 to 0.1875
- step_weight: bfloat16 [1024, 32], P('dp', 'tensor'), may hold values from -0.1875 to 0.1875
- state_weight: bfloat16 [1024, 256], P(('dp', 'tensor')), may hold values from -0.1875 to 0.1875
- conv_inner: bfloat16 [4, 2048], P(None, 'tensor'), may hold values from -3 to 3
- conv_inner_bias: bfloat16 [2048], P('tensor'), may hold values from -0.5 to 0.5
- conv_state: bfloat16 [4, 256], P(None, ('dp', 'tensor')), may hold values from -3 to 3
- conv_state_bias: bfloat16 [256], P(('dp', 'tensor')), may hold values from -0.5 to 0.5
- step_bias: bfloat16 [32], P('tensor'), may hold values from -5 to -1
- decay_log: bfloat16 [32], P('tensor'), may hold values from -2 to 1.5
- skip_gain: bfloat16 [32], P('tensor'), may hold values from 0.5 to 1.5
- norm_gain: bfloat16 [2048], P('tensor'), may hold values from 0.5 to 1.5
- output_weight: bfloat16 [2048, 1024], P('tensor', 'dp'), may hold values from -0.125 to 0.125
Outputs:
- block_out: bfloat16 [4096, 1024], P(('dp', 'tensor'))
- tokens_grad: float32 [4096, 1024], P(('dp', 'tensor'))
- pre_gain_grad: float32 [1024], P(('dp', 'tensor'))
- input_weight_grad: float32 [1024, 2, 2048], P('dp', None, 'tensor')
- step_weight_grad: float32 [1024, 32], P('dp', 'tensor')
- state_weight_grad: float32 [1024, 256], P(('dp', 'tensor'))
- conv_inner_grad: float32 [4, 2048], P(None, 'tensor')
- conv_inner_bias_grad: float32 [2048], P('tensor')
- conv_state_grad: float32 [4, 256], P(None, ('dp', 'tensor'))
- conv_state_bias_grad: float32 [256], P(('dp', 'tensor'))
- step_bias_grad: float32 [32], P('tensor')
- decay_log_grad: float32 [32], P('tensor')
- skip_gain_grad: float32 [32], P('tensor')
- norm_gain_grad: float32 [2048], P('tensor')
- output_weight_grad: float32 [2048, 1024], P('tensor', 'dp')
Inputs may be any that keep to these rules, and one draw needn't show every extreme that they name: Row g lists the lengths of the 4 sequences packed in order from the start of group g; empty slots are 0, the lengths of a row add up to at most 512, and the rows after them are padding.
All inputs are finite; a program needn't handle non-finite values.
Results may differ from a plain program's by a relative error of at most 0.0095.
Values may be sent and summed in bfloat16 or wider, within the bound.
No kernel may reach another device: no remote copies, remote signals or barrier semaphores. Data moves between devices by JAX's collectives and lax.ppermute only.
A program may use at most 128 MiB of HBM per device.

v0:
```python
import functools

import jax
import jax.numpy as jnp
from jax import lax
from jax.experimental import pallas as pl
from jax.experimental.pallas import tpu as pltpu
from jax.sharding import PartitionSpec as P

epsilon = 1e-05
highest = lax.Precision.HIGHEST
f32 = jnp.float32
bf16 = jnp.bfloat16
span = 256
pad = 8
head_rows = 16
head_width = 64
vmem_bytes = 52 * 1024 * 1024


def mm(a, b, over=(1, 0)):
    dims = (((over[0],), (over[1],)), ((), ()))
    return lax.dot_general(a, b, dims, preferred_element_type=f32)


def mm_exact(a, b, over=(1, 0)):
    dims = (((over[0],), (over[1],)), ((), ()))
    return lax.dot_general(a, b, dims, preferred_element_type=f32, precision=highest)


def sigmoid(v):
    return 1.0 / (1.0 + jnp.exp(-v))


def ends_of(lengths_ref):
    ends, total = [], None
    for slot in range(lengths_ref.shape[1]):
        here = lengths_ref[0, slot]
        total = here if total is None else total + here
        ends.append(total)
    return ends


def segment_of(places, ends):
    segment = jnp.zeros(places.shape, jnp.int32)
    for end in ends:
        segment = segment + jnp.where(places >= end, 1, 0)
    return segment


def iota(shape, dim):
    return lax.broadcasted_iota(jnp.int32, shape, dim)


def write_masks(mask_ref, ends):
    rows = mask_ref.shape[1] - pad
    places = iota((rows, 128), 0)
    segment = segment_of(places, ends)
    for shift in range(1, mask_ref.shape[0] + 1):
        same = (segment_of(places - shift, ends) == segment) & (places >= shift)
        mask_ref[shift - 1, :rows, :] = jnp.where(same, 1.0, 0.0)
        mask_ref[shift - 1, rows:, :] = jnp.zeros((pad, 128), f32)


def shifted_rows(x_ref, mask_ref, at, cols, shift, tall):
    part = x_ref[pad + at - shift : pad + at - shift + tall, cols]
    if shift == 0:
        return part
    return part * mask_ref[shift - 1, at : at + tall, :]


def conv_pre(x_ref, mask_ref, taps_ref, bias_ref, at, cols, tall):
    taps = taps_ref.shape[0]
    shifted = [shifted_rows(x_ref, mask_ref, at, cols, s, tall) for s in range(taps)]
    total = bias_ref[:, cols]
    for s in range(taps):
        total = total + taps_ref[taps - 1 - s : taps - s, cols] * shifted[s]
    return total, shifted


def column_loop(width, step):
    def one(c, carry):
        step(pl.ds(pl.multiple_of(c * 128, 128), 128))
        return carry

    lax.fori_loop(0, width // 128, one, 0)


def row_loop(rows, tall, step):
    def one(r, carry):
        step(pl.multiple_of(r * tall, tall))
        return carry

    lax.fori_loop(0, rows // tall, one, 0)


class Block:
    def __init__(self, b, ends, step_col, step_row, rate_col, rate_row, state_ref):
        low, top = b * span, (b + 1) * span
        states = state_ref.shape[1] // 2
        lower = jnp.where(iota((span, span), 0) >= iota((span, span), 1), 1.0, 0.0)
        self.rows = slice(low, top)
        self.step = step_col[low:top]
        self.step_row = step_row[:, low:top]
        self.cum = mm_exact(lower, rate_col[low:top])
        self.cum_row = mm_exact(rate_row[:, low:top], lower, (1, 1))
        self.inputs = state_ref[low:top, :states].astype(bf16)
        self.outputs = state_ref[low:top, states:].astype(bf16)
        segment = segment_of(iota((span, 1), 0) + low, ends)
        segment_row = segment_of(iota((1, span), 1) + low, ends)
        edge = sum(jnp.where(span - 1 >= end, 1, 0) for end in ends)
        self.near_edge = jnp.where(segment == edge, 1.0, 0.0)
        self.mask = jnp.where(segment == segment_row, lower, 0.0)
        self.contact = mm(self.outputs, self.inputs, (1, 1)) * self.mask

    def decay(self, h):
        gap = self.cum[:, h : h + 1] - self.cum_row[h : h + 1, :]
        return jnp.exp(jnp.minimum(gap, 0.0))

    def from_edge(self, h):
        return jnp.exp(self.cum[:, h : h + 1]) * self.near_edge

    def to_edge(self, h):
        last = self.cum[span - 1 : span, h : h + 1]
        return jnp.exp(last - self.cum[:, h : h + 1]) * self.near_edge


def wide(low_half, left, right):
    return jnp.where(low_half, left, right)


def step_sizes(raw_col, raw_row, bias_ref, bias_col_ref, log_ref, log_col_ref):
    def soft(v):
        return jnp.maximum(v, 0.0) + jnp.log1p(jnp.exp(-jnp.abs(v)))

    step_col = soft(raw_col + bias_ref[...])
    step_row = soft(raw_row + bias_col_ref[...])
    rate_col = -step_col * jnp.exp(log_ref[...])
    rate_row = -step_row * jnp.exp(log_col_ref[...])
    return step_col, step_row, rate_col, rate_row


def forward_kernel(fast, place_ref, lengths_ref, *refs):
    n_rows = 4 if fast else 1
    n_msg = 8 if fast else 4
    row_refs, msg_refs, refs = refs[:n_rows], refs[n_rows : n_rows + n_msg], refs[n_rows + n_msg :]
    (taps_ref, bias_ref, step_bias_ref, step_bias_col_ref, log_ref, log_col_ref, skip_ref) = refs[:7]
    (
        rows_ref,
        normed_ref,
        weight_ref,
        state_weight_ref,
        step_weight_ref,
        small_ref,
        gate_ref,
        raw_ref,
        state_raw_ref,
        step_col_ref,
        step_row_ref,
        act_ref,
        state_ref,
        mixed_ref,
    ) = refs[7:21]
    mask_ref, state_taps_ref, state_bias_ref = refs[21:]
    total = rows_ref.shape[0]
    channels = gate_ref.shape[1]
    ends = ends_of(lengths_ref)

    if fast:
        depth_part = 128
        small = jnp.zeros(small_ref.shape, f32)
        share = state_weight_ref.shape[0] // 32
        for slot in range(8):
            msg = msg_refs[slot]
            index = place_ref[4 + slot]
            at = pl.multiple_of(index * depth_part, depth_part)
            weight_ref[pl.ds(at, depth_part), :] = msg[:depth_part, :]
            for member in range(4):
                inner = pl.multiple_of(at + place_ref[member] * share, share)
                state_weight_ref[pl.ds(inner, share), :] = msg[
                    depth_part : depth_part + share, 256 * member : 256 * (member + 1)
                ]
            tail = depth_part + share
            small = small + msg[tail : tail + 16, :256].astype(f32)
            step_weight_ref[:, pl.ds(at, depth_part)] = msg[tail : tail + 16, 256:384]
        small_ref[...] = small
    else:
        weight_ref[...] = msg_refs[0][...]
        state_weight_ref[...] = msg_refs[1][...]
        step_weight_ref[...] = msg_refs[2][...]
        small_ref[...] = msg_refs[3][...].astype(f32)
    gain = jnp.concatenate([small_ref[i : i + 1, :] for i in range(4)], axis=1)
    taps = taps_ref.shape[0]
    state_taps_ref[...] = small_ref[4 : 4 + taps, :]
    state_bias_ref[...] = small_ref[4 + taps : 5 + taps, :]

    tall = total // n_rows
    for member in range(n_rows):
        at = pl.multiple_of(place_ref[member] * tall, tall) if fast else 0
        own = row_refs[member]
        rows_ref[pl.ds(at, tall), :] = own[...]
        value = own[...].astype(f32)
        scale = lax.rsqrt(jnp.mean(value * value, axis=1, keepdims=True) + epsilon)
        normed_ref[pl.ds(at, tall), :] = (value * scale * gain).astype(bf16)

    raw_ref[:pad, :] = jnp.zeros((pad, channels), f32)
    state_raw_ref[:pad, :] = jnp.zeros((pad, state_raw_ref.shape[1]), f32)

    def project(at):
        part = normed_ref[pl.ds(at, 128), :]
        both = mm(part, weight_ref[...])
        gate_ref[pl.ds(at, 128), :] = both[:, :channels]
        raw_ref[pl.ds(at + pad, 128), :] = both[:, channels:]
        state_raw_ref[pl.ds(at + pad, 128), :] = mm(part, state_weight_ref[...])
        step_col_ref[pl.ds(at, 128), :] = mm(part, step_weight_ref[...], (1, 1))

    row_loop(total, 128, project)
    step_row_ref[...] = mm(step_weight_ref[...], normed_ref[...], (1, 1))

    write_masks(mask_ref, ends)

    def activate(x_ref, out_ref, own_taps, own_bias):
        def column(cols):
            for at in range(0, total, 128):
                pre, _ = conv_pre(x_ref, mask_ref, own_taps, own_bias, at, cols, 128)
                out_ref[at : at + 128, cols] = pre * sigmoid(pre)

        column_loop(out_ref.shape[1], column)

    activate(raw_ref, act_ref, taps_ref, bias_ref)
    activate(state_raw_ref, state_ref, state_taps_ref, state_bias_ref)

    steps = step_sizes(
        step_col_ref[...],
        step_row_ref[...],
        step_bias_ref,
        step_bias_col_ref,
        log_ref,
        log_col_ref,
    )
    low_half = iota((span, 128), 1) < head_width
    held = []
    for b in range(total // span):
        block = Block(b, ends, *steps, state_ref)
        for i in range(channels // 128):
            cols = slice(128 * i, 128 * (i + 1))
            pair = (2 * i, 2 * i + 1)
            x = act_ref[block.rows, cols]
            step_wide = wide(low_half, *(block.step[:, h : h + 1] for h in pair))
            x_step = (x * step_wide).astype(bf16)
            y = [mm((block.decay(h) * block.contact).astype(bf16), x_step) for h in pair]
            y = wide(low_half, *y) + skip_ref[:, cols] * x
            if b == 0:
                reach = wide(low_half, *(block.to_edge(h) for h in pair))
                weighted = (x * step_wide * reach).astype(bf16)
                held.append(mm(block.inputs, weighted, (0, 0)).astype(bf16))
            else:
                reach = wide(low_half, *(block.from_edge(h) for h in pair))
                y = y + reach * mm(block.outputs, held[i])
            mixed_ref[block.rows, cols] = y


def grad_in_kernel(fast, place_ref, lengths_ref, *refs):
    n_rows = 4 if fast else 1
    n_msg = 8 if fast else 1
    row_refs, out_refs, refs = refs[:n_rows], refs[n_rows : n_rows + n_msg], refs[n_rows + n_msg :]
    gate_ref, mixed_ref, norm_ref, rows_ref, weight_ref, grad_ref, sums_ref, wide_ref = refs
    total = rows_ref.shape[0]
    ends = ends_of(lengths_ref)
    tall = total // n_rows
    for member in range(n_rows):
        at = pl.multiple_of(place_ref[member] * tall, tall) if fast else 0
        rows_ref[pl.ds(at, tall), :] = row_refs[member][...]
    if fast:
        for slot in range(8):
            at = pl.multiple_of(place_ref[4 + slot] * 128, 128)
            weight_ref[:, pl.ds(at, 128)] = out_refs[slot][...]
    else:
        weight_ref[...] = out_refs[0][...]

    def part(at):
        rows = pl.ds(at, 128)
        valid = jnp.where(iota((128, 1), 0) + at < ends[-1], 1.0, 0.0)
        grad = mm(rows_ref[rows, :], weight_ref[...], (1, 1)) * valid
        grad_ref[rows, :] = grad
        gate = gate_ref[rows, :]
        gated = mixed_ref[rows, :] * (gate * sigmoid(gate))
        square = jnp.sum(gated * gated, axis=1, keepdims=True)
        cross = jnp.sum(grad * norm_ref[...] * gated, axis=1, keepdims=True)
        lane = iota((128, 128), 1)
        wide_ref[rows, :] = jnp.where(lane == 0, square, jnp.where(lane == 1, cross, 0.0))

    row_loop(total, 128, part)
    for at in range(0, total, 128):
        sums_ref[:, at : at + 128] = wide_ref[at : at + 128, :].T[:8, :]


def norm_kernel(inner_total, lengths_ref, *refs):
    (sums_ref, gate_ref, mixed_ref, grad_ref, norm_ref, weight_ref, rows_ref, normed_ref) = refs[:8]
    partial_ref, msg_ref, grad_gate_ref, grad_mixed_ref, norm_grad_ref = refs[8:13]
    wide_ref, out_rows_ref = refs[13:]
    total, channels = gate_ref.shape
    ends = ends_of(lengths_ref)
    for at in range(0, total, 128):
        tile = jnp.concatenate([sums_ref[:, at : at + 128]] * 16, axis=0)
        wide_ref[at : at + 128, :] = tile.T
    norm_grad_ref[...] = jnp.zeros(norm_grad_ref.shape, f32)

    def part(at):
        rows = pl.ds(at, 128)
        valid = jnp.where(iota((128, 1), 0) + at < ends[-1], 1.0, 0.0)
        scale = lax.rsqrt(wide_ref[rows, 0:1] / inner_total + epsilon)
        cross = wide_ref[rows, 1:2]
        gate = gate_ref[rows, :]
        mixed = mixed_ref[rows, :]
        sig = sigmoid(gate)
        gate_act = gate * sig
        gated = mixed * gate_act
        grad = grad_ref[rows, :]
        norm = norm_ref[...]
        hat = gated * scale
        out_rows_ref[rows, :] = (hat * norm * valid).astype(bf16)
        norm_grad_ref[...] += jnp.sum(grad * hat, axis=0, keepdims=True)
        grad_gated = scale * (grad * norm) - gated * (scale * scale * scale * cross / inner_total)
        grad_mixed_ref[rows, :] = grad_gated * gate_act
        grad_gate = grad_gated * mixed * sig * (1.0 + gate * (1.0 - sig))
        grad_gate_ref[rows, :] = grad_gate.astype(bf16)
        partial_ref[rows, :] = mm(out_rows_ref[rows, :], weight_ref[...]).astype(bf16)

    row_loop(total, 128, part)

    chunks, tall = msg_ref.shape[0], msg_ref.shape[1] // 2

    def chunk(c):
        cols = pl.ds(pl.multiple_of(c * tall, tall), tall)
        msg_ref[c, :tall, :] = mm(normed_ref[:, cols], grad_gate_ref[...], (0, 0)).astype(bf16)
        msg_ref[c, tall:, :] = mm(rows_ref[:, cols], out_rows_ref[...], (0, 0)).astype(bf16)

    def one(c, carry):
        chunk(c)
        return carry

    lax.fori_loop(0, chunks, one, 0)


def backward_kernel(lengths_ref, *refs):
    (
        grad_mixed_ref,
        act_ref,
        state_ref,
        raw_ref,
        state_raw_ref,
        step_col_ref,
        step_row_ref,
        grad_gate_ref,
        normed_ref,
        rows_ref,
        weight_ref,
        state_weight_ref,
        step_weight_ref,
        small_ref,
        taps_ref,
        bias_ref,
        step_bias_ref,
        step_bias_col_ref,
        log_ref,
        log_col_ref,
        skip_ref,
    ) = refs[:21]
    (
        msg_ref,
        state_part_ref,
        step_part_ref,
        gain_part_ref,
        grad_normed_ref,
        inner_sums_ref,
        head_sums_ref,
        state_sums_ref,
    ) = refs[21:29]
    (
        mask_ref,
        state_taps_ref,
        state_bias_ref,
        acc_ref,
        grad_act_ref,
        grad_state_ref,
        pre_ref,
        state_pre_ref,
        grad_inner_ref,
        grad_state_low_ref,
    ) = refs[29:]
    total, channels = grad_mixed_ref.shape
    states = state_ref.shape[1] // 2
    ends = ends_of(lengths_ref)
    taps = taps_ref.shape[0]
    state_taps_ref[...] = small_ref[4 : 4 + taps, :]
    state_bias_ref[...] = small_ref[4 + taps : 5 + taps, :]
    write_masks(mask_ref, ends)
    raw_row = step_row_ref[...]
    steps = step_sizes(
        step_col_ref[...], raw_row, step_bias_ref, step_bias_col_ref, log_ref, log_col_ref
    )
    rate_row = steps[3]
    low_half = iota((span, 128), 1) < head_width
    lower = jnp.where(iota((span, span), 0) >= iota((span, span), 1), 1.0, 0.0)
    blocks = [Block(b, ends, *steps, state_ref) for b in range(total // span)]
    first, second = blocks
    row_sums, step_rows, out_sums, in_sums = [], [], None, None
    grad_out = jnp.zeros((span, states), f32)
    grad_in = jnp.zeros((span, states), f32)
    head_of = iota((head_rows, 128), 0)
    lane_head = iota((head_rows, 128), 1) // head_width

    for b, block in enumerate(blocks):
        acc_ref[...] = jnp.zeros((span, span), f32)
        row_sum = jnp.zeros((span, 128), f32)
        step_grad = jnp.zeros((head_rows, span), f32)
        lane = iota((span, 128), 1)
        head_row = iota((head_rows, span), 0)
        for i in range(channels // 128):
            cols = slice(128 * i, 128 * (i + 1))
            pair = (2 * i, 2 * i + 1)
            x = act_ref[block.rows, cols]
            x_low = x.astype(bf16)
            grad = grad_mixed_ref[block.rows, cols]
            grad_low = grad.astype(bf16)
            halves = (
                jnp.where(low_half, grad, 0.0).astype(bf16),
                jnp.where(low_half, 0.0, grad).astype(bf16),
            )
            step_wide = wide(low_half, *(block.step[:, h : h + 1] for h in pair))
            grads = []
            for h, half in zip(pair, halves):
                decay = block.decay(h)
                spread = mm(half, x_low, (1, 1)) * decay
                stepped = spread * block.step_row[h : h + 1, :]
                acc_ref[...] += stepped
                row_here = jnp.sum(stepped * block.contact, axis=1, keepdims=True)
                row_sum = jnp.where(lane == h, row_here, row_sum)
                step_here = jnp.sum(spread * block.contact, axis=0, keepdims=True)
                step_grad = jnp.where(head_row == h, step_here, step_grad)
                grads.append(mm((decay * block.contact).astype(bf16), grad_low, (0, 0)))
            grad_act = wide(low_half, *grads) * step_wide + skip_ref[:, cols] * grad
            picks = jnp.where(lane_head + 2 * i == head_of, 1.0, 0.0)
            if b == 0:
                reach = wide(low_half, *(second.from_edge(h) for h in pair))
                lead = (grad_mixed_ref[second.rows, cols] * reach).astype(bf16)
                edge = wide(low_half, *(block.to_edge(h) for h in pair))
                weighted = (x * step_wide * edge).astype(bf16)
                held = mm(block.inputs, weighted, (0, 0)).astype(bf16)
                held_grad = mm(second.outputs, lead, (0, 0)).astype(bf16)
                grad_out = grad_out + mm(lead, held, (1, 1))
                grad_in = grad_in + mm(weighted, held_grad, (1, 1))
                back = mm(block.inputs, held_grad) * edge
                grad_act = grad_act + back * step_wide
                ahead = mm(second.outputs, held)
                out_here = mm_exact(picks, lead.astype(f32) * ahead, (1, 1))
                in_here = mm_exact(picks, x * back, (1, 1))
                out_sums = out_here if out_sums is None else out_sums + out_here
                in_sums = in_here if in_sums is None else in_sums + in_here
            grad_act_ref[block.rows, cols] = grad_act
        table = (acc_ref[...] * block.mask).astype(bf16)
        grad_c = mm(table, block.inputs)
        grad_b = mm(table, block.outputs, (0, 0))
        if b == 0:
            grad_b = grad_b + grad_in
        else:
            grad_c = grad_c + grad_out
        grad_state_ref[block.rows, :states] = grad_b
        grad_state_ref[block.rows, states:] = grad_c
        row_sums.append(row_sum)
        step_rows.append(step_grad)

    rate_grads = []
    for b, block in enumerate(blocks):
        column = step_rows[b] * block.step_row
        crossing = mm_exact(row_sums[b], lower, (0, 0))[:head_rows] - mm_exact(column, lower)
        if b == 0:
            crossing = crossing + mm_exact(in_sums * block.step_row, 1.0 - lower)
        else:
            crossing = crossing + mm_exact(out_sums, lower)
        rate_grads.append(crossing)
    step_rows[0] = step_rows[0] + in_sums
    rate_grad = jnp.concatenate(rate_grads, axis=1)
    step_grad = jnp.concatenate(step_rows, axis=1) - rate_grad * jnp.exp(log_col_ref[...])
    step_grad = step_grad * sigmoid(raw_row + step_bias_col_ref[...])
    decay_sum = jnp.sum(rate_grad * rate_row, axis=1, keepdims=True)
    bias_sum = jnp.sum(step_grad, axis=1, keepdims=True)
    lane = iota((head_rows, 128), 1)
    head_sums_ref[...] = jnp.where(lane == 0, bias_sum, jnp.where(lane == 1, decay_sum, 0.0))
    step_grad_low = step_grad.astype(bf16)

    def conv_back(x_ref, grad_ref, held_ref, out_ref, sums_ref, own_taps, own_bias, skips):
        held_ref[total:, :] = jnp.zeros((pad, held_ref.shape[1]), f32)

        def column(cols):
            sums = [jnp.zeros((1, 128), f32) for _ in range(taps + 2)]
            for at in range(0, total, 128):
                pre, shifted = conv_pre(x_ref, mask_ref, own_taps, own_bias, at, cols, 128)
                sig = sigmoid(pre)
                grad = grad_ref[at : at + 128, cols] * sig * (1.0 + pre * (1.0 - sig))
                held_ref[at : at + 128, cols] = grad
                for s in range(taps):
                    sums[taps - 1 - s] += jnp.sum(grad * shifted[s], axis=0, keepdims=True)
                sums[taps] += jnp.sum(grad, axis=0, keepdims=True)
                if skips:
                    act = act_ref[at : at + 128, cols]
                    over = grad_mixed_ref[at : at + 128, cols] * act
                    sums[taps + 1] += jnp.sum(over, axis=0, keepdims=True)
            for t, value in enumerate(sums):
                sums_ref[t : t + 1, cols] = value
            for at in range(0, total, 128):
                back = own_taps[taps - 1 : taps, cols] * held_ref[at : at + 128, cols]
                for s in range(1, taps):
                    part = held_ref[at + s : at + s + 128, cols]
                    part = part * mask_ref[s - 1, at + s : at + s + 128, :]
                    back = back + own_taps[taps - 1 - s : taps - s, cols] * part
                out_ref[at : at + 128, cols] = back.astype(bf16)

        column_loop(out_ref.shape[1], column)

    inner_sums_ref[...] = jnp.zeros(inner_sums_ref.shape, f32)
    state_sums_ref[...] = jnp.zeros(state_sums_ref.shape, f32)
    conv_back(
        raw_ref, grad_act_ref, pre_ref, grad_inner_ref, inner_sums_ref, taps_ref, bias_ref, True
    )
    conv_back(
        state_raw_ref,
        grad_state_ref,
        state_pre_ref,
        grad_state_low_ref,
        state_sums_ref,
        state_taps_ref,
        state_bias_ref,
        False,
    )

    chunks, tall = msg_ref.shape[0], msg_ref.shape[1]

    def chunk(c, carry):
        at = pl.multiple_of(c * tall, tall)
        part = normed_ref[:, pl.ds(at, tall)]
        msg_ref[c] = mm(part, grad_inner_ref[...], (0, 0)).astype(bf16)
        state_part_ref[pl.ds(at, tall), :] = mm(part, grad_state_low_ref[...], (0, 0)).astype(bf16)
        return carry

    lax.fori_loop(0, chunks, chunk, 0)
    step_part_ref[...] = mm(step_grad_low, normed_ref[...])
    step_back = step_grad.T.astype(bf16)
    gain_part_ref[...] = jnp.zeros(gain_part_ref.shape, f32)
    for at in range(0, total, 128):
        rows = slice(at, at + 128)
        grad = mm(grad_gate_ref[rows, :], weight_ref[:, :channels], (1, 1))
        grad = grad + mm(grad_inner_ref[rows, :], weight_ref[:, channels:], (1, 1))
        grad = grad + mm(grad_state_low_ref[rows, :], state_weight_ref[...], (1, 1))
        grad = grad + mm(step_back[rows, :], step_weight_ref[...])
        grad_normed_ref[rows, :] = grad.astype(bf16)
        value = rows_ref[rows, :].astype(f32)
        scale = lax.rsqrt(jnp.mean(value * value, axis=1, keepdims=True) + epsilon)
        gain_part_ref[...] += jnp.sum(grad * (value * scale), axis=0, keepdims=True)


def call(kernel, scalars, arrays, outs, scratch):
    smem = pl.BlockSpec(memory_space=pltpu.SMEM)
    vmem = pl.BlockSpec(memory_space=pltpu.VMEM)
    return pl.pallas_call(
        kernel,
        out_shape=[jax.ShapeDtypeStruct(shape, kind) for shape, kind in outs],
        in_specs=[smem] * len(scalars) + [vmem] * len(arrays),
        out_specs=[vmem] * len(outs),
        scratch_shapes=[pltpu.VMEM(shape, kind) for shape, kind in scratch],
        compiler_params=pltpu.CompilerParams(vmem_limit_bytes=vmem_bytes),
    )(*scalars, *arrays)


def ring_ok(n_dp, n_tensor):
    return n_dp == 8 and n_tensor == 4


ring_order = (0, 2, 4, 6, 7, 5, 3, 1)


def ring_place(index):
    high, low = index // 2, index % 2
    return jnp.where(low == 0, high, 7 - high)


def ring_index(place):
    place = lax.rem(place + 16, 8)
    return jnp.where(place < 4, 2 * place, 2 * (7 - place) + 1)


def ring_send(value, forward):
    pairs = []
    for place in range(8):
        other = (place + (1 if forward else 7)) % 8
        pairs.append((ring_order[place], ring_order[other]))
    return lax.ppermute(value, "dp", pairs)


def ring_gather(value):
    me = ring_place(lax.axis_index("dp"))
    pieces = [(value, ring_index(me))]
    ahead, back = value, value
    for step in range(1, 5):
        ahead = ring_send(ahead, True)
        pieces.append((ahead, ring_index(me - step)))
        if step < 4:
            back = ring_send(back, False)
            pieces.append((back, ring_index(me + step)))
    return pieces


def ring_scatter(parts):
    me = ring_place(lax.axis_index("dp"))

    def own(place):
        return lax.dynamic_index_in_dim(parts, ring_index(place), 0, keepdims=False).astype(f32)

    total = own(me)
    for forward, steps in ((True, 4), (False, 3)):
        sign = 1 if forward else -1
        held = own(me + sign * steps)
        for step in range(1, steps + 1):
            got = ring_send(held.astype(bf16), forward).astype(f32)
            if step < steps:
                held = got + own(me + sign * (steps - step))
            else:
                total = total + got
    return total


def dp_others(value):
    got = []
    for shift in range(1, 8):
        pairs = [(i, (i + shift) % 8) for i in range(8)]
        got.append(lax.ppermute(value, "dp", pairs))
    return got


def tensor_swap(value, bit):
    return lax.ppermute(value, "tensor", [(i, i ^ bit) for i in range(4)])


def tensor_gather(value):
    near = tensor_swap(value, 1)
    far = tensor_swap(value, 2)
    return [value, near, far, tensor_swap(far, 1)]


def tensor_scatter(parts):
    me = lax.axis_index("tensor")
    core, across = me % 2, me // 2
    split = parts.reshape((2, 2) + parts.shape[1:])
    give = lax.dynamic_index_in_dim(split, 1 - core, 1, keepdims=False)
    keep = lax.dynamic_index_in_dim(split, core, 1, keepdims=False)
    got = tensor_swap(give, 1)
    half = keep.astype(f32) + got.astype(f32)
    give = lax.dynamic_index_in_dim(half, 1 - across, 0, keepdims=False)
    keep = lax.dynamic_index_in_dim(half, across, 0, keepdims=False)
    got = tensor_swap(give.astype(bf16), 2)
    return keep + got.astype(f32)


def body(
    tokens,
    lengths,
    cotangent,
    pre_gain,
    input_weight,
    step_weight,
    state_weight,
    conv_inner,
    conv_inner_bias,
    conv_state,
    conv_state_bias,
    step_bias,
    decay_log,
    skip_gain,
    norm_gain,
    output_weight,
):
    n_dp, n_tensor = lax.axis_size("dp"), lax.axis_size("tensor")
    fast = ring_ok(n_dp, n_tensor)
    owners = n_dp * n_tensor
    me = lax.axis_index("tensor")
    owner = lax.axis_index("dp") * n_tensor + me
    own_rows, depth = tokens.shape
    total = own_rows * n_tensor
    states = state_weight.shape[1]
    heads = step_weight.shape[1]
    share = state_weight.shape[0]
    taps = conv_state.shape[0]
    channels = input_weight.shape[2]
    inner_total = channels * n_tensor

    def placed(value, whole):
        zeros = jnp.zeros(value.shape[:-1] + (whole,), value.dtype)
        start = (0,) * (value.ndim - 1) + (owner * value.shape[-1],)
        return lax.dynamic_update_slice(zeros, value, start)

    small = jnp.concatenate(
        [
            placed(pre_gain, depth).reshape(-1, states),
            placed(conv_state, states),
            placed(conv_state_bias[None], states),
        ],
        axis=0,
    )
    small = jnp.pad(small, ((0, 16 - small.shape[0]), (0, 0)))
    step_rows = jnp.pad(step_weight.T, ((0, head_rows - heads), (0, 0)))
    input_flat = input_weight.reshape(input_weight.shape[0], -1)
    if fast:
        shared = tensor_gather(jnp.concatenate([state_weight, small], axis=0))
        beside = jnp.concatenate([piece[:share] for piece in shared], axis=1)
        small = shared[0][share:] + shared[1][share:] + shared[2][share:] + shared[3][share:]
        tail = jnp.concatenate([small, step_rows], axis=1)
        tail = jnp.pad(tail, ((0, 0), (0, depth - tail.shape[1])))
        msg = ring_gather(jnp.concatenate([input_flat, beside, tail], axis=0))
        out_msg = ring_gather(output_weight)
        row_pieces = tensor_gather(tokens)
        grad_pieces = tensor_gather(cotangent)
        weight_pieces = [piece for piece, _ in msg]
        out_pieces = [piece for piece, _ in out_msg]
        place = jnp.stack([me, me ^ 1, me ^ 2, me ^ 3] + [index for _, index in msg])
    else:
        row_pieces = [lax.all_gather(tokens, "tensor", axis=0, tiled=True)]
        grad_pieces = [lax.all_gather(cotangent, "tensor", axis=0, tiled=True)]
        weight_pieces = [
            lax.all_gather(input_flat, "dp", axis=0, tiled=True),
            lax.all_gather(state_weight, ("dp", "tensor"), axis=0, tiled=True),
            lax.all_gather(step_rows, "dp", axis=1, tiled=True),
            lax.psum(small, ("dp", "tensor")),
        ]
        out_pieces = [lax.all_gather(output_weight, "dp", axis=1, tiled=True)]
        place = jnp.zeros((12,), jnp.int32)
    place = place.astype(jnp.int32)

    def row(value):
        return value.astype(f32).reshape(1, -1)

    def head(value):
        return jnp.pad(value.astype(f32), (0, head_rows - heads))

    taps_float = conv_inner.astype(f32)
    scan_params = [
        taps_float,
        row(conv_inner_bias),
        head(step_bias)[None, :],
        head(step_bias)[:, None],
        head(decay_log)[None, :],
        head(decay_log)[:, None],
        row(jnp.repeat(skip_gain, channels // heads)),
    ]
    masks = ((taps - 1, total + pad, 128), f32)
    state_taps = [((taps, states), f32), ((1, states), f32)]
    (
        rows,
        normed,
        weight_full,
        state_full,
        step_full,
        small_full,
        gate,
        raw,
        state_raw,
        step_col,
        step_row,
        act,
        state_act,
        mixed,
    ) = call(
        functools.partial(forward_kernel, fast),
        [place, lengths],
        row_pieces + weight_pieces + scan_params,
        [
            ((total, depth), bf16),
            ((total, depth), bf16),
            ((depth, 2 * channels), bf16),
            ((depth, states), bf16),
            ((head_rows, depth), bf16),
            ((16, states), f32),
            ((total, channels), f32),
            ((total + pad, channels), f32),
            ((total + pad, states), f32),
            ((total, head_rows), f32),
            ((head_rows, total), f32),
            ((total, channels), f32),
            ((total, states), f32),
            ((total, channels), f32),
        ],
        [masks] + state_taps,
    )
    norm_row = row(norm_gain)
    grad_rows, output_full, grad_normalized, sums = call(
        functools.partial(grad_in_kernel, fast),
        [place, lengths],
        grad_pieces + out_pieces + [gate, mixed, norm_row],
        [
            ((total, depth), bf16),
            ((channels, depth), bf16),
            ((total, channels), f32),
            ((8, total), f32),
        ],
        [((total, 128), f32)],
    )
    if fast:
        sums = sums + tensor_swap(sums, 1)
        sums = sums + tensor_swap(sums, 2)
    else:
        sums = lax.psum(sums, "tensor")
    chunks = 8
    tall = depth // chunks
    partial_out, gate_msg, grad_gate, grad_mixed, norm_grad = call(
        functools.partial(norm_kernel, inner_total),
        [lengths],
        [sums, gate, mixed, grad_normalized, norm_row, output_full, grad_rows, normed],
        [
            ((total, depth), bf16),
            ((chunks, 2 * tall, channels), bf16),
            ((total, channels), bf16),
            ((total, channels), f32),
            ((1, channels), f32),
        ],
        [((total, 128), f32), ((total, channels), bf16)],
    )
    (
        inner_msg,
        state_part,
        step_part,
        gain_part,
        grad_normed,
        inner_sums,
        head_sums,
        state_sums,
    ) = call(
        backward_kernel,
        [lengths],
        [
            grad_mixed,
            act,
            state_act,
            raw,
            state_raw,
            step_col,
            step_row,
            grad_gate,
            normed,
            rows,
            weight_full,
            state_full,
            step_full,
            small_full,
        ]
        + scan_params,
        [
            ((chunks, tall, channels), bf16),
            ((depth, states), bf16),
            ((head_rows, depth), f32),
            ((1, depth), f32),
            ((total, depth), bf16),
            ((8, channels), f32),
            ((head_rows, 128), f32),
            ((8, states), f32),
        ],
        [
            masks,
            *state_taps,
            ((span, span), f32),
            ((total, channels), f32),
            ((total, states), f32),
            ((total + pad, channels), f32),
            ((total + pad, states), f32),
            ((total, channels), bf16),
            ((total, states), bf16),
        ],
    )

    token_float = tokens.astype(f32)
    gain_full = small_full[: depth // states].reshape(1, depth)

    def lay(value):
        value = value.reshape(owners, -1)
        return jnp.pad(value, ((0, 0), (0, states - value.shape[1])))[:, None, :].astype(bf16)

    conv_state_owned = state_sums[:taps].reshape(taps, owners, -1).transpose(1, 0, 2)
    shared_part = jnp.concatenate(
        [
            state_part.reshape(owners, share, states),
            lay(gain_part),
            lay(conv_state_owned),
            lay(state_sums[taps]),
        ],
        axis=1,
    )
    shared_part = jnp.pad(shared_part, ((0, 0), (0, -shared_part.shape[1] % 8), (0, 0)))
    if fast:
        mixed_rows = tensor_scatter(partial_out.reshape((n_tensor, -1, depth)))
        grad_local = tensor_scatter(grad_normed.reshape((n_tensor, -1, depth)))
        by_tensor = shared_part.reshape((n_dp, n_tensor) + shared_part.shape[1:])
        shared_mine = ring_scatter(tensor_scatter(by_tensor.transpose(1, 0, 2, 3)))
        gate_out = ring_scatter(gate_msg)
        gate_grad, output_grad = gate_out[:tall], gate_out[tall:].T
        inner_grad = ring_scatter(inner_msg)
        step_chunks = step_part[:heads].reshape(heads, n_dp, tall).transpose(1, 0, 2)
        step_grad = ring_scatter(step_chunks).T
    else:
        mixed_rows = lax.psum_scatter(
            partial_out, "tensor", scatter_dimension=0, tiled=True
        ).astype(f32)
        grad_local = lax.psum_scatter(
            grad_normed, "tensor", scatter_dimension=0, tiled=True
        ).astype(f32)
        shared_mine = lax.psum_scatter(
            shared_part.astype(f32), ("dp", "tensor"), scatter_dimension=0, tiled=True
        )[0]
        both = gate_msg.astype(f32)
        gate_grad, output_grad, inner_grad = (
            lax.psum_scatter(part.reshape(depth, channels), "dp", scatter_dimension=0, tiled=True)
            for part in (both[:, :tall], both[:, tall:], inner_msg.astype(f32))
        )
        output_grad = output_grad.T
        step_grad = lax.psum_scatter(step_part[:heads].T, "dp", scatter_dimension=0, tiled=True)
    input_grad = jnp.stack([gate_grad, inner_grad], axis=1)
    block_out = (token_float + mixed_rows).astype(bf16)
    scale = lax.rsqrt(jnp.mean(token_float * token_float, axis=1, keepdims=True) + epsilon)
    grad_scaled = grad_local * gain_full
    along = jnp.sum(grad_scaled * token_float, axis=1, keepdims=True) / depth
    tokens_grad = (
        scale * grad_scaled
        - token_float * (scale * scale * scale * along)
        + cotangent.astype(f32)
    )
    state_grad = shared_mine[:share]
    pre_gain_grad = shared_mine[share, : depth // owners]
    conv_state_grad = shared_mine[share + 1, : taps * (states // owners)].reshape(taps, -1)
    conv_state_bias_grad = shared_mine[share + 2, : states // owners]

    head_part = jnp.pad(head_sums[:, :2].T, ((0, 0), (0, channels - head_rows)))
    sums = jnp.concatenate([inner_sums, norm_grad, head_part], axis=0)
    if fast:
        for other in dp_others(sums):
            sums = sums + other
    else:
        sums = lax.psum(sums, "dp")
    skip_grad = sums[taps + 1].reshape(heads, -1).sum(axis=1)
    return (
        block_out,
        tokens_grad,
        pre_gain_grad,
        input_grad,
        step_grad,
        state_grad,
        sums[:taps],
        sums[taps],
        conv_state_grad,
        conv_state_bias_grad,
        sums[9, :heads],
        sums[10, :heads],
        skip_grad,
        sums[8],
        output_grad,
    )


def solution(mesh):
    in_specs = (
        P(("dp", "tensor"), None),
        P("dp", None),
        P(("dp", "tensor"), None),
        P(("dp", "tensor")),
        P("dp", None, "tensor"),
        P("dp", "tensor"),
        P(("dp", "tensor"), None),
        P(None, "tensor"),
        P("tensor"),
        P(None, ("dp", "tensor")),
        P(("dp", "tensor")),
        P("tensor"),
        P("tensor"),
        P("tensor"),
        P("tensor"),
        P("tensor", "dp"),
    )
    out_specs = (
        P(("dp", "tensor"), None),
        P(("dp", "tensor"), None),
        P(("dp", "tensor")),
        P("dp", None, "tensor"),
        P("dp", "tensor"),
        P(("dp", "tensor"), None),
        P(None, "tensor"),
        P("tensor"),
        P(None, ("dp", "tensor")),
        P(("dp", "tensor")),
        P("tensor"),
        P("tensor"),
        P("tensor"),
        P("tensor"),
        P("tensor", "dp"),
    )
    return jax.shard_map(body, mesh=mesh, in_specs=in_specs, out_specs=out_specs, check_vma=False)
```

profile of v0, /device:TPU:0, one launch (start us, length us, event | category | flops | bytes accessed | tf_op | source)
XLA Modules:
  0.0 214.5 jit_solution(9305922710898319717)
XLA Ops:
  4.2 3.1 %collective-permute-start.14 = (bf16[48,256]{1,0:T(8,128)(2,1)S(1)}, bf16[48,256]{1,0:T(8,128)(2,1)S(1)}, u32[]{:S(2)}, u32[]{:S(2)}) collective-permute-start(bf16[48,256]{1,0:T(8,128)(2,1)S(1)} %pad_maximum_fusion.1), channel_id=1, source_target_pairs={{0,2},{1,3},{2,0},{3,1},{4,6},{5,7},{6,4},{7,5},{8,10},{9,11},{10,... | collective-permute-start | bytes 73736 | tf_op jit(solution)/shard_map/ppermute | solution.py:642
  7.3 1.8 collective-permute-done.14
  11.7 2.2 %collective-permute-start.16 = (bf16[176,1024]{1,0:T(8,128)(2,1)S(1)}, bf16[176,1024]{1,0:T(8,128)(2,1)S(1)}, u32[]{:S(2)}, u32[]{:S(2)}) collective-permute-start(bf16[176,1024]{1,0:T(8,128)(2,1)S(1)} %fusion.20.refs_4_), channel_id=1, source_target_pairs={{0,8},{8,16},{16,24},{24,28},{28,20},{20,12},{12,4},{4,0},{1,9},{9... | collective-permute-start | bytes 1081352 | tf_op jit(solution)/shard_map/ppermute | solution.py:598
  13.9 8.9 %collective-permute-done.16.refs_5_ = bf16[176,1024]{1,0:T(8,128)(2,1)S(1)} collective-permute-done((bf16[176,1024]{1,0:T(8,128)(2,1)S(1)}, bf16[176,1024]{1,0:T(8,128)(2,1)S(1)}, u32[]{:S(2)}, u32[]{:S(2)}) %collective-permute-start.16) | collective-permute-done | bytes 360480 | tf_op jit(solution)/shard_map/ppermute | solution.py:598
  22.8 1.8 collective-permute-start.18
  24.8 1.8 collective-permute-start.3
  28.1 6.0 %collective-permute-done.18.refs_7_ = bf16[176,1024]{1,0:T(8,128)(2,1)S(1)} collective-permute-done((bf16[176,1024]{1,0:T(8,128)(2,1)S(1)}, bf16[176,1024]{1,0:T(8,128)(2,1)S(1)}, u32[]{:S(2)}, u32[]{:S(2)}) %collective-permute-start.18) | collective-permute-done | bytes 360480 | tf_op jit(solution)/shard_map/ppermute | solution.py:598
  34.1 1.8 collective-permute-start.20
  36.9 1.8 collective-permute-start.4
  38.7 3.2 %collective-permute-done.4.refs_6_ = bf16[512,128]{1,0:T(8,128)(2,1)S(1)} collective-permute-done((bf16[512,128]{1,0:T(8,128)(2,1)S(1)}, bf16[512,128]{1,0:T(8,128)(2,1)S(1)}, u32[]{:S(2)}, u32[]{:S(2)}) %collective-permute-start.4) | collective-permute-done | bytes 131104 | tf_op jit(solution)/shard_map/ppermute | solution.py:598
  41.9 1.8 collective-permute-start.5
  47.4 2.9 %collective-permute-done.6.refs_8_ = bf16[512,128]{1,0:T(8,128)(2,1)S(1)} collective-permute-done((bf16[512,128]{1,0:T(8,128)(2,1)S(1)}, bf16[512,128]{1,0:T(8,128)(2,1)S(1)}, u32[]{:S(2)}, u32[]{:S(2)}) %collective-permute-start.6) | collective-permute-done | bytes 131104 | tf_op jit(solution)/shard_map/ppermute | solution.py:598
  53.4 3.3 %collective-permute-done.7.refs_9_ = bf16[512,128]{1,0:T(8,128)(2,1)S(1)} collective-permute-done((bf16[512,128]{1,0:T(8,128)(2,1)S(1)}, bf16[512,128]{1,0:T(8,128)(2,1)S(1)}, u32[]{:S(2)}, u32[]{:S(2)}) %collective-permute-start.7) | collective-permute-done | bytes 131104 | tf_op jit(solution)/shard_map/ppermute | solution.py:598
  64.3 11.3 %shard_map.271 = (bf16[512,1024]{1,0:T(8,128)(2,1)}, bf16[512,1024]{1,0:T(8,128)(2,1)}, bf16[1024,1024]{1,0:T(8,128)(2,1)}, bf16[1024,256]{1,0:T(8,128)(2,1)}, b...) custom-call(s32[12]{0:T(128)S(1)} %copy-done.17, ...), custom_call_target="tpu_custom_call" | custom-call | tf_op jit(solution)/shard_map/pallas_call | solution.py:566
  75.6 5.5 %shard_map.272 = (bf16[512,1024]{1,0:T(8,128)(2,1)}, bf16[512,1024]{1,0:T(8,128)(2,1)}, f32[512,512]{1,0:T(8,128)}, f32[8,512]{1,0:T(8,128)S(1)}) custom-call(s32[12]{0:T(128)S(1)} %copy-done.17, s32[1,4]{1,0:T(1,128)S(1)} %copy-done.11, bf16[128,1024]{1,0:T(8,128)(2,1)S(1)} %copy-done.1, bf16[128,1024]{1,0:T(8,128)(2,1)S(1)} %collective-permute-done.refs_1_, ...), custom_call_target="tpu_custom_call" | custom-call | tf_op jit(solution)/shard_map/pallas_call | solution.py:566
  84.1 2.0 collective-permute-done.24
  86.2 9.3 %shard_map.273 = (bf16[512,1024]{1,0:T(8,128)(2,1)S(1)}, bf16[8,256,512]{2,1,0:T(8,128)(2,1)}, bf16[512,512]{1,0:T(8,128)(2,1)S(1)}, f32[512,512]{1,0:T(8,128)}, f32[1,512]{1,0:T(1,128)S(1)}) custom-call(s32[1,4]{1,0:T(1,128)S(1)} %copy-done.12, f32[8,512]{1,0:T(8,128)S(1)} %add.478.refs_0_, f32[512,512]{1,0:T(8,128)} %get-tuple-element.46.refs_12_.refs_1_, ...), custom_call_target="tpu_custom_call" | custom-call | tf_op jit(solution)/shard_map/pallas_call | solution.py:566
  96.3 23.3 %shard_map.274 = (bf16[8,128,512]{2,1,0:T(8,128)(2,1)}, bf16[1024,256]{1,0:T(8,128)(2,1)S(1)}, f32[16,1024]{1,0:T(8,128)S(1)}, f32[1,1024]{1,0:T(1,128)S(1)}, bf...) custom-call(s32[1,4]{1,0:T(1,128)S(1)} %copy-done.12, ...), custom_call_target="tpu_custom_call" | custom-call | tf_op jit(solution)/shard_map/pallas_call | solution.py:566
  123.5 3.1 %collective-permute-start.61 = (f32[11,512]{1,0:T(8,128)}, f32[11,512]{1,0:T(8,128)S(1)}, u32[]{:S(2)}, u32[]{:S(2)}) collective-permute-start(f32[11,512]{1,0:T(8,128)} %select_maximum_fusion), channel_id=1, source_target_pairs={{0,12},{4,16},{8,20},{12,24},{16,28},{20,0},{24,4},{28,8},{1,13},{... | collective-permute-start | bytes 67592 | tf_op jit(solution)/shard_map/ppermute | solution.py:637
  126.7 2.0 collective-permute-start.56
  128.7 1.8 dynamic-slice_bitcast_fusion.4
  131.7 1.9 dynamic-slice_bitcast_fusion
  135.3 1.8 collective-permute-start.57
  142.6 1.9 collective-permute-start.62
  144.5 2.2 %collective-permute-start.63 = (f32[11,512]{1,0:T(8,128)}, f32[11,512]{1,0:T(8,128)S(1)}, u32[]{:S(2)}, u32[]{:S(2)}) collective-permute-start(f32[11,512]{1,0:T(8,128)} %select_maximum_fusion), channel_id=1, source_target_pairs={{0,20},{4,24},{8,28},{12,0},{16,4},{20,8},{24,12},{28,16},{1,21},{... | collective-permute-start | bytes 67592 | tf_op jit(solution)/shard_map/ppermute | solution.py:637
  162.3 2.2 %collective-permute-start.30 = (bf16[8,40,256]{2,1,0:T(8,128)(2,1)S(1)}, bf16[8,40,256]{2,1,0:T(8,128)(2,1)S(1)}, u32[]{:S(2)}, u32[]{:S(2)}) collective-permute-start(bf16[8,40,256]{2,1,0:T(8,128)(2,1)S(1)} %fusion.30), channel_id=1, source_target_pairs={{0,2},{1,3},{2,0},{3,1},{4,6},{5,7},{6,4},{7,5},{8,10},{9,11},{10,... | collective-permute-start | bytes 491528 | tf_op jit(solution)/shard_map/ppermute | solution.py:642
  169.7 2.1 collective-permute-done.47
  174.3 4.4 %collective-permute-done.31 = bf16[40,256]{1,0:T(8,128)(2,1)S(1)} collective-permute-done((bf16[40,256]{1,0:T(8,128)(2,1)S(1)}, bf16[40,256]{1,0:T(8,128)(2,1)S(1)}, u32[]{:S(2)}, u32[]{:S(2)}) %collective-permute-start.31) | collective-permute-done | bytes 20512 | tf_op jit(solution)/shard_map/ppermute | solution.py:598
  181.9 2.0 fusion.16
  193.2 2.0 collective-permute-start.26
  197.4 1.8 collective-permute-done.34
  207.3 3.0 %collective-permute-done.41 = bf16[256,512]{1,0:T(8,128)(2,1)S(1)} collective-permute-done((bf16[256,512]{1,0:T(8,128)(2,1)S(1)}, bf16[256,512]{1,0:T(8,128)(2,1)S(1)}, u32[]{:S(2)}, u32[]{:S(2)}) %collective-permute-start.41) | collective-permute-done | bytes 262176 | tf_op jit(solution)/shard_map/ppermute | solution.py:598
  (270 shorter events, 89.3 us)
Async XLA Ops:
  11.7 11.0 %collective-permute-start.16 = (bf16[176,1024]{1,0:T(8,128)(2,1)S(1)}, bf16[176,1024]{1,0:T(8,128)(2,1)S(1)}, u32[]{:S(2)}, u32[]{:S(2)}) collective-permute-start(bf16[176,1024]{1,0:T(8,128)(2,1)S(1)} %fusion.20.refs_4_), channel_id=1, source_target_pairs={{0,8},{8,16},{16,24},{24,28},{28,20},{20,12},{12,4},{4,0},{1,9},{9... | collective-permute-start | bytes 1081352 | tf_op jit(solution)/shard_map/ppermute | solution.py:598
  13.9 10.7 %collective-permute-start.17 = (bf16[176,1024]{1,0:T(8,128)(2,1)S(1)}, bf16[176,1024]{1,0:T(8,128)(2,1)S(1)}, u32[]{:S(2)}, u32[]{:S(2)}) collective-permute-start(bf16[176,1024]{1,0:T(8,128)(2,1)S(1)} %fusion.20.refs_4_), channel_id=1, source_target_pairs={{0,4},{8,0},{16,8},{24,16},{28,24},{20,28},{12,20},{4,12},{1,5},{9... | collective-permute-start | bytes 1081352 | tf_op jit(solution)/shard_map/ppermute | solution.py:598
  22.8 11.3 %collective-permute-start.18 = (bf16[176,1024]{1,0:T(8,128)(2,1)S(1)}, bf16[176,1024]{1,0:T(8,128)(2,1)S(1)}, u32[]{:S(2)}, u32[]{:S(2)}) collective-permute-start(bf16[176,1024]{1,0:T(8,128)(2,1)S(1)} %collective-permute-done.16.refs_5_), channel_id=1, source_target_pairs={{0,8},{8,16},{16,24},{24,28},{28,20},{20,12},{12,4},{4,0},{1,9},{9... | collective-permute-start | bytes 1081352 | tf_op jit(solution)/shard_map/ppermute | solution.py:598
  24.6 21.1 %collective-permute-start.19 = (bf16[176,1024]{1,0:T(8,128)(2,1)S(1)}, bf16[176,1024]{1,0:T(8,128)(2,1)S(1)}, u32[]{:S(2)}, u32[]{:S(2)}) collective-permute-start(bf16[176,1024]{1,0:T(8,128)(2,1)S(1)} %collective-permute-done.17.refs_6_), channel_id=1, source_target_pairs={{0,4},{8,0},{16,8},{24,16},{28,24},{20,28},{12,20},{4,12},{1,5},{9... | collective-permute-start | bytes 1081352 | tf_op jit(solution)/shard_map/ppermute | solution.py:598
  24.8 12.1 %collective-permute-start.3 = (bf16[512,128]{1,0:T(8,128)(2,1)S(1)}, bf16[512,128]{1,0:T(8,128)(2,1)S(1)}, u32[]{:S(2)}, u32[]{:S(2)}) collective-permute-start(bf16[512,128]{1,0:T(8,128)(2,1)S(1)} %copy-done.4), channel_id=1, source_target_pairs={{0,8},{8,16},{16,24},{24,28},{28,20},{20,12},{12,4},{4,0},{1,9},{9... | collective-permute-start | bytes 393224 | tf_op jit(solution)/shard_map/ppermute | solution.py:598
  26.6 17.1 %collective-permute-start.11 = (bf16[128,1024]{1,0:T(8,128)(2,1)S(1)}, bf16[128,1024]{1,0:T(8,128)(2,1)S(1)}, u32[]{:S(2)}, u32[]{:S(2)}) collective-permute-start(bf16[128,1024]{1,0:T(8,128)(2,1)S(1)} %copy-done), channel_id=1, source_target_pairs={{0,2},{1,3},{2,0},{3,1},{4,6},{5,7},{6,4},{7,5},{8,10},{9,11},{10,... | collective-permute-start | bytes 786440 | tf_op jit(solution)/shard_map/ppermute | solution.py:642
  28.1 17.1 %collective-permute-start.10 = (bf16[128,1024]{1,0:T(8,128)(2,1)S(1)}, bf16[128,1024]{1,0:T(8,128)(2,1)S(1)}, u32[]{:S(2)}, u32[]{:S(2)}) collective-permute-start(bf16[128,1024]{1,0:T(8,128)(2,1)S(1)} %copy-done), channel_id=1, source_target_pairs={{0,1},{1,0},{2,3},{3,2},{4,5},{5,4},{6,7},{7,6},{8,9},{9,8},{10,11... | collective-permute-start | bytes 786440 | tf_op jit(solution)/shard_map/ppermute | solution.py:642
  34.1 17.8 %collective-permute-start.20 = (bf16[176,1024]{1,0:T(8,128)(2,1)S(1)}, bf16[176,1024]{1,0:T(8,128)(2,1)}, u32[]{:S(2)}, u32[]{:S(2)}) collective-permute-start(bf16[176,1024]{1,0:T(8,128)(2,1)S(1)} %collective-permute-done.18.refs_7_), channel_id=1, source_target_pairs={{0,8},{8,16},{16,24},{24,28},{28,20},{20,12},{12,4},{4,0},{1,9},{9... | collective-permute-start | bytes 1081352 | tf_op jit(solution)/shard_map/ppermute | solution.py:598
  43.7 9.8 %collective-permute-start.1 = (bf16[128,1024]{1,0:T(8,128)(2,1)S(1)}, bf16[128,1024]{1,0:T(8,128)(2,1)S(1)}, u32[]{:S(2)}, u32[]{:S(2)}) collective-permute-start(bf16[128,1024]{1,0:T(8,128)(2,1)S(1)} %copy-done.1), channel_id=1, source_target_pairs={{0,2},{1,3},{2,0},{3,1},{4,6},{5,7},{6,4},{7,5},{8,10},{9,11},{10,... | collective-permute-start | bytes 786440 | tf_op jit(solution)/shard_map/ppermute | solution.py:642
  45.6 11.6 %collective-permute-start.21 = (bf16[176,1024]{1,0:T(8,128)(2,1)S(1)}, bf16[176,1024]{1,0:T(8,128)(2,1)S(1)}, u32[]{:S(2)}, u32[]{:S(2)}) collective-permute-start(bf16[176,1024]{1,0:T(8,128)(2,1)S(1)} %collective-permute-done.19.refs_8_), channel_id=1, source_target_pairs={{0,4},{8,0},{16,8},{24,16},{28,24},{20,28},{12,20},{4,12},{1,5},{9... | collective-permute-start | bytes 1081352 | tf_op jit(solution)/shard_map/ppermute | solution.py:598
  47.4 9.4 %collective-permute-start.12 = (bf16[128,1024]{1,0:T(8,128)(2,1)S(1)}, bf16[128,1024]{1,0:T(8,128)(2,1)S(1)}, u32[]{:S(2)}, u32[]{:S(2)}) collective-permute-start(bf16[128,1024]{1,0:T(8,128)(2,1)S(1)} %collective-permute-done.11.refs_2_), channel_id=1, source_target_pairs={{0,1},{1,0},{2,3},{3,2},{4,5},{5,4},{6,7},{7,6},{8,9},{9,8},{10,11... | collective-permute-start | bytes 786440 | tf_op jit(solution)/shard_map/ppermute | solution.py:642
  51.9 9.8 %collective-permute-start.22 = (bf16[176,1024]{1,0:T(8,128)(2,1)}, bf16[176,1024]{1,0:T(8,128)(2,1)}, u32[]{:S(2)}, u32[]{:S(2)}) collective-permute-start(bf16[176,1024]{1,0:T(8,128)(2,1)} %collective-permute-done.20.refs_9_), channel_id=1, source_target_pairs={{0,8},{8,16},{16,24},{24,28},{28,20},{20,12},{12,4},{4,0},{1,9},{9... | collective-permute-start | bytes 1081352 | tf_op jit(solution)/shard_map/ppermute | solution.py:598
  53.4 22.1 %collective-permute-start = (bf16[128,1024]{1,0:T(8,128)(2,1)S(1)}, bf16[128,1024]{1,0:T(8,128)(2,1)S(1)}, u32[]{:S(2)}, u32[]{:S(2)}) collective-permute-start(bf16[128,1024]{1,0:T(8,128)(2,1)S(1)} %copy-done.1), channel_id=1, source_target_pairs={{0,1},{1,0},{2,3},{3,2},{4,5},{5,4},{6,7},{7,6},{8,9},{9,8},{10,11... | collective-permute-start | bytes 786440 | tf_op jit(solution)/shard_map/ppermute | solution.py:642
  56.7 18.9 %collective-permute-start.2 = (bf16[128,1024]{1,0:T(8,128)(2,1)S(1)}, bf16[128,1024]{1,0:T(8,128)(2,1)}, u32[]{:S(2)}, u32[]{:S(2)}) collective-permute-start(bf16[128,1024]{1,0:T(8,128)(2,1)S(1)} %collective-permute-done.1.refs_2_), channel_id=1, source_target_pairs={{0,1},{1,0},{2,3},{3,2},{4,5},{5,4},{6,7},{7,6},{8,9},{9,8},{10,11... | collective-permute-start | bytes 786440 | tf_op jit(solution)/shard_map/ppermute | solution.py:642
  56.7 18.8 %collective-permute-start.8 = (bf16[512,128]{1,0:T(8,128)(2,1)S(1)}, bf16[512,128]{1,0:T(8,128)(2,1)S(1)}, u32[]{:S(2)}, u32[]{:S(2)}) collective-permute-start(bf16[512,128]{1,0:T(8,128)(2,1)S(1)} %collective-permute-done.6.refs_8_), channel_id=1, source_target_pairs={{0,4},{8,0},{16,8},{24,16},{28,24},{20,28},{12,20},{4,12},{1,5},{9... | collective-permute-start | bytes 393224 | tf_op jit(solution)/shard_map/ppermute | solution.py:598
  58.0 17.6 %collective-permute-start.9 = (bf16[512,128]{1,0:T(8,128)(2,1)S(1)}, bf16[512,128]{1,0:T(8,128)(2,1)S(1)}, u32[]{:S(2)}, u32[]{:S(2)}) collective-permute-start(bf16[512,128]{1,0:T(8,128)(2,1)S(1)} %collective-permute-done.7.refs_9_), channel_id=1, source_target_pairs={{0,8},{8,16},{16,24},{24,28},{28,20},{20,12},{12,4},{4,0},{1,9},{9... | collective-permute-start | bytes 393224 | tf_op jit(solution)/shard_map/ppermute | solution.py:598
  120.3 26.4 %collective-permute-start.59 = (f32[11,512]{1,0:T(8,128)}, f32[11,512]{1,0:T(8,128)S(1)}, u32[]{:S(2)}, u32[]{:S(2)}) collective-permute-start(f32[11,512]{1,0:T(8,128)} %select_maximum_fusion), channel_id=1, source_target_pairs={{0,4},{4,8},{8,12},{12,16},{16,20},{20,24},{24,28},{28,0},{1,5},{5... | collective-permute-start | bytes 67592 | tf_op jit(solution)/shard_map/ppermute | solution.py:637
  122.0 26.1 %collective-permute-start.60 = (f32[11,512]{1,0:T(8,128)}, f32[11,512]{1,0:T(8,128)S(1)}, u32[]{:S(2)}, u32[]{:S(2)}) collective-permute-start(f32[11,512]{1,0:T(8,128)} %select_maximum_fusion), channel_id=1, source_target_pairs={{0,8},{4,12},{8,16},{12,20},{16,24},{20,28},{24,0},{28,4},{1,9},{5... | collective-permute-start | bytes 67592 | tf_op jit(solution)/shard_map/ppermute | solution.py:637
  123.5 26.1 %collective-permute-start.61 = (f32[11,512]{1,0:T(8,128)}, f32[11,512]{1,0:T(8,128)S(1)}, u32[]{:S(2)}, u32[]{:S(2)}) collective-permute-start(f32[11,512]{1,0:T(8,128)} %select_maximum_fusion), channel_id=1, source_target_pairs={{0,12},{4,16},{8,20},{12,24},{16,28},{20,0},{24,4},{28,8},{1,13},{... | collective-permute-start | bytes 67592 | tf_op jit(solution)/shard_map/ppermute | solution.py:637
  142.6 7.9 %collective-permute-start.62 = (f32[11,512]{1,0:T(8,128)}, f32[11,512]{1,0:T(8,128)S(1)}, u32[]{:S(2)}, u32[]{:S(2)}) collective-permute-start(f32[11,512]{1,0:T(8,128)} %select_maximum_fusion), channel_id=1, source_target_pairs={{0,16},{4,20},{8,24},{12,28},{16,0},{20,4},{24,8},{28,12},{1,17},{... | collective-permute-start | bytes 67592 | tf_op jit(solution)/shard_map/ppermute | solution.py:637
  144.5 7.1 %collective-permute-start.63 = (f32[11,512]{1,0:T(8,128)}, f32[11,512]{1,0:T(8,128)S(1)}, u32[]{:S(2)}, u32[]{:S(2)}) collective-permute-start(f32[11,512]{1,0:T(8,128)} %select_maximum_fusion), channel_id=1, source_target_pairs={{0,20},{4,24},{8,28},{12,0},{16,4},{20,8},{24,12},{28,16},{1,21},{... | collective-permute-start | bytes 67592 | tf_op jit(solution)/shard_map/ppermute | solution.py:637
  149.6 8.9 %collective-permute-start.38 = (bf16[256,512]{1,0:T(8,128)(2,1)}, bf16[256,512]{1,0:T(8,128)(2,1)}, u32[]{:S(2)}, u32[]{:S(2)}) collective-permute-start(bf16[256,512]{1,0:T(8,128)(2,1)} %get-tuple-element.143), channel_id=1, source_target_pairs={{0,8},{8,16},{16,24},{24,28},{28,20},{20,12},{12,4},{4,0},{1,9},{9... | collective-permute-start | bytes 786440 | tf_op jit(solution)/shard_map/ppermute | solution.py:598
  150.6 29.1 %collective-permute-start.42 = (bf16[256,512]{1,0:T(8,128)(2,1)S(1)}, bf16[256,512]{1,0:T(8,128)(2,1)}, u32[]{:S(2)}, u32[]{:S(2)}) collective-permute-start(bf16[256,512]{1,0:T(8,128)(2,1)S(1)} %get-tuple-element.144), channel_id=1, source_target_pairs={{0,4},{8,0},{16,8},{24,16},{28,24},{20,28},{12,20},{4,12},{1,5},{9... | collective-permute-start | bytes 786440 | tf_op jit(solution)/shard_map/ppermute | solution.py:598
  152.7 9.7 %collective-permute-start.49 = (bf16[128,512]{1,0:T(8,128)(2,1)}, bf16[128,512]{1,0:T(8,128)(2,1)}, u32[]{:S(2)}, u32[]{:S(2)}) collective-permute-start(bf16[128,512]{1,0:T(8,128)(2,1)} %get-tuple-element.150), channel_id=1, source_target_pairs={{0,4},{8,0},{16,8},{24,16},{28,24},{20,28},{12,20},{4,12},{1,5},{9... | collective-permute-start | bytes 393224 | tf_op jit(solution)/shard_map/ppermute | solution.py:598
  157.6 26.3 %collective-permute-start.25 = (bf16[2,128,1024]{2,1,0:T(8,128)(2,1)S(1)}, bf16[2,128,1024]{2,1,0:T(8,128)(2,1)S(1)}, u32[]{:S(2)}, u32[]{:S(2)}) collective-permute-start(bf16[2,128,1024]{2,1,0:T(8,128)(2,1)S(1)} %dynamic-slice_bitcast_fusion.1), channel_id=1, source_target_pairs={{0,1},{1,0},{2,3},{3,2},{4,5},{5,4},{6,7},{7,6},{8,9},{9,8},{10,11... | collective-permute-start | bytes 1572872 | tf_op jit(solution)/shard_map/ppermute | solution.py:642
  158.6 26.5 %collective-permute-start.27 = (bf16[2,128,1024]{2,1,0:T(8,128)(2,1)}, bf16[2,128,1024]{2,1,0:T(8,128)(2,1)S(1)}, u32[]{:S(2)}, u32[]{:S(2)}) collective-permute-start(bf16[2,128,1024]{2,1,0:T(8,128)(2,1)} %dynamic-slice_bitcast_fusion), channel_id=1, source_target_pairs={{0,1},{1,0},{2,3},{3,2},{4,5},{5,4},{6,7},{7,6},{8,9},{9,8},{10,11... | collective-permute-start | bytes 1572872 | tf_op jit(solution)/shard_map/ppermute | solution.py:642
  171.8 9.0 %collective-permute-start.39 = (bf16[256,512]{1,0:T(8,128)(2,1)S(1)}, bf16[256,512]{1,0:T(8,128)(2,1)S(1)}, u32[]{:S(2)}, u32[]{:S(2)}) collective-permute-start(bf16[256,512]{1,0:T(8,128)(2,1)S(1)} %fusion.17), channel_id=1, source_target_pairs={{0,8},{8,16},{16,24},{24,28},{28,20},{20,12},{12,4},{4,0},{1,9},{9... | collective-permute-start | bytes 786440 | tf_op jit(solution)/shard_map/ppermute | solution.py:598
  178.7 16.6 %collective-permute-start.48 = (bf16[128,512]{1,0:T(8,128)(2,1)S(1)}, bf16[128,512]{1,0:T(8,128)(2,1)S(1)}, u32[]{:S(2)}, u32[]{:S(2)}) collective-permute-start(bf16[128,512]{1,0:T(8,128)(2,1)S(1)} %get-tuple-element.145), channel_id=1, source_target_pairs={{0,8},{8,16},{16,24},{24,28},{28,20},{20,12},{12,4},{4,0},{1,9},{9... | collective-permute-start | bytes 393224 | tf_op jit(solution)/shard_map/ppermute | solution.py:598
  179.7 16.5 %collective-permute-start.51 = (bf16[128,512]{1,0:T(8,128)(2,1)S(1)}, bf16[128,512]{1,0:T(8,128)(2,1)S(1)}, u32[]{:S(2)}, u32[]{:S(2)}) collective-permute-start(bf16[128,512]{1,0:T(8,128)(2,1)S(1)} %get-tuple-element.146), channel_id=1, source_target_pairs={{0,4},{8,0},{16,8},{24,16},{28,24},{20,28},{12,20},{4,12},{1,5},{9... | collective-permute-start | bytes 393224 | tf_op jit(solution)/shard_map/ppermute | solution.py:598
  185.0 17.5 %collective-permute-start.40 = (bf16[256,512]{1,0:T(8,128)(2,1)}, bf16[256,512]{1,0:T(8,128)(2,1)}, u32[]{:S(2)}, u32[]{:S(2)}) collective-permute-start(bf16[256,512]{1,0:T(8,128)(2,1)} %get-tuple-element.141), channel_id=1, source_target_pairs={{0,8},{8,16},{16,24},{24,28},{28,20},{20,12},{12,4},{4,0},{1,9},{9... | collective-permute-start | bytes 786440 | tf_op jit(solution)/shard_map/ppermute | solution.py:598
  191.9 10.6 %collective-permute-start.43 = (bf16[256,512]{1,0:T(8,128)(2,1)}, bf16[256,512]{1,0:T(8,128)(2,1)}, u32[]{:S(2)}, u32[]{:S(2)}) collective-permute-start(bf16[256,512]{1,0:T(8,128)(2,1)} %get-tuple-element.142), channel_id=1, source_target_pairs={{0,4},{8,0},{16,8},{24,16},{28,24},{20,28},{12,20},{4,12},{1,5},{9... | collective-permute-start | bytes 786440 | tf_op jit(solution)/shard_map/ppermute | solution.py:598
  193.2 12.9 %collective-permute-start.26 = (bf16[128,1024]{1,0:T(8,128)(2,1)}, bf16[128,1024]{1,0:T(8,128)(2,1)S(1)}, u32[]{:S(2)}, u32[]{:S(2)}) collective-permute-start(bf16[128,1024]{1,0:T(8,128)(2,1)} %fusion.21), channel_id=1, source_target_pairs={{0,2},{1,3},{2,0},{3,1},{4,6},{5,7},{6,4},{7,5},{8,10},{9,11},{10,... | collective-permute-start | bytes 786440 | tf_op jit(solution)/shard_map/ppermute | solution.py:642
  (69 other events, 848.7 us)
where the time goes:
time: 215 us
  starting transfers between devices  71.2 us (33%)
  waiting for transfers between devices  52.7 us (25%)
  Pallas kernels  49.4 us (23%)
  local copies, waits for them, and re-layouts  23.2 us (11%)
  other arithmetic  16.6 us (8%)
    pallas_call x4, Pallas kernels, call(): pl.pallas_call(kernel, out_shape=[jax.ShapeDtypeStruct(shape, kind) for s...  49.4 us
    ppermute x42, waiting for transfers between devices, ring_send(): return lax.ppermute(value, 'dp', pairs)  46.7 us
    ppermute x42, starting transfers between devices, ring_send(): return lax.ppermute(value, 'dp', pairs)  46.5 us
    ppermute x7, starting transfers between devices, dp_others(): got.append(lax.ppermute(value, 'dp', pairs))  12.6 us
    ppermute x17, starting transfers between devices, tensor_swap(): return lax.ppermute(value, 'tensor', [(i, i ^ bit) for i in range(4)])  12.1 us
    unnamed x76, local copies, waits for them, and re-layouts  7.98 us
    convert_element_type x12, other arithmetic, ring_scatter(): got = ring_send(held.astype(bf16), forward).astype(f32)  6.48 us
    ppermute x17, waiting for transfers between devices, tensor_swap(): return lax.ppermute(value, 'tensor', [(i, i ^ bit) for i in range(4)])  5.97 us
  transfers between devices with their start and end apart: 66, of which 25 were waited for; matrix products, arithmetic and copies ran while one was open for 13% of the time, Pallas kernels for 5%

commit v1 on v0

--- a/solution.py
+++ b/solution.py
@@ -15,7 +15,7 @@
 pad = 8
 head_rows = 16
 head_width = 64
-vmem_bytes = 52 * 1024 * 1024
+vmem_bytes = 32 * 1024 * 1024
 
 
 def mm(a, b, over=(1, 0)):
@@ -152,7 +152,6 @@
         state_weight_ref,
         step_weight_ref,
         small_ref,
-        gate_ref,
         raw_ref,
         state_raw_ref,
         step_col_ref,
@@ -160,10 +159,10 @@
         act_ref,
         state_ref,
         mixed_ref,
-    ) = refs[7:21]
-    mask_ref, state_taps_ref, state_bias_ref = refs[21:]
+    ) = refs[7:20]
+    mask_ref, state_taps_ref, state_bias_ref = refs[20:]
     total = rows_ref.shape[0]
-    channels = gate_ref.shape[1]
+    channels = act_ref.shape[1]
     ends = ends_of(lengths_ref)
 
     if fast:
@@ -176,11 +175,12 @@
             at = pl.multiple_of(index * depth_part, depth_part)
             weight_ref[pl.ds(at, depth_part), :] = msg[:depth_part, :]
             for member in range(4):
-                inner = pl.multiple_of(at + place_ref[member] * share, share)
+                inner = pl.multiple_of(at + member * share, share)
+                high, low = depth_part + share * (member // 2), 256 * (member % 2)
                 state_weight_ref[pl.ds(inner, share), :] = msg[
-                    depth_part : depth_part + share, 256 * member : 256 * (member + 1)
+                    high : high + share, low : low + 256
                 ]
-            tail = depth_part + share
+            tail = depth_part + 2 * share
             small = small + msg[tail : tail + 16, :256].astype(f32)
             step_weight_ref[:, pl.ds(at, depth_part)] = msg[tail : tail + 16, 256:384]
         small_ref[...] = small
@@ -197,9 +197,9 @@
     tall = total // n_rows
     for member in range(n_rows):
         at = pl.multiple_of(place_ref[member] * tall, tall) if fast else 0
-        own = row_refs[member]
-        rows_ref[pl.ds(at, tall), :] = own[...]
-        value = own[...].astype(f32)
+        own = row_refs[member][:tall, :]
+        rows_ref[pl.ds(at, tall), :] = own
+        value = own.astype(f32)
         scale = lax.rsqrt(jnp.mean(value * value, axis=1, keepdims=True) + epsilon)
         normed_ref[pl.ds(at, tall), :] = (value * scale * gain).astype(bf16)
 
@@ -208,9 +208,7 @@
 
     def project(at):
         part = normed_ref[pl.ds(at, 128), :]
-        both = mm(part, weight_ref[...])
-        gate_ref[pl.ds(at, 128), :] = both[:, :channels]
-        raw_ref[pl.ds(at + pad, 128), :] = both[:, channels:]
+        raw_ref[pl.ds(at + pad, 128), :] = mm(part, weight_ref[...])
         state_raw_ref[pl.ds(at + pad, 128), :] = mm(part, state_weight_ref[...])
         step_col_ref[pl.ds(at, 128), :] = mm(part, step_weight_ref[...], (1, 1))
 
@@ -262,28 +260,32 @@
 
 def grad_in_kernel(fast, place_ref, lengths_ref, *refs):
     n_rows = 4 if fast else 1
-    n_msg = 8 if fast else 1
-    row_refs, out_refs, refs = refs[:n_rows], refs[n_rows : n_rows + n_msg], refs[n_rows + n_msg :]
-    gate_ref, mixed_ref, norm_ref, rows_ref, weight_ref, grad_ref, sums_ref, wide_ref = refs
+    n_msg = 8 if fast else 2
+    row_refs, msg_refs, refs = refs[:n_rows], refs[n_rows : n_rows + n_msg], refs[n_rows + n_msg :]
+    normed_ref, mixed_ref, norm_ref = refs[:3]
+    rows_ref, gate_weight_ref, out_weight_ref, gate_ref, grad_ref, sums_ref, wide_ref = refs[3:]
     total = rows_ref.shape[0]
     ends = ends_of(lengths_ref)
     tall = total // n_rows
     for member in range(n_rows):
         at = pl.multiple_of(place_ref[member] * tall, tall) if fast else 0
-        rows_ref[pl.ds(at, tall), :] = row_refs[member][...]
+        rows_ref[pl.ds(at, tall), :] = row_refs[member][-tall:, :]
     if fast:
         for slot in range(8):
             at = pl.multiple_of(place_ref[4 + slot] * 128, 128)
-            weight_ref[:, pl.ds(at, 128)] = out_refs[slot][...]
+            gate_weight_ref[pl.ds(at, 128), :] = msg_refs[slot][:128, :]
+            out_weight_ref[pl.ds(at, 128), :] = msg_refs[slot][128:, :]
     else:
-        weight_ref[...] = out_refs[0][...]
+        gate_weight_ref[...] = msg_refs[0][...]
+        out_weight_ref[...] = msg_refs[1][...]
 
     def part(at):
         rows = pl.ds(at, 128)
         valid = jnp.where(iota((128, 1), 0) + at < ends[-1], 1.0, 0.0)
-        grad = mm(rows_ref[rows, :], weight_ref[...], (1, 1)) * valid
+        grad = mm(rows_ref[rows, :], out_weight_ref[...]) * valid
         grad_ref[rows, :] = grad
-        gate = gate_ref[rows, :]
+        gate = mm(normed_ref[rows, :], gate_weight_ref[...])
+        gate_ref[rows, :] = gate
         gated = mixed_ref[rows, :] * (gate * sigmoid(gate))
         square = jnp.sum(gated * gated, axis=1, keepdims=True)
         cross = jnp.sum(grad * norm_ref[...] * gated, axis=1, keepdims=True)
@@ -325,7 +327,7 @@
         grad_mixed_ref[rows, :] = grad_gated * gate_act
         grad_gate = grad_gated * mixed * sig * (1.0 + gate * (1.0 - sig))
         grad_gate_ref[rows, :] = grad_gate.astype(bf16)
-        partial_ref[rows, :] = mm(out_rows_ref[rows, :], weight_ref[...]).astype(bf16)
+        partial_ref[rows, :] = mm(out_rows_ref[rows, :], weight_ref[...], (1, 1)).astype(bf16)
 
     row_loop(total, 128, part)
 
@@ -355,10 +357,12 @@
         grad_gate_ref,
         normed_ref,
         rows_ref,
+        gate_weight_ref,
         weight_ref,
         state_weight_ref,
         step_weight_ref,
         small_ref,
+        norm_grad_ref,
         taps_ref,
         bias_ref,
         step_bias_ref,
@@ -366,17 +370,15 @@
         log_ref,
         log_col_ref,
         skip_ref,
-    ) = refs[:21]
+    ) = refs[:23]
     (
         msg_ref,
         state_part_ref,
-        step_part_ref,
         gain_part_ref,
         grad_normed_ref,
         inner_sums_ref,
-        head_sums_ref,
         state_sums_ref,
-    ) = refs[21:29]
+    ) = refs[23:29]
     (
         mask_ref,
         state_taps_ref,
@@ -487,7 +489,8 @@
     decay_sum = jnp.sum(rate_grad * rate_row, axis=1, keepdims=True)
     bias_sum = jnp.sum(step_grad, axis=1, keepdims=True)
     lane = iota((head_rows, 128), 1)
-    head_sums_ref[...] = jnp.where(lane == 0, bias_sum, jnp.where(lane == 1, decay_sum, 0.0))
+    head_sums = jnp.where(lane == 0, bias_sum, jnp.where(lane == 1, decay_sum, 0.0))
+    head_sums = jnp.concatenate([head_sums] * (128 // head_rows), axis=0).T
     step_grad_low = step_grad.astype(bf16)
 
     def conv_back(x_ref, grad_ref, held_ref, out_ref, sums_ref, own_taps, own_bias, skips):
@@ -520,6 +523,8 @@
         column_loop(out_ref.shape[1], column)
 
     inner_sums_ref[...] = jnp.zeros(inner_sums_ref.shape, f32)
+    inner_sums_ref[6:7, :] = norm_grad_ref[...]
+    inner_sums_ref[8:10, :128] = head_sums[:2, :]
     state_sums_ref[...] = jnp.zeros(state_sums_ref.shape, f32)
     conv_back(
         raw_ref, grad_act_ref, pre_ref, grad_inner_ref, inner_sums_ref, taps_ref, bias_ref, True
@@ -535,23 +540,24 @@
         False,
     )
 
-    chunks, tall = msg_ref.shape[0], msg_ref.shape[1]
+    chunks, tall = msg_ref.shape[0], msg_ref.shape[1] - head_rows
+    msg_ref[...] = jnp.zeros(msg_ref.shape, bf16)
 
     def chunk(c, carry):
         at = pl.multiple_of(c * tall, tall)
         part = normed_ref[:, pl.ds(at, tall)]
-        msg_ref[c] = mm(part, grad_inner_ref[...], (0, 0)).astype(bf16)
+        msg_ref[c, :tall, :] = mm(part, grad_inner_ref[...], (0, 0)).astype(bf16)
+        msg_ref[c, tall:, :tall] = mm(step_grad_low, part).astype(bf16)
         state_part_ref[pl.ds(at, tall), :] = mm(part, grad_state_low_ref[...], (0, 0)).astype(bf16)
         return carry
 
     lax.fori_loop(0, chunks, chunk, 0)
-    step_part_ref[...] = mm(step_grad_low, normed_ref[...])
     step_back = step_grad.T.astype(bf16)
     gain_part_ref[...] = jnp.zeros(gain_part_ref.shape, f32)
     for at in range(0, total, 128):
         rows = slice(at, at + 128)
-        grad = mm(grad_gate_ref[rows, :], weight_ref[:, :channels], (1, 1))
-        grad = grad + mm(grad_inner_ref[rows, :], weight_ref[:, channels:], (1, 1))
+        grad = mm(grad_gate_ref[rows, :], gate_weight_ref[...], (1, 1))
+        grad = grad + mm(grad_inner_ref[rows, :], weight_ref[...], (1, 1))
         grad = grad + mm(grad_state_low_ref[rows, :], state_weight_ref[...], (1, 1))
         grad = grad + mm(step_back[rows, :], step_weight_ref[...])
         grad_normed_ref[rows, :] = grad.astype(bf16)
@@ -560,7 +566,7 @@
         gain_part_ref[...] += jnp.sum(grad * (value * scale), axis=0, keepdims=True)
 
 
-def call(kernel, scalars, arrays, outs, scratch):
+def call(kernel, micros, scalars, arrays, outs, scratch):
     smem = pl.BlockSpec(memory_space=pltpu.SMEM)
     vmem = pl.BlockSpec(memory_space=pltpu.VMEM)
     return pl.pallas_call(
@@ -570,6 +576,9 @@
         out_specs=[vmem] * len(outs),
         scratch_shapes=[pltpu.VMEM(shape, kind) for shape, kind in scratch],
         compiler_params=pltpu.CompilerParams(vmem_limit_bytes=vmem_bytes),
+        cost_estimate=pl.CostEstimate(
+            flops=int(micros * 1.1e9), bytes_accessed=1 << 20, transcendentals=0
+        ),
     )(*scalars, *arrays)
 
 
@@ -628,14 +637,6 @@
             else:
                 total = total + got
     return total
-
-
-def dp_others(value):
-    got = []
-    for shift in range(1, 8):
-        pairs = [(i, (i + shift) % 8) for i in range(8)]
-        got.append(lax.ppermute(value, "dp", pairs))
-    return got
 
 
 def tensor_swap(value, bit):
@@ -709,30 +710,38 @@
     )
     small = jnp.pad(small, ((0, 16 - small.shape[0]), (0, 0)))
     step_rows = jnp.pad(step_weight.T, ((0, head_rows - heads), (0, 0)))
-    input_flat = input_weight.reshape(input_weight.shape[0], -1)
+    gate_weight, inner_weight = input_weight[:, 0], input_weight[:, 1]
     if fast:
-        shared = tensor_gather(jnp.concatenate([state_weight, small], axis=0))
-        beside = jnp.concatenate([piece[:share] for piece in shared], axis=1)
-        small = shared[0][share:] + shared[1][share:] + shared[2][share:] + shared[3][share:]
+        late = ring_gather(jnp.concatenate([gate_weight, output_weight.T], axis=0))
+        shared = jnp.concatenate([state_weight, small], axis=0)
+        shared = lax.all_to_all(
+            jnp.broadcast_to(shared, (4,) + shared.shape), "tensor", 0, 0, tiled=True
+        )
+        small = shared[0, share:] + shared[1, share:] + shared[2, share:] + shared[3, share:]
         tail = jnp.concatenate([small, step_rows], axis=1)
-        tail = jnp.pad(tail, ((0, 0), (0, depth - tail.shape[1])))
-        msg = ring_gather(jnp.concatenate([input_flat, beside, tail], axis=0))
-        out_msg = ring_gather(output_weight)
-        row_pieces = tensor_gather(tokens)
-        grad_pieces = tensor_gather(cotangent)
+        tail = jnp.pad(tail, ((0, 0), (0, channels - tail.shape[1])))
+        beside = [
+            jnp.concatenate([shared[i, :share], shared[i + 1, :share]], axis=1) for i in (0, 2)
+        ]
+        msg = ring_gather(jnp.concatenate([inner_weight, *beside, tail], axis=0))
+        row_pieces = tensor_gather(jnp.concatenate([tokens, cotangent], axis=0))
+        grad_pieces = row_pieces
         weight_pieces = [piece for piece, _ in msg]
-        out_pieces = [piece for piece, _ in out_msg]
+        late_pieces = [piece for piece, _ in late]
         place = jnp.stack([me, me ^ 1, me ^ 2, me ^ 3] + [index for _, index in msg])
     else:
         row_pieces = [lax.all_gather(tokens, "tensor", axis=0, tiled=True)]
         grad_pieces = [lax.all_gather(cotangent, "tensor", axis=0, tiled=True)]
         weight_pieces = [
-            lax.all_gather(input_flat, "dp", axis=0, tiled=True),
+            lax.all_gather(inner_weight, "dp", axis=0, tiled=True),
             lax.all_gather(state_weight, ("dp", "tensor"), axis=0, tiled=True),
             lax.all_gather(step_rows, "dp", axis=1, tiled=True),
             lax.psum(small, ("dp", "tensor")),
         ]
-        out_pieces = [lax.all_gather(output_weight, "dp", axis=1, tiled=True)]
+        late_pieces = [
+            lax.all_gather(gate_weight, "dp", axis=0, tiled=True),
+            lax.all_gather(output_weight.T, "dp", axis=0, tiled=True),
+        ]
         place = jnp.zeros((12,), jnp.int32)
     place = place.astype(jnp.int32)
 
@@ -757,11 +766,10 @@
     (
         rows,
         normed,
-        weight_full,
+        inner_full,
         state_full,
         step_full,
         small_full,
-        gate,
         raw,
         state_raw,
         step_col,
@@ -771,16 +779,16 @@
         mixed,
     ) = call(
         functools.partial(forward_kernel, fast),
+        12,
         [place, lengths],
         row_pieces + weight_pieces + scan_params,
         [
             ((total, depth), bf16),
             ((total, depth), bf16),
-            ((depth, 2 * channels), bf16),
+            ((depth, channels), bf16),
             ((depth, states), bf16),
             ((head_rows, depth), bf16),
             ((16, states), f32),
-            ((total, channels), f32),
             ((total + pad, channels), f32),
             ((total + pad, states), f32),
             ((total, head_rows), f32),
@@ -792,13 +800,16 @@
         [masks] + state_taps,
     )
     norm_row = row(norm_gain)
-    grad_rows, output_full, grad_normalized, sums = call(
+    grad_rows, gate_full, output_full, gate, grad_normalized, sums = call(
         functools.partial(grad_in_kernel, fast),
+        5,
         [place, lengths],
-        grad_pieces + out_pieces + [gate, mixed, norm_row],
+        grad_pieces + late_pieces + [normed, mixed, norm_row],
         [
             ((total, depth), bf16),
-            ((channels, depth), bf16),
+            ((depth, channels), bf16),
+            ((depth, channels), bf16),
+            ((total, channels), f32),
             ((total, channels), f32),
             ((8, total), f32),
         ],
@@ -813,6 +824,7 @@
     tall = depth // chunks
     partial_out, gate_msg, grad_gate, grad_mixed, norm_grad = call(
         functools.partial(norm_kernel, inner_total),
+        9,
         [lengths],
         [sums, gate, mixed, grad_normalized, norm_row, output_full, grad_rows, normed],
         [
@@ -827,14 +839,13 @@
     (
         inner_msg,
         state_part,
-        step_part,
         gain_part,
         grad_normed,
-        inner_sums,
-        head_sums,
+        sums,
         state_sums,
     ) = call(
         backward_kernel,
+        23,
         [lengths],
         [
             grad_mixed,
@@ -847,20 +858,20 @@
             grad_gate,
             normed,
             rows,
-            weight_full,
+            gate_full,
+            inner_full,
             state_full,
             step_full,
             small_full,
+            norm_grad,
         ]
         + scan_params,
         [
-            ((chunks, tall, channels), bf16),
+            ((chunks, tall + head_rows, channels), bf16),
             ((depth, states), bf16),
-            ((head_rows, depth), f32),
             ((1, depth), f32),
             ((total, depth), bf16),
-            ((8, channels), f32),
-            ((head_rows, 128), f32),
+            ((16, channels), f32),
             ((8, states), f32),
         ],
         [
@@ -897,13 +908,16 @@
     if fast:
         mixed_rows = tensor_scatter(partial_out.reshape((n_tensor, -1, depth)))
         grad_local = tensor_scatter(grad_normed.reshape((n_tensor, -1, depth)))
-        by_tensor = shared_part.reshape((n_dp, n_tensor) + shared_part.shape[1:])
-        shared_mine = ring_scatter(tensor_scatter(by_tensor.transpose(1, 0, 2, 3)))
+        shared_mine = lax.all_to_all(shared_part, ("dp", "tensor"), 0, 0, tiled=True)
+        shared_mine = jnp.sum(shared_mine.astype(f32), axis=0)
         gate_out = ring_scatter(gate_msg)
         gate_grad, output_grad = gate_out[:tall], gate_out[tall:].T
-        inner_grad = ring_scatter(inner_msg)
-        step_chunks = step_part[:heads].reshape(heads, n_dp, tall).transpose(1, 0, 2)
-        step_grad = ring_scatter(step_chunks).T
+        inner_out = ring_scatter(inner_msg)
+        inner_grad, step_grad = inner_out[:tall], inner_out[tall : tall + heads, :tall].T
+        sums = lax.all_to_all(
+            jnp.broadcast_to(sums, (n_dp,) + sums.shape), "dp", 0, 0, tiled=True
+        )
+        sums = jnp.sum(sums, axis=0)
     else:
         mixed_rows = lax.psum_scatter(
             partial_out, "tensor", scatter_dimension=0, tiled=True
@@ -914,13 +928,16 @@
         shared_mine = lax.psum_scatter(
             shared_part.astype(f32), ("dp", "tensor"), scatter_dimension=0, tiled=True
         )[0]
-        both = gate_msg.astype(f32)
+        both, inner_float = gate_msg.astype(f32), inner_msg.astype(f32)
         gate_grad, output_grad, inner_grad = (
             lax.psum_scatter(part.reshape(depth, channels), "dp", scatter_dimension=0, tiled=True)
-            for part in (both[:, :tall], both[:, tall:], inner_msg.astype(f32))
+            for part in (both[:, :tall], both[:, tall:], inner_float[:, :tall])
         )
         output_grad = output_grad.T
-        step_grad = lax.psum_scatter(step_part[:heads].T, "dp", scatter_dimension=0, tiled=True)
+        step_part = inner_float[:, tall : tall + heads, :tall].transpose(0, 2, 1)
+        step_part = step_part.reshape(depth, heads)
+        step_grad = lax.psum_scatter(step_part, "dp", scatter_dimension=0, tiled=True)
+        sums = lax.psum(sums, "dp")
     input_grad = jnp.stack([gate_grad, inner_grad], axis=1)
     block_out = (token_float + mixed_rows).astype(bf16)
     scale = lax.rsqrt(jnp.mean(token_float * token_float, axis=1, keepdims=True) + epsilon)
@@ -936,13 +953,6 @@
     conv_state_grad = shared_mine[share + 1, : taps * (states // owners)].reshape(taps, -1)
     conv_state_bias_grad = shared_mine[share + 2, : states // owners]
 
-    head_part = jnp.pad(head_sums[:, :2].T, ((0, 0), (0, channels - head_rows)))
-    sums = jnp.concatenate([inner_sums, norm_grad, head_part], axis=0)
-    if fast:
-        for other in dp_others(sums):
-            sums = sums + other
-    else:
-        sums = lax.psum(sums, "dp")
     skip_grad = sums[taps + 1].reshape(heads, -1).sum(axis=1)
     return (
         block_out,
@@ -955,10 +965,10 @@
         sums[taps],
         conv_state_grad,
         conv_state_bias_grad,
+        sums[8, :heads],
         sums[9, :heads],
-        sums[10, :heads],
         skip_grad,
-        sums[8],
+        sums[6],
         output_grad,
     )
 

time: 215 us -> 205 us (0.953)
  local copies, waits for them, and re-layouts: 23.2 us -> 47.1 us
  starting transfers between devices: 71.2 us -> 56.6 us
  Pallas kernels: 49.4 us -> 38.7 us
  waiting for transfers between devices: 52.7 us -> 43.5 us
    unnamed x76 -> x116, local copies, waits for them, and re-layouts: 7.98 us -> 27.7 us
    ppermute x42 -> x28, waiting for transfers between devices: 46.7 us -> 31.6 us  [ring_send(): return lax.ppermute(value, 'dp', pairs)]
    all_to_all x0 -> x3, starting transfers between devices: none -> 14.2 us  [the longest x1 6.04 us: body(): lax.all_to_all(jnp.broadcast_to(sums, (n_dp,) + sums.shape), 'dp', 0, 0,...]
    ppermute x7 -> x0, starting transfers between devices: 12.6 us -> none  [dp_others(): got.append(lax.ppermute(value, 'dp', pairs))]
    pallas_call x4, Pallas kernels: 49.4 us -> 38.7 us  [call(): pl.pallas_call(kernel, out_shape=[jax.ShapeDtypeStruct(shape, kind) for s...]
    ppermute x42 -> x28, starting transfers between devices: 46.5 us -> 37.8 us  [ring_send(): return lax.ppermute(value, 'dp', pairs)]
    ppermute x17 -> x9, starting transfers between devices: 12.1 us -> 4.6 us  [tensor_swap(): return lax.ppermute(value, 'tensor', [(i, i ^ bit) for i in range(4)])]
    ppermute x17 -> x9, waiting for transfers between devices: 5.97 us -> 11.8 us  [tensor_swap(): return lax.ppermute(value, 'tensor', [(i, i ^ bit) for i in range(4)])]
  transfers between devices with their start and end apart: 66 -> 40, of which waited for: 25 -> 17; matrix products, arithmetic and copies ran while one was open for 13% -> 15% of each run, Pallas kernels for 5% -> 4%
where the time goes in v1:
time: 205 us; the launch traced here: 204 us
  starting transfers between devices  56.6 us (28%)
  local copies, waits for them, and re-layouts  47.1 us (23%)
  waiting for transfers between devices  43.5 us (21%)
  Pallas kernels  38.7 us (19%)
  other arithmetic  16.3 us (8%)
    pallas_call x4, Pallas kernels, call(): pl.pallas_call(kernel, out_shape=[jax.ShapeDtypeStruct(shape, kind) for s...  38.7 us
    ppermute x28, starting transfers between devices, ring_send(): return lax.ppermute(value, 'dp', pairs)  37.8 us
    ppermute x28, waiting for transfers between devices, ring_send(): return lax.ppermute(value, 'dp', pairs)  31.6 us
    unnamed x116, local copies, waits for them, and re-layouts  27.7 us
    ppermute x9, waiting for transfers between devices, tensor_swap(): return lax.ppermute(value, 'tensor', [(i, i ^ bit) for i in range(4)])  11.8 us
    all_to_all x1, starting transfers between devices, body(): lax.all_to_all(jnp.broadcast_to(sums, (n_dp,) + sums.shape), 'dp', 0, 0,...  6.04 us
    convert_element_type x6, other arithmetic, ring_scatter(): got = ring_send(held.astype(bf16), forward).astype(f32)  5.83 us
    ppermute x9, starting transfers between devices, tensor_swap(): return lax.ppermute(value, 'tensor', [(i, i ^ bit) for i in range(4)])  4.6 us
  transfers between devices with their start and end apart: 40, of which 17 were waited for; matrix products, arithmetic and copies ran while one was open for 15% of the time, Pallas kernels for 4%

profile of v1, /device:TPU:0, one launch (start us, length us, event | category | flops | bytes accessed | tf_op | source)
XLA Modules:
  0.0 203.5 jit_solution(9373601346641973895)
XLA Ops:
  4.6 4.5 %all-to-all-start = ((bf16[4,48,256]{2,1,0:T(8,128)(2,1)}), bf16[4,48,256]{2,1,0:T(8,128)(2,1)S(1)}, u32[]{:S(2)}, u32[]{:S(2)}) async-start(bf16[4,48,256]{2,1,0:T(8,128)(2,1)} %broadcast_in_dim.42), calls=%async_computation | async-start | bytes 196608 | tf_op jit(solution)/shard_map/all_to_all | solution.py:717
  11.1 2.1 %collective-permute-start.1 = (bf16[256,1024]{1,0:T(8,128)(2,1)S(1)}, bf16[256,1024]{1,0:T(8,128)(2,1)S(1)}, u32[]{:S(2)}, u32[]{:S(2)}) collective-permute-start(bf16[256,1024]{1,0:T(8,128)(2,1)S(1)} %constant_dynamic-update-slice_fusion.refs_0_), channel_id=1, source_target_pairs={{0,2},{1,3},{2,0},{3,1},{4,6},{5,7},{6,4},{7,5},{8,10},{9,11},{10,... | collective-permute-start | bytes 1572872 | tf_op jit(solution)/shard_map/ppermute | solution.py:643
  13.8 2.1 %collective-permute-start.3 = (bf16[256,512]{1,0:T(8,128)(2,1)S(1)}, bf16[256,512]{1,0:T(8,128)(2,1)S(1)}, u32[]{:S(2)}, u32[]{:S(2)}) collective-permute-start(bf16[256,512]{1,0:T(8,128)(2,1)S(1)} %pad_maximum_fusion.1.refs_4_), channel_id=1, source_target_pairs={{0,8},{8,16},{16,24},{24,28},{28,20},{20,12},{12,4},{4,0},{1,9},{9... | collective-permute-start | bytes 786440 | tf_op jit(solution)/shard_map/ppermute | solution.py:607
  18.1 4.9 %collective-permute-done.3.refs_5_ = bf16[256,512]{1,0:T(8,128)(2,1)S(1)} collective-permute-done((bf16[256,512]{1,0:T(8,128)(2,1)S(1)}, bf16[256,512]{1,0:T(8,128)(2,1)S(1)}, u32[]{:S(2)}, u32[]{:S(2)}) %collective-permute-start.3) | collective-permute-done | bytes 262176 | tf_op jit(solution)/shard_map/ppermute | solution.py:607
  23.0 2.1 %collective-permute-start.11 = (bf16[208,512]{1,0:T(8,128)(2,1)S(1)}, bf16[208,512]{1,0:T(8,128)(2,1)S(1)}, u32[]{:S(2)}, u32[]{:S(2)}) collective-permute-start(bf16[208,512]{1,0:T(8,128)(2,1)S(1)} %fusion.28.refs_4_), channel_id=1, source_target_pairs={{0,4},{8,0},{16,8},{24,16},{28,24},{20,28},{12,20},{4,12},{1,5},{9... | collective-permute-start | bytes 638984 | tf_op jit(solution)/shard_map/ppermute | solution.py:607
  26.8 1.8 collective-permute-start.12
  32.0 2.9 %collective-permute-done.12.refs_7_ = bf16[208,512]{1,0:T(8,128)(2,1)S(1)} collective-permute-done((bf16[208,512]{1,0:T(8,128)(2,1)S(1)}, bf16[208,512]{1,0:T(8,128)(2,1)S(1)}, u32[]{:S(2)}, u32[]{:S(2)}) %collective-permute-start.12) | collective-permute-done | bytes 213024 | tf_op jit(solution)/shard_map/ppermute | solution.py:607
  35.0 1.8 collective-permute-start.14
  40.7 1.8 collective-permute-start.7
  42.7 2.5 %collective-permute-done.14.refs_9_ = bf16[208,512]{1,0:T(8,128)(2,1)} collective-permute-done((bf16[208,512]{1,0:T(8,128)(2,1)S(1)}, bf16[208,512]{1,0:T(8,128)(2,1)}, u32[]{:S(2)}, u32[]{:S(2)}) %collective-permute-start.14) | collective-permute-done | bytes 213024 | tf_op jit(solution)/shard_map/ppermute | solution.py:607
  45.3 1.8 collective-permute-start.16
  48.4 2.5 %collective-permute-done.7.refs_9_ = bf16[256,512]{1,0:T(8,128)(2,1)} collective-permute-done((bf16[256,512]{1,0:T(8,128)(2,1)}, bf16[256,512]{1,0:T(8,128)(2,1)}, u32[]{:S(2)}, u32[]{:S(2)}) %collective-permute-start.7) | collective-permute-done | bytes 262176 | tf_op jit(solution)/shard_map/ppermute | solution.py:607
  50.9 1.8 collective-permute-start.9
  52.7 2.8 %collective-permute-done.16.refs_11_ = bf16[208,512]{1,0:T(8,128)(2,1)} collective-permute-done((bf16[208,512]{1,0:T(8,128)(2,1)}, bf16[208,512]{1,0:T(8,128)(2,1)}, u32[]{:S(2)}, u32[]{:S(2)}) %collective-permute-start.16) | collective-permute-done | bytes 213024 | tf_op jit(solution)/shard_map/ppermute | solution.py:607
  58.2 9.2 %shard_map.271 = (bf16[512,1024]{1,0:T(8,128)(2,1)S(1)}, bf16[512,1024]{1,0:T(8,128)(2,1)S(1)}, bf16[1024,512]{1,0:T(8,128)(2,1)S(1)}, bf16[1024,256]{1,0:T(8,12...) custom-call(s32[12]{0:T(128)S(1)} %stack.60.place_ref, ...), custom_call_target="tpu_custom_call" | custom-call | flops 13200000000 | bytes 1048576 | tf_op jit(solution)/shard_map/pallas_call | solution.py:572
  71.9 4.4 %shard_map.272 = (bf16[512,1024]{1,0:T(8,128)(2,1)S(1)}, bf16[1024,512]{1,0:T(8,128)(2,1)S(1)}, bf16[1024,512]{1,0:T(8,128)(2,1)S(1)}, f32[512,512]{1,0:T(8,128)...) custom-call(s32[12]{0:T(128)S(1)} %stack.60.place_ref, s32[1,4]{1,0:T(1,128)S(1)} %copy-done.11, ...), custom_call_target="tpu_custom_call" | custom-call | flops 5500000256 | bytes 1048576 | tf_op jit(solution)/shard_map/pallas_call | solution.py:572
  83.0 3.4 %collective-permute-done.18 = f32[8,512]{1,0:T(8,128)S(1)} collective-permute-done((f32[8,512]{1,0:T(8,128)S(1)}, f32[8,512]{1,0:T(8,128)S(1)}, u32[]{:S(2)}, u32[]{:S(2)}) %collective-permute-start.18) | collective-permute-done | bytes 16416 | tf_op jit(solution)/shard_map/ppermute | solution.py:643
  93.8 5.9 %shard_map.273 = (bf16[512,1024]{1,0:T(8,128)(2,1)S(1)}, bf16[8,256,512]{2,1,0:T(8,128)(2,1)S(1)}, bf16[512,512]{1,0:T(8,128)(2,1)S(1)}, f32[512,512]{1,0:T(8,128)S(1)}, f32[1,512]{1,0:T(1,128)S(1)}) custom-call(s32[1,4]{1,0:T(1,128)S(1)} %copy-done.11, f32[8,512]{1,0:T(8,128)S(1)} %add.340.refs_0_, f32[512,512]{1,0:T(8,128)S(1)} %copy-done.24, ...), custom_call_target="tpu_custom_call" | custom-call | flops 9900000256 | bytes 1048576 | tf_op jit(solution)/shard_map/pallas_call | solution.py:572
  100.8 19.1 %shard_map.274 = (bf16[8,144,512]{2,1,0:T(8,128)(2,1)S(1)}, bf16[1024,256]{1,0:T(8,128)(2,1)S(1)}, f32[1,1024]{1,0:T(1,128)S(1)}, bf16[512,1024]{1,0:T(8,128)(2,...) custom-call(s32[1,4]{1,0:T(1,128)S(1)} %copy-done.11, f32[512,512]{1,0:T(8,128)S(1)} %get-tuple-element.53.refs_0_, ...), custom_call_target="tpu_custom_call" | custom-call | flops 25300000768 | bytes 1048576 | tf_op jit(solution)/shard_map/pallas_call | solution.py:572
  122.6 1.8 collective-permute-start.23
  129.8 1.9 dynamic-slice_bitcast_fusion.1
  132.4 6.0 %all-to-all-start.2 = ((f32[8,16,512]{2,1,0:T(8,128)}), f32[8,16,512]{2,1,0:T(8,128)S(1)}, u32[]{:S(2)}, u32[]{:S(2)}) async-start(f32[8,16,512]{2,1,0:T(8,128)} %broadcast_in_dim.48), calls=%async_computation.2 | async-start | bytes 524288 | tf_op jit(solution)/shard_map/all_to_all | solution.py:917
  139.5 2.1 %collective-permute-start.31 = (bf16[144,512]{1,0:T(8,128)(2,1)S(1)}, bf16[144,512]{1,0:T(8,128)(2,1)S(1)}, u32[]{:S(2)}, u32[]{:S(2)}) collective-permute-start(bf16[144,512]{1,0:T(8,128)(2,1)S(1)} %fusion.24), channel_id=1, source_target_pairs={{0,8},{8,16},{16,24},{24,28},{28,20},{20,12},{12,4},{4,0},{1,9},{9... | collective-permute-start | bytes 442376 | tf_op jit(solution)/shard_map/ppermute | solution.py:607
  141.6 2.1 %fusion.6 = bf16[32,40,256]{2,1,0:T(8,128)(2,1)} fusion(bf16[32,1,256]{2,1,0:T(2,128)(2,1)} %copy.73, bf16[32,1,256]{2,1,0:T(2,128)(2,1)} %copy.72, bf16[32,1,256]{2,1,0:T(2,128)(2,1)} %copy.71, bf16[32,32,256]{2,1,0:T(8,128)(2,1)} %bitcast.151), kind=kLoop, calls=%fused_computation.14 | loop fusion | flops 4259840 | bytes 1228800 | tf_op jit(solution)/shard_map/concatenate | solution.py:898
  144.5 2.9 %collective-permute-done.31 = bf16[144,512]{1,0:T(8,128)(2,1)S(1)} collective-permute-done((bf16[144,512]{1,0:T(8,128)(2,1)S(1)}, bf16[144,512]{1,0:T(8,128)(2,1)S(1)}, u32[]{:S(2)}, u32[]{:S(2)}) %collective-permute-start.31) | collective-permute-done | bytes 147488 | tf_op jit(solution)/shard_map/ppermute | solution.py:607
  148.5 2.1 %collective-permute-start.32 = (bf16[144,512]{1,0:T(8,128)(2,1)S(1)}, bf16[144,512]{1,0:T(8,128)(2,1)S(1)}, u32[]{:S(2)}, u32[]{:S(2)}) collective-permute-start(bf16[144,512]{1,0:T(8,128)(2,1)S(1)} %get-tuple-element.130), channel_id=1, source_target_pairs={{0,8},{8,16},{16,24},{24,28},{28,20},{20,12},{12,4},{4,0},{1,9},{9... | collective-permute-start | bytes 442376 | tf_op jit(solution)/shard_map/ppermute | solution.py:607
  157.4 2.0 collective-permute-start.33
  159.4 3.6 %all-to-all-start.1 = ((bf16[32,40,256]{2,1,0:T(8,128)(2,1)}), bf16[32,40,256]{2,1,0:T(8,128)(2,1)}, u32[]{:S(2)}, u32[]{:S(2)}) async-start(bf16[32,40,256]{2,1,0:T(8,128)(2,1)} %fusion.6), calls=%async_computation.1 | async-start | bytes 1310720 | tf_op jit(solution)/shard_map/all_to_all | solution.py:911
  179.8 7.2 %collective-permute-done.22 = bf16[128,1024]{1,0:T(8,128)(2,1)S(1)} collective-permute-done((bf16[128,1024]{1,0:T(8,128)(2,1)S(1)}, bf16[128,1024]{1,0:T(8,128)(2,1)S(1)}, u32[]{:S(2)}, u32[]{:S(2)}) %collective-permute-start.22) | collective-permute-done | bytes 262176 | tf_op jit(solution)/shard_map/ppermute | solution.py:643
  187.5 2.8 %collective-permute-start.26 = (bf16[256,512]{1,0:T(8,128)(2,1)S(1)}, bf16[256,512]{1,0:T(8,128)(2,1)S(1)}, u32[]{:S(2)}, u32[]{:S(2)}) collective-permute-start(bf16[256,512]{1,0:T(8,128)(2,1)S(1)} %get-tuple-element.122), channel_id=1, source_target_pairs={{0,8},{8,16},{16,24},{24,28},{28,20},{20,12},{12,4},{4,0},{1,9},{9... | collective-permute-start | bytes 786440 | tf_op jit(solution)/shard_map/ppermute | solution.py:607
  191.4 4.2 %collective-permute-done.26 = bf16[256,512]{1,0:T(8,128)(2,1)S(1)} collective-permute-done((bf16[256,512]{1,0:T(8,128)(2,1)S(1)}, bf16[256,512]{1,0:T(8,128)(2,1)S(1)}, u32[]{:S(2)}, u32[]{:S(2)}) %collective-permute-start.26) | collective-permute-done | bytes 262176 | tf_op jit(solution)/shard_map/ppermute | solution.py:607
  195.6 2.2 %collective-permute-done.29 = bf16[256,512]{1,0:T(8,128)(2,1)S(1)} collective-permute-done((bf16[256,512]{1,0:T(8,128)(2,1)S(1)}, bf16[256,512]{1,0:T(8,128)(2,1)S(1)}, u32[]{:S(2)}, u32[]{:S(2)}) %collective-permute-start.29) | collective-permute-done | bytes 262176 | tf_op jit(solution)/shard_map/ppermute | solution.py:607
  (246 shorter events, 83.7 us)
Async XLA Ops:
  4.6 11.4 %all-to-all-start = ((bf16[4,48,256]{2,1,0:T(8,128)(2,1)}), bf16[4,48,256]{2,1,0:T(8,128)(2,1)S(1)}, u32[]{:S(2)}, u32[]{:S(2)}) async-start(bf16[4,48,256]{2,1,0:T(8,128)(2,1)} %broadcast_in_dim.42), calls=%async_computation | async-start | bytes 196608 | tf_op jit(solution)/shard_map/all_to_all | solution.py:717
  11.1 19.6 %collective-permute-start.1 = (bf16[256,1024]{1,0:T(8,128)(2,1)S(1)}, bf16[256,1024]{1,0:T(8,128)(2,1)S(1)}, u32[]{:S(2)}, u32[]{:S(2)}) collective-permute-start(bf16[256,1024]{1,0:T(8,128)(2,1)S(1)} %constant_dynamic-update-slice_fusion.refs_0_), channel_id=1, source_target_pairs={{0,2},{1,3},{2,0},{3,1},{4,6},{5,7},{6,4},{7,5},{8,10},{9,11},{10,... | collective-permute-start | bytes 1572872 | tf_op jit(solution)/shard_map/ppermute | solution.py:643
  13.8 9.2 %collective-permute-start.3 = (bf16[256,512]{1,0:T(8,128)(2,1)S(1)}, bf16[256,512]{1,0:T(8,128)(2,1)S(1)}, u32[]{:S(2)}, u32[]{:S(2)}) collective-permute-start(bf16[256,512]{1,0:T(8,128)(2,1)S(1)} %pad_maximum_fusion.1.refs_4_), channel_id=1, source_target_pairs={{0,8},{8,16},{16,24},{24,28},{28,20},{20,12},{12,4},{4,0},{1,9},{9... | collective-permute-start | bytes 786440 | tf_op jit(solution)/shard_map/ppermute | solution.py:607
  16.0 10.7 %collective-permute-start.10 = (bf16[208,512]{1,0:T(8,128)(2,1)S(1)}, bf16[208,512]{1,0:T(8,128)(2,1)S(1)}, u32[]{:S(2)}, u32[]{:S(2)}) collective-permute-start(bf16[208,512]{1,0:T(8,128)(2,1)S(1)} %fusion.28.refs_4_), channel_id=1, source_target_pairs={{0,8},{8,16},{16,24},{24,28},{28,20},{20,12},{12,4},{4,0},{1,9},{9... | collective-permute-start | bytes 638984 | tf_op jit(solution)/shard_map/ppermute | solution.py:607
  17.5 11.8 %collective-permute-start.4 = (bf16[256,512]{1,0:T(8,128)(2,1)S(1)}, bf16[256,512]{1,0:T(8,128)(2,1)S(1)}, u32[]{:S(2)}, u32[]{:S(2)}) collective-permute-start(bf16[256,512]{1,0:T(8,128)(2,1)S(1)} %pad_maximum_fusion.1.refs_4_), channel_id=1, source_target_pairs={{0,4},{8,0},{16,8},{24,16},{28,24},{20,28},{12,20},{4,12},{1,5},{9... | collective-permute-start | bytes 786440 | tf_op jit(solution)/shard_map/ppermute | solution.py:607
  18.1 24.4 %collective-permute-start = (bf16[256,1024]{1,0:T(8,128)(2,1)S(1)}, bf16[256,1024]{1,0:T(8,128)(2,1)S(1)}, u32[]{:S(2)}, u32[]{:S(2)}) collective-permute-start(bf16[256,1024]{1,0:T(8,128)(2,1)S(1)} %constant_dynamic-update-slice_fusion.refs_0_), channel_id=1, source_target_pairs={{0,1},{1,0},{2,3},{3,2},{4,5},{5,4},{6,7},{7,6},{8,9},{9,8},{10,11... | collective-permute-start | bytes 1572872 | tf_op jit(solution)/shard_map/ppermute | solution.py:643
  26.8 8.2 %collective-permute-start.12 = (bf16[208,512]{1,0:T(8,128)(2,1)S(1)}, bf16[208,512]{1,0:T(8,128)(2,1)S(1)}, u32[]{:S(2)}, u32[]{:S(2)}) collective-permute-start(bf16[208,512]{1,0:T(8,128)(2,1)S(1)} %collective-permute-done.10.refs_5_), channel_id=1, source_target_pairs={{0,8},{8,16},{16,24},{24,28},{28,20},{20,12},{12,4},{4,0},{1,9},{9... | collective-permute-start | bytes 638984 | tf_op jit(solution)/shard_map/ppermute | solution.py:607
  29.3 11.4 %collective-permute-start.5 = (bf16[256,512]{1,0:T(8,128)(2,1)S(1)}, bf16[256,512]{1,0:T(8,128)(2,1)}, u32[]{:S(2)}, u32[]{:S(2)}) collective-permute-start(bf16[256,512]{1,0:T(8,128)(2,1)S(1)} %collective-permute-done.3.refs_5_), channel_id=1, source_target_pairs={{0,8},{8,16},{16,24},{24,28},{28,20},{20,12},{12,4},{4,0},{1,9},{9... | collective-permute-start | bytes 786440 | tf_op jit(solution)/shard_map/ppermute | solution.py:607
  30.6 24.8 %collective-permute-start.2 = (bf16[256,1024]{1,0:T(8,128)(2,1)S(1)}, bf16[256,1024]{1,0:T(8,128)(2,1)S(1)}, u32[]{:S(2)}, u32[]{:S(2)}) collective-permute-start(bf16[256,1024]{1,0:T(8,128)(2,1)S(1)} %collective-permute-done.1.refs_2_), channel_id=1, source_target_pairs={{0,1},{1,0},{2,3},{3,2},{4,5},{5,4},{6,7},{7,6},{8,9},{9,8},{10,11... | collective-permute-start | bytes 1572872 | tf_op jit(solution)/shard_map/ppermute | solution.py:643
  35.0 10.3 %collective-permute-start.14 = (bf16[208,512]{1,0:T(8,128)(2,1)S(1)}, bf16[208,512]{1,0:T(8,128)(2,1)}, u32[]{:S(2)}, u32[]{:S(2)}) collective-permute-start(bf16[208,512]{1,0:T(8,128)(2,1)S(1)} %collective-permute-done.12.refs_7_), channel_id=1, source_target_pairs={{0,8},{8,16},{16,24},{24,28},{28,20},{20,12},{12,4},{4,0},{1,9},{9... | collective-permute-start | bytes 638984 | tf_op jit(solution)/shard_map/ppermute | solution.py:607
  38.4 9.3 %collective-permute-start.6 = (bf16[256,512]{1,0:T(8,128)(2,1)S(1)}, bf16[256,512]{1,0:T(8,128)(2,1)}, u32[]{:S(2)}, u32[]{:S(2)}) collective-permute-start(bf16[256,512]{1,0:T(8,128)(2,1)S(1)} %collective-permute-done.4.refs_6_), channel_id=1, source_target_pairs={{0,4},{8,0},{16,8},{24,16},{28,24},{20,28},{12,20},{4,12},{1,5},{9... | collective-permute-start | bytes 786440 | tf_op jit(solution)/shard_map/ppermute | solution.py:607
  40.7 10.2 %collective-permute-start.7 = (bf16[256,512]{1,0:T(8,128)(2,1)}, bf16[256,512]{1,0:T(8,128)(2,1)}, u32[]{:S(2)}, u32[]{:S(2)}) collective-permute-start(bf16[256,512]{1,0:T(8,128)(2,1)} %collective-permute-done.5.refs_7_), channel_id=1, source_target_pairs={{0,8},{8,16},{16,24},{24,28},{28,20},{20,12},{12,4},{4,0},{1,9},{9... | collective-permute-start | bytes 786440 | tf_op jit(solution)/shard_map/ppermute | solution.py:607
  42.5 10.2 %collective-permute-start.15 = (bf16[208,512]{1,0:T(8,128)(2,1)}, bf16[208,512]{1,0:T(8,128)(2,1)}, u32[]{:S(2)}, u32[]{:S(2)}) collective-permute-start(bf16[208,512]{1,0:T(8,128)(2,1)} %collective-permute-done.13.refs_8_), channel_id=1, source_target_pairs={{0,4},{8,0},{16,8},{24,16},{28,24},{20,28},{12,20},{4,12},{1,5},{9... | collective-permute-start | bytes 638984 | tf_op jit(solution)/shard_map/ppermute | solution.py:607
  45.3 10.2 %collective-permute-start.16 = (bf16[208,512]{1,0:T(8,128)(2,1)}, bf16[208,512]{1,0:T(8,128)(2,1)}, u32[]{:S(2)}, u32[]{:S(2)}) collective-permute-start(bf16[208,512]{1,0:T(8,128)(2,1)} %collective-permute-done.14.refs_9_), channel_id=1, source_target_pairs={{0,8},{8,16},{16,24},{24,28},{28,20},{20,12},{12,4},{4,0},{1,9},{9... | collective-permute-start | bytes 638984 | tf_op jit(solution)/shard_map/ppermute | solution.py:607
  47.8 24.1 %collective-permute-start.8 = (bf16[256,512]{1,0:T(8,128)(2,1)}, bf16[256,512]{1,0:T(8,128)(2,1)S(1)}, u32[]{:S(2)}, u32[]{:S(2)}) collective-permute-start(bf16[256,512]{1,0:T(8,128)(2,1)} %collective-permute-done.6.refs_8_), channel_id=1, source_target_pairs={{0,4},{8,0},{16,8},{24,16},{28,24},{20,28},{12,20},{4,12},{1,5},{9... | collective-permute-start | bytes 786440 | tf_op jit(solution)/shard_map/ppermute | solution.py:607
  50.9 21.0 %collective-permute-start.9 = (bf16[256,512]{1,0:T(8,128)(2,1)}, bf16[256,512]{1,0:T(8,128)(2,1)S(1)}, u32[]{:S(2)}, u32[]{:S(2)}) collective-permute-start(bf16[256,512]{1,0:T(8,128)(2,1)} %collective-permute-done.7.refs_9_), channel_id=1, source_target_pairs={{0,8},{8,16},{16,24},{24,28},{28,20},{20,12},{12,4},{4,0},{1,9},{9... | collective-permute-start | bytes 786440 | tf_op jit(solution)/shard_map/ppermute | solution.py:607
  122.6 28.0 %collective-permute-start.23 = (bf16[256,512]{1,0:T(8,128)(2,1)}, bf16[256,512]{1,0:T(8,128)(2,1)}, u32[]{:S(2)}, u32[]{:S(2)}) collective-permute-start(bf16[256,512]{1,0:T(8,128)(2,1)} %get-tuple-element.126), channel_id=1, source_target_pairs={{0,8},{8,16},{16,24},{24,28},{28,20},{20,12},{12,4},{4,0},{1,9},{9... | collective-permute-start | bytes 786440 | tf_op jit(solution)/shard_map/ppermute | solution.py:607
  124.4 50.0 %collective-permute-start.27 = (bf16[256,512]{1,0:T(8,128)(2,1)}, bf16[256,512]{1,0:T(8,128)(2,1)}, u32[]{:S(2)}, u32[]{:S(2)}) collective-permute-start(bf16[256,512]{1,0:T(8,128)(2,1)} %get-tuple-element.127), channel_id=1, source_target_pairs={{0,4},{8,0},{16,8},{24,16},{28,24},{20,28},{12,20},{4,12},{1,5},{9... | collective-permute-start | bytes 786440 | tf_op jit(solution)/shard_map/ppermute | solution.py:607
  125.3 13.1 %collective-permute-start.30 = (bf16[144,512]{1,0:T(8,128)(2,1)}, bf16[144,512]{1,0:T(8,128)(2,1)}, u32[]{:S(2)}, u32[]{:S(2)}) collective-permute-start(bf16[144,512]{1,0:T(8,128)(2,1)} %get-tuple-element.132), channel_id=1, source_target_pairs={{0,8},{8,16},{16,24},{24,28},{28,20},{20,12},{12,4},{4,0},{1,9},{9... | collective-permute-start | bytes 442376 | tf_op jit(solution)/shard_map/ppermute | solution.py:607
  127.1 17.4 %collective-permute-start.34 = (bf16[144,512]{1,0:T(8,128)(2,1)}, bf16[144,512]{1,0:T(8,128)(2,1)}, u32[]{:S(2)}, u32[]{:S(2)}) collective-permute-start(bf16[144,512]{1,0:T(8,128)(2,1)} %get-tuple-element.133), channel_id=1, source_target_pairs={{0,4},{8,0},{16,8},{24,16},{28,24},{20,28},{12,20},{4,12},{1,5},{9... | collective-permute-start | bytes 442376 | tf_op jit(solution)/shard_map/ppermute | solution.py:607
  131.7 36.7 %collective-permute-start.19 = (bf16[2,128,1024]{2,1,0:T(8,128)(2,1)}, bf16[2,128,1024]{2,1,0:T(8,128)(2,1)}, u32[]{:S(2)}, u32[]{:S(2)}) collective-permute-start(bf16[2,128,1024]{2,1,0:T(8,128)(2,1)} %dynamic-slice_bitcast_fusion.1), channel_id=1, source_target_pairs={{0,1},{1,0},{2,3},{3,2},{4,5},{5,4},{6,7},{7,6},{8,9},{9,8},{10,11... | collective-permute-start | bytes 1572872 | tf_op jit(solution)/shard_map/ppermute | solution.py:643
  132.4 27.0 %all-to-all-start.2 = ((f32[8,16,512]{2,1,0:T(8,128)}), f32[8,16,512]{2,1,0:T(8,128)S(1)}, u32[]{:S(2)}, u32[]{:S(2)}) async-start(f32[8,16,512]{2,1,0:T(8,128)} %broadcast_in_dim.48), calls=%async_computation.2 | async-start | bytes 524288 | tf_op jit(solution)/shard_map/all_to_all | solution.py:917
  144.5 27.0 %collective-permute-start.21 = (bf16[2,128,1024]{2,1,0:T(8,128)(2,1)}, bf16[2,128,1024]{2,1,0:T(8,128)(2,1)}, u32[]{:S(2)}, u32[]{:S(2)}) collective-permute-start(bf16[2,128,1024]{2,1,0:T(8,128)(2,1)} %dynamic-slice_bitcast_fusion), channel_id=1, source_target_pairs={{0,1},{1,0},{2,3},{3,2},{4,5},{5,4},{6,7},{7,6},{8,9},{9,8},{10,11... | collective-permute-start | bytes 1572872 | tf_op jit(solution)/shard_map/ppermute | solution.py:643
  154.8 20.2 %collective-permute-start.24 = (bf16[256,512]{1,0:T(8,128)(2,1)}, bf16[256,512]{1,0:T(8,128)(2,1)}, u32[]{:S(2)}, u32[]{:S(2)}) collective-permute-start(bf16[256,512]{1,0:T(8,128)(2,1)} %fusion.16), channel_id=1, source_target_pairs={{0,8},{8,16},{16,24},{24,28},{28,20},{20,12},{12,4},{4,0},{1,9},{9... | collective-permute-start | bytes 786440 | tf_op jit(solution)/shard_map/ppermute | solution.py:607
  157.4 19.2 %collective-permute-start.33 = (bf16[144,512]{1,0:T(8,128)(2,1)}, bf16[144,512]{1,0:T(8,128)(2,1)}, u32[]{:S(2)}, u32[]{:S(2)}) collective-permute-start(bf16[144,512]{1,0:T(8,128)(2,1)} %get-tuple-element.128), channel_id=1, source_target_pairs={{0,8},{8,16},{16,24},{24,28},{28,20},{20,12},{12,4},{4,0},{1,9},{9... | collective-permute-start | bytes 442376 | tf_op jit(solution)/shard_map/ppermute | solution.py:607
  159.4 40.7 %all-to-all-start.1 = ((bf16[32,40,256]{2,1,0:T(8,128)(2,1)}), bf16[32,40,256]{2,1,0:T(8,128)(2,1)}, u32[]{:S(2)}, u32[]{:S(2)}) async-start(bf16[32,40,256]{2,1,0:T(8,128)(2,1)} %fusion.6), calls=%async_computation.1 | async-start | bytes 1310720 | tf_op jit(solution)/shard_map/all_to_all | solution.py:911
  168.4 9.9 %collective-permute-start.36 = (bf16[144,512]{1,0:T(8,128)(2,1)}, bf16[144,512]{1,0:T(8,128)(2,1)S(1)}, u32[]{:S(2)}, u32[]{:S(2)}) collective-permute-start(bf16[144,512]{1,0:T(8,128)(2,1)} %get-tuple-element.129), channel_id=1, source_target_pairs={{0,4},{8,0},{16,8},{24,16},{28,24},{20,28},{12,20},{4,12},{1,5},{9... | collective-permute-start | bytes 442376 | tf_op jit(solution)/shard_map/ppermute | solution.py:607
  171.6 18.7 %collective-permute-start.20 = (bf16[128,1024]{1,0:T(8,128)(2,1)S(1)}, bf16[128,1024]{1,0:T(8,128)(2,1)S(1)}, u32[]{:S(2)}, u32[]{:S(2)}) collective-permute-start(bf16[128,1024]{1,0:T(8,128)(2,1)S(1)} %fusion.26), channel_id=1, source_target_pairs={{0,2},{1,3},{2,0},{3,1},{4,6},{5,7},{6,4},{7,5},{8,10},{9,11},{10,... | collective-permute-start | bytes 786440 | tf_op jit(solution)/shard_map/ppermute | solution.py:643
  174.4 12.7 %collective-permute-start.22 = (bf16[128,1024]{1,0:T(8,128)(2,1)S(1)}, bf16[128,1024]{1,0:T(8,128)(2,1)S(1)}, u32[]{:S(2)}, u32[]{:S(2)}) collective-permute-start(bf16[128,1024]{1,0:T(8,128)(2,1)S(1)} %fusion.27), channel_id=1, source_target_pairs={{0,2},{1,3},{2,0},{3,1},{4,6},{5,7},{6,4},{7,5},{8,10},{9,11},{10,... | collective-permute-start | bytes 786440 | tf_op jit(solution)/shard_map/ppermute | solution.py:643
  176.2 11.1 %collective-permute-start.25 = (bf16[256,512]{1,0:T(8,128)(2,1)S(1)}, bf16[256,512]{1,0:T(8,128)(2,1)S(1)}, u32[]{:S(2)}, u32[]{:S(2)}) collective-permute-start(bf16[256,512]{1,0:T(8,128)(2,1)S(1)} %get-tuple-element.124), channel_id=1, source_target_pairs={{0,8},{8,16},{16,24},{24,28},{28,20},{20,12},{12,4},{4,0},{1,9},{9... | collective-permute-start | bytes 786440 | tf_op jit(solution)/shard_map/ppermute | solution.py:607
  176.6 10.8 %collective-permute-start.28 = (bf16[256,512]{1,0:T(8,128)(2,1)S(1)}, bf16[256,512]{1,0:T(8,128)(2,1)S(1)}, u32[]{:S(2)}, u32[]{:S(2)}) collective-permute-start(bf16[256,512]{1,0:T(8,128)(2,1)S(1)} %get-tuple-element.125), channel_id=1, source_target_pairs={{0,4},{8,0},{16,8},{24,16},{28,24},{20,28},{12,20},{4,12},{1,5},{9... | collective-permute-start | bytes 786440 | tf_op jit(solution)/shard_map/ppermute | solution.py:607
  187.5 8.1 %collective-permute-start.26 = (bf16[256,512]{1,0:T(8,128)(2,1)S(1)}, bf16[256,512]{1,0:T(8,128)(2,1)S(1)}, u32[]{:S(2)}, u32[]{:S(2)}) collective-permute-start(bf16[256,512]{1,0:T(8,128)(2,1)S(1)} %get-tuple-element.122), channel_id=1, source_target_pairs={{0,8},{8,16},{16,24},{24,28},{28,20},{20,12},{12,4},{4,0},{1,9},{9... | collective-permute-start | bytes 786440 | tf_op jit(solution)/shard_map/ppermute | solution.py:607
  (62 other events, 461.8 us)

commit v2 on v1

--- a/solution.py
+++ b/solution.py
@@ -15,7 +15,7 @@
 pad = 8
 head_rows = 16
 head_width = 64
-vmem_bytes = 32 * 1024 * 1024
+vmem_bytes = 54 * 1024 * 1024
 
 
 def mm(a, b, over=(1, 0)):
@@ -92,6 +92,17 @@
         return carry
 
     lax.fori_loop(0, rows // tall, one, 0)
+
+
+def for_chunks(place_ref, give_ref, keep_ref, step):
+    side = place_ref[8]
+
+    def one(c, carry):
+        step(c, 1 - side, give_ref)
+        step(c, side, keep_ref)
+        return carry
+
+    lax.fori_loop(0, give_ref.shape[0], one, 0)
 
 
 class Block:
@@ -141,12 +152,10 @@
 
 
 def forward_kernel(fast, place_ref, lengths_ref, *refs):
-    n_rows = 4 if fast else 1
     n_msg = 8 if fast else 4
-    row_refs, msg_refs, refs = refs[:n_rows], refs[n_rows : n_rows + n_msg], refs[n_rows + n_msg :]
+    rows_ref, msg_refs, refs = refs[0], refs[1 : 1 + n_msg], refs[1 + n_msg :]
     (taps_ref, bias_ref, step_bias_ref, step_bias_col_ref, log_ref, log_col_ref, skip_ref) = refs[:7]
     (
-        rows_ref,
         normed_ref,
         weight_ref,
         state_weight_ref,
@@ -159,8 +168,8 @@
         act_ref,
         state_ref,
         mixed_ref,
-    ) = refs[7:20]
-    mask_ref, state_taps_ref, state_bias_ref = refs[20:]
+    ) = refs[7:19]
+    mask_ref, state_taps_ref, state_bias_ref = refs[19:]
     total = rows_ref.shape[0]
     channels = act_ref.shape[1]
     ends = ends_of(lengths_ref)
@@ -171,7 +180,7 @@
         share = state_weight_ref.shape[0] // 32
         for slot in range(8):
             msg = msg_refs[slot]
-            index = place_ref[4 + slot]
+            index = place_ref[slot]
             at = pl.multiple_of(index * depth_part, depth_part)
             weight_ref[pl.ds(at, depth_part), :] = msg[:depth_part, :]
             for member in range(4):
@@ -194,14 +203,12 @@
     state_taps_ref[...] = small_ref[4 : 4 + taps, :]
     state_bias_ref[...] = small_ref[4 + taps : 5 + taps, :]
 
-    tall = total // n_rows
-    for member in range(n_rows):
-        at = pl.multiple_of(place_ref[member] * tall, tall) if fast else 0
-        own = row_refs[member][:tall, :]
-        rows_ref[pl.ds(at, tall), :] = own
-        value = own.astype(f32)
+    def norm(at):
+        value = rows_ref[pl.ds(at, 128), :].astype(f32)
         scale = lax.rsqrt(jnp.mean(value * value, axis=1, keepdims=True) + epsilon)
-        normed_ref[pl.ds(at, tall), :] = (value * scale * gain).astype(bf16)
+        normed_ref[pl.ds(at, 128), :] = (value * scale * gain).astype(bf16)
+
+    row_loop(total, 128, norm)
 
     raw_ref[:pad, :] = jnp.zeros((pad, channels), f32)
     state_raw_ref[:pad, :] = jnp.zeros((pad, state_raw_ref.shape[1]), f32)
@@ -259,20 +266,15 @@
 
 
 def grad_in_kernel(fast, place_ref, lengths_ref, *refs):
-    n_rows = 4 if fast else 1
     n_msg = 8 if fast else 2
-    row_refs, msg_refs, refs = refs[:n_rows], refs[n_rows : n_rows + n_msg], refs[n_rows + n_msg :]
+    rows_ref, msg_refs, refs = refs[0], refs[1 : 1 + n_msg], refs[1 + n_msg :]
     normed_ref, mixed_ref, norm_ref = refs[:3]
-    rows_ref, gate_weight_ref, out_weight_ref, gate_ref, grad_ref, sums_ref, wide_ref = refs[3:]
+    gate_weight_ref, out_weight_ref, gate_ref, grad_ref, sums_ref, wide_ref = refs[3:]
     total = rows_ref.shape[0]
     ends = ends_of(lengths_ref)
-    tall = total // n_rows
-    for member in range(n_rows):
-        at = pl.multiple_of(place_ref[member] * tall, tall) if fast else 0
-        rows_ref[pl.ds(at, tall), :] = row_refs[member][-tall:, :]
     if fast:
         for slot in range(8):
-            at = pl.multiple_of(place_ref[4 + slot] * 128, 128)
+            at = pl.multiple_of(place_ref[slot] * 128, 128)
             gate_weight_ref[pl.ds(at, 128), :] = msg_refs[slot][:128, :]
             out_weight_ref[pl.ds(at, 128), :] = msg_refs[slot][128:, :]
     else:
@@ -297,10 +299,10 @@
         sums_ref[:, at : at + 128] = wide_ref[at : at + 128, :].T[:8, :]
 
 
-def norm_kernel(inner_total, lengths_ref, *refs):
+def norm_kernel(inner_total, place_ref, lengths_ref, *refs):
     (sums_ref, gate_ref, mixed_ref, grad_ref, norm_ref, weight_ref, rows_ref, normed_ref) = refs[:8]
-    partial_ref, msg_ref, grad_gate_ref, grad_mixed_ref, norm_grad_ref = refs[8:13]
-    wide_ref, out_rows_ref = refs[13:]
+    partial_ref, give_ref, keep_ref, grad_gate_ref, grad_mixed_ref, norm_grad_ref = refs[8:14]
+    wide_ref, out_rows_ref = refs[14:]
     total, channels = gate_ref.shape
     ends = ends_of(lengths_ref)
     for at in range(0, total, 128):
@@ -331,73 +333,24 @@
 
     row_loop(total, 128, part)
 
-    chunks, tall = msg_ref.shape[0], msg_ref.shape[1] // 2
-
-    def chunk(c):
-        cols = pl.ds(pl.multiple_of(c * tall, tall), tall)
+    tall = give_ref.shape[1] // 2
+
+    def chunk(c, side, msg_ref):
+        cols = pl.ds(pl.multiple_of((2 * c + side) * tall, tall), tall)
         msg_ref[c, :tall, :] = mm(normed_ref[:, cols], grad_gate_ref[...], (0, 0)).astype(bf16)
         msg_ref[c, tall:, :] = mm(rows_ref[:, cols], out_rows_ref[...], (0, 0)).astype(bf16)
 
-    def one(c, carry):
-        chunk(c)
-        return carry
-
-    lax.fori_loop(0, chunks, one, 0)
-
-
-def backward_kernel(lengths_ref, *refs):
-    (
-        grad_mixed_ref,
-        act_ref,
-        state_ref,
-        raw_ref,
-        state_raw_ref,
-        step_col_ref,
-        step_row_ref,
-        grad_gate_ref,
-        normed_ref,
-        rows_ref,
-        gate_weight_ref,
-        weight_ref,
-        state_weight_ref,
-        step_weight_ref,
-        small_ref,
-        norm_grad_ref,
-        taps_ref,
-        bias_ref,
-        step_bias_ref,
-        step_bias_col_ref,
-        log_ref,
-        log_col_ref,
-        skip_ref,
-    ) = refs[:23]
-    (
-        msg_ref,
-        state_part_ref,
-        gain_part_ref,
-        grad_normed_ref,
-        inner_sums_ref,
-        state_sums_ref,
-    ) = refs[23:29]
-    (
-        mask_ref,
-        state_taps_ref,
-        state_bias_ref,
-        acc_ref,
-        grad_act_ref,
-        grad_state_ref,
-        pre_ref,
-        state_pre_ref,
-        grad_inner_ref,
-        grad_state_low_ref,
-    ) = refs[29:]
+    for_chunks(place_ref, give_ref, keep_ref, chunk)
+
+
+def scan_back_kernel(lengths_ref, *refs):
+    grad_mixed_ref, act_ref, state_ref, step_col_ref, step_row_ref = refs[:5]
+    step_bias_ref, step_bias_col_ref, log_ref, log_col_ref, skip_ref = refs[5:10]
+    grad_act_ref, grad_state_ref, step_grad_ref, sums_ref, acc_ref = refs[10:]
     total, channels = grad_mixed_ref.shape
     states = state_ref.shape[1] // 2
     ends = ends_of(lengths_ref)
-    taps = taps_ref.shape[0]
-    state_taps_ref[...] = small_ref[4 : 4 + taps, :]
-    state_bias_ref[...] = small_ref[4 + taps : 5 + taps, :]
-    write_masks(mask_ref, ends)
+    sums_ref[...] = jnp.zeros(sums_ref.shape, f32)
     raw_row = step_row_ref[...]
     steps = step_sizes(
         step_col_ref[...], raw_row, step_bias_ref, step_bias_col_ref, log_ref, log_col_ref
@@ -443,6 +396,7 @@
                 step_grad = jnp.where(head_row == h, step_here, step_grad)
                 grads.append(mm((decay * block.contact).astype(bf16), grad_low, (0, 0)))
             grad_act = wide(low_half, *grads) * step_wide + skip_ref[:, cols] * grad
+            sums_ref[2:3, cols] += jnp.sum(grad * x, axis=0, keepdims=True)
             picks = jnp.where(lane_head + 2 * i == head_of, 1.0, 0.0)
             if b == 0:
                 reach = wide(low_half, *(second.from_edge(h) for h in pair))
@@ -491,13 +445,62 @@
     lane = iota((head_rows, 128), 1)
     head_sums = jnp.where(lane == 0, bias_sum, jnp.where(lane == 1, decay_sum, 0.0))
     head_sums = jnp.concatenate([head_sums] * (128 // head_rows), axis=0).T
+    sums_ref[0:2, :128] = head_sums[:2, :]
+    step_grad_ref[...] = step_grad
+
+
+def backward_kernel(place_ref, lengths_ref, *refs):
+    (
+        grad_act_ref,
+        grad_state_ref,
+        step_grad_ref,
+        head_sums_ref,
+        raw_ref,
+        state_raw_ref,
+        grad_gate_ref,
+        normed_ref,
+        rows_ref,
+        gate_weight_ref,
+        weight_ref,
+        state_weight_ref,
+        step_weight_ref,
+        small_ref,
+        norm_grad_ref,
+        taps_ref,
+        bias_ref,
+    ) = refs[:17]
+    (
+        give_ref,
+        keep_ref,
+        state_part_ref,
+        gain_part_ref,
+        grad_normed_ref,
+        inner_sums_ref,
+        state_sums_ref,
+    ) = refs[17:24]
+    (
+        mask_ref,
+        state_taps_ref,
+        state_bias_ref,
+        pre_ref,
+        state_pre_ref,
+        grad_inner_ref,
+        grad_state_low_ref,
+    ) = refs[24:]
+    total = grad_act_ref.shape[0]
+    ends = ends_of(lengths_ref)
+    taps = taps_ref.shape[0]
+    state_taps_ref[...] = small_ref[4 : 4 + taps, :]
+    state_bias_ref[...] = small_ref[4 + taps : 5 + taps, :]
+    write_masks(mask_ref, ends)
+    step_grad = step_grad_ref[...]
     step_grad_low = step_grad.astype(bf16)
 
-    def conv_back(x_ref, grad_ref, held_ref, out_ref, sums_ref, own_taps, own_bias, skips):
+    def conv_back(x_ref, grad_ref, held_ref, out_ref, sums_ref, own_taps, own_bias):
         held_ref[total:, :] = jnp.zeros((pad, held_ref.shape[1]), f32)
 
         def column(cols):
-            sums = [jnp.zeros((1, 128), f32) for _ in range(taps + 2)]
+            sums = [jnp.zeros((1, 128), f32) for _ in range(taps + 1)]
             for at in range(0, total, 128):
                 pre, shifted = conv_pre(x_ref, mask_ref, own_taps, own_bias, at, cols, 128)
                 sig = sigmoid(pre)
@@ -506,10 +509,6 @@
                 for s in range(taps):
                     sums[taps - 1 - s] += jnp.sum(grad * shifted[s], axis=0, keepdims=True)
                 sums[taps] += jnp.sum(grad, axis=0, keepdims=True)
-                if skips:
-                    act = act_ref[at : at + 128, cols]
-                    over = grad_mixed_ref[at : at + 128, cols] * act
-                    sums[taps + 1] += jnp.sum(over, axis=0, keepdims=True)
             for t, value in enumerate(sums):
                 sums_ref[t : t + 1, cols] = value
             for at in range(0, total, 128):
@@ -524,10 +523,10 @@
 
     inner_sums_ref[...] = jnp.zeros(inner_sums_ref.shape, f32)
     inner_sums_ref[6:7, :] = norm_grad_ref[...]
-    inner_sums_ref[8:10, :128] = head_sums[:2, :]
+    inner_sums_ref[7:10, :] = head_sums_ref[:3, :]
     state_sums_ref[...] = jnp.zeros(state_sums_ref.shape, f32)
     conv_back(
-        raw_ref, grad_act_ref, pre_ref, grad_inner_ref, inner_sums_ref, taps_ref, bias_ref, True
+        raw_ref, grad_act_ref, pre_ref, grad_inner_ref, inner_sums_ref, taps_ref, bias_ref
     )
     conv_back(
         state_raw_ref,
@@ -537,21 +536,20 @@
         state_sums_ref,
         state_taps_ref,
         state_bias_ref,
-        False,
-    )
-
-    chunks, tall = msg_ref.shape[0], msg_ref.shape[1] - head_rows
-    msg_ref[...] = jnp.zeros(msg_ref.shape, bf16)
-
-    def chunk(c, carry):
-        at = pl.multiple_of(c * tall, tall)
+    )
+
+    tall = give_ref.shape[1] - head_rows
+    give_ref[...] = jnp.zeros(give_ref.shape, bf16)
+    keep_ref[...] = jnp.zeros(keep_ref.shape, bf16)
+
+    def chunk(c, side, msg_ref):
+        at = pl.multiple_of((2 * c + side) * tall, tall)
         part = normed_ref[:, pl.ds(at, tall)]
         msg_ref[c, :tall, :] = mm(part, grad_inner_ref[...], (0, 0)).astype(bf16)
         msg_ref[c, tall:, :tall] = mm(step_grad_low, part).astype(bf16)
         state_part_ref[pl.ds(at, tall), :] = mm(part, grad_state_low_ref[...], (0, 0)).astype(bf16)
-        return carry
-
-    lax.fori_loop(0, chunks, chunk, 0)
+
+    for_chunks(place_ref, give_ref, keep_ref, chunk)
     step_back = step_grad.T.astype(bf16)
     gain_part_ref[...] = jnp.zeros(gain_part_ref.shape, f32)
     for at in range(0, total, 128):
@@ -620,47 +618,18 @@
     return pieces
 
 
-def ring_scatter(parts):
-    me = ring_place(lax.axis_index("dp"))
-
-    def own(place):
-        return lax.dynamic_index_in_dim(parts, ring_index(place), 0, keepdims=False).astype(f32)
-
-    total = own(me)
-    for forward, steps in ((True, 4), (False, 3)):
-        sign = 1 if forward else -1
-        held = own(me + sign * steps)
-        for step in range(1, steps + 1):
-            got = ring_send(held.astype(bf16), forward).astype(f32)
-            if step < steps:
-                held = got + own(me + sign * (steps - step))
-            else:
-                total = total + got
-    return total
+def side_sum(give, keep):
+    got = lax.ppermute(give, "dp", [(i, i ^ 1) for i in range(8)])
+    return (keep.astype(f32) + got.astype(f32)).astype(bf16)
+
+
+def line_blocks(half):
+    lines = [[0, 2, 4, 6], [1, 3, 5, 7]]
+    return lax.all_to_all(half, "dp", 0, 0, axis_index_groups=lines, tiled=True)
 
 
 def tensor_swap(value, bit):
     return lax.ppermute(value, "tensor", [(i, i ^ bit) for i in range(4)])
-
-
-def tensor_gather(value):
-    near = tensor_swap(value, 1)
-    far = tensor_swap(value, 2)
-    return [value, near, far, tensor_swap(far, 1)]
-
-
-def tensor_scatter(parts):
-    me = lax.axis_index("tensor")
-    core, across = me % 2, me // 2
-    split = parts.reshape((2, 2) + parts.shape[1:])
-    give = lax.dynamic_index_in_dim(split, 1 - core, 1, keepdims=False)
-    keep = lax.dynamic_index_in_dim(split, core, 1, keepdims=False)
-    got = tensor_swap(give, 1)
-    half = keep.astype(f32) + got.astype(f32)
-    give = lax.dynamic_index_in_dim(half, 1 - across, 0, keepdims=False)
-    keep = lax.dynamic_index_in_dim(half, across, 0, keepdims=False)
-    got = tensor_swap(give.astype(bf16), 2)
-    return keep + got.astype(f32)
 
 
 def body(
@@ -696,9 +665,10 @@
     inner_total = channels * n_tensor
 
     def placed(value, whole):
-        zeros = jnp.zeros(value.shape[:-1] + (whole,), value.dtype)
-        start = (0,) * (value.ndim - 1) + (owner * value.shape[-1],)
-        return lax.dynamic_update_slice(zeros, value, start)
+        width = value.shape[-1]
+        mine = jnp.arange(whole, dtype=jnp.int32) // width == owner
+        spread = jnp.tile(value, (1,) * (value.ndim - 1) + (whole // width,))
+        return jnp.where(mine, spread, jnp.zeros((), value.dtype))
 
     small = jnp.concatenate(
         [
@@ -711,9 +681,13 @@
     small = jnp.pad(small, ((0, 16 - small.shape[0]), (0, 0)))
     step_rows = jnp.pad(step_weight.T, ((0, head_rows - heads), (0, 0)))
     gate_weight, inner_weight = input_weight[:, 0], input_weight[:, 1]
+    rows = lax.all_gather(tokens, "tensor", axis=0, tiled=True)
+    grad_rows = lax.all_gather(cotangent, "tensor", axis=0, tiled=True)
     if fast:
-        late = ring_gather(jnp.concatenate([gate_weight, output_weight.T], axis=0))
+        late = jnp.concatenate([gate_weight, output_weight.T], axis=0)
         shared = jnp.concatenate([state_weight, small], axis=0)
+        late, shared = lax.optimization_barrier((late, shared))
+        late = ring_gather(late)
         shared = lax.all_to_all(
             jnp.broadcast_to(shared, (4,) + shared.shape), "tensor", 0, 0, tiled=True
         )
@@ -724,14 +698,10 @@
             jnp.concatenate([shared[i, :share], shared[i + 1, :share]], axis=1) for i in (0, 2)
         ]
         msg = ring_gather(jnp.concatenate([inner_weight, *beside, tail], axis=0))
-        row_pieces = tensor_gather(jnp.concatenate([tokens, cotangent], axis=0))
-        grad_pieces = row_pieces
         weight_pieces = [piece for piece, _ in msg]
         late_pieces = [piece for piece, _ in late]
-        place = jnp.stack([me, me ^ 1, me ^ 2, me ^ 3] + [index for _, index in msg])
+        place = jnp.stack([index for _, index in msg] + [lax.axis_index("dp") % 2])
     else:
-        row_pieces = [lax.all_gather(tokens, "tensor", axis=0, tiled=True)]
-        grad_pieces = [lax.all_gather(cotangent, "tensor", axis=0, tiled=True)]
         weight_pieces = [
             lax.all_gather(inner_weight, "dp", axis=0, tiled=True),
             lax.all_gather(state_weight, ("dp", "tensor"), axis=0, tiled=True),
@@ -742,7 +712,7 @@
             lax.all_gather(gate_weight, "dp", axis=0, tiled=True),
             lax.all_gather(output_weight.T, "dp", axis=0, tiled=True),
         ]
-        place = jnp.zeros((12,), jnp.int32)
+        place = jnp.zeros((9,), jnp.int32)
     place = place.astype(jnp.int32)
 
     def row(value):
@@ -763,8 +733,8 @@
     ]
     masks = ((taps - 1, total + pad, 128), f32)
     state_taps = [((taps, states), f32), ((1, states), f32)]
+    rows, grad_rows = lax.optimization_barrier((rows, grad_rows))
     (
-        rows,
         normed,
         inner_full,
         state_full,
@@ -781,9 +751,8 @@
         functools.partial(forward_kernel, fast),
         12,
         [place, lengths],
-        row_pieces + weight_pieces + scan_params,
+        [rows] + weight_pieces + scan_params,
         [
-            ((total, depth), bf16),
             ((total, depth), bf16),
             ((depth, channels), bf16),
             ((depth, states), bf16),
@@ -800,13 +769,12 @@
         [masks] + state_taps,
     )
     norm_row = row(norm_gain)
-    grad_rows, gate_full, output_full, gate, grad_normalized, sums = call(
+    gate_full, output_full, gate, grad_normalized, sums = call(
         functools.partial(grad_in_kernel, fast),
         5,
         [place, lengths],
-        grad_pieces + late_pieces + [normed, mixed, norm_row],
+        [grad_rows] + late_pieces + [normed, mixed, norm_row],
         [
-            ((total, depth), bf16),
             ((depth, channels), bf16),
             ((depth, channels), bf16),
             ((total, channels), f32),
@@ -822,22 +790,41 @@
         sums = lax.psum(sums, "tensor")
     chunks = 8
     tall = depth // chunks
-    partial_out, gate_msg, grad_gate, grad_mixed, norm_grad = call(
+    partial_out, gate_give, gate_keep, grad_gate, grad_mixed, norm_grad = call(
         functools.partial(norm_kernel, inner_total),
         9,
-        [lengths],
+        [place, lengths],
         [sums, gate, mixed, grad_normalized, norm_row, output_full, grad_rows, normed],
         [
             ((total, depth), bf16),
-            ((chunks, 2 * tall, channels), bf16),
+            ((chunks // 2, 2 * tall, channels), bf16),
+            ((chunks // 2, 2 * tall, channels), bf16),
             ((total, channels), bf16),
             ((total, channels), f32),
             ((1, channels), f32),
         ],
         [((total, 128), f32), ((total, channels), bf16)],
     )
+    grad_act, grad_state, step_grad, head_sums = call(
+        scan_back_kernel,
+        13,
+        [lengths],
+        [grad_mixed, act, state_act, step_col, step_row] + scan_params[2:],
+        [
+            ((total, channels), f32),
+            ((total, states), f32),
+            ((head_rows, total), f32),
+            ((8, channels), f32),
+        ],
+        [((span, span), f32)],
+    )
+    if fast:
+        gate_half = side_sum(gate_give, gate_keep)
+        grad_act, gate_half = lax.optimization_barrier((grad_act, gate_half))
+        gate_blocks = line_blocks(gate_half)
     (
-        inner_msg,
+        inner_give,
+        inner_keep,
         state_part,
         gain_part,
         grad_normed,
@@ -845,16 +832,15 @@
         state_sums,
     ) = call(
         backward_kernel,
-        23,
-        [lengths],
+        9,
+        [place, lengths],
         [
-            grad_mixed,
-            act,
-            state_act,
+            grad_act,
+            grad_state,
+            step_grad,
+            head_sums,
             raw,
             state_raw,
-            step_col,
-            step_row,
             grad_gate,
             normed,
             rows,
@@ -865,9 +851,10 @@
             small_full,
             norm_grad,
         ]
-        + scan_params,
+        + scan_params[:2],
         [
-            ((chunks, tall + head_rows, channels), bf16),
+            ((chunks // 2, tall + head_rows, channels), bf16),
+            ((chunks // 2, tall + head_rows, channels), bf16),
             ((depth, states), bf16),
             ((1, depth), f32),
             ((total, depth), bf16),
@@ -877,9 +864,6 @@
         [
             masks,
             *state_taps,
-            ((span, span), f32),
-            ((total, channels), f32),
-            ((total, states), f32),
             ((total + pad, channels), f32),
             ((total + pad, states), f32),
             ((total, channels), bf16),
@@ -905,30 +889,31 @@
         axis=1,
     )
     shared_part = jnp.pad(shared_part, ((0, 0), (0, -shared_part.shape[1] % 8), (0, 0)))
+    mixed_rows = lax.psum_scatter(partial_out, "tensor", scatter_dimension=0, tiled=True)
+    grad_normed, mixed_rows = lax.optimization_barrier((grad_normed, mixed_rows))
+    grad_local = lax.psum_scatter(grad_normed, "tensor", scatter_dimension=0, tiled=True)
+    mixed_rows, grad_local = mixed_rows.astype(f32), grad_local.astype(f32)
     if fast:
-        mixed_rows = tensor_scatter(partial_out.reshape((n_tensor, -1, depth)))
-        grad_local = tensor_scatter(grad_normed.reshape((n_tensor, -1, depth)))
         shared_mine = lax.all_to_all(shared_part, ("dp", "tensor"), 0, 0, tiled=True)
         shared_mine = jnp.sum(shared_mine.astype(f32), axis=0)
-        gate_out = ring_scatter(gate_msg)
+        inner_half = side_sum(inner_give, inner_keep)
+        inner_half, gate_blocks = lax.optimization_barrier((inner_half, gate_blocks))
+        gate_out = jnp.sum(gate_blocks.astype(f32), axis=0)
         gate_grad, output_grad = gate_out[:tall], gate_out[tall:].T
-        inner_out = ring_scatter(inner_msg)
+        inner_out = jnp.sum(line_blocks(inner_half).astype(f32), axis=0)
         inner_grad, step_grad = inner_out[:tall], inner_out[tall : tall + heads, :tall].T
         sums = lax.all_to_all(
             jnp.broadcast_to(sums, (n_dp,) + sums.shape), "dp", 0, 0, tiled=True
         )
         sums = jnp.sum(sums, axis=0)
     else:
-        mixed_rows = lax.psum_scatter(
-            partial_out, "tensor", scatter_dimension=0, tiled=True
-        ).astype(f32)
-        grad_local = lax.psum_scatter(
-            grad_normed, "tensor", scatter_dimension=0, tiled=True
-        ).astype(f32)
         shared_mine = lax.psum_scatter(
             shared_part.astype(f32), ("dp", "tensor"), scatter_dimension=0, tiled=True
         )[0]
-        both, inner_float = gate_msg.astype(f32), inner_msg.astype(f32)
+        both, inner_float = (
+            jnp.stack([keep, give], axis=1).reshape((chunks,) + keep.shape[1:]).astype(f32)
+            for keep, give in ((gate_keep, gate_give), (inner_keep, inner_give))
+        )
         gate_grad, output_grad, inner_grad = (
             lax.psum_scatter(part.reshape(depth, channels), "dp", scatter_dimension=0, tiled=True)
             for part in (both[:, :tall], both[:, tall:], inner_float[:, :tall])
@@ -953,7 +938,7 @@
     conv_state_grad = shared_mine[share + 1, : taps * (states // owners)].reshape(taps, -1)
     conv_state_bias_grad = shared_mine[share + 2, : states // owners]
 
-    skip_grad = sums[taps + 1].reshape(heads, -1).sum(axis=1)
+    skip_grad = sums[9].reshape(heads, -1).sum(axis=1)
     return (
         block_out,
         tokens_grad,
@@ -965,8 +950,8 @@
         sums[taps],
         conv_state_grad,
         conv_state_bias_grad,
+        sums[7, :heads],
         sums[8, :heads],
-        sums[9, :heads],
         skip_grad,
         sums[6],
         output_grad,

time: 205 us -> 235 us (1.15)
  waiting for transfers between devices: 43.5 us -> 90.1 us
  local copies, waits for them, and re-layouts: 47.1 us -> 17.1 us
  starting transfers between devices: 56.6 us -> 36.4 us
  blocking collectives: 0 us -> 14.3 us
  between operations: 1.39 us -> 14.4 us
  Pallas kernels: 38.7 us -> 50.9 us
  other arithmetic: 16.3 us -> 11.3 us
    ppermute x0 -> x2, waiting for transfers between devices: none -> 31.9 us  [side_sum(): got = lax.ppermute(give, 'dp', [(i, i ^ 1) for i in range(8)])]
    all_to_all x1 -> x2, waiting for transfers between devices: 0.01 us -> 31 us  [line_blocks(): return lax.all_to_all(half, 'dp', 0, 0, axis_index_groups=lines, tiled=True)]
    unnamed x116 -> x69, local copies, waits for them, and re-layouts: 27.7 us -> 3.85 us
    ppermute x28 -> x14, starting transfers between devices: 37.8 us -> 16.8 us  [ring_send(): return lax.ppermute(value, 'dp', pairs)]
    ppermute x28 -> x14, waiting for transfers between devices: 31.6 us -> 16.9 us  [ring_send(): return lax.ppermute(value, 'dp', pairs)]
    all_to_all x0 -> x1, blocking collectives: none -> 14.3 us  [body(): lax.all_to_all(jnp.broadcast_to(sums, (n_dp,) + sums.shape), 'dp', 0, 0,...]
    pallas_call x4 -> x5, Pallas kernels: 38.7 us -> 50.9 us  [call(): pl.pallas_call(kernel, out_shape=[jax.ShapeDtypeStruct(shape, kind) for s...]
    ppermute x9 -> x2, waiting for transfers between devices: 11.8 us -> 4.83 us  [tensor_swap(): return lax.ppermute(value, 'tensor', [(i, i ^ bit) for i in range(4)])]
  transfers between devices with their start and end apart: 40 -> 26, of which waited for: 17 -> 13; matrix products, arithmetic and copies ran while one was open for 15% -> 9% of each run, Pallas kernels for 4% -> 9%
where the time goes in v2:
time: 235 us; the launch traced here: 234 us
  waiting for transfers between devices  90.1 us (38%)
  Pallas kernels  50.9 us (22%)
  starting transfers between devices  36.4 us (15%)
  local copies, waits for them, and re-layouts  17.1 us (7%)
  between operations  14.4 us (6%)
  blocking collectives  14.3 us (6%)
  other arithmetic  11.3 us (5%)
    pallas_call x5, Pallas kernels, call(): pl.pallas_call(kernel, out_shape=[jax.ShapeDtypeStruct(shape, kind) for s...  50.9 us
    ppermute x2, waiting for transfers between devices, side_sum(): got = lax.ppermute(give, 'dp', [(i, i ^ 1) for i in range(8)])  31.9 us
    all_to_all x2, waiting for transfers between devices, line_blocks(): return lax.all_to_all(half, 'dp', 0, 0, axis_index_groups=lines, tiled=True)  31 us
    ppermute x14, waiting for transfers between devices, ring_send(): return lax.ppermute(value, 'dp', pairs)  16.9 us
    ppermute x14, starting transfers between devices, ring_send(): return lax.ppermute(value, 'dp', pairs)  16.8 us
    all_to_all x1, blocking collectives, body(): lax.all_to_all(jnp.broadcast_to(sums, (n_dp,) + sums.shape), 'dp', 0, 0,...  14.3 us
    all_to_all x2, starting transfers between devices, line_blocks(): return lax.all_to_all(half, 'dp', 0, 0, axis_index_groups=lines, tiled=True)  8.37 us
    ppermute x2, waiting for transfers between devices, tensor_swap(): return lax.ppermute(value, 'tensor', [(i, i ^ bit) for i in range(4)])  4.83 us
  transfers between devices with their start and end apart: 26, of which 13 were waited for; matrix products, arithmetic and copies ran while one was open for 9% of the time, Pallas kernels for 9%

profile of v2, /device:TPU:0, one launch (start us, length us, event | category | flops | bytes accessed | tf_op | source)
XLA Modules:
  0.0 234.4 jit_solution(16276588005897908799)
XLA Ops:
  12.8 4.2 %all-to-all-start = ((bf16[4,48,256]{2,1,0:T(8,128)(2,1)}), bf16[4,48,256]{2,1,0:T(8,128)(2,1)S(1)}, u32[]{:S(2)}, u32[]{:S(2)}) async-start(bf16[4,48,256]{2,1,0:T(8,128)(2,1)} %broadcast_in_dim.45), calls=%async_computation | async-start | bytes 196608 | tf_op jit(solution)/shard_map/all_to_all | solution.py:691
  17.7 3.5 %all-to-all-done = bf16[4,48,256]{2,1,0:T(8,128)(2,1)S(1)} async-done(((bf16[4,48,256]{2,1,0:T(8,128)(2,1)}), bf16[4,48,256]{2,1,0:T(8,128)(2,1)S(1)}, u32[]{:S(2)}, u32[]{:S(2)}) %all-to-all-start) | async-done | bytes 98336 | tf_op jit(solution)/shard_map/all_to_all | solution.py:691
  21.3 2.1 collective-permute-start.7
  23.5 1.7 collective-permute-start
  25.5 4.0 %collective-permute-done.7.refs_2_ = bf16[208,512]{1,0:T(8,128)(2,1)S(1)} collective-permute-done((bf16[208,512]{1,0:T(8,128)(2,1)S(1)}, bf16[208,512]{1,0:T(8,128)(2,1)S(1)}, u32[]{:S(2)}, u32[]{:S(2)}) %collective-permute-start.7) | collective-permute-done | bytes 213024 | tf_op jit(solution)/shard_map/ppermute | solution.py:605
  29.5 2.1 collective-permute-start.9
  31.7 3.5 %collective-permute-done.refs_2_ = bf16[256,512]{1,0:T(8,128)(2,1)S(1)} collective-permute-done((bf16[256,512]{1,0:T(8,128)(2,1)S(1)}, bf16[256,512]{1,0:T(8,128)(2,1)S(1)}, u32[]{:S(2)}, u32[]{:S(2)}) %collective-permute-start) | collective-permute-done | bytes 262176 | tf_op jit(solution)/shard_map/ppermute | solution.py:605
  35.2 2.1 collective-permute-start.2
  37.3 2.4 %collective-permute-done.9.refs_4_ = bf16[208,512]{1,0:T(8,128)(2,1)S(1)} collective-permute-done((bf16[208,512]{1,0:T(8,128)(2,1)S(1)}, bf16[208,512]{1,0:T(8,128)(2,1)S(1)}, u32[]{:S(2)}, u32[]{:S(2)}) %collective-permute-start.9) | collective-permute-done | bytes 213024 | tf_op jit(solution)/shard_map/ppermute | solution.py:605
  39.7 2.1 collective-permute-start.11
  41.9 3.5 %collective-permute-done.2.refs_4_ = bf16[256,512]{1,0:T(8,128)(2,1)S(1)} collective-permute-done((bf16[256,512]{1,0:T(8,128)(2,1)S(1)}, bf16[256,512]{1,0:T(8,128)(2,1)S(1)}, u32[]{:S(2)}, u32[]{:S(2)}) %collective-permute-start.2) | collective-permute-done | bytes 262176 | tf_op jit(solution)/shard_map/ppermute | solution.py:605
  45.3 2.1 collective-permute-start.4
  47.5 2.4 %collective-permute-done.11.refs_6_ = bf16[208,512]{1,0:T(8,128)(2,1)S(1)} collective-permute-done((bf16[208,512]{1,0:T(8,128)(2,1)S(1)}, bf16[208,512]{1,0:T(8,128)(2,1)S(1)}, u32[]{:S(2)}, u32[]{:S(2)}) %collective-permute-start.11) | collective-permute-done | bytes 213024 | tf_op jit(solution)/shard_map/ppermute | solution.py:605
  49.9 2.1 collective-permute-start.13
  57.1 2.0 collective-permute-start.6
  60.2 10.9 %shard_map.271 = (bf16[512,1024]{1,0:T(8,128)(2,1)}, bf16[1024,512]{1,0:T(8,128)(2,1)}, bf16[1024,256]{1,0:T(8,128)(2,1)}, bf16[16,1024]{1,0:T(8,128)(2,1)}, f32...) custom-call(s32[9]{0:T(128)} %stack.48.place_ref, ...), custom_call_target="tpu_custom_call" | custom-call | flops 13200000000 | bytes 1048576 | tf_op jit(solution)/shard_map/pallas_call | solution.py:570
  72.1 6.4 %shard_map.272 = (bf16[1024,512]{1,0:T(8,128)(2,1)}, bf16[1024,512]{1,0:T(8,128)(2,1)}, f32[512,512]{1,0:T(8,128)}, f32[512,512]{1,0:T(8,128)}, f32[8,512]{1,0:T(8,128)}) custom-call(s32[9]{0:T(128)} %stack.48.place_ref, s32[1,4]{1,0:T(1,128)} %lengths_ref.9, bf16[512,1024]{1,0:T(8,128)(2,1)} %all-gather.5.cloned.1.call-done.refs_0_.refs_6_, ...), custom_call_target="tpu_custom_call" | custom-call | flops 5500000256 | bytes 1048576 | tf_op jit(solution)/shard_map/pallas_call | solution.py:570
  80.9 3.4 %collective-permute-done.15 = f32[8,512]{1,0:T(8,128)S(1)} collective-permute-done((f32[8,512]{1,0:T(8,128)S(1)}, f32[8,512]{1,0:T(8,128)S(1)}, u32[]{:S(2)}, u32[]{:S(2)}) %collective-permute-start.15) | collective-permute-done | bytes 16416 | tf_op jit(solution)/shard_map/ppermute | solution.py:632
  84.9 8.9 %shard_map.273 = (bf16[512,1024]{1,0:T(8,128)(2,1)}, bf16[4,256,512]{2,1,0:T(8,128)(2,1)}, bf16[4,256,512]{2,1,0:T(8,128)(2,1)}, bf16[512,512]{1,0:T(8,128)(2,1)}, f32[512,512]{1,0:T(8,128)}, /*index=5*/f32[1,512]{1,0:T(1,128)}) custom-call(s32[9]{0:T(128)} %stack.48.place_ref, s32[1,4]{1,0:T(1,128)} %lengths_ref.9, f32[8,512]{1,0:T(8,128)} %add.186.refs_0_, ...), custom_call_target="tpu_custom_call" | custom-call | flops 9900000256 | bytes 1048576 | tf_op jit(solution)/shard_map/pallas_call | solution.py:570
  93.8 2.1 collective-permute-start.16
  95.9 10.0 %shard_map.274 = (f32[512,512]{1,0:T(8,128)}, f32[512,256]{1,0:T(8,128)}, f32[16,512]{1,0:T(8,128)}, f32[8,512]{1,0:T(8,128)}) custom-call(s32[1,4]{1,0:T(1,128)} %lengths_ref.9, f32[512,512]{1,0:T(8,128)} %get-tuple-element.69.refs_0_, f32[512,512]{1,0:T(8,128)} %get-tuple-element.70.refs_1_, f32[512,256]{1,0:T(8,128)} %get-tuple-element.71.refs_2_, ...), custom_call_target="tpu_custom_call" | custom-call | flops 14300000256 | bytes 1048576 | tf_op jit(solution)/shard_map/pallas_call | solution.py:570
  105.9 12.6 %collective-permute-done.16 = bf16[4,256,512]{2,1,0:T(8,128)(2,1)S(1)} collective-permute-done((bf16[4,256,512]{2,1,0:T(8,128)(2,1)}, bf16[4,256,512]{2,1,0:T(8,128)(2,1)S(1)}, u32[]{:S(2)}, u32[]{:S(2)}) %collective-permute-start.16) | collective-permute-done | bytes 1048608 | tf_op jit(solution)/shard_map/ppermute | solution.py:622
  119.7 14.7 %shard_map.275 = (bf16[4,144,512]{2,1,0:T(8,128)(2,1)}, bf16[4,144,512]{2,1,0:T(8,128)(2,1)}, bf16[1024,256]{1,0:T(8,128)(2,1)}, f32[1,1024]{1,0:T(1,128)}, bf16...) custom-call(s32[9]{0:T(128)} %stack.48.place_ref, s32[1,4]{1,0:T(1,128)} %lengths_ref.9, ...), custom_call_target="tpu_custom_call" | custom-call | flops 9900000256 | bytes 1048576 | tf_op jit(solution)/shard_map/pallas_call | solution.py:570
  135.2 14.3 %all_to_all.25 = f32[8,16,512]{2,1,0:T(8,128)S(1)} all-to-all(f32[8,16,512]{2,1,0:T(8,128)S(1)} %broadcast_in_dim.51), channel_id=1, replica_groups=mesh['dp'=8,'tensor'=4] {'dp'}, dimensions={0} | all-to-all | bytes 524288 | tf_op jit(solution)/shard_map/all_to_all | solution.py:905
  149.5 3.6 %all-to-all-start.2 = ((bf16[4,256,512]{2,1,0:T(8,128)(2,1)}), bf16[4,256,512]{2,1,0:T(8,128)(2,1)S(1)}, u32[]{:S(2)}, u32[]{:S(2)}) async-start(bf16[4,256,512]{2,1,0:T(8,128)(2,1)} %add_convert_fusion), calls=%async_computation.4 | async-start | bytes 2097152 | tf_op jit(solution)/shard_map/all_to_all | solution.py:628
  155.6 20.5 %all-to-all-done.2 = bf16[4,256,512]{2,1,0:T(8,128)(2,1)S(1)} async-done(((bf16[4,256,512]{2,1,0:T(8,128)(2,1)}), bf16[4,256,512]{2,1,0:T(8,128)(2,1)S(1)}, u32[]{:S(2)}, u32[]{:S(2)}) %all-to-all-start.2) | async-done | bytes 1048608 | tf_op jit(solution)/shard_map/all_to_all | solution.py:628
  176.1 2.6 %all-to-all-start.1 = ((bf16[32,40,256]{2,1,0:T(8,128)(2,1)}), bf16[32,40,256]{2,1,0:T(8,128)(2,1)S(1)}, u32[]{:S(2)}, u32[]{:S(2)}) async-start(bf16[32,40,256]{2,1,0:T(8,128)(2,1)} %fusion.6), calls=%async_computation.3 | async-start | bytes 1310720 | tf_op jit(solution)/shard_map/all_to_all | solution.py:897
  178.8 1.7 collective-permute-start.17
  181.8 19.3 %collective-permute-done.17 = bf16[4,144,512]{2,1,0:T(8,128)(2,1)S(1)} collective-permute-done((bf16[4,144,512]{2,1,0:T(8,128)(2,1)}, bf16[4,144,512]{2,1,0:T(8,128)(2,1)S(1)}, u32[]{:S(2)}, u32[]{:S(2)}) %collective-permute-start.17) | collective-permute-done | bytes 589856 | tf_op jit(solution)/shard_map/ppermute | solution.py:622
  202.1 4.7 %all-to-all-start.3 = ((bf16[4,144,512]{2,1,0:T(8,128)(2,1)}), bf16[4,144,512]{2,1,0:T(8,128)(2,1)S(1)}, u32[]{:S(2)}, u32[]{:S(2)}) async-start(bf16[4,144,512]{2,1,0:T(8,128)(2,1)} %add_convert_fusion.1), calls=%async_computation.5 | async-start | bytes 1179648 | tf_op jit(solution)/shard_map/all_to_all | solution.py:628
  212.1 10.5 %all-to-all-done.3 = bf16[4,144,512]{2,1,0:T(8,128)(2,1)S(1)} async-done(((bf16[4,144,512]{2,1,0:T(8,128)(2,1)}), bf16[4,144,512]{2,1,0:T(8,128)(2,1)S(1)}, u32[]{:S(2)}, u32[]{:S(2)}) %all-to-all-start.3) | async-done | bytes 589856 | tf_op jit(solution)/shard_map/all_to_all | solution.py:628
  225.8 2.0 fusion.11
  (166 shorter events, 31.7 us)
Async XLA Ops:
  7.2 52.0 %all-gather.3.cloned.1.call-start = ((), (), s32[]{:S(2)}) async-start(), calls=%async_computation.7 | async-start | bytes 1310720 | tf_op jit(solution)/shard_map/all_gather | solution.py:684
  12.0 41.9 %copy-start.11 = (bf16[4,512]{1,0:T(4,128)(2,1)S(1)}, bf16[4,512]{1,0:T(4,128)(2,1)}, u32[]{:S(2)}) copy-start(bf16[4,512]{1,0:T(4,128)(2,1)} %param.23) | copy-start | bytes 12292
  12.1 59.1 %copy-start.6 = (bf16[256,512]{1,0:T(8,128)(2,1)}, bf16[256,512]{1,0:T(8,128)(2,1)S(1)}, u32[]{:S(2)}) copy-start(bf16[256,512]{1,0:T(8,128)(2,1)S(1)} %pad_maximum_fusion.1.refs_1_) | copy-start | bytes 786436
  12.1 42.5 %copy-start.16 = (bf16[8]{0:T(256)(128)(2,1)S(1)}, bf16[8]{0:T(256)(128)(2,1)}, u32[]{:S(2)}) copy-start(bf16[8]{0:T(256)(128)(2,1)} %param.29) | copy-start | bytes 52
  12.1 43.2 %copy-start.14 = (bf16[512]{0:T(512)(128)(2,1)S(1)}, bf16[512]{0:T(512)(128)(2,1)}, u32[]{:S(2)}) copy-start(bf16[512]{0:T(512)(128)(2,1)} %param.24) | copy-start | bytes 3076
  12.1 43.8 %copy-start.15 = (bf16[512]{0:T(512)(128)(2,1)S(1)}, bf16[512]{0:T(512)(128)(2,1)}, u32[]{:S(2)}) copy-start(bf16[512]{0:T(512)(128)(2,1)} %param.30) | copy-start | bytes 3076
  12.8 8.5 %all-to-all-start = ((bf16[4,48,256]{2,1,0:T(8,128)(2,1)}), bf16[4,48,256]{2,1,0:T(8,128)(2,1)S(1)}, u32[]{:S(2)}, u32[]{:S(2)}) async-start(bf16[4,48,256]{2,1,0:T(8,128)(2,1)} %broadcast_in_dim.45), calls=%async_computation | async-start | bytes 196608 | tf_op jit(solution)/shard_map/all_to_all | solution.py:691
  17.0 42.2 %all-gather.5.cloned.1.call-start = ((), (), s32[]{:S(2)}) async-start(), calls=%async_computation.8 | async-start | bytes 1310720 | tf_op jit(solution)/shard_map/all_gather | solution.py:685
  21.3 8.2 %collective-permute-start.7 = (bf16[208,512]{1,0:T(8,128)(2,1)S(1)}, bf16[208,512]{1,0:T(8,128)(2,1)S(1)}, u32[]{:S(2)}, u32[]{:S(2)}) collective-permute-start(bf16[208,512]{1,0:T(8,128)(2,1)S(1)} %fusion.13.refs_1_), channel_id=1, source_target_pairs={{0,8},{8,16},{16,24},{24,28},{28,20},{20,12},{12,4},{4,0},{1,9},{9... | collective-permute-start | bytes 638984 | tf_op jit(solution)/shard_map/ppermute | solution.py:605
  23.5 11.7 %collective-permute-start = (bf16[256,512]{1,0:T(8,128)(2,1)S(1)}, bf16[256,512]{1,0:T(8,128)(2,1)S(1)}, u32[]{:S(2)}, u32[]{:S(2)}) collective-permute-start(bf16[256,512]{1,0:T(8,128)(2,1)S(1)} %pad_maximum_fusion.1.refs_1_), channel_id=1, source_target_pairs={{0,8},{8,16},{16,24},{24,28},{28,20},{20,12},{12,4},{4,0},{1,9},{9... | collective-permute-start | bytes 786440 | tf_op jit(solution)/shard_map/ppermute | solution.py:605
  25.1 12.1 %collective-permute-start.8 = (bf16[208,512]{1,0:T(8,128)(2,1)S(1)}, bf16[208,512]{1,0:T(8,128)(2,1)S(1)}, u32[]{:S(2)}, u32[]{:S(2)}) collective-permute-start(bf16[208,512]{1,0:T(8,128)(2,1)S(1)} %fusion.13.refs_1_), channel_id=1, source_target_pairs={{0,4},{8,0},{16,8},{24,16},{28,24},{20,28},{12,20},{4,12},{1,5},{9... | collective-permute-start | bytes 638984 | tf_op jit(solution)/shard_map/ppermute | solution.py:605
  29.5 10.2 %collective-permute-start.9 = (bf16[208,512]{1,0:T(8,128)(2,1)S(1)}, bf16[208,512]{1,0:T(8,128)(2,1)S(1)}, u32[]{:S(2)}, u32[]{:S(2)}) collective-permute-start(bf16[208,512]{1,0:T(8,128)(2,1)S(1)} %collective-permute-done.7.refs_2_), channel_id=1, source_target_pairs={{0,8},{8,16},{16,24},{24,28},{28,20},{20,12},{12,4},{4,0},{1,9},{9... | collective-permute-start | bytes 638984 | tf_op jit(solution)/shard_map/ppermute | solution.py:605
  31.7 10.2 %collective-permute-start.1 = (bf16[256,512]{1,0:T(8,128)(2,1)S(1)}, bf16[256,512]{1,0:T(8,128)(2,1)S(1)}, u32[]{:S(2)}, u32[]{:S(2)}) collective-permute-start(bf16[256,512]{1,0:T(8,128)(2,1)S(1)} %pad_maximum_fusion.1.refs_1_), channel_id=1, source_target_pairs={{0,4},{8,0},{16,8},{24,16},{28,24},{20,28},{12,20},{4,12},{1,5},{9... | collective-permute-start | bytes 786440 | tf_op jit(solution)/shard_map/ppermute | solution.py:605
  35.2 10.2 %collective-permute-start.2 = (bf16[256,512]{1,0:T(8,128)(2,1)S(1)}, bf16[256,512]{1,0:T(8,128)(2,1)S(1)}, u32[]{:S(2)}, u32[]{:S(2)}) collective-permute-start(bf16[256,512]{1,0:T(8,128)(2,1)S(1)} %collective-permute-done.refs_2_), channel_id=1, source_target_pairs={{0,8},{8,16},{16,24},{24,28},{28,20},{20,12},{12,4},{4,0},{1,9},{9... | collective-permute-start | bytes 786440 | tf_op jit(solution)/shard_map/ppermute | solution.py:605
  37.3 10.2 %collective-permute-start.10 = (bf16[208,512]{1,0:T(8,128)(2,1)S(1)}, bf16[208,512]{1,0:T(8,128)(2,1)S(1)}, u32[]{:S(2)}, u32[]{:S(2)}) collective-permute-start(bf16[208,512]{1,0:T(8,128)(2,1)S(1)} %collective-permute-done.8.refs_3_), channel_id=1, source_target_pairs={{0,4},{8,0},{16,8},{24,16},{28,24},{20,28},{12,20},{4,12},{1,5},{9... | collective-permute-start | bytes 638984 | tf_op jit(solution)/shard_map/ppermute | solution.py:605
  39.7 10.2 %collective-permute-start.11 = (bf16[208,512]{1,0:T(8,128)(2,1)S(1)}, bf16[208,512]{1,0:T(8,128)(2,1)S(1)}, u32[]{:S(2)}, u32[]{:S(2)}) collective-permute-start(bf16[208,512]{1,0:T(8,128)(2,1)S(1)} %collective-permute-done.9.refs_4_), channel_id=1, source_target_pairs={{0,8},{8,16},{16,24},{24,28},{28,20},{20,12},{12,4},{4,0},{1,9},{9... | collective-permute-start | bytes 638984 | tf_op jit(solution)/shard_map/ppermute | solution.py:605
  41.9 15.3 %collective-permute-start.3 = (bf16[256,512]{1,0:T(8,128)(2,1)S(1)}, bf16[256,512]{1,0:T(8,128)(2,1)S(1)}, u32[]{:S(2)}, u32[]{:S(2)}) collective-permute-start(bf16[256,512]{1,0:T(8,128)(2,1)S(1)} %collective-permute-done.1.refs_3_), channel_id=1, source_target_pairs={{0,4},{8,0},{16,8},{24,16},{28,24},{20,28},{12,20},{4,12},{1,5},{9... | collective-permute-start | bytes 786440 | tf_op jit(solution)/shard_map/ppermute | solution.py:605
  45.3 11.8 %collective-permute-start.4 = (bf16[256,512]{1,0:T(8,128)(2,1)S(1)}, bf16[256,512]{1,0:T(8,128)(2,1)S(1)}, u32[]{:S(2)}, u32[]{:S(2)}) collective-permute-start(bf16[256,512]{1,0:T(8,128)(2,1)S(1)} %collective-permute-done.2.refs_4_), channel_id=1, source_target_pairs={{0,8},{8,16},{16,24},{24,28},{28,20},{20,12},{12,4},{4,0},{1,9},{9... | collective-permute-start | bytes 786440 | tf_op jit(solution)/shard_map/ppermute | solution.py:605
  47.5 11.7 %collective-permute-start.12 = (bf16[208,512]{1,0:T(8,128)(2,1)S(1)}, bf16[208,512]{1,0:T(8,128)(2,1)}, u32[]{:S(2)}, u32[]{:S(2)}) collective-permute-start(bf16[208,512]{1,0:T(8,128)(2,1)S(1)} %collective-permute-done.10.refs_5_), channel_id=1, source_target_pairs={{0,4},{8,0},{16,8},{24,16},{28,24},{20,28},{12,20},{4,12},{1,5},{9... | collective-permute-start | bytes 638984 | tf_op jit(solution)/shard_map/ppermute | solution.py:605
  49.9 10.3 %collective-permute-start.13 = (bf16[208,512]{1,0:T(8,128)(2,1)S(1)}, bf16[208,512]{1,0:T(8,128)(2,1)}, u32[]{:S(2)}, u32[]{:S(2)}) collective-permute-start(bf16[208,512]{1,0:T(8,128)(2,1)S(1)} %collective-permute-done.11.refs_6_), channel_id=1, source_target_pairs={{0,8},{8,16},{16,24},{24,28},{28,20},{20,12},{12,4},{4,0},{1,9},{9... | collective-permute-start | bytes 638984 | tf_op jit(solution)/shard_map/ppermute | solution.py:605
  57.1 14.1 %collective-permute-start.5 = (bf16[256,512]{1,0:T(8,128)(2,1)S(1)}, bf16[256,512]{1,0:T(8,128)(2,1)S(1)}, u32[]{:S(2)}, u32[]{:S(2)}) collective-permute-start(bf16[256,512]{1,0:T(8,128)(2,1)S(1)} %collective-permute-done.3.refs_5_), channel_id=1, source_target_pairs={{0,4},{8,0},{16,8},{24,16},{28,24},{20,28},{12,20},{4,12},{1,5},{9... | collective-permute-start | bytes 786440 | tf_op jit(solution)/shard_map/ppermute | solution.py:605
  57.1 14.1 %collective-permute-start.6 = (bf16[256,512]{1,0:T(8,128)(2,1)S(1)}, bf16[256,512]{1,0:T(8,128)(2,1)S(1)}, u32[]{:S(2)}, u32[]{:S(2)}) collective-permute-start(bf16[256,512]{1,0:T(8,128)(2,1)S(1)} %collective-permute-done.4.refs_6_), channel_id=1, source_target_pairs={{0,8},{8,16},{16,24},{24,28},{28,20},{20,12},{12,4},{4,0},{1,9},{9... | collective-permute-start | bytes 786440 | tf_op jit(solution)/shard_map/ppermute | solution.py:605
  78.5 1.4 collective-permute-start.14
  80.6 3.7 %collective-permute-start.15 = (f32[8,512]{1,0:T(8,128)S(1)}, f32[8,512]{1,0:T(8,128)S(1)}, u32[]{:S(2)}, u32[]{:S(2)}) collective-permute-start(f32[8,512]{1,0:T(8,128)S(1)} %add.185), channel_id=1, source_target_pairs={{0,2},{1,3},{2,0},{3,1},{4,6},{5,7},{6,4},{7,5},{8,10},{9,11},{10,... | collective-permute-start | bytes 49160 | tf_op jit(solution)/shard_map/ppermute | solution.py:632
  93.8 24.6 %collective-permute-start.16 = (bf16[4,256,512]{2,1,0:T(8,128)(2,1)}, bf16[4,256,512]{2,1,0:T(8,128)(2,1)S(1)}, u32[]{:S(2)}, u32[]{:S(2)}) collective-permute-start(bf16[4,256,512]{2,1,0:T(8,128)(2,1)} %get-tuple-element.76), channel_id=1, source_target_pairs={{0,4},{4,0},{8,12},{12,8},{16,20},{20,16},{24,28},{28,24},{1,5},{5... | collective-permute-start | bytes 3145736 | tf_op jit(solution)/shard_map/ppermute | solution.py:622
  149.5 26.6 %all-to-all-start.2 = ((bf16[4,256,512]{2,1,0:T(8,128)(2,1)}), bf16[4,256,512]{2,1,0:T(8,128)(2,1)S(1)}, u32[]{:S(2)}, u32[]{:S(2)}) async-start(bf16[4,256,512]{2,1,0:T(8,128)(2,1)} %add_convert_fusion), calls=%async_computation.4 | async-start | bytes 2097152 | tf_op jit(solution)/shard_map/all_to_all | solution.py:628
  153.2 28.6 %reduce-scatter.3.cloned.1.call-start = ((), (), s32[]{:S(2)}) async-start(), calls=%async_computation.9 | async-start | bytes 1310720 | tf_op jit(solution)/shard_map/reduce_scatter | solution.py:892
  155.6 45.5 %copy-start.3 = (bf16[4,144,512]{2,1,0:T(8,128)(2,1)S(1)}, bf16[4,144,512]{2,1,0:T(8,128)(2,1)}, u32[]{:S(2)}) copy-start(bf16[4,144,512]{2,1,0:T(8,128)(2,1)} %get-tuple-element.97) | copy-start | bytes 1769476
  176.1 26.0 %all-to-all-start.1 = ((bf16[32,40,256]{2,1,0:T(8,128)(2,1)}), bf16[32,40,256]{2,1,0:T(8,128)(2,1)S(1)}, u32[]{:S(2)}, u32[]{:S(2)}) async-start(bf16[32,40,256]{2,1,0:T(8,128)(2,1)} %fusion.6), calls=%async_computation.3 | async-start | bytes 1310720 | tf_op jit(solution)/shard_map/all_to_all | solution.py:897
  178.7 45.9 %reduce-scatter.5.cloned.1.call-start = ((), (), s32[]{:S(2)}) async-start(), calls=%async_computation.10 | async-start | bytes 1310720 | tf_op jit(solution)/shard_map/reduce_scatter | solution.py:894
  178.8 22.4 %collective-permute-start.17 = (bf16[4,144,512]{2,1,0:T(8,128)(2,1)}, bf16[4,144,512]{2,1,0:T(8,128)(2,1)S(1)}, u32[]{:S(2)}, u32[]{:S(2)}) collective-permute-start(bf16[4,144,512]{2,1,0:T(8,128)(2,1)} %get-tuple-element.98), channel_id=1, source_target_pairs={{0,4},{4,0},{8,12},{12,8},{16,20},{20,16},{24,28},{28,24},{1,5},{5... | collective-permute-start | bytes 1769480 | tf_op jit(solution)/shard_map/ppermute | solution.py:622
  202.1 20.5 %all-to-all-start.3 = ((bf16[4,144,512]{2,1,0:T(8,128)(2,1)}), bf16[4,144,512]{2,1,0:T(8,128)(2,1)S(1)}, u32[]{:S(2)}, u32[]{:S(2)}) async-start(bf16[4,144,512]{2,1,0:T(8,128)(2,1)} %add_convert_fusion.1), calls=%async_computation.5 | async-start | bytes 1179648 | tf_op jit(solution)/shard_map/all_to_all | solution.py:628
  (25 other events, 393.6 us)
Sparse Core Ops, SparseCore 0:
  9.6 19.4 all-gather.2
  30.6 16.8 all-gather.4
  156.5 24.3 reduce-scatter.2
  183.5 24.8 reduce-scatter.4

commit v3 on v2

--- a/solution.py
+++ b/solution.py
@@ -92,17 +92,6 @@
         return carry
 
     lax.fori_loop(0, rows // tall, one, 0)
-
-
-def for_chunks(place_ref, give_ref, keep_ref, step):
-    side = place_ref[8]
-
-    def one(c, carry):
-        step(c, 1 - side, give_ref)
-        step(c, side, keep_ref)
-        return carry
-
-    lax.fori_loop(0, give_ref.shape[0], one, 0)
 
 
 class Block:
@@ -153,9 +142,11 @@
 
 def forward_kernel(fast, place_ref, lengths_ref, *refs):
     n_msg = 8 if fast else 4
-    rows_ref, msg_refs, refs = refs[0], refs[1 : 1 + n_msg], refs[1 + n_msg :]
+    n_rows = 4 if fast else 1
+    row_refs, msg_refs, refs = refs[:n_rows], refs[n_rows : n_rows + n_msg], refs[n_rows + n_msg :]
     (taps_ref, bias_ref, step_bias_ref, step_bias_col_ref, log_ref, log_col_ref, skip_ref) = refs[:7]
     (
+        rows_ref,
         normed_ref,
         weight_ref,
         state_weight_ref,
@@ -168,8 +159,8 @@
         act_ref,
         state_ref,
         mixed_ref,
-    ) = refs[7:19]
-    mask_ref, state_taps_ref, state_bias_ref = refs[19:]
+    ) = refs[7:20]
+    mask_ref, state_taps_ref, state_bias_ref = refs[20:]
     total = rows_ref.shape[0]
     channels = act_ref.shape[1]
     ends = ends_of(lengths_ref)
@@ -203,12 +194,14 @@
     state_taps_ref[...] = small_ref[4 : 4 + taps, :]
     state_bias_ref[...] = small_ref[4 + taps : 5 + taps, :]
 
-    def norm(at):
-        value = rows_ref[pl.ds(at, 128), :].astype(f32)
+    tall = total // n_rows
+    for member in range(n_rows):
+        at = pl.multiple_of(place_ref[8 + member] * tall, tall) if fast else 0
+        own = row_refs[member][:tall, :]
+        rows_ref[pl.ds(at, tall), :] = own
+        value = own.astype(f32)
         scale = lax.rsqrt(jnp.mean(value * value, axis=1, keepdims=True) + epsilon)
-        normed_ref[pl.ds(at, 128), :] = (value * scale * gain).astype(bf16)
-
-    row_loop(total, 128, norm)
+        normed_ref[pl.ds(at, tall), :] = (value * scale * gain).astype(bf16)
 
     raw_ref[:pad, :] = jnp.zeros((pad, channels), f32)
     state_raw_ref[:pad, :] = jnp.zeros((pad, state_raw_ref.shape[1]), f32)
@@ -266,12 +259,17 @@
 
 
 def grad_in_kernel(fast, place_ref, lengths_ref, *refs):
+    n_rows = 4 if fast else 1
     n_msg = 8 if fast else 2
-    rows_ref, msg_refs, refs = refs[0], refs[1 : 1 + n_msg], refs[1 + n_msg :]
+    row_refs, msg_refs, refs = refs[:n_rows], refs[n_rows : n_rows + n_msg], refs[n_rows + n_msg :]
     normed_ref, mixed_ref, norm_ref = refs[:3]
-    gate_weight_ref, out_weight_ref, gate_ref, grad_ref, sums_ref, wide_ref = refs[3:]
+    rows_ref, gate_weight_ref, out_weight_ref, gate_ref, grad_ref, sums_ref, wide_ref = refs[3:]
     total = rows_ref.shape[0]
     ends = ends_of(lengths_ref)
+    tall = total // n_rows
+    for member in range(n_rows):
+        at = pl.multiple_of(place_ref[8 + member] * tall, tall) if fast else 0
+        rows_ref[pl.ds(at, tall), :] = row_refs[member][-tall:, :]
     if fast:
         for slot in range(8):
             at = pl.multiple_of(place_ref[slot] * 128, 128)
@@ -301,8 +299,9 @@
 
 def norm_kernel(inner_total, place_ref, lengths_ref, *refs):
     (sums_ref, gate_ref, mixed_ref, grad_ref, norm_ref, weight_ref, rows_ref, normed_ref) = refs[:8]
-    partial_ref, give_ref, keep_ref, grad_gate_ref, grad_mixed_ref, norm_grad_ref = refs[8:14]
-    wide_ref, out_rows_ref = refs[14:]
+    chunk_refs = refs[8:16]
+    partial_ref, grad_gate_ref, grad_mixed_ref, norm_grad_ref = refs[16:20]
+    wide_ref, out_rows_ref = refs[20:]
     total, channels = gate_ref.shape
     ends = ends_of(lengths_ref)
     for at in range(0, total, 128):
@@ -333,21 +332,18 @@
 
     row_loop(total, 128, part)
 
-    tall = give_ref.shape[1] // 2
-
-    def chunk(c, side, msg_ref):
-        cols = pl.ds(pl.multiple_of((2 * c + side) * tall, tall), tall)
-        msg_ref[c, :tall, :] = mm(normed_ref[:, cols], grad_gate_ref[...], (0, 0)).astype(bf16)
-        msg_ref[c, tall:, :] = mm(rows_ref[:, cols], out_rows_ref[...], (0, 0)).astype(bf16)
-
-    for_chunks(place_ref, give_ref, keep_ref, chunk)
-
-
-def scan_back_kernel(lengths_ref, *refs):
+    tall = chunk_refs[0].shape[0] // 2
+    for slot, chunk_ref in enumerate(chunk_refs):
+        cols = pl.ds(pl.multiple_of(place_ref[slot] * tall, tall), tall)
+        chunk_ref[:tall, :] = mm(normed_ref[:, cols], grad_gate_ref[...], (0, 0)).astype(bf16)
+        chunk_ref[tall:, :] = mm(rows_ref[:, cols], out_rows_ref[...], (0, 0)).astype(bf16)
+
+
+def scan_back_kernel(first_pair, lengths_ref, *refs):
     grad_mixed_ref, act_ref, state_ref, step_col_ref, step_row_ref = refs[:5]
     step_bias_ref, step_bias_col_ref, log_ref, log_col_ref, skip_ref = refs[5:10]
     grad_act_ref, grad_state_ref, step_grad_ref, sums_ref, acc_ref = refs[10:]
-    total, channels = grad_mixed_ref.shape
+    total, own_width = grad_act_ref.shape
     states = state_ref.shape[1] // 2
     ends = ends_of(lengths_ref)
     sums_ref[...] = jnp.zeros(sums_ref.shape, f32)
@@ -372,8 +368,9 @@
         step_grad = jnp.zeros((head_rows, span), f32)
         lane = iota((span, 128), 1)
         head_row = iota((head_rows, span), 0)
-        for i in range(channels // 128):
+        for i in range(first_pair, first_pair + own_width // 128):
             cols = slice(128 * i, 128 * (i + 1))
+            own_cols = slice(128 * (i - first_pair), 128 * (i - first_pair + 1))
             pair = (2 * i, 2 * i + 1)
             x = act_ref[block.rows, cols]
             x_low = x.astype(bf16)
@@ -396,7 +393,7 @@
                 step_grad = jnp.where(head_row == h, step_here, step_grad)
                 grads.append(mm((decay * block.contact).astype(bf16), grad_low, (0, 0)))
             grad_act = wide(low_half, *grads) * step_wide + skip_ref[:, cols] * grad
-            sums_ref[2:3, cols] += jnp.sum(grad * x, axis=0, keepdims=True)
+            sums_ref[2:3, own_cols] += jnp.sum(grad * x, axis=0, keepdims=True)
             picks = jnp.where(lane_head + 2 * i == head_of, 1.0, 0.0)
             if b == 0:
                 reach = wide(low_half, *(second.from_edge(h) for h in pair))
@@ -414,7 +411,7 @@
                 in_here = mm_exact(picks, x * back, (1, 1))
                 out_sums = out_here if out_sums is None else out_sums + out_here
                 in_sums = in_here if in_sums is None else in_sums + in_here
-            grad_act_ref[block.rows, cols] = grad_act
+            grad_act_ref[block.rows, own_cols] = grad_act
         table = (acc_ref[...] * block.mask).astype(bf16)
         grad_c = mm(table, block.inputs)
         grad_b = mm(table, block.outputs, (0, 0))
@@ -449,52 +446,43 @@
     step_grad_ref[...] = step_grad
 
 
-def backward_kernel(place_ref, lengths_ref, *refs):
+def conv_back_kernel(lengths_ref, *refs):
+    act_refs, state_refs, step_refs, head_refs, refs = (
+        refs[0:2],
+        refs[2:4],
+        refs[4:6],
+        refs[6:8],
+        refs[8:],
+    )
+    raw_ref, state_raw_ref, normed_ref, small_ref, norm_grad_ref, taps_ref, bias_ref = refs[:7]
     (
-        grad_act_ref,
-        grad_state_ref,
-        step_grad_ref,
-        head_sums_ref,
-        raw_ref,
-        state_raw_ref,
-        grad_gate_ref,
-        normed_ref,
-        rows_ref,
-        gate_weight_ref,
-        weight_ref,
-        state_weight_ref,
-        step_weight_ref,
-        small_ref,
-        norm_grad_ref,
-        taps_ref,
-        bias_ref,
-    ) = refs[:17]
-    (
-        give_ref,
-        keep_ref,
+        grad_inner_ref,
+        grad_state_low_ref,
+        step_low_ref,
         state_part_ref,
-        gain_part_ref,
-        grad_normed_ref,
         inner_sums_ref,
         state_sums_ref,
-    ) = refs[17:24]
+    ) = refs[7:13]
     (
         mask_ref,
         state_taps_ref,
         state_bias_ref,
+        grad_act_ref,
+        grad_state_ref,
         pre_ref,
         state_pre_ref,
-        grad_inner_ref,
-        grad_state_low_ref,
-    ) = refs[24:]
-    total = grad_act_ref.shape[0]
+    ) = refs[13:]
+    total, channels = grad_inner_ref.shape
     ends = ends_of(lengths_ref)
     taps = taps_ref.shape[0]
+    half = channels // 2
     state_taps_ref[...] = small_ref[4 : 4 + taps, :]
     state_bias_ref[...] = small_ref[4 + taps : 5 + taps, :]
     write_masks(mask_ref, ends)
-    step_grad = step_grad_ref[...]
-    step_grad_low = step_grad.astype(bf16)
+    grad_act_ref[:, :half] = act_refs[0][...]
+    grad_act_ref[:, half:] = act_refs[1][...]
+    grad_state_ref[...] = state_refs[0][...] + state_refs[1][...]
+    step_low_ref[...] = (step_refs[0][...] + step_refs[1][...]).astype(bf16)
 
     def conv_back(x_ref, grad_ref, held_ref, out_ref, sums_ref, own_taps, own_bias):
         held_ref[total:, :] = jnp.zeros((pad, held_ref.shape[1]), f32)
@@ -523,7 +511,9 @@
 
     inner_sums_ref[...] = jnp.zeros(inner_sums_ref.shape, f32)
     inner_sums_ref[6:7, :] = norm_grad_ref[...]
-    inner_sums_ref[7:10, :] = head_sums_ref[:3, :]
+    inner_sums_ref[7:9, :half] = head_refs[0][:2, :] + head_refs[1][:2, :]
+    inner_sums_ref[9:10, :half] = head_refs[0][2:3, :]
+    inner_sums_ref[9:10, half:] = head_refs[1][2:3, :]
     state_sums_ref[...] = jnp.zeros(state_sums_ref.shape, f32)
     conv_back(
         raw_ref, grad_act_ref, pre_ref, grad_inner_ref, inner_sums_ref, taps_ref, bias_ref
@@ -538,30 +528,86 @@
         state_bias_ref,
     )
 
-    tall = give_ref.shape[1] - head_rows
-    give_ref[...] = jnp.zeros(give_ref.shape, bf16)
-    keep_ref[...] = jnp.zeros(keep_ref.shape, bf16)
-
-    def chunk(c, side, msg_ref):
-        at = pl.multiple_of((2 * c + side) * tall, tall)
-        part = normed_ref[:, pl.ds(at, tall)]
+    def chunk(at):
+        part = normed_ref[:, pl.ds(at, 256)]
+        state_part_ref[pl.ds(at, 256), :] = mm(part, grad_state_low_ref[...], (0, 0)).astype(bf16)
+
+    row_loop(normed_ref.shape[1], 256, chunk)
+
+
+def project_back_kernel(*refs):
+    (
+        grad_gate_ref,
+        grad_inner_ref,
+        grad_state_low_ref,
+        step_low_ref,
+        normed_ref,
+        rows_ref,
+        gate_weight_ref,
+        weight_ref,
+        state_weight_ref,
+        step_weight_ref,
+        msg_ref,
+        gain_part_ref,
+        grad_normed_ref,
+    ) = refs
+    total = rows_ref.shape[0]
+    tall = msg_ref.shape[1] - head_rows
+    step_low = step_low_ref[...]
+
+    def chunk(c, carry):
+        part = normed_ref[:, pl.ds(pl.multiple_of(c * tall, tall), tall)]
         msg_ref[c, :tall, :] = mm(part, grad_inner_ref[...], (0, 0)).astype(bf16)
-        msg_ref[c, tall:, :tall] = mm(step_grad_low, part).astype(bf16)
-        state_part_ref[pl.ds(at, tall), :] = mm(part, grad_state_low_ref[...], (0, 0)).astype(bf16)
-
-    for_chunks(place_ref, give_ref, keep_ref, chunk)
-    step_back = step_grad.T.astype(bf16)
+        msg_ref[c, tall:, :tall] = mm(step_low, part).astype(bf16)
+        msg_ref[c, tall:, tall:] = jnp.zeros((head_rows, msg_ref.shape[2] - tall), bf16)
+        return carry
+
+    lax.fori_loop(0, msg_ref.shape[0], chunk, 0)
     gain_part_ref[...] = jnp.zeros(gain_part_ref.shape, f32)
-    for at in range(0, total, 128):
-        rows = slice(at, at + 128)
+
+    def back(at):
+        rows = pl.ds(at, 128)
         grad = mm(grad_gate_ref[rows, :], gate_weight_ref[...], (1, 1))
         grad = grad + mm(grad_inner_ref[rows, :], weight_ref[...], (1, 1))
         grad = grad + mm(grad_state_low_ref[rows, :], state_weight_ref[...], (1, 1))
-        grad = grad + mm(step_back[rows, :], step_weight_ref[...])
+        grad = grad + mm(step_low_ref[:, rows], step_weight_ref[...], (0, 0))
         grad_normed_ref[rows, :] = grad.astype(bf16)
         value = rows_ref[rows, :].astype(f32)
         scale = lax.rsqrt(jnp.mean(value * value, axis=1, keepdims=True) + epsilon)
         gain_part_ref[...] += jnp.sum(grad * (value * scale), axis=0, keepdims=True)
+
+    row_loop(total, 128, back)
+
+
+def prepare_kernel(place_ref, *refs):
+    (gain_ref, taps_ref, bias_ref, state_ref, step_ref, input_ref, out_ref) = refs[:7]
+    shared_ref, step_rows_ref, inner_ref, late_ref = refs[7:]
+    owner = place_ref[0]
+    share, states = state_ref.shape
+    depth_part = input_ref.shape[0]
+    channels = out_ref.shape[0]
+    shared_ref[...] = jnp.zeros(shared_ref.shape, bf16)
+    shared_ref[:share, :] = state_ref[...]
+
+    def placed(value, at):
+        width = value.shape[1]
+        pick = iota((width, states), 1) - at == iota((width, states), 0)
+        return mm(value, jnp.where(pick, 1.0, 0.0).astype(bf16))
+
+    start = owner * gain_ref.shape[1]
+    gain = jnp.concatenate(
+        [placed(gain_ref[...], start - states * i) for i in range(4)]
+        + [placed(taps_ref[...], owner * taps_ref.shape[1])]
+        + [placed(bias_ref[...], owner * bias_ref.shape[1])]
+        + [jnp.zeros((7, states), f32)],
+        axis=0,
+    )
+    shared_ref[share:, :] = gain.astype(bf16)
+    step_rows_ref[...] = jnp.zeros(step_rows_ref.shape, bf16)
+    step_rows_ref[: step_ref.shape[0], :] = step_ref[...]
+    late_ref[:depth_part, :] = input_ref[:, :channels]
+    late_ref[depth_part:, :] = out_ref[...].astype(f32).T.astype(bf16)
+    inner_ref[...] = input_ref[:, channels:]
 
 
 def call(kernel, micros, scalars, arrays, outs, scratch):
@@ -618,14 +664,28 @@
     return pieces
 
 
-def side_sum(give, keep):
-    got = lax.ppermute(give, "dp", [(i, i ^ 1) for i in range(8)])
-    return (keep.astype(f32) + got.astype(f32)).astype(bf16)
-
-
-def line_blocks(half):
-    lines = [[0, 2, 4, 6], [1, 3, 5, 7]]
-    return lax.all_to_all(half, "dp", 0, 0, axis_index_groups=lines, tiled=True)
+def ring_step(held):
+    return ring_send(held[0], True), ring_send(held[1], False)
+
+
+def add_low(got, own):
+    return (got.astype(f32) + own.astype(f32)).astype(bf16)
+
+
+def ordered(first, then):
+    return lax.optimization_barrier((first, then))
+
+
+def tensor_gather(value):
+    near = tensor_swap(value, 1)
+    far = tensor_swap(value, 2)
+    return [value, near, far, tensor_swap(far, 1)]
+
+
+def tensor_sum(value, depth):
+    parts = value.reshape(4, -1, depth)
+    parts = lax.all_to_all(parts, "tensor", 0, 0, tiled=True)
+    return jnp.sum(parts.astype(f32), axis=0)
 
 
 def tensor_swap(value, bit):
@@ -664,30 +724,31 @@
     channels = input_weight.shape[2]
     inner_total = channels * n_tensor
 
-    def placed(value, whole):
-        width = value.shape[-1]
-        mine = jnp.arange(whole, dtype=jnp.int32) // width == owner
-        spread = jnp.tile(value, (1,) * (value.ndim - 1) + (whole // width,))
-        return jnp.where(mine, spread, jnp.zeros((), value.dtype))
-
-    small = jnp.concatenate(
+    input_flat = input_weight.reshape(input_weight.shape[0], -1)
+    owner_place = jnp.stack([owner, owners]).astype(jnp.int32)
+    shared, step_rows, inner_weight, late = call(
+        prepare_kernel,
+        2,
+        [owner_place],
         [
-            placed(pre_gain, depth).reshape(-1, states),
-            placed(conv_state, states),
-            placed(conv_state_bias[None], states),
+            pre_gain[None, :],
+            conv_state,
+            conv_state_bias[None, :],
+            state_weight,
+            step_weight.T,
+            input_flat,
+            output_weight,
         ],
-        axis=0,
-    )
-    small = jnp.pad(small, ((0, 16 - small.shape[0]), (0, 0)))
-    step_rows = jnp.pad(step_weight.T, ((0, head_rows - heads), (0, 0)))
-    gate_weight, inner_weight = input_weight[:, 0], input_weight[:, 1]
-    rows = lax.all_gather(tokens, "tensor", axis=0, tiled=True)
-    grad_rows = lax.all_gather(cotangent, "tensor", axis=0, tiled=True)
+        [
+            ((share + 16, states), bf16),
+            ((head_rows, step_weight.shape[0]), bf16),
+            ((input_weight.shape[0], channels), bf16),
+            ((input_weight.shape[0] + output_weight.shape[1], channels), bf16),
+        ],
+        [],
+    )
     if fast:
-        late = jnp.concatenate([gate_weight, output_weight.T], axis=0)
-        shared = jnp.concatenate([state_weight, small], axis=0)
-        late, shared = lax.optimization_barrier((late, shared))
-        late = ring_gather(late)
+        late_one = ring_step((late, late))
         shared = lax.all_to_all(
             jnp.broadcast_to(shared, (4,) + shared.shape), "tensor", 0, 0, tiled=True
         )
@@ -697,22 +758,36 @@
         beside = [
             jnp.concatenate([shared[i, :share], shared[i + 1, :share]], axis=1) for i in (0, 2)
         ]
-        msg = ring_gather(jnp.concatenate([inner_weight, *beside, tail], axis=0))
+        msg = jnp.concatenate([inner_weight, *beside, tail], axis=0)
+        late_one, msg = ordered(late_one, msg)
+        msg = ring_gather(msg)
+        late_pieces = [late, *late_one]
+        held = late_one
+        for step in range(2, 5):
+            if step < 4:
+                held = ring_step(held)
+                late_pieces += held
+            else:
+                late_pieces.append(ring_send(held[0], True))
+        row_pieces = tensor_gather(jnp.concatenate([tokens, cotangent], axis=0))
+        grad_pieces = row_pieces
         weight_pieces = [piece for piece, _ in msg]
-        late_pieces = [piece for piece, _ in late]
-        place = jnp.stack([index for _, index in msg] + [lax.axis_index("dp") % 2])
+        place = jnp.stack([index for _, index in msg] + [me, me ^ 1, me ^ 2, me ^ 3])
     else:
+        row_pieces = [lax.all_gather(tokens, "tensor", axis=0, tiled=True)]
+        grad_pieces = [lax.all_gather(cotangent, "tensor", axis=0, tiled=True)]
+        gate_weight = late[: input_weight.shape[0]]
         weight_pieces = [
             lax.all_gather(inner_weight, "dp", axis=0, tiled=True),
             lax.all_gather(state_weight, ("dp", "tensor"), axis=0, tiled=True),
             lax.all_gather(step_rows, "dp", axis=1, tiled=True),
-            lax.psum(small, ("dp", "tensor")),
+            lax.psum(shared[share:], ("dp", "tensor")),
         ]
         late_pieces = [
             lax.all_gather(gate_weight, "dp", axis=0, tiled=True),
-            lax.all_gather(output_weight.T, "dp", axis=0, tiled=True),
+            lax.all_gather(late[input_weight.shape[0] :], "dp", axis=0, tiled=True),
         ]
-        place = jnp.zeros((9,), jnp.int32)
+        place = jnp.arange(12)
     place = place.astype(jnp.int32)
 
     def row(value):
@@ -733,8 +808,8 @@
     ]
     masks = ((taps - 1, total + pad, 128), f32)
     state_taps = [((taps, states), f32), ((1, states), f32)]
-    rows, grad_rows = lax.optimization_barrier((rows, grad_rows))
     (
+        rows,
         normed,
         inner_full,
         state_full,
@@ -751,8 +826,9 @@
         functools.partial(forward_kernel, fast),
         12,
         [place, lengths],
-        [rows] + weight_pieces + scan_params,
+        row_pieces + weight_pieces + scan_params,
         [
+            ((total, depth), bf16),
             ((total, depth), bf16),
             ((depth, channels), bf16),
             ((depth, states), bf16),
@@ -769,12 +845,13 @@
         [masks] + state_taps,
     )
     norm_row = row(norm_gain)
-    gate_full, output_full, gate, grad_normalized, sums = call(
+    grad_rows, gate_full, output_full, gate, grad_normalized, sums = call(
         functools.partial(grad_in_kernel, fast),
         5,
         [place, lengths],
-        [grad_rows] + late_pieces + [normed, mixed, norm_row],
+        grad_pieces + late_pieces + [normed, mixed, norm_row],
         [
+            ((total, depth), bf16),
             ((depth, channels), bf16),
             ((depth, channels), bf16),
             ((total, channels), f32),
@@ -790,87 +867,105 @@
         sums = lax.psum(sums, "tensor")
     chunks = 8
     tall = depth // chunks
-    partial_out, gate_give, gate_keep, grad_gate, grad_mixed, norm_grad = call(
+    norm_outs = call(
         functools.partial(norm_kernel, inner_total),
         9,
         [place, lengths],
         [sums, gate, mixed, grad_normalized, norm_row, output_full, grad_rows, normed],
-        [
+        [((2 * tall, channels), bf16)] * chunks
+        + [
             ((total, depth), bf16),
-            ((chunks // 2, 2 * tall, channels), bf16),
-            ((chunks // 2, 2 * tall, channels), bf16),
             ((total, channels), bf16),
             ((total, channels), f32),
             ((1, channels), f32),
         ],
         [((total, 128), f32), ((total, channels), bf16)],
     )
-    grad_act, grad_state, step_grad, head_sums = call(
-        scan_back_kernel,
-        13,
+    gate_chunks = norm_outs[:chunks]
+    partial_out, grad_gate, grad_mixed, norm_grad = norm_outs[chunks:]
+
+    def scan_back(first_pair, grad):
+        return call(
+            functools.partial(scan_back_kernel, first_pair),
+            6,
+            [lengths],
+            [grad, act, state_act, step_col, step_row] + scan_params[2:],
+            [
+                ((total, channels // 2), f32),
+                ((total, states), f32),
+                ((head_rows, total), f32),
+                ((8, channels // 2), f32),
+            ],
+            [((span, span), f32)],
+        )
+
+    if fast:
+        got = ring_step((gate_chunks[7], gate_chunks[5]))
+        held = add_low(got[0], gate_chunks[6]), add_low(got[1], gate_chunks[3])
+    first = scan_back(0, grad_mixed)
+    if fast:
+        held, grad_mixed = ordered(held, grad_mixed)
+        got = ring_step(held)
+        held = add_low(got[0], gate_chunks[4]), add_low(got[1], gate_chunks[1])
+    second = scan_back(channels // 256, grad_mixed)
+    if fast:
+        held, raw = ordered(held, raw)
+        got = ring_step(held)
+        held, last = add_low(got[0], gate_chunks[2]), got[1]
+    backs = [part for pair in zip(first, second) for part in pair]
+    grad_inner, grad_state_low, step_low, state_part, sums, state_sums = call(
+        conv_back_kernel,
+        7,
         [lengths],
-        [grad_mixed, act, state_act, step_col, step_row] + scan_params[2:],
+        backs + [raw, state_raw, normed, small_full, norm_grad] + scan_params[:2],
         [
+            ((total, channels), bf16),
+            ((total, states), bf16),
+            ((head_rows, total), bf16),
+            ((depth, states), bf16),
+            ((16, channels), f32),
+            ((8, states), f32),
+        ],
+        [
+            masks,
+            *state_taps,
             ((total, channels), f32),
             ((total, states), f32),
-            ((head_rows, total), f32),
-            ((8, channels), f32),
+            ((total + pad, channels), f32),
+            ((total + pad, states), f32),
         ],
-        [((span, span), f32)],
     )
     if fast:
-        gate_half = side_sum(gate_give, gate_keep)
-        grad_act, gate_half = lax.optimization_barrier((grad_act, gate_half))
-        gate_blocks = line_blocks(gate_half)
-    (
-        inner_give,
-        inner_keep,
-        state_part,
-        gain_part,
-        grad_normed,
-        sums,
-        state_sums,
-    ) = call(
-        backward_kernel,
-        9,
-        [place, lengths],
+        mixed_rows = tensor_sum(partial_out, depth)
+        (held, mixed_rows), grad_inner = ordered((held, mixed_rows), grad_inner)
+        gate_out = gate_chunks[0].astype(f32) + last.astype(f32)
+        gate_out = gate_out + ring_send(held, True).astype(f32)
+    inner_msg, gain_part, grad_normed = call(
+        project_back_kernel,
+        6,
+        [],
         [
-            grad_act,
-            grad_state,
-            step_grad,
-            head_sums,
-            raw,
-            state_raw,
             grad_gate,
+            grad_inner,
+            grad_state_low,
+            step_low,
             normed,
             rows,
             gate_full,
             inner_full,
             state_full,
             step_full,
-            small_full,
-            norm_grad,
-        ]
-        + scan_params[:2],
+        ],
         [
-            ((chunks // 2, tall + head_rows, channels), bf16),
-            ((chunks // 2, tall + head_rows, channels), bf16),
-            ((depth, states), bf16),
+            ((chunks, tall + head_rows, channels), bf16),
             ((1, depth), f32),
             ((total, depth), bf16),
-            ((16, channels), f32),
-            ((8, states), f32),
         ],
-        [
-            masks,
-            *state_taps,
-            ((total + pad, channels), f32),
-            ((total + pad, states), f32),
-            ((total, channels), bf16),
-            ((total, states), bf16),
-        ],
-    )
-
+        [],
+    )
+
+    if fast:
+        inner_msg, sums = ordered(inner_msg, sums)
     token_float = tokens.astype(f32)
     gain_full = small_full[: depth // states].reshape(1, depth)
 
@@ -889,18 +984,13 @@
         axis=1,
     )
     shared_part = jnp.pad(shared_part, ((0, 0), (0, -shared_part.shape[1] % 8), (0, 0)))
-    mixed_rows = lax.psum_scatter(partial_out, "tensor", scatter_dimension=0, tiled=True)
-    grad_normed, mixed_rows = lax.optimization_barrier((grad_normed, mixed_rows))
-    grad_local = lax.psum_scatter(grad_normed, "tensor", scatter_dimension=0, tiled=True)
-    mixed_rows, grad_local = mixed_rows.astype(f32), grad_local.astype(f32)
     if fast:
         shared_mine = lax.all_to_all(shared_part, ("dp", "tensor"), 0, 0, tiled=True)
         shared_mine = jnp.sum(shared_mine.astype(f32), axis=0)
-        inner_half = side_sum(inner_give, inner_keep)
-        inner_half, gate_blocks = lax.optimization_barrier((inner_half, gate_blocks))
-        gate_out = jnp.sum(gate_blocks.astype(f32), axis=0)
         gate_grad, output_grad = gate_out[:tall], gate_out[tall:].T
-        inner_out = jnp.sum(line_blocks(inner_half).astype(f32), axis=0)
+        inner_out = lax.all_to_all(inner_msg, "dp", 0, 0, tiled=True)
+        inner_out = jnp.sum(inner_out.astype(f32), axis=0)
+        grad_local = tensor_sum(grad_normed, depth)
         inner_grad, step_grad = inner_out[:tall], inner_out[tall : tall + heads, :tall].T
         sums = lax.all_to_all(
             jnp.broadcast_to(sums, (n_dp,) + sums.shape), "dp", 0, 0, tiled=True
@@ -910,10 +1000,11 @@
         shared_mine = lax.psum_scatter(
             shared_part.astype(f32), ("dp", "tensor"), scatter_dimension=0, tiled=True
         )[0]
-        both, inner_float = (
-            jnp.stack([keep, give], axis=1).reshape((chunks,) + keep.shape[1:]).astype(f32)
-            for keep, give in ((gate_keep, gate_give), (inner_keep, inner_give))
+        mixed_rows, grad_local = (
+            lax.psum_scatter(part, "tensor", scatter_dimension=0, tiled=True).astype(f32)
+            for part in (partial_out, grad_normed)
         )
+        both, inner_float = jnp.stack(gate_chunks).astype(f32), inner_msg.astype(f32)
         gate_grad, output_grad, inner_grad = (
             lax.psum_scatter(part.reshape(depth, channels), "dp", scatter_dimension=0, tiled=True)
             for part in (both[:, :tall], both[:, tall:], inner_float[:, :tall])

time: 235 us -> 219 us (0.932)
  waiting for transfers between devices: 90.1 us -> 67.4 us
  between operations: 14.4 us -> 1.22 us
  Pallas kernels: 50.9 us -> 60.4 us
  starting transfers between devices: 36.4 us -> 45.7 us
    ppermute x2 -> x0, waiting for transfers between devices: 31.9 us -> none  [side_sum(): got = lax.ppermute(give, 'dp', [(i, i ^ 1) for i in range(8)])]
    all_to_all x1, waiting for transfers between devices: 0.01 us -> 15.5 us  [body(): lax.all_to_all(shared_part, ('dp', 'tensor'), 0, 0, tiled=True)]
    pallas_call x5 -> x8, Pallas kernels: 50.9 us -> 60.4 us  [call(): pl.pallas_call(kernel, out_shape=[jax.ShapeDtypeStruct(shape, kind) for s...]
    ppermute x14 -> x21, starting transfers between devices: 16.8 us -> 26.1 us  [ring_send(): return lax.ppermute(value, 'dp', pairs)]
    ppermute x2 -> x0, starting transfers between devices: 3.79 us -> none  [side_sum(): got = lax.ppermute(give, 'dp', [(i, i ^ 1) for i in range(8)])]
    unnamed x69 -> x72, local copies, waits for them, and re-layouts: 3.85 us -> 6.96 us
    all_to_all x2 -> x3, starting transfers between devices: 8.37 us -> 11.1 us  [the longest x2 7.56 us: tensor_sum(): parts = lax.all_to_all(parts, 'tensor', 0, 0, tiled=True)]
    ppermute x14 -> x21, waiting for transfers between devices: 16.9 us -> 14.8 us  [ring_send(): return lax.ppermute(value, 'dp', pairs)]
  transfers between devices with their start and end apart: 26 -> 31, of which waited for: 13 -> 13; matrix products, arithmetic and copies ran while one was open for 9% -> 10% of each run, Pallas kernels for 9% -> 15%
where the time goes in v3:
time: 219 us; the launch traced here: 218 us
  waiting for transfers between devices  67.4 us (31%)
  Pallas kernels  60.4 us (28%)
  starting transfers between devices  45.7 us (21%)
  local copies, waits for them, and re-layouts  17.2 us (8%)
  blocking collectives  13.4 us (6%)
  other arithmetic  12.6 us (6%)
    pallas_call x8, Pallas kernels, call(): pl.pallas_call(kernel, out_shape=[jax.ShapeDtypeStruct(shape, kind) for s...  60.4 us
    ppermute x21, starting transfers between devices, ring_send(): return lax.ppermute(value, 'dp', pairs)  26.1 us
    all_to_all x1, waiting for transfers between devices, body(): inner_out = lax.all_to_all(inner_msg, 'dp', 0, 0, tiled=True)  16.9 us
    all_to_all x1, waiting for transfers between devices, body(): lax.all_to_all(shared_part, ('dp', 'tensor'), 0, 0, tiled=True)  15.5 us
    ppermute x21, waiting for transfers between devices, ring_send(): return lax.ppermute(value, 'dp', pairs)  14.8 us
    all_to_all x1, blocking collectives, body(): lax.all_to_all(jnp.broadcast_to(sums, (n_dp,) + sums.shape), 'dp', 0, 0,...  13.4 us
    all_to_all x2, waiting for transfers between devices, tensor_sum(): parts = lax.all_to_all(parts, 'tensor', 0, 0, tiled=True)  12.5 us
    all_to_all x2, starting transfers between devices, tensor_sum(): parts = lax.all_to_all(parts, 'tensor', 0, 0, tiled=True)  7.56 us
  transfers between devices with their start and end apart: 31, of which 13 were waited for; matrix products, arithmetic and copies ran while one was open for 10% of the time, Pallas kernels for 15%

profile of v3, /device:TPU:0, one launch (start us, length us, event | category | flops | bytes accessed | tf_op | source)
XLA Modules:
  0.0 218.1 jit_solution(4018882515540095830)
XLA Ops:
  2.9 2.0 shard_map.271
  5.0 3.1 %collective-permute-start.3 = (bf16[256,512]{1,0:T(8,128)(2,1)}, bf16[256,512]{1,0:T(8,128)(2,1)S(1)}, u32[]{:S(2)}, u32[]{:S(2)}) collective-permute-start(bf16[256,512]{1,0:T(8,128)(2,1)} %get-tuple-element.81.refs_4_), channel_id=1, source_target_pairs={{0,8},{8,16},{16,24},{24,28},{28,20},{20,12},{12,4},{4,0},{1,9},{9... | collective-permute-start | bytes 786440 | tf_op jit(solution)/shard_map/ppermute | solution.py:651
  9.4 3.3 %all-to-all-start = ((bf16[4,48,256]{2,1,0:T(8,128)(2,1)}), bf16[4,48,256]{2,1,0:T(8,128)(2,1)S(1)}, u32[]{:S(2)}, u32[]{:S(2)}) async-start(bf16[4,48,256]{2,1,0:T(8,128)(2,1)} %broadcast_in_dim.34), calls=%async_computation | async-start | bytes 196608 | tf_op jit(solution)/shard_map/all_to_all | solution.py:752
  12.8 2.0 collective-permute-start.1
  14.9 2.6 %all-to-all-done = bf16[4,48,256]{2,1,0:T(8,128)(2,1)S(1)} async-done(((bf16[4,48,256]{2,1,0:T(8,128)(2,1)}), bf16[4,48,256]{2,1,0:T(8,128)(2,1)S(1)}, u32[]{:S(2)}, u32[]{:S(2)}) %all-to-all-start) | async-done | bytes 98336 | tf_op jit(solution)/shard_map/all_to_all | solution.py:752
  17.6 2.1 collective-permute-start.10
  19.7 4.6 %collective-permute-done.10.refs_5_ = bf16[208,512]{1,0:T(8,128)(2,1)S(1)} collective-permute-done((bf16[208,512]{1,0:T(8,128)(2,1)S(1)}, bf16[208,512]{1,0:T(8,128)(2,1)S(1)}, u32[]{:S(2)}, u32[]{:S(2)}) %collective-permute-start.10) | collective-permute-done | bytes 213024 | tf_op jit(solution)/shard_map/ppermute | solution.py:651
  24.3 1.8 collective-permute-start.12
  28.2 2.0 collective-permute-start.13
  30.3 2.2 %collective-permute-done.12.refs_7_ = bf16[208,512]{1,0:T(8,128)(2,1)S(1)} collective-permute-done((bf16[208,512]{1,0:T(8,128)(2,1)S(1)}, bf16[208,512]{1,0:T(8,128)(2,1)S(1)}, u32[]{:S(2)}, u32[]{:S(2)}) %collective-permute-start.12) | collective-permute-done | bytes 213024 | tf_op jit(solution)/shard_map/ppermute | solution.py:651
  32.5 1.8 collective-permute-start.14
  34.5 3.7 %collective-permute-done.5.refs_7_ = bf16[256,512]{1,0:T(8,128)(2,1)} collective-permute-done((bf16[256,512]{1,0:T(8,128)(2,1)S(1)}, bf16[256,512]{1,0:T(8,128)(2,1)}, u32[]{:S(2)}, u32[]{:S(2)}) %collective-permute-start.5) | collective-permute-done | bytes 262176 | tf_op jit(solution)/shard_map/ppermute | solution.py:651
  38.2 1.8 collective-permute-start.7
  40.3 2.5 %collective-permute-done.14.refs_9_ = bf16[208,512]{1,0:T(8,128)(2,1)} collective-permute-done((bf16[208,512]{1,0:T(8,128)(2,1)S(1)}, bf16[208,512]{1,0:T(8,128)(2,1)}, u32[]{:S(2)}, u32[]{:S(2)}) %collective-permute-start.14) | collective-permute-done | bytes 213024 | tf_op jit(solution)/shard_map/ppermute | solution.py:651
  42.8 1.8 collective-permute-start.16
  50.0 1.8 collective-permute-start.9
  53.0 11.0 %shard_map.272 = (bf16[512,1024]{1,0:T(8,128)(2,1)}, bf16[512,1024]{1,0:T(8,128)(2,1)}, bf16[1024,512]{1,0:T(8,128)(2,1)}, bf16[1024,256]{1,0:T(8,128)(2,1)}, bf...) custom-call(s32[12]{0:T(128)} %stack.66.place_ref, ...), custom_call_target="tpu_custom_call" | custom-call | flops 13200000000 | bytes 1048576 | tf_op jit(solution)/shard_map/pallas_call | solution.py:616
  64.8 7.2 %shard_map.273 = (bf16[512,1024]{1,0:T(8,128)(2,1)}, bf16[1024,512]{1,0:T(8,128)(2,1)}, bf16[1024,512]{1,0:T(8,128)(2,1)}, f32[512,512]{1,0:T(8,128)}, f32[512,512]{1,0:T(8,128)}, /*index=5*/f32[8,512]{1,0:T(8,128)}) custom-call(s32[12]{0:T(128)} %stack.66.place_ref, s32[1,4]{1,0:T(1,128)} %lengths_ref.11, bf16[256,1024]{1,0:T(8,128)(2,1)} %copy-done.11, ...), custom_call_target="tpu_custom_call" | custom-call | flops 5500000256 | bytes 1048576 | tf_op jit(solution)/shard_map/pallas_call | solution.py:616
  74.8 3.2 %collective-permute-done.18 = f32[8,512]{1,0:T(8,128)S(1)} collective-permute-done((f32[8,512]{1,0:T(8,128)S(1)}, f32[8,512]{1,0:T(8,128)S(1)}, u32[]{:S(2)}, u32[]{:S(2)}) %collective-permute-start.18) | collective-permute-done | bytes 16416 | tf_op jit(solution)/shard_map/ppermute | solution.py:692
  78.6 8.1 %shard_map.274 = (bf16[256,512]{1,0:T(8,128)(2,1)}, bf16[256,512]{1,0:T(8,128)(2,1)}, bf16[256,512]{1,0:T(8,128)(2,1)}, bf16[256,512]{1,0:T(8,128)(2,1)}, bf16[2...) custom-call(s32[12]{0:T(128)} %stack.66.place_ref, ...), custom_call_target="tpu_custom_call" | custom-call | flops 9900000256 | bytes 1048576 | tf_op jit(solution)/shard_map/pallas_call | solution.py:616
  88.8 3.7 %all-to-all-start.1 = ((bf16[4,128,1024]{2,1,0:T(8,128)(2,1)}), bf16[4,128,1024]{2,1,0:T(8,128)(2,1)S(1)}, u32[]{:S(2)}, u32[]{:S(2)}) async-start(bf16[4,128,1024]{2,1,0:T(8,128)(2,1)} %bitcast.70), calls=%async_computation.1 | async-start | bytes 2097152 | tf_op jit(solution)/shard_map/all_to_all | solution.py:687
  92.5 6.5 %shard_map.275 = (f32[512,256]{1,0:T(8,128)}, f32[512,256]{1,0:T(8,128)}, f32[16,512]{1,0:T(8,128)}, f32[8,256]{1,0:T(8,128)}) custom-call(s32[1,4]{1,0:T(1,128)} %lengths_ref.11, f32[512,512]{1,0:T(8,128)} %get-tuple-element.113.refs_0_, f32[512,512]{1,0:T(8,128)} %get-tuple-element.108.refs_1_, f32[512,256]{1,0:T(8,128)} %get-tuple-element.109.refs_2_, ...), custom_call_target="tpu_custom_call" | custom-call | flops 6600000000 | bytes 1048576 | tf_op jit(solution)/shard_map/pallas_call | solution.py:616
  101.3 6.5 %shard_map.276 = (f32[512,256]{1,0:T(8,128)}, f32[512,256]{1,0:T(8,128)}, f32[16,512]{1,0:T(8,128)}, f32[8,256]{1,0:T(8,128)}) custom-call(s32[1,4]{1,0:T(1,128)} %lengths_ref.11, f32[512,512]{1,0:T(8,128)} %get-tuple-element.113.refs_0_, f32[512,512]{1,0:T(8,128)} %get-tuple-element.108.refs_1_, f32[512,256]{1,0:T(8,128)} %get-tuple-element.109.refs_2_, ...), custom_call_target="tpu_custom_call" | custom-call | flops 6600000000 | bytes 1048576 | tf_op jit(solution)/shard_map/pallas_call | solution.py:616
  110.5 9.0 %shard_map.277 = (bf16[512,512]{1,0:T(8,128)(2,1)}, bf16[512,256]{1,0:T(8,128)(2,1)}, bf16[16,512]{1,0:T(8,128)(2,1)}, bf16[1024,256]{1,0:T(8,128)(2,1)}, f32[16,512]{1,0:T(8,128)}, /*index=5*/f32[8,256]{1,0:T(8,128)}) custom-call(s32[1,4]{1,0:T(1,128)} %lengths_ref.11, f32[512,256]{1,0:T(8,128)} %get-tuple-element.112.refs_0_, ...), custom_call_target="tpu_custom_call" | custom-call | flops 7699999744 | bytes 1048576 | tf_op jit(solution)/shard_map/pallas_call | solution.py:616
  121.3 10.1 %shard_map.278 = (bf16[8,144,512]{2,1,0:T(8,128)(2,1)}, f32[1,1024]{1,0:T(1,128)}, bf16[512,1024]{1,0:T(8,128)(2,1)}) custom-call(bf16[512,512]{1,0:T(8,128)(2,1)} %get-tuple-element.127.refs_0_, bf16[512,512]{1,0:T(8,128)(2,1)} %get-tuple-element.128.refs_1_, bf16[512,256]{1,0:T(8,128)(2,1)} %get-tuple-element.129.refs_2_, ...), custom_call_target="tpu_custom_call" | custom-call | flops 6600000000 | bytes 1048576 | tf_op jit(solution)/shard_map/pallas_call | solution.py:616
  131.4 13.4 %all_to_all.30 = f32[8,16,512]{2,1,0:T(8,128)} all-to-all(f32[8,16,512]{2,1,0:T(8,128)S(1)} %broadcast_in_dim.40), channel_id=1, replica_groups=mesh['dp'=8,'tensor'=4] {'dp'}, dimensions={0} | all-to-all | bytes 524288 | tf_op jit(solution)/shard_map/all_to_all | solution.py:995
  144.8 3.9 %all-to-all-start.2 = ((bf16[4,128,1024]{2,1,0:T(8,128)(2,1)}), bf16[4,128,1024]{2,1,0:T(8,128)(2,1)S(1)}, u32[]{:S(2)}, u32[]{:S(2)}) async-start(bf16[4,128,1024]{2,1,0:T(8,128)(2,1)} %bitcast.71), calls=%async_computation.2 | async-start | bytes 2097152 | tf_op jit(solution)/shard_map/all_to_all | solution.py:687
  150.4 12.5 %all-to-all-done.2 = bf16[4,128,1024]{2,1,0:T(8,128)(2,1)S(1)} async-done(((bf16[4,128,1024]{2,1,0:T(8,128)(2,1)}), bf16[4,128,1024]{2,1,0:T(8,128)(2,1)S(1)}, u32[]{:S(2)}, u32[]{:S(2)}) %all-to-all-start.2) | async-done | bytes 1048608 | tf_op jit(solution)/shard_map/all_to_all | solution.py:687
  162.9 2.6 %all-to-all-start.3 = ((bf16[32,40,256]{2,1,0:T(8,128)(2,1)}), bf16[32,40,256]{2,1,0:T(8,128)(2,1)S(1)}, u32[]{:S(2)}, u32[]{:S(2)}) async-start(bf16[32,40,256]{2,1,0:T(8,128)(2,1)} %fusion.6), calls=%async_computation.3 | async-start | bytes 1310720 | tf_op jit(solution)/shard_map/all_to_all | solution.py:988
  168.3 15.5 %all-to-all-done.3 = bf16[32,40,256]{2,1,0:T(8,128)(2,1)S(1)} async-done(((bf16[32,40,256]{2,1,0:T(8,128)(2,1)}), bf16[32,40,256]{2,1,0:T(8,128)(2,1)S(1)}, u32[]{:S(2)}, u32[]{:S(2)}) %all-to-all-start.3) | async-done | bytes 655392 | tf_op jit(solution)/shard_map/all_to_all | solution.py:988
  183.8 3.6 %all-to-all-start.4 = ((bf16[8,144,512]{2,1,0:T(8,128)(2,1)}), bf16[8,144,512]{2,1,0:T(8,128)(2,1)S(1)}, u32[]{:S(2)}, u32[]{:S(2)}) async-start(bf16[8,144,512]{2,1,0:T(8,128)(2,1)} %get-tuple-element.145), calls=%async_computation.4 | async-start | bytes 2359296 | tf_op jit(solution)/shard_map/all_to_all | solution.py:991
  199.1 16.9 %all-to-all-done.4 = bf16[8,144,512]{2,1,0:T(8,128)(2,1)S(1)} async-done(((bf16[8,144,512]{2,1,0:T(8,128)(2,1)}), bf16[8,144,512]{2,1,0:T(8,128)(2,1)S(1)}, u32[]{:S(2)}, u32[]{:S(2)}) %all-to-all-start.4) | async-done | bytes 1179680 | tf_op jit(solution)/shard_map/all_to_all | solution.py:991
  (172 shorter events, 44.1 us)
Async XLA Ops:
  5.0 12.6 %collective-permute-start.3 = (bf16[256,512]{1,0:T(8,128)(2,1)}, bf16[256,512]{1,0:T(8,128)(2,1)S(1)}, u32[]{:S(2)}, u32[]{:S(2)}) collective-permute-start(bf16[256,512]{1,0:T(8,128)(2,1)} %get-tuple-element.81.refs_4_), channel_id=1, source_target_pairs={{0,8},{8,16},{16,24},{24,28},{28,20},{20,12},{12,4},{4,0},{1,9},{9... | collective-permute-start | bytes 786440 | tf_op jit(solution)/shard_map/ppermute | solution.py:651
  8.0 9.5 %collective-permute-start.4 = (bf16[256,512]{1,0:T(8,128)(2,1)}, bf16[256,512]{1,0:T(8,128)(2,1)S(1)}, u32[]{:S(2)}, u32[]{:S(2)}) collective-permute-start(bf16[256,512]{1,0:T(8,128)(2,1)} %get-tuple-element.81.refs_4_), channel_id=1, source_target_pairs={{0,4},{8,0},{16,8},{24,16},{28,24},{20,28},{12,20},{4,12},{1,5},{9... | collective-permute-start | bytes 786440 | tf_op jit(solution)/shard_map/ppermute | solution.py:651
  9.4 8.0 %all-to-all-start = ((bf16[4,48,256]{2,1,0:T(8,128)(2,1)}), bf16[4,48,256]{2,1,0:T(8,128)(2,1)S(1)}, u32[]{:S(2)}, u32[]{:S(2)}) async-start(bf16[4,48,256]{2,1,0:T(8,128)(2,1)} %broadcast_in_dim.34), calls=%async_computation | async-start | bytes 196608 | tf_op jit(solution)/shard_map/all_to_all | solution.py:752
  12.8 15.4 %collective-permute-start.1 = (bf16[256,1024]{1,0:T(8,128)(2,1)S(1)}, bf16[256,1024]{1,0:T(8,128)(2,1)S(1)}, u32[]{:S(2)}, u32[]{:S(2)}) collective-permute-start(bf16[256,1024]{1,0:T(8,128)(2,1)S(1)} %constant_dynamic-update-slice_fusion.refs_0_), channel_id=1, source_target_pairs={{0,2},{1,3},{2,0},{3,1},{4,6},{5,7},{6,4},{7,5},{8,10},{9,11},{10,... | collective-permute-start | bytes 1572872 | tf_op jit(solution)/shard_map/ppermute | solution.py:692
  17.6 46.4 %copy-start.26 = (bf16[256,512]{1,0:T(8,128)(2,1)}, bf16[256,512]{1,0:T(8,128)(2,1)S(1)}, u32[]{:S(2)}) copy-start(bf16[256,512]{1,0:T(8,128)(2,1)S(1)} %collective-permute-done.3.refs_5_) | copy-start | bytes 786436
  17.6 6.7 %collective-permute-start.10 = (bf16[208,512]{1,0:T(8,128)(2,1)S(1)}, bf16[208,512]{1,0:T(8,128)(2,1)S(1)}, u32[]{:S(2)}, u32[]{:S(2)}) collective-permute-start(bf16[208,512]{1,0:T(8,128)(2,1)S(1)} %pad_maximum_fusion.1.refs_4_), channel_id=1, source_target_pairs={{0,8},{8,16},{16,24},{24,28},{28,20},{20,12},{12,4},{4,0},{1,9},{9... | collective-permute-start | bytes 638984 | tf_op jit(solution)/shard_map/ppermute | solution.py:651
  19.7 14.6 %collective-permute-start = (bf16[256,1024]{1,0:T(8,128)(2,1)S(1)}, bf16[256,1024]{1,0:T(8,128)(2,1)S(1)}, u32[]{:S(2)}, u32[]{:S(2)}) collective-permute-start(bf16[256,1024]{1,0:T(8,128)(2,1)S(1)} %constant_dynamic-update-slice_fusion.refs_0_), channel_id=1, source_target_pairs={{0,1},{1,0},{2,3},{3,2},{4,5},{5,4},{6,7},{7,6},{8,9},{9,8},{10,11... | collective-permute-start | bytes 1572872 | tf_op jit(solution)/shard_map/ppermute | solution.py:692
  19.7 8.6 %collective-permute-start.11 = (bf16[208,512]{1,0:T(8,128)(2,1)S(1)}, bf16[208,512]{1,0:T(8,128)(2,1)S(1)}, u32[]{:S(2)}, u32[]{:S(2)}) collective-permute-start(bf16[208,512]{1,0:T(8,128)(2,1)S(1)} %pad_maximum_fusion.1.refs_4_), channel_id=1, source_target_pairs={{0,4},{8,0},{16,8},{24,16},{28,24},{20,28},{12,20},{4,12},{1,5},{9... | collective-permute-start | bytes 638984 | tf_op jit(solution)/shard_map/ppermute | solution.py:651
  24.3 8.2 %collective-permute-start.12 = (bf16[208,512]{1,0:T(8,128)(2,1)S(1)}, bf16[208,512]{1,0:T(8,128)(2,1)S(1)}, u32[]{:S(2)}, u32[]{:S(2)}) collective-permute-start(bf16[208,512]{1,0:T(8,128)(2,1)S(1)} %collective-permute-done.10.refs_5_), channel_id=1, source_target_pairs={{0,8},{8,16},{16,24},{24,28},{28,20},{20,12},{12,4},{4,0},{1,9},{9... | collective-permute-start | bytes 638984 | tf_op jit(solution)/shard_map/ppermute | solution.py:651
  26.1 12.1 %collective-permute-start.5 = (bf16[256,512]{1,0:T(8,128)(2,1)S(1)}, bf16[256,512]{1,0:T(8,128)(2,1)}, u32[]{:S(2)}, u32[]{:S(2)}) collective-permute-start(bf16[256,512]{1,0:T(8,128)(2,1)S(1)} %collective-permute-done.3.refs_5_), channel_id=1, source_target_pairs={{0,8},{8,16},{16,24},{24,28},{28,20},{20,12},{12,4},{4,0},{1,9},{9... | collective-permute-start | bytes 786440 | tf_op jit(solution)/shard_map/ppermute | solution.py:651
  28.2 23.5 %collective-permute-start.2 = (bf16[256,1024]{1,0:T(8,128)(2,1)S(1)}, bf16[256,1024]{1,0:T(8,128)(2,1)S(1)}, u32[]{:S(2)}, u32[]{:S(2)}) collective-permute-start(bf16[256,1024]{1,0:T(8,128)(2,1)S(1)} %collective-permute-done.1.refs_2_), channel_id=1, source_target_pairs={{0,1},{1,0},{2,3},{3,2},{4,5},{5,4},{6,7},{7,6},{8,9},{9,8},{10,11... | collective-permute-start | bytes 1572872 | tf_op jit(solution)/shard_map/ppermute | solution.py:692
  28.2 11.8 %collective-permute-start.13 = (bf16[208,512]{1,0:T(8,128)(2,1)S(1)}, bf16[208,512]{1,0:T(8,128)(2,1)}, u32[]{:S(2)}, u32[]{:S(2)}) collective-permute-start(bf16[208,512]{1,0:T(8,128)(2,1)S(1)} %collective-permute-done.11.refs_6_), channel_id=1, source_target_pairs={{0,4},{8,0},{16,8},{24,16},{28,24},{20,28},{12,20},{4,12},{1,5},{9... | collective-permute-start | bytes 638984 | tf_op jit(solution)/shard_map/ppermute | solution.py:651
  32.5 10.3 %collective-permute-start.14 = (bf16[208,512]{1,0:T(8,128)(2,1)S(1)}, bf16[208,512]{1,0:T(8,128)(2,1)}, u32[]{:S(2)}, u32[]{:S(2)}) collective-permute-start(bf16[208,512]{1,0:T(8,128)(2,1)S(1)} %collective-permute-done.12.refs_7_), channel_id=1, source_target_pairs={{0,8},{8,16},{16,24},{24,28},{28,20},{20,12},{12,4},{4,0},{1,9},{9... | collective-permute-start | bytes 638984 | tf_op jit(solution)/shard_map/ppermute | solution.py:651
  34.3 15.4 %collective-permute-start.6 = (bf16[256,512]{1,0:T(8,128)(2,1)S(1)}, bf16[256,512]{1,0:T(8,128)(2,1)}, u32[]{:S(2)}, u32[]{:S(2)}) collective-permute-start(bf16[256,512]{1,0:T(8,128)(2,1)S(1)} %collective-permute-done.4.refs_6_), channel_id=1, source_target_pairs={{0,4},{8,0},{16,8},{24,16},{28,24},{20,28},{12,20},{4,12},{1,5},{9... | collective-permute-start | bytes 786440 | tf_op jit(solution)/shard_map/ppermute | solution.py:651
  38.2 11.7 %collective-permute-start.7 = (bf16[256,512]{1,0:T(8,128)(2,1)}, bf16[256,512]{1,0:T(8,128)(2,1)}, u32[]{:S(2)}, u32[]{:S(2)}) collective-permute-start(bf16[256,512]{1,0:T(8,128)(2,1)} %collective-permute-done.5.refs_7_), channel_id=1, source_target_pairs={{0,8},{8,16},{16,24},{24,28},{28,20},{20,12},{12,4},{4,0},{1,9},{9... | collective-permute-start | bytes 786440 | tf_op jit(solution)/shard_map/ppermute | solution.py:651
  40.0 11.7 %collective-permute-start.15 = (bf16[208,512]{1,0:T(8,128)(2,1)}, bf16[208,512]{1,0:T(8,128)(2,1)}, u32[]{:S(2)}, u32[]{:S(2)}) collective-permute-start(bf16[208,512]{1,0:T(8,128)(2,1)} %collective-permute-done.13.refs_8_), channel_id=1, source_target_pairs={{0,4},{8,0},{16,8},{24,16},{28,24},{20,28},{12,20},{4,12},{1,5},{9... | collective-permute-start | bytes 638984 | tf_op jit(solution)/shard_map/ppermute | solution.py:651
  42.8 10.2 %collective-permute-start.16 = (bf16[208,512]{1,0:T(8,128)(2,1)}, bf16[208,512]{1,0:T(8,128)(2,1)}, u32[]{:S(2)}, u32[]{:S(2)}) collective-permute-start(bf16[208,512]{1,0:T(8,128)(2,1)} %collective-permute-done.14.refs_9_), channel_id=1, source_target_pairs={{0,8},{8,16},{16,24},{24,28},{28,20},{20,12},{12,4},{4,0},{1,9},{9... | collective-permute-start | bytes 638984 | tf_op jit(solution)/shard_map/ppermute | solution.py:651
  49.7 14.3 %collective-permute-start.8 = (bf16[256,512]{1,0:T(8,128)(2,1)}, bf16[256,512]{1,0:T(8,128)(2,1)S(1)}, u32[]{:S(2)}, u32[]{:S(2)}) collective-permute-start(bf16[256,512]{1,0:T(8,128)(2,1)} %collective-permute-done.6.refs_8_), channel_id=1, source_target_pairs={{0,4},{8,0},{16,8},{24,16},{28,24},{20,28},{12,20},{4,12},{1,5},{9... | collective-permute-start | bytes 786440 | tf_op jit(solution)/shard_map/ppermute | solution.py:651
  50.0 14.1 %collective-permute-start.9 = (bf16[256,512]{1,0:T(8,128)(2,1)}, bf16[256,512]{1,0:T(8,128)(2,1)S(1)}, u32[]{:S(2)}, u32[]{:S(2)}) collective-permute-start(bf16[256,512]{1,0:T(8,128)(2,1)} %collective-permute-done.7.refs_9_), channel_id=1, source_target_pairs={{0,8},{8,16},{16,24},{24,28},{28,20},{20,12},{12,4},{4,0},{1,9},{9... | collective-permute-start | bytes 786440 | tf_op jit(solution)/shard_map/ppermute | solution.py:651
  72.1 1.5 collective-permute-start.17
  74.3 3.7 %collective-permute-start.18 = (f32[8,512]{1,0:T(8,128)S(1)}, f32[8,512]{1,0:T(8,128)S(1)}, u32[]{:S(2)}, u32[]{:S(2)}) collective-permute-start(f32[8,512]{1,0:T(8,128)S(1)} %add.174), channel_id=1, source_target_pairs={{0,2},{1,3},{2,0},{3,1},{4,6},{5,7},{6,4},{7,5},{8,10},{9,11},{10,... | collective-permute-start | bytes 49160 | tf_op jit(solution)/shard_map/ppermute | solution.py:692
  86.7 12.3 %collective-permute-start.20 = (bf16[256,512]{1,0:T(8,128)(2,1)}, bf16[256,512]{1,0:T(8,128)(2,1)S(1)}, u32[]{:S(2)}, u32[]{:S(2)}) collective-permute-start(bf16[256,512]{1,0:T(8,128)(2,1)} %get-tuple-element.97), channel_id=1, source_target_pairs={{0,4},{8,0},{16,8},{24,16},{28,24},{20,28},{12,20},{4,12},{1,5},{9... | collective-permute-start | bytes 786440 | tf_op jit(solution)/shard_map/ppermute | solution.py:651
  88.4 10.7 %collective-permute-start.19 = (bf16[256,512]{1,0:T(8,128)(2,1)}, bf16[256,512]{1,0:T(8,128)(2,1)S(1)}, u32[]{:S(2)}, u32[]{:S(2)}) collective-permute-start(bf16[256,512]{1,0:T(8,128)(2,1)} %get-tuple-element.95), channel_id=1, source_target_pairs={{0,8},{8,16},{16,24},{24,28},{28,20},{20,12},{12,4},{4,0},{1,9},{9... | collective-permute-start | bytes 786440 | tf_op jit(solution)/shard_map/ppermute | solution.py:651
  88.8 31.5 %all-to-all-start.1 = ((bf16[4,128,1024]{2,1,0:T(8,128)(2,1)}), bf16[4,128,1024]{2,1,0:T(8,128)(2,1)S(1)}, u32[]{:S(2)}, u32[]{:S(2)}) async-start(bf16[4,128,1024]{2,1,0:T(8,128)(2,1)} %bitcast.70), calls=%async_computation.1 | async-start | bytes 2097152 | tf_op jit(solution)/shard_map/all_to_all | solution.py:687
  99.2 8.6 %collective-permute-start.22 = (bf16[256,512]{1,0:T(8,128)(2,1)S(1)}, bf16[256,512]{1,0:T(8,128)(2,1)S(1)}, u32[]{:S(2)}, u32[]{:S(2)}) collective-permute-start(bf16[256,512]{1,0:T(8,128)(2,1)S(1)} %add_convert_fusion.3), channel_id=1, source_target_pairs={{0,4},{8,0},{16,8},{24,16},{28,24},{20,28},{12,20},{4,12},{1,5},{9... | collective-permute-start | bytes 786440 | tf_op jit(solution)/shard_map/ppermute | solution.py:651
  100.9 8.2 %collective-permute-start.21 = (bf16[256,512]{1,0:T(8,128)(2,1)S(1)}, bf16[256,512]{1,0:T(8,128)(2,1)S(1)}, u32[]{:S(2)}, u32[]{:S(2)}) collective-permute-start(bf16[256,512]{1,0:T(8,128)(2,1)S(1)} %add_convert_fusion.4), channel_id=1, source_target_pairs={{0,8},{8,16},{16,24},{24,28},{28,20},{20,12},{12,4},{4,0},{1,9},{9... | collective-permute-start | bytes 786440 | tf_op jit(solution)/shard_map/ppermute | solution.py:651
  109.2 10.3 %collective-permute-start.23 = (bf16[256,512]{1,0:T(8,128)(2,1)S(1)}, bf16[256,512]{1,0:T(8,128)(2,1)S(1)}, u32[]{:S(2)}, u32[]{:S(2)}) collective-permute-start(bf16[256,512]{1,0:T(8,128)(2,1)S(1)} %add_convert_fusion.2), channel_id=1, source_target_pairs={{0,8},{8,16},{16,24},{24,28},{28,20},{20,12},{12,4},{4,0},{1,9},{9... | collective-permute-start | bytes 786440 | tf_op jit(solution)/shard_map/ppermute | solution.py:651
  144.8 18.1 %all-to-all-start.2 = ((bf16[4,128,1024]{2,1,0:T(8,128)(2,1)}), bf16[4,128,1024]{2,1,0:T(8,128)(2,1)S(1)}, u32[]{:S(2)}, u32[]{:S(2)}) async-start(bf16[4,128,1024]{2,1,0:T(8,128)(2,1)} %bitcast.71), calls=%async_computation.2 | async-start | bytes 2097152 | tf_op jit(solution)/shard_map/all_to_all | solution.py:687
  162.9 20.9 %all-to-all-start.3 = ((bf16[32,40,256]{2,1,0:T(8,128)(2,1)}), bf16[32,40,256]{2,1,0:T(8,128)(2,1)S(1)}, u32[]{:S(2)}, u32[]{:S(2)}) async-start(bf16[32,40,256]{2,1,0:T(8,128)(2,1)} %fusion.6), calls=%async_computation.3 | async-start | bytes 1310720 | tf_op jit(solution)/shard_map/all_to_all | solution.py:988
  165.5 21.8 %collective-permute-start.24 = (bf16[256,512]{1,0:T(8,128)(2,1)}, bf16[256,512]{1,0:T(8,128)(2,1)}, u32[]{:S(2)}, u32[]{:S(2)}) collective-permute-start(bf16[256,512]{1,0:T(8,128)(2,1)} %add_convert_fusion.1), channel_id=1, source_target_pairs={{0,4},{8,0},{16,8},{24,16},{28,24},{20,28},{12,20},{4,12},{1,5},{9... | collective-permute-start | bytes 786440 | tf_op jit(solution)/shard_map/ppermute | solution.py:651
  167.3 20.1 %collective-permute-start.25 = (bf16[256,512]{1,0:T(8,128)(2,1)}, bf16[256,512]{1,0:T(8,128)(2,1)}, u32[]{:S(2)}, u32[]{:S(2)}) collective-permute-start(bf16[256,512]{1,0:T(8,128)(2,1)} %add_convert_fusion), channel_id=1, source_target_pairs={{0,8},{8,16},{16,24},{24,28},{28,20},{20,12},{12,4},{4,0},{1,9},{9... | collective-permute-start | bytes 786440 | tf_op jit(solution)/shard_map/ppermute | solution.py:651
  183.8 32.2 %all-to-all-start.4 = ((bf16[8,144,512]{2,1,0:T(8,128)(2,1)}), bf16[8,144,512]{2,1,0:T(8,128)(2,1)S(1)}, u32[]{:S(2)}, u32[]{:S(2)}) async-start(bf16[8,144,512]{2,1,0:T(8,128)(2,1)} %get-tuple-element.145), calls=%async_computation.4 | async-start | bytes 2359296 | tf_op jit(solution)/shard_map/all_to_all | solution.py:991
  (32 other events, 580.9 us)

commit v4 on v3

--- a/solution.py
+++ b/solution.py
@@ -144,7 +144,7 @@
     n_msg = 8 if fast else 4
     n_rows = 4 if fast else 1
     row_refs, msg_refs, refs = refs[:n_rows], refs[n_rows : n_rows + n_msg], refs[n_rows + n_msg :]
-    (taps_ref, bias_ref, step_bias_ref, step_bias_col_ref, log_ref, log_col_ref, skip_ref) = refs[:7]
+    taps_ref, bias_ref = refs[:2]
     (
         rows_ref,
         normed_ref,
@@ -158,9 +158,8 @@
         step_row_ref,
         act_ref,
         state_ref,
-        mixed_ref,
-    ) = refs[7:20]
-    mask_ref, state_taps_ref, state_bias_ref = refs[20:]
+    ) = refs[2:14]
+    mask_ref, state_taps_ref, state_bias_ref = refs[14:]
     total = rows_ref.shape[0]
     channels = act_ref.shape[1]
     ends = ends_of(lengths_ref)
@@ -175,7 +174,7 @@
             at = pl.multiple_of(index * depth_part, depth_part)
             weight_ref[pl.ds(at, depth_part), :] = msg[:depth_part, :]
             for member in range(4):
-                inner = pl.multiple_of(at + member * share, share)
+                inner = pl.multiple_of(at + place_ref[8 + member] * share, share)
                 high, low = depth_part + share * (member // 2), 256 * (member % 2)
                 state_weight_ref[pl.ds(inner, share), :] = msg[
                     high : high + share, low : low + 256
@@ -228,6 +227,12 @@
     activate(raw_ref, act_ref, taps_ref, bias_ref)
     activate(state_raw_ref, state_ref, state_taps_ref, state_bias_ref)
 
+
+def scan_kernel(lengths_ref, *refs):
+    act_ref, state_ref, step_col_ref, step_row_ref = refs[:4]
+    step_bias_ref, step_bias_col_ref, log_ref, log_col_ref, skip_ref, mixed_ref = refs[4:]
+    total, channels = act_ref.shape
+    ends = ends_of(lengths_ref)
     steps = step_sizes(
         step_col_ref[...],
         step_row_ref[...],
@@ -298,14 +303,17 @@
 
 
 def norm_kernel(inner_total, place_ref, lengths_ref, *refs):
-    (sums_ref, gate_ref, mixed_ref, grad_ref, norm_ref, weight_ref, rows_ref, normed_ref) = refs[:8]
-    chunk_refs = refs[8:16]
-    partial_ref, grad_gate_ref, grad_mixed_ref, norm_grad_ref = refs[16:20]
-    wide_ref, out_rows_ref = refs[20:]
+    n_sums = len(refs) - 21
+    sums_refs, refs = refs[:n_sums], refs[n_sums:]
+    gate_ref, mixed_ref, grad_ref, norm_ref, weight_ref, rows_ref, normed_ref = refs[:7]
+    chunk_refs = refs[7:15]
+    partial_ref, grad_gate_ref, grad_mixed_ref, norm_grad_ref = refs[15:19]
+    wide_ref, out_rows_ref = refs[19:]
     total, channels = gate_ref.shape
     ends = ends_of(lengths_ref)
     for at in range(0, total, 128):
-        tile = jnp.concatenate([sums_ref[:, at : at + 128]] * 16, axis=0)
+        tile = sum(ref[:, at : at + 128] for ref in sums_refs)
+        tile = jnp.concatenate([tile] * 16, axis=0)
         wide_ref[at : at + 128, :] = tile.T
     norm_grad_ref[...] = jnp.zeros(norm_grad_ref.shape, f32)
 
@@ -446,147 +454,162 @@
     step_grad_ref[...] = step_grad
 
 
-def conv_back_kernel(lengths_ref, *refs):
-    act_refs, state_refs, step_refs, head_refs, refs = (
-        refs[0:2],
-        refs[2:4],
-        refs[4:6],
-        refs[6:8],
-        refs[8:],
-    )
-    raw_ref, state_raw_ref, normed_ref, small_ref, norm_grad_ref, taps_ref, bias_ref = refs[:7]
-    (
-        grad_inner_ref,
-        grad_state_low_ref,
-        step_low_ref,
-        state_part_ref,
-        inner_sums_ref,
-        state_sums_ref,
-    ) = refs[7:13]
-    (
+def conv_back(x_ref, mask_ref, grad_ref, held_ref, out_ref, sums_ref, own_taps, own_bias):
+    total, taps = out_ref.shape[0], own_taps.shape[0]
+    held_ref[total:, :] = jnp.zeros((pad, held_ref.shape[1]), f32)
+
+    def column(cols):
+        sums = [jnp.zeros((1, 128), f32) for _ in range(taps + 1)]
+        for at in range(0, total, 128):
+            pre, shifted = conv_pre(x_ref, mask_ref, own_taps, own_bias, at, cols, 128)
+            sig = sigmoid(pre)
+            grad = grad_ref[at : at + 128, cols] * sig * (1.0 + pre * (1.0 - sig))
+            held_ref[at : at + 128, cols] = grad
+            for s in range(taps):
+                sums[taps - 1 - s] += jnp.sum(grad * shifted[s], axis=0, keepdims=True)
+            sums[taps] += jnp.sum(grad, axis=0, keepdims=True)
+        for t, value in enumerate(sums):
+            sums_ref[t : t + 1, cols] = value
+        for at in range(0, total, 128):
+            back = own_taps[taps - 1 : taps, cols] * held_ref[at : at + 128, cols]
+            for s in range(1, taps):
+                part = held_ref[at + s : at + s + 128, cols]
+                part = part * mask_ref[s - 1, at + s : at + s + 128, :]
+                back = back + own_taps[taps - 1 - s : taps - s, cols] * part
+            out_ref[at : at + 128, cols] = back.astype(bf16)
+
+    column_loop(out_ref.shape[1], column)
+
+
+def state_back_kernel(fast, place_ref, lengths_ref, *refs):
+    state_refs, step_refs, refs = refs[0:2], refs[2:4], refs[4:]
+    state_raw_ref, normed_ref, small_ref, grad_state_low_ref, step_low_ref = refs[:5]
+    n_out = 4 if fast else 2
+    out_refs, refs = refs[5 : 5 + n_out], refs[5 + n_out :]
+    mask_ref, taps_ref, bias_ref, grad_state_ref, pre_ref, part_ref, sums_ref = refs
+    taps = taps_ref.shape[0]
+    taps_ref[...] = small_ref[4 : 4 + taps, :]
+    bias_ref[...] = small_ref[4 + taps : 5 + taps, :]
+    write_masks(mask_ref, ends_of(lengths_ref))
+    grad_state_ref[...] = state_refs[0][...] + state_refs[1][...]
+    step_low_ref[...] = (step_refs[0][...] + step_refs[1][...]).astype(bf16)
+    sums_ref[...] = jnp.zeros(sums_ref.shape, f32)
+    conv_back(
+        state_raw_ref,
         mask_ref,
-        state_taps_ref,
-        state_bias_ref,
-        grad_act_ref,
         grad_state_ref,
         pre_ref,
-        state_pre_ref,
-    ) = refs[13:]
-    total, channels = grad_inner_ref.shape
-    ends = ends_of(lengths_ref)
-    taps = taps_ref.shape[0]
-    half = channels // 2
-    state_taps_ref[...] = small_ref[4 : 4 + taps, :]
-    state_bias_ref[...] = small_ref[4 + taps : 5 + taps, :]
-    write_masks(mask_ref, ends)
+        grad_state_low_ref,
+        sums_ref,
+        taps_ref,
+        bias_ref,
+    )
+
+    def chunk(at):
+        part = normed_ref[:, pl.ds(at, 256)]
+        part_ref[pl.ds(at, 256), :] = mm(part, grad_state_low_ref[...], (0, 0)).astype(bf16)
+
+    depth = normed_ref.shape[1]
+    row_loop(depth, 256, chunk)
+    if fast:
+        share = depth // 32
+        for member, out_ref in enumerate(out_refs):
+            for c in range(8):
+                at = pl.multiple_of((4 * c + place_ref[8 + member]) * share, share)
+                out_ref[share * c : share * (c + 1), :] = part_ref[pl.ds(at, share), :]
+            out_ref[8 * share :, :] = sums_ref[...].astype(bf16)
+    else:
+        out_refs[0][...] = part_ref[...]
+        out_refs[1][...] = sums_ref[...]
+
+
+def inner_back_kernel(lengths_ref, *refs):
+    act_refs, head_refs, refs = refs[0:2], refs[2:4], refs[4:]
+    raw_ref, norm_grad_ref, taps_ref, bias_ref, grad_inner_ref, sums_ref = refs[:6]
+    mask_ref, grad_act_ref, pre_ref = refs[6:]
+    half = grad_inner_ref.shape[1] // 2
+    write_masks(mask_ref, ends_of(lengths_ref))
     grad_act_ref[:, :half] = act_refs[0][...]
     grad_act_ref[:, half:] = act_refs[1][...]
-    grad_state_ref[...] = state_refs[0][...] + state_refs[1][...]
-    step_low_ref[...] = (step_refs[0][...] + step_refs[1][...]).astype(bf16)
-
-    def conv_back(x_ref, grad_ref, held_ref, out_ref, sums_ref, own_taps, own_bias):
-        held_ref[total:, :] = jnp.zeros((pad, held_ref.shape[1]), f32)
-
-        def column(cols):
-            sums = [jnp.zeros((1, 128), f32) for _ in range(taps + 1)]
-            for at in range(0, total, 128):
-                pre, shifted = conv_pre(x_ref, mask_ref, own_taps, own_bias, at, cols, 128)
-                sig = sigmoid(pre)
-                grad = grad_ref[at : at + 128, cols] * sig * (1.0 + pre * (1.0 - sig))
-                held_ref[at : at + 128, cols] = grad
-                for s in range(taps):
-                    sums[taps - 1 - s] += jnp.sum(grad * shifted[s], axis=0, keepdims=True)
-                sums[taps] += jnp.sum(grad, axis=0, keepdims=True)
-            for t, value in enumerate(sums):
-                sums_ref[t : t + 1, cols] = value
-            for at in range(0, total, 128):
-                back = own_taps[taps - 1 : taps, cols] * held_ref[at : at + 128, cols]
-                for s in range(1, taps):
-                    part = held_ref[at + s : at + s + 128, cols]
-                    part = part * mask_ref[s - 1, at + s : at + s + 128, :]
-                    back = back + own_taps[taps - 1 - s : taps - s, cols] * part
-                out_ref[at : at + 128, cols] = back.astype(bf16)
-
-        column_loop(out_ref.shape[1], column)
-
-    inner_sums_ref[...] = jnp.zeros(inner_sums_ref.shape, f32)
-    inner_sums_ref[6:7, :] = norm_grad_ref[...]
-    inner_sums_ref[7:9, :half] = head_refs[0][:2, :] + head_refs[1][:2, :]
-    inner_sums_ref[9:10, :half] = head_refs[0][2:3, :]
-    inner_sums_ref[9:10, half:] = head_refs[1][2:3, :]
-    state_sums_ref[...] = jnp.zeros(state_sums_ref.shape, f32)
+    sums_ref[...] = jnp.zeros(sums_ref.shape, f32)
+    sums_ref[6:7, :] = norm_grad_ref[...]
+    sums_ref[7:9, :half] = head_refs[0][:2, :] + head_refs[1][:2, :]
+    sums_ref[9:10, :half] = head_refs[0][2:3, :]
+    sums_ref[9:10, half:] = head_refs[1][2:3, :]
     conv_back(
-        raw_ref, grad_act_ref, pre_ref, grad_inner_ref, inner_sums_ref, taps_ref, bias_ref
-    )
-    conv_back(
-        state_raw_ref,
-        grad_state_ref,
-        state_pre_ref,
-        grad_state_low_ref,
-        state_sums_ref,
-        state_taps_ref,
-        state_bias_ref,
-    )
-
-    def chunk(at):
-        part = normed_ref[:, pl.ds(at, 256)]
-        state_part_ref[pl.ds(at, 256), :] = mm(part, grad_state_low_ref[...], (0, 0)).astype(bf16)
-
-    row_loop(normed_ref.shape[1], 256, chunk)
-
-
-def project_back_kernel(*refs):
+        raw_ref,
+        mask_ref,
+        grad_act_ref,
+        pre_ref,
+        grad_inner_ref,
+        sums_ref,
+        taps_ref,
+        bias_ref,
+    )
+
+
+def message_kernel(fast, *refs):
+    grad_inner_ref, step_low_ref, normed_ref = refs[:3]
+    msg_ref = refs[-1]
+    chunks = msg_ref.shape[0]
+    tall = normed_ref.shape[1] // chunks
+    step_low = step_low_ref[...]
+    tail = tall + head_rows
+
+    def chunk(c, carry):
+        part = normed_ref[:, pl.ds(pl.multiple_of(c * tall, tall), tall)]
+        msg_ref[c, :tall, :] = mm(part, grad_inner_ref[...], (0, 0)).astype(bf16)
+        msg_ref[c, tall:tail, :tall] = mm(step_low, part).astype(bf16)
+        msg_ref[c, tall:tail, tall:] = jnp.zeros((head_rows, msg_ref.shape[2] - tall), bf16)
+        return carry
+
+    lax.fori_loop(0, chunks, chunk, 0)
+    if fast:
+        sums_ref, state_refs = refs[3], refs[4:8]
+
+        def state_rows(low, high):
+            return sum(ref[low:high, :].astype(f32) for ref in state_refs)
+
+        states = state_refs[0].shape[1]
+        share = (state_refs[0].shape[0] - 16) // chunks
+        shared = state_rows(share * chunks, share * chunks + 5)
+        shared = jnp.concatenate([shared, jnp.zeros((5, states), f32)], axis=1)
+        sums = jnp.concatenate([sums_ref[:10, :], shared, jnp.zeros((1, 2 * states), f32)], axis=0)
+        sums = sums.astype(bf16)
+        for c in range(chunks):
+            low = share * c
+            part = jnp.concatenate(
+                [state_rows(low, low + 16), state_rows(low + 16, low + 32)], axis=1
+            )
+            msg_ref[c, tail : tail + 16, :] = part.astype(bf16)
+            msg_ref[c, tail + 16 :, :] = sums
+
+
+def project_back_kernel(fast, place_ref, *refs):
     (
         grad_gate_ref,
         grad_inner_ref,
         grad_state_low_ref,
         step_low_ref,
-        normed_ref,
-        rows_ref,
         gate_weight_ref,
         weight_ref,
         state_weight_ref,
         step_weight_ref,
-        msg_ref,
-        gain_part_ref,
-        grad_normed_ref,
-    ) = refs
-    total = rows_ref.shape[0]
-    tall = msg_ref.shape[1] - head_rows
-    step_low = step_low_ref[...]
-
-    def chunk(c, carry):
-        part = normed_ref[:, pl.ds(pl.multiple_of(c * tall, tall), tall)]
-        msg_ref[c, :tall, :] = mm(part, grad_inner_ref[...], (0, 0)).astype(bf16)
-        msg_ref[c, tall:, :tall] = mm(step_low, part).astype(bf16)
-        msg_ref[c, tall:, tall:] = jnp.zeros((head_rows, msg_ref.shape[2] - tall), bf16)
-        return carry
-
-    lax.fori_loop(0, msg_ref.shape[0], chunk, 0)
-    gain_part_ref[...] = jnp.zeros(gain_part_ref.shape, f32)
-
-    def back(at):
+    ) = refs[:8]
+    out_refs = refs[8:]
+    for member in range(4):
+        at = pl.multiple_of(place_ref[8 + member] * 128, 128) if fast else 128 * member
         rows = pl.ds(at, 128)
         grad = mm(grad_gate_ref[rows, :], gate_weight_ref[...], (1, 1))
         grad = grad + mm(grad_inner_ref[rows, :], weight_ref[...], (1, 1))
         grad = grad + mm(grad_state_low_ref[rows, :], state_weight_ref[...], (1, 1))
         grad = grad + mm(step_low_ref[:, rows], step_weight_ref[...], (0, 0))
-        grad_normed_ref[rows, :] = grad.astype(bf16)
-        value = rows_ref[rows, :].astype(f32)
-        scale = lax.rsqrt(jnp.mean(value * value, axis=1, keepdims=True) + epsilon)
-        gain_part_ref[...] += jnp.sum(grad * (value * scale), axis=0, keepdims=True)
-
-    row_loop(total, 128, back)
-
-
-def prepare_kernel(place_ref, *refs):
-    (gain_ref, taps_ref, bias_ref, state_ref, step_ref, input_ref, out_ref) = refs[:7]
-    shared_ref, step_rows_ref, inner_ref, late_ref = refs[7:]
+        out_refs[member % 2][member // 2] = grad.astype(bf16)
+
+
+def prepare_kernel(place_ref, gain_ref, taps_ref, bias_ref, state_ref, shared_ref):
     owner = place_ref[0]
     share, states = state_ref.shape
-    depth_part = input_ref.shape[0]
-    channels = out_ref.shape[0]
-    shared_ref[...] = jnp.zeros(shared_ref.shape, bf16)
     shared_ref[:share, :] = state_ref[...]
 
     def placed(value, at):
@@ -595,19 +618,54 @@
         return mm(value, jnp.where(pick, 1.0, 0.0).astype(bf16))
 
     start = owner * gain_ref.shape[1]
-    gain = jnp.concatenate(
+    small = jnp.concatenate(
         [placed(gain_ref[...], start - states * i) for i in range(4)]
         + [placed(taps_ref[...], owner * taps_ref.shape[1])]
         + [placed(bias_ref[...], owner * bias_ref.shape[1])]
         + [jnp.zeros((7, states), f32)],
         axis=0,
     )
-    shared_ref[share:, :] = gain.astype(bf16)
-    step_rows_ref[...] = jnp.zeros(step_rows_ref.shape, bf16)
-    step_rows_ref[: step_ref.shape[0], :] = step_ref[...]
-    late_ref[:depth_part, :] = input_ref[:, :channels]
+    shared_ref[share:, :] = small.astype(bf16)
+
+
+def prepare_late_kernel(*refs):
+    input_ref, out_ref, taps_ref, bias_ref, step_bias_ref, log_ref, skip_ref, norm_ref = refs[:8]
+    late_ref, outs = refs[8], refs[9:]
+    depth_part = input_ref.shape[0]
+    late_ref[:depth_part, :] = input_ref[:, 0, :]
     late_ref[depth_part:, :] = out_ref[...].astype(f32).T.astype(bf16)
-    inner_ref[...] = input_ref[:, channels:]
+    heads = step_bias_ref.shape[1]
+    pick = jnp.where(iota((heads, head_rows), 0) == iota((heads, head_rows), 1), 1.0, 0.0)
+    square = iota((head_rows, head_rows), 0) == iota((head_rows, head_rows), 1)
+
+    def both(value_ref, row_ref, col_ref):
+        row = mm_exact(value_ref[...].astype(f32), pick)
+        row_ref[...] = row
+        col_ref[...] = jnp.sum(jnp.where(square, row, 0.0), axis=1, keepdims=True)
+
+    outs[0][...] = taps_ref[...].astype(f32)
+    outs[1][...] = bias_ref[...].astype(f32)
+    both(step_bias_ref, outs[2], outs[3])
+    both(log_ref, outs[4], outs[5])
+    channels = norm_ref.shape[1]
+    own = iota((heads, channels), 1) // (channels // heads) == iota((heads, channels), 0)
+    outs[6][...] = mm_exact(skip_ref[...].astype(f32), jnp.where(own, 1.0, 0.0))
+    outs[7][...] = norm_ref[...].astype(f32)
+
+
+def assemble_kernel(input_ref, step_ref, *refs):
+    shared_refs, msg_ref = refs[:4], refs[4]
+    depth_part, _, channels = input_ref.shape
+    share = shared_refs[0].shape[0] - 16
+    tail = depth_part + 2 * share
+    msg_ref[:depth_part, :] = input_ref[:, 1, :]
+    for member, ref in enumerate(shared_refs):
+        high, low = depth_part + share * (member // 2), 256 * (member % 2)
+        msg_ref[high : high + share, low : low + 256] = ref[:share, :]
+    small = sum(ref[share:, :].astype(f32) for ref in shared_refs)
+    msg_ref[tail:, :256] = small.astype(bf16)
+    msg_ref[tail:, 256:384] = step_ref[...]
+    msg_ref[tail:, 384:] = jnp.zeros((16, channels - 384), bf16)
 
 
 def call(kernel, micros, scalars, arrays, outs, scratch):
@@ -664,6 +722,10 @@
     return pieces
 
 
+def dp_swap(value, bit):
+    return lax.ppermute(value, "dp", [(i, i ^ bit) for i in range(8)])
+
+
 def ring_step(held):
     return ring_send(held[0], True), ring_send(held[1], False)
 
@@ -680,6 +742,10 @@
     near = tensor_swap(value, 1)
     far = tensor_swap(value, 2)
     return [value, near, far, tensor_swap(far, 1)]
+
+
+def tensor_direct(value):
+    return [value] + [tensor_swap(value, bit) for bit in range(1, 4)]
 
 
 def tensor_sum(value, depth):
@@ -724,59 +790,68 @@
     channels = input_weight.shape[2]
     inner_total = channels * n_tensor
 
-    input_flat = input_weight.reshape(input_weight.shape[0], -1)
     owner_place = jnp.stack([owner, owners]).astype(jnp.int32)
-    shared, step_rows, inner_weight, late = call(
+    (shared,) = call(
         prepare_kernel,
+        1,
+        [owner_place],
+        [pre_gain[None, :], conv_state, conv_state_bias[None, :], state_weight],
+        [((share + 16, states), bf16)],
+        [],
+    )
+    step_rows = jnp.pad(step_weight.T, ((0, head_rows - heads), (0, 0)))
+    late, *params = call(
+        prepare_late_kernel,
         2,
-        [owner_place],
+        [],
         [
-            pre_gain[None, :],
-            conv_state,
-            conv_state_bias[None, :],
-            state_weight,
-            step_weight.T,
-            input_flat,
+            input_weight,
             output_weight,
+            conv_inner,
+            conv_inner_bias[None, :],
+            step_bias[None, :],
+            decay_log[None, :],
+            skip_gain[None, :],
+            norm_gain[None, :],
         ],
         [
-            ((share + 16, states), bf16),
-            ((head_rows, step_weight.shape[0]), bf16),
-            ((input_weight.shape[0], channels), bf16),
             ((input_weight.shape[0] + output_weight.shape[1], channels), bf16),
+            ((taps, channels), f32),
+            ((1, channels), f32),
+            ((1, head_rows), f32),
+            ((head_rows, 1), f32),
+            ((1, head_rows), f32),
+            ((head_rows, 1), f32),
+            ((1, channels), f32),
+            ((1, channels), f32),
         ],
         [],
     )
-    if fast:
+    conv_params, head_params, norm_row = params[:2], params[2:7], params[7]
+    if fast:
+        shared = tensor_direct(shared)
         late_one = ring_step((late, late))
-        shared = lax.all_to_all(
-            jnp.broadcast_to(shared, (4,) + shared.shape), "tensor", 0, 0, tiled=True
+        (msg,) = call(
+            assemble_kernel,
+            1,
+            [],
+            [input_weight, step_rows, *shared],
+            [((input_weight.shape[0] + 2 * share + 16, channels), bf16)],
+            [],
         )
-        small = shared[0, share:] + shared[1, share:] + shared[2, share:] + shared[3, share:]
-        tail = jnp.concatenate([small, step_rows], axis=1)
-        tail = jnp.pad(tail, ((0, 0), (0, channels - tail.shape[1])))
-        beside = [
-            jnp.concatenate([shared[i, :share], shared[i + 1, :share]], axis=1) for i in (0, 2)
-        ]
-        msg = jnp.concatenate([inner_weight, *beside, tail], axis=0)
         late_one, msg = ordered(late_one, msg)
         msg = ring_gather(msg)
-        late_pieces = [late, *late_one]
-        held = late_one
-        for step in range(2, 5):
-            if step < 4:
-                held = ring_step(held)
-                late_pieces += held
-            else:
-                late_pieces.append(ring_send(held[0], True))
+        weight_pieces, late_one = ordered([piece for piece, _ in msg], late_one)
+        late_two = ring_step(late_one)
+        late_three = ring_step(late_two)
+        late_pieces = [late, *late_one, *late_two, *late_three, ring_send(late_three[0], True)]
         row_pieces = tensor_gather(jnp.concatenate([tokens, cotangent], axis=0))
         grad_pieces = row_pieces
-        weight_pieces = [piece for piece, _ in msg]
         place = jnp.stack([index for _, index in msg] + [me, me ^ 1, me ^ 2, me ^ 3])
     else:
         row_pieces = [lax.all_gather(tokens, "tensor", axis=0, tiled=True)]
         grad_pieces = [lax.all_gather(cotangent, "tensor", axis=0, tiled=True)]
-        gate_weight = late[: input_weight.shape[0]]
+        gate_weight, inner_weight = late[: input_weight.shape[0]], input_weight[:, 1]
         weight_pieces = [
             lax.all_gather(inner_weight, "dp", axis=0, tiled=True),
             lax.all_gather(state_weight, ("dp", "tensor"), axis=0, tiled=True),
@@ -787,25 +862,9 @@
             lax.all_gather(gate_weight, "dp", axis=0, tiled=True),
             lax.all_gather(late[input_weight.shape[0] :], "dp", axis=0, tiled=True),
         ]
-        place = jnp.arange(12)
+        place = jnp.concatenate([jnp.arange(8), jnp.arange(4)])
     place = place.astype(jnp.int32)
 
-    def row(value):
-        return value.astype(f32).reshape(1, -1)
-
-    def head(value):
-        return jnp.pad(value.astype(f32), (0, head_rows - heads))
-
-    taps_float = conv_inner.astype(f32)
-    scan_params = [
-        taps_float,
-        row(conv_inner_bias),
-        head(step_bias)[None, :],
-        head(step_bias)[:, None],
-        head(decay_log)[None, :],
-        head(decay_log)[:, None],
-        row(jnp.repeat(skip_gain, channels // heads)),
-    ]
     masks = ((taps - 1, total + pad, 128), f32)
     state_taps = [((taps, states), f32), ((1, states), f32)]
     (
@@ -821,12 +880,11 @@
         step_row,
         act,
         state_act,
-        mixed,
     ) = call(
         functools.partial(forward_kernel, fast),
-        12,
+        6,
         [place, lengths],
-        row_pieces + weight_pieces + scan_params,
+        row_pieces + weight_pieces + conv_params,
         [
             ((total, depth), bf16),
             ((total, depth), bf16),
@@ -840,11 +898,20 @@
             ((head_rows, total), f32),
             ((total, channels), f32),
             ((total, states), f32),
-            ((total, channels), f32),
         ],
         [masks] + state_taps,
     )
-    norm_row = row(norm_gain)
+    if fast:
+        late_two, act = ordered(late_two, act)
+        late_pieces[3:5] = late_two
+    (mixed,) = call(
+        scan_kernel,
+        5,
+        [lengths],
+        [act, state_act, step_col, step_row] + head_params,
+        [((total, channels), f32)],
+        [],
+    )
     grad_rows, gate_full, output_full, gate, grad_normalized, sums = call(
         functools.partial(grad_in_kernel, fast),
         5,
@@ -861,17 +928,16 @@
         [((total, 128), f32)],
     )
     if fast:
-        sums = sums + tensor_swap(sums, 1)
-        sums = sums + tensor_swap(sums, 2)
+        sums = tensor_direct(sums)
     else:
-        sums = lax.psum(sums, "tensor")
+        sums = [lax.psum(sums, "tensor")]
     chunks = 8
     tall = depth // chunks
     norm_outs = call(
         functools.partial(norm_kernel, inner_total),
         9,
         [place, lengths],
-        [sums, gate, mixed, grad_normalized, norm_row, output_full, grad_rows, normed],
+        [*sums, gate, mixed, grad_normalized, norm_row, output_full, grad_rows, normed],
         [((2 * tall, channels), bf16)] * chunks
         + [
             ((total, depth), bf16),
@@ -889,7 +955,7 @@
             functools.partial(scan_back_kernel, first_pair),
             6,
             [lengths],
-            [grad, act, state_act, step_col, step_row] + scan_params[2:],
+            [grad, act, state_act, step_col, step_row] + head_params,
             [
                 ((total, channels // 2), f32),
                 ((total, states), f32),
@@ -909,97 +975,108 @@
         held = add_low(got[0], gate_chunks[4]), add_low(got[1], gate_chunks[1])
     second = scan_back(channels // 256, grad_mixed)
     if fast:
-        held, raw = ordered(held, raw)
+        held, state_raw = ordered(held, state_raw)
         got = ring_step(held)
         held, last = add_low(got[0], gate_chunks[2]), got[1]
-    backs = [part for pair in zip(first, second) for part in pair]
-    grad_inner, grad_state_low, step_low, state_part, sums, state_sums = call(
-        conv_back_kernel,
-        7,
-        [lengths],
-        backs + [raw, state_raw, normed, small_full, norm_grad] + scan_params[:2],
-        [
-            ((total, channels), bf16),
-            ((total, states), bf16),
-            ((head_rows, total), bf16),
-            ((depth, states), bf16),
-            ((16, channels), f32),
-            ((8, states), f32),
-        ],
+    share_rows = depth // 4 + 16
+    state_outs = call(
+        functools.partial(state_back_kernel, fast),
+        4,
+        [place, lengths],
+        [first[1], second[1], first[2], second[2], state_raw, normed, small_full],
+        [((total, states), bf16), ((head_rows, total), bf16)]
+        + (
+            [((share_rows, states), bf16)] * 4
+            if fast
+            else [((depth, states), bf16), ((16, states), f32)]
+        ),
         [
             masks,
             *state_taps,
-            ((total, channels), f32),
             ((total, states), f32),
-            ((total + pad, channels), f32),
             ((total + pad, states), f32),
+            ((depth, states), bf16),
+            ((16, states), f32),
         ],
     )
-    if fast:
-        mixed_rows = tensor_sum(partial_out, depth)
-        (held, mixed_rows), grad_inner = ordered((held, mixed_rows), grad_inner)
+    grad_state_low, step_low = state_outs[:2]
+    state_parts = state_outs[2:]
+    if fast:
+        state_parts = [state_parts[0]] + [tensor_swap(state_parts[i], i) for i in range(1, 4)]
+    if fast:
+        (held, last), raw = ordered((held, last), raw)
         gate_out = gate_chunks[0].astype(f32) + last.astype(f32)
         gate_out = gate_out + ring_send(held, True).astype(f32)
-    inner_msg, gain_part, grad_normed = call(
-        project_back_kernel,
+    grad_inner, sums = call(
+        inner_back_kernel,
         6,
+        [lengths],
+        [first[0], second[0], first[3], second[3], raw, norm_grad] + conv_params,
+        [((total, channels), bf16), ((16, channels), f32)],
+        [masks, ((total, channels), f32), ((total + pad, channels), f32)],
+    )
+    if fast:
+        mixed_rows = tensor_sum(partial_out, depth)
+        (gate_out, mixed_rows), grad_inner = ordered((gate_out, mixed_rows), grad_inner)
+    msg_rows = tall + head_rows + (32 if fast else 0)
+    (inner_msg,) = call(
+        functools.partial(message_kernel, fast),
+        5,
         [],
+        [grad_inner, step_low, normed] + ([sums, *state_parts] if fast else []),
+        [((chunks, msg_rows, channels), bf16)],
+        [],
+    )
+    if fast:
+        inner_msg, grad_inner = ordered(inner_msg, grad_inner)
+    keep_rows, give_rows = call(
+        functools.partial(project_back_kernel, fast),
+        6,
+        [place],
         [
             grad_gate,
             grad_inner,
             grad_state_low,
             step_low,
-            normed,
-            rows,
             gate_full,
             inner_full,
             state_full,
             step_full,
         ],
-        [
-            ((chunks, tall + head_rows, channels), bf16),
-            ((1, depth), f32),
-            ((total, depth), bf16),
-        ],
+        [((2, 128, depth), bf16)] * 2,
         [],
     )
 
-    if fast:
-        inner_msg, sums = ordered(inner_msg, sums)
     token_float = tokens.astype(f32)
     gain_full = small_full[: depth // states].reshape(1, depth)
 
-    def lay(value):
-        value = value.reshape(owners, -1)
-        return jnp.pad(value, ((0, 0), (0, states - value.shape[1])))[:, None, :].astype(bf16)
-
-    conv_state_owned = state_sums[:taps].reshape(taps, owners, -1).transpose(1, 0, 2)
-    shared_part = jnp.concatenate(
-        [
-            state_part.reshape(owners, share, states),
-            lay(gain_part),
-            lay(conv_state_owned),
-            lay(state_sums[taps]),
-        ],
-        axis=1,
-    )
-    shared_part = jnp.pad(shared_part, ((0, 0), (0, -shared_part.shape[1] % 8), (0, 0)))
-    if fast:
-        shared_mine = lax.all_to_all(shared_part, ("dp", "tensor"), 0, 0, tiled=True)
-        shared_mine = jnp.sum(shared_mine.astype(f32), axis=0)
+    if fast:
+        got = tensor_swap(give_rows, 1)
+        far = tensor_swap(add_low(keep_rows[1], got[1]), 2)
+        grad_local = keep_rows[0].astype(f32) + got[0].astype(f32) + far.astype(f32)
         gate_grad, output_grad = gate_out[:tall], gate_out[tall:].T
         inner_out = lax.all_to_all(inner_msg, "dp", 0, 0, tiled=True)
         inner_out = jnp.sum(inner_out.astype(f32), axis=0)
-        grad_local = tensor_sum(grad_normed, depth)
+        tail = tall + head_rows
+        state_grad = inner_out[tail : tail + 16]
+        state_grad = jnp.concatenate([state_grad[:, :states], state_grad[:, states:]], axis=0)
+        sums = inner_out[tail + 16 :]
+        width = states // owners
+        conv_state_sum = lax.dynamic_slice(
+            sums, (10, owner * width), (taps + 1, width)
+        )
+        conv_state_grad, conv_state_bias_grad = conv_state_sum[:taps], conv_state_sum[taps]
         inner_grad, step_grad = inner_out[:tall], inner_out[tall : tall + heads, :tall].T
-        sums = lax.all_to_all(
-            jnp.broadcast_to(sums, (n_dp,) + sums.shape), "dp", 0, 0, tiled=True
+    else:
+        state_part, state_sums = state_parts
+        state_grad = lax.psum_scatter(
+            state_part.astype(f32), ("dp", "tensor"), scatter_dimension=0, tiled=True
         )
-        sums = jnp.sum(sums, axis=0)
-    else:
-        shared_mine = lax.psum_scatter(
-            shared_part.astype(f32), ("dp", "tensor"), scatter_dimension=0, tiled=True
-        )[0]
+        conv_state_sum = lax.psum_scatter(
+            state_sums[: taps + 1], ("dp", "tensor"), scatter_dimension=1, tiled=True
+        )
+        conv_state_grad, conv_state_bias_grad = conv_state_sum[:taps], conv_state_sum[taps]
+        grad_normed = jnp.stack([keep_rows, give_rows], axis=1).reshape(total, depth)
         mixed_rows, grad_local = (
             lax.psum_scatter(part, "tensor", scatter_dimension=0, tiled=True).astype(f32)
             for part in (partial_out, grad_normed)
@@ -1015,6 +1092,15 @@
         step_grad = lax.psum_scatter(step_part, "dp", scatter_dimension=0, tiled=True)
         sums = lax.psum(sums, "dp")
     input_grad = jnp.stack([gate_grad, inner_grad], axis=1)
+    own_gain = jnp.sum(input_weight.astype(f32) * input_grad, axis=(1, 2))
+    own_gain = own_gain + jnp.sum(step_weight.astype(f32) * step_grad, axis=1)
+    state_gain = jnp.sum(state_weight.astype(f32) * state_grad, axis=1)
+    if fast:
+        own_gain = sum(tensor_direct(own_gain))
+        own_gain = lax.dynamic_slice(own_gain, (me * share,), (share,))
+    else:
+        own_gain = lax.psum_scatter(own_gain, "tensor", scatter_dimension=0, tiled=True)
+    pre_gain_grad = (own_gain + state_gain) / pre_gain.astype(f32)
     block_out = (token_float + mixed_rows).astype(bf16)
     scale = lax.rsqrt(jnp.mean(token_float * token_float, axis=1, keepdims=True) + epsilon)
     grad_scaled = grad_local * gain_full
@@ -1024,11 +1110,6 @@
         - token_float * (scale * scale * scale * along)
         + cotangent.astype(f32)
     )
-    state_grad = shared_mine[:share]
-    pre_gain_grad = shared_mine[share, : depth // owners]
-    conv_state_grad = shared_mine[share + 1, : taps * (states // owners)].reshape(taps, -1)
-    conv_state_bias_grad = shared_mine[share + 2, : states // owners]
-
     skip_grad = sums[9].reshape(heads, -1).sum(axis=1)
     return (
         block_out,

time: 219 us -> 190 us (0.87)
  waiting for transfers between devices: 67.4 us -> 47.8 us
  blocking collectives: 13.4 us -> 0 us
  Pallas kernels: 60.4 us -> 72.3 us
  other arithmetic: 12.6 us -> 9.34 us
    all_to_all x2 -> x0, waiting for transfers between devices: 18.1 us -> none  [the longest x1 15.5 us: body(): lax.all_to_all(shared_part, ('dp', 'tensor'), 0, 0, tiled=True)]
    all_to_all x1 -> x0, blocking collectives: 13.4 us -> none  [body(): lax.all_to_all(jnp.broadcast_to(sums, (n_dp,) + sums.shape), 'dp', 0, 0,...]
    all_to_all x2 -> x1, waiting for transfers between devices: 12.5 us -> 0.01 us  [tensor_sum(): parts = lax.all_to_all(parts, 'tensor', 0, 0, tiled=True)]
    pallas_call x8 -> x13, Pallas kernels: 60.4 us -> 72.3 us  [call(): pl.pallas_call(kernel, out_shape=[jax.ShapeDtypeStruct(shape, kind) for s...]
    ppermute x21, waiting for transfers between devices: 14.8 us -> 25.7 us  [ring_send(): return lax.ppermute(value, 'dp', pairs)]
    ppermute x5 -> x17, starting transfers between devices: 2.62 us -> 11.4 us  [tensor_swap(): return lax.ppermute(value, 'tensor', [(i, i ^ bit) for i in range(4)])]
    all_to_all x2 -> x0, starting transfers between devices: 5.92 us -> none  [the longest x1 3.3 us: body(): lax.all_to_all(jnp.broadcast_to(shared, (4,) + shared.shape), 'tensor', 0...]
    ppermute x5 -> x17, waiting for transfers between devices: 5.15 us -> 10.8 us  [tensor_swap(): return lax.ppermute(value, 'tensor', [(i, i ^ bit) for i in range(4)])]
  transfers between devices with their start and end apart: 31 -> 40, of which waited for: 13 -> 16; matrix products, arithmetic and copies ran while one was open for 10% -> 8% of each run, Pallas kernels for 15% -> 26%
where the time goes in v4:
time: 190 us; the launch traced here: 189 us
  Pallas kernels  72.3 us (38%)
  waiting for transfers between devices  47.8 us (25%)
  starting transfers between devices  43.6 us (23%)
  local copies, waits for them, and re-layouts  15.1 us (8%)
  other arithmetic  9.34 us (5%)
    pallas_call x13, Pallas kernels, call(): pl.pallas_call(kernel, out_shape=[jax.ShapeDtypeStruct(shape, kind) for s...  72.3 us
    ppermute x21, waiting for transfers between devices, ring_send(): return lax.ppermute(value, 'dp', pairs)  25.7 us
    ppermute x21, starting transfers between devices, ring_send(): return lax.ppermute(value, 'dp', pairs)  23.2 us
    ppermute x17, starting transfers between devices, tensor_swap(): return lax.ppermute(value, 'tensor', [(i, i ^ bit) for i in range(4)])  11.4 us
    all_to_all x1, waiting for transfers between devices, body(): inner_out = lax.all_to_all(inner_msg, 'dp', 0, 0, tiled=True)  11.2 us
    ppermute x17, waiting for transfers between devices, tensor_swap(): return lax.ppermute(value, 'tensor', [(i, i ^ bit) for i in range(4)])  10.8 us
    unnamed x83, local copies, waits for them, and re-layouts  8 us
    all_to_all x1, starting transfers between devices, body(): inner_out = lax.all_to_all(inner_msg, 'dp', 0, 0, tiled=True)  5.32 us
  transfers between devices with their start and end apart: 40, of which 16 were waited for; matrix products, arithmetic and copies ran while one was open for 8% of the time, Pallas kernels for 26%

profile of v4, /device:TPU:0, one launch (start us, length us, event | category | flops | bytes accessed | tf_op | source)
XLA Modules:
  0.0 189.2 jit_solution(10046982427369803322)
XLA Ops:
  3.2 2.3 %shard_map.271 = (bf16[256,512]{1,0:T(8,128)(2,1)}, f32[4,512]{1,0:T(4,128)}, f32[1,512]{1,0:T(1,128)}, f32[1,16]{1,0:T(1,128)}, f32[16,1]{1,0:T(8,128)}, /*inde...) custom-call(bf16[128,2,512]{2,1,0:T(2,128)(2,1)} %input_ref.1, bf16[512,128]{1,0:T(8,128)(2,1)} %refs_1_.1, ...), custom_call_target="tpu_custom_call" | custom-call | flops 2200000000 | bytes 1048576 | tf_op jit(solution)/shard_map/pallas_call | solution.py:674
  5.4 3.1 %collective-permute-start.3 = (bf16[256,512]{1,0:T(8,128)(2,1)}, bf16[256,512]{1,0:T(8,128)(2,1)S(1)}, u32[]{:S(2)}, u32[]{:S(2)}) collective-permute-start(bf16[256,512]{1,0:T(8,128)(2,1)} %get-tuple-element.101.refs_4_), channel_id=1, source_target_pairs={{0,8},{8,16},{16,24},{24,28},{28,20},{20,12},{12,4},{4,0},{1,9},{9... | collective-permute-start | bytes 786440 | tf_op jit(solution)/shard_map/ppermute | solution.py:709
  10.7 1.9 %collective-permute-start.6 = (bf16[48,256]{1,0:T(8,128)(2,1)}, bf16[48,256]{1,0:T(8,128)(2,1)S(1)}, u32[]{:S(2)}, u32[]{:S(2)}) collective-permute-start(bf16[48,256]{1,0:T(8,128)(2,1)} %shard_map.272.refs_0_), channel_id=1, source_target_pairs={{0,2},{1,3},{2,0},{3,1},{4,6},{5,7},{6,4},{7,5},{8,10},{9,11},{10,... | collective-permute-start | bytes 73736 | tf_op jit(solution)/shard_map/ppermute | solution.py:758
  16.7 2.0 %shard_map.273.refs_4_ = bf16[208,512]{1,0:T(8,128)(2,1)} custom-call(bf16[128,2,512]{2,1,0:T(2,128)(2,1)} %input_ref.1, bf16[16,128]{1,0:T(8,128)(2,1)} %pad.4.step_ref, bf16[48,256]{1,0:T(8,128)(2,1)} %shard_map.272.refs_0_, bf16[48,256]{1,0:T(8,128)(2,1)} %copy-done.33, bf16[48,256]{1,0:T(8,128)(2,1)} %copy-done.34, bf16[48,256]{1,0:T(8,128)(2,1)} %copy-done.35), custom_call_target="tpu_custom_call" | custom-call | flops 1100000000 | bytes 1048576 | tf_op jit(solution)/shard_map/pallas_call | solution.py:674
  22.1 4.5 %collective-permute-done.8.refs_5_ = bf16[208,512]{1,0:T(8,128)(2,1)S(1)} collective-permute-done((bf16[208,512]{1,0:T(8,128)(2,1)}, bf16[208,512]{1,0:T(8,128)(2,1)S(1)}, u32[]{:S(2)}, u32[]{:S(2)}) %collective-permute-start.8) | collective-permute-done | bytes 213024 | tf_op jit(solution)/shard_map/ppermute | solution.py:709
  28.7 4.8 %collective-permute-done.10.refs_7_ = bf16[208,512]{1,0:T(8,128)(2,1)S(1)} collective-permute-done((bf16[208,512]{1,0:T(8,128)(2,1)S(1)}, bf16[208,512]{1,0:T(8,128)(2,1)S(1)}, u32[]{:S(2)}, u32[]{:S(2)}) %collective-permute-start.10) | collective-permute-done | bytes 213024 | tf_op jit(solution)/shard_map/ppermute | solution.py:709
  36.1 3.5 %collective-permute-done.12.refs_9_ = bf16[208,512]{1,0:T(8,128)(2,1)S(1)} collective-permute-done((bf16[208,512]{1,0:T(8,128)(2,1)S(1)}, bf16[208,512]{1,0:T(8,128)(2,1)S(1)}, u32[]{:S(2)}, u32[]{:S(2)}) %collective-permute-start.12) | collective-permute-done | bytes 213024 | tf_op jit(solution)/shard_map/ppermute | solution.py:709
  41.1 1.7 collective-permute-done.13.refs_10_
  42.8 2.6 %collective-permute-done.14.refs_11_ = bf16[208,512]{1,0:T(8,128)(2,1)S(1)} collective-permute-done((bf16[208,512]{1,0:T(8,128)(2,1)S(1)}, bf16[208,512]{1,0:T(8,128)(2,1)S(1)}, u32[]{:S(2)}, u32[]{:S(2)}) %collective-permute-start.14) | collective-permute-done | bytes 213024 | tf_op jit(solution)/shard_map/ppermute | solution.py:709
  48.8 4.8 %collective-permute-done.15.refs_7_ = bf16[256,512]{1,0:T(8,128)(2,1)S(1)} collective-permute-done((bf16[256,512]{1,0:T(8,128)(2,1)S(1)}, bf16[256,512]{1,0:T(8,128)(2,1)S(1)}, u32[]{:S(2)}, u32[]{:S(2)}) %collective-permute-start.15) | collective-permute-done | bytes 262176 | tf_op jit(solution)/shard_map/ppermute | solution.py:709
  56.1 9.6 %shard_map.274 = (bf16[512,1024]{1,0:T(8,128)(2,1)}, bf16[512,1024]{1,0:T(8,128)(2,1)}, bf16[1024,512]{1,0:T(8,128)(2,1)}, bf16[1024,256]{1,0:T(8,128)(2,1)}, bf...) custom-call(s32[12]{0:T(128)} %stack.66.place_ref, ...), custom_call_target="tpu_custom_call" | custom-call | flops 6600000000 | bytes 1048576 | tf_op jit(solution)/shard_map/pallas_call | solution.py:674
  67.8 5.5 %shard_map.275.refs_13_.refs_5_ = f32[512,512]{1,0:T(8,128)} custom-call(s32[1,4]{1,0:T(1,128)} %lengths_ref.15, f32[512,512]{1,0:T(8,128)} %get-tuple-element.121.refs_0_.refs_1_, f32[512,256]{1,0:T(8,128)} %get-tuple-element.122.refs_1_.refs_2_, f32[512,16]{1,0:T(8,128)} %get-tuple-element.123.refs_2_.refs_3_, ...), custom_call_target="tpu_custom_call" | custom-call | flops 5500000256 | bytes 1048576 | tf_op jit(solution)/shard_map/pallas_call | solution.py:674
  74.2 7.3 %shard_map.276 = (bf16[512,1024]{1,0:T(8,128)(2,1)}, bf16[1024,512]{1,0:T(8,128)(2,1)}, bf16[1024,512]{1,0:T(8,128)(2,1)}, f32[512,512]{1,0:T(8,128)}, f32[512,512]{1,0:T(8,128)}, /*index=5*/f32[8,512]{1,0:T(8,128)}) custom-call(s32[12]{0:T(128)} %stack.66.place_ref, s32[1,4]{1,0:T(1,128)} %lengths_ref.15, bf16[256,1024]{1,0:T(8,128)(2,1)} %copy-done.11, ...), custom_call_target="tpu_custom_call" | custom-call | flops 5500000256 | bytes 1048576 | tf_op jit(solution)/shard_map/pallas_call | solution.py:674
  83.4 2.3 %collective-permute-done.21.refs_2_ = f32[8,512]{1,0:T(8,128)S(1)} collective-permute-done((f32[8,512]{1,0:T(8,128)}, f32[8,512]{1,0:T(8,128)S(1)}, u32[]{:S(2)}, u32[]{:S(2)}) %collective-permute-start.21) | collective-permute-done | bytes 16416 | tf_op jit(solution)/shard_map/ppermute | solution.py:758
  86.3 8.3 %shard_map.277 = (bf16[256,512]{1,0:T(8,128)(2,1)}, bf16[256,512]{1,0:T(8,128)(2,1)}, bf16[256,512]{1,0:T(8,128)(2,1)}, bf16[256,512]{1,0:T(8,128)(2,1)}, bf16[2...) custom-call(s32[12]{0:T(128)} %stack.66.place_ref, ...), custom_call_target="tpu_custom_call" | custom-call | flops 9900000256 | bytes 1048576 | tf_op jit(solution)/shard_map/pallas_call | solution.py:674
  96.7 6.4 %shard_map.278 = (f32[512,256]{1,0:T(8,128)}, f32[512,256]{1,0:T(8,128)}, f32[16,512]{1,0:T(8,128)}, f32[8,256]{1,0:T(8,128)}) custom-call(s32[1,4]{1,0:T(1,128)} %lengths_ref.15, f32[512,512]{1,0:T(8,128)} %get-tuple-element.155.refs_0_, f32[512,512]{1,0:T(8,128)} %get-tuple-element.121.refs_0_.refs_1_, f32[512,256]{1,0:T(8,128)} %get-tuple-element.122.refs_1_.refs_2_, ...), custom_call_target="tpu_custom_call" | custom-call | flops 6600000000 | bytes 1048576 | tf_op jit(solution)/shard_map/pallas_call | solution.py:674
  103.2 3.7 %all-to-all-start = ((bf16[4,128,1024]{2,1,0:T(8,128)(2,1)}), bf16[4,128,1024]{2,1,0:T(8,128)(2,1)S(1)}, u32[]{:S(2)}, u32[]{:S(2)}) async-start(bf16[4,128,1024]{2,1,0:T(8,128)(2,1)} %bitcast.19), calls=%async_computation | async-start | bytes 2097152 | tf_op jit(solution)/shard_map/all_to_all | solution.py:753
  109.1 6.5 %shard_map.279 = (f32[512,256]{1,0:T(8,128)}, f32[512,256]{1,0:T(8,128)}, f32[16,512]{1,0:T(8,128)}, f32[8,256]{1,0:T(8,128)}) custom-call(s32[1,4]{1,0:T(1,128)} %lengths_ref.15, f32[512,512]{1,0:T(8,128)} %get-tuple-element.155.refs_0_, f32[512,512]{1,0:T(8,128)} %get-tuple-element.121.refs_0_.refs_1_, f32[512,256]{1,0:T(8,128)} %get-tuple-element.122.refs_1_.refs_2_, ...), custom_call_target="tpu_custom_call" | custom-call | flops 6600000000 | bytes 1048576 | tf_op jit(solution)/shard_map/pallas_call | solution.py:674
  119.2 5.7 %shard_map.281 = (bf16[512,256]{1,0:T(8,128)(2,1)}, bf16[16,512]{1,0:T(8,128)(2,1)}, bf16[272,256]{1,0:T(8,128)(2,1)}, bf16[272,256]{1,0:T(8,128)(2,1)}, bf16[27...) custom-call(s32[12]{0:T(128)} %stack.66.place_ref, s32[1,4]{1,0:T(1,128)} %lengths_ref.15, ...), custom_call_target="tpu_custom_call" | custom-call | flops 4400000000 | bytes 1048576 | tf_op jit(solution)/shard_map/pallas_call | solution.py:674
  124.9 1.7 collective-permute-start.31
  127.7 5.6 %shard_map.280 = (bf16[512,512]{1,0:T(8,128)(2,1)}, f32[16,512]{1,0:T(8,128)}) custom-call(s32[1,4]{1,0:T(1,128)} %lengths_ref.15, f32[512,256]{1,0:T(8,128)} %get-tuple-element.154.refs_0_, f32[512,256]{1,0:T(8,128)} %get-tuple-element.156.refs_1_, f32[8,256]{1,0:T(8,128)} %get-tuple-element.157.refs_2_, f32[8,256]{1,0:T(8,128)} %get-tuple-element.158.refs_3_, ...), custom_call_target="tpu_custom_call" | custom-call | flops 6600000000 | bytes 1048576 | tf_op jit(solution)/shard_map/pallas_call | solution.py:674
  133.5 2.1 %collective-permute-done.29 = bf16[256,512]{1,0:T(8,128)(2,1)S(1)} collective-permute-done((bf16[256,512]{1,0:T(8,128)(2,1)S(1)}, bf16[256,512]{1,0:T(8,128)(2,1)S(1)}, u32[]{:S(2)}, u32[]{:S(2)}) %collective-permute-start.29) | collective-permute-done | bytes 262176 | tf_op jit(solution)/shard_map/ppermute | solution.py:709
  136.4 5.0 %shard_map.282 = bf16[8,176,512]{2,1,0:T(8,128)(2,1)} custom-call(bf16[512,512]{1,0:T(8,128)(2,1)} %get-tuple-element.177.refs_0_.refs_1_, bf16[16,512]{1,0:T(8,128)(2,1)} %get-tuple-element.171.refs_1_.refs_3_, bf16[512,1024]{1,0:T(8,128)(2,1)} %get-tuple-element.120.refs_12_.refs_10_.refs_5_.refs_2_, f32[16,512]{1,0:T(8,128)} %get-tuple-element.172.refs_3_, ...), custom_call_target="tpu_custom_call" | custom-call | flops 5500000256 | bytes 1048576 | tf_op jit(solution)/shard_map/pallas_call | solution.py:674
  141.4 5.3 %all-to-all-start.1 = ((bf16[8,176,512]{2,1,0:T(8,128)(2,1)}), bf16[8,176,512]{2,1,0:T(8,128)(2,1)S(1)}, u32[]{:S(2)}, u32[]{:S(2)}) async-start(bf16[8,176,512]{2,1,0:T(8,128)(2,1)} %shard_map.282), calls=%async_computation.1 | async-start | bytes 2883584 | tf_op jit(solution)/shard_map/all_to_all | solution.py:1058
  146.7 6.6 %shard_map.283 = (bf16[2,128,1024]{2,1,0:T(8,128)(2,1)}, bf16[2,128,1024]{2,1,0:T(8,128)(2,1)}) custom-call(s32[12]{0:T(128)} %stack.66.place_ref, bf16[512,512]{1,0:T(8,128)(2,1)} %get-tuple-element.163.refs_0_, bf16[512,512]{1,0:T(8,128)(2,1)} %get-tuple-element.177.refs_0_.refs_1_, bf16[512,256]{1,0:T(8,128)(2,1)} %get-tuple-element.178.refs_2_, ...), custom_call_target="tpu_custom_call" | custom-call | flops 6600000000 | bytes 1048576 | tf_op jit(solution)/shard_map/pallas_call | solution.py:674
  153.3 2.2 %collective-permute-done.33 = bf16[2,128,1024]{2,1,0:T(8,128)(2,1)} collective-permute-done((bf16[2,128,1024]{2,1,0:T(8,128)(2,1)}, bf16[2,128,1024]{2,1,0:T(8,128)(2,1)}, u32[]{:S(2)}, u32[]{:S(2)}) %collective-permute-start.33) | collective-permute-done | bytes 524320 | tf_op jit(solution)/shard_map/ppermute | solution.py:758
  155.6 1.8 fusion.6
  160.6 1.8 copy.33
  162.4 3.6 %collective-permute-done.34 = bf16[128,1024]{1,0:T(8,128)(2,1)S(1)} collective-permute-done((bf16[128,1024]{1,0:T(8,128)(2,1)}, bf16[128,1024]{1,0:T(8,128)(2,1)S(1)}, u32[]{:S(2)}, u32[]{:S(2)}) %collective-permute-start.34) | collective-permute-done | bytes 262176 | tf_op jit(solution)/shard_map/ppermute | solution.py:758
  167.2 2.2 %fusion.4 = (f32[128,1024]{1,0:T(8,128)}, bf16[128,1024]{1,0:T(8,128)(2,1)}) fusion(bf16[128,1024]{1,0:T(8,128)(2,1)S(1)} %copy-done, bf16[128,1024]{1,0:T(8,128)(2,1)} %param.18, bf16[128,1024]{1,0:T(8,128)(2,1)S(1)} %collective-permute-done.34, f32[128]{0:T(128)S(1)} %get-tuple-element.222, f32[1024]{0:T(1024)S(1)} %bitcast.51, ...), kind=kLoop, calls=%fused_computation.10 | loop fusion | flops 1835008 | bytes 2626560 | tf_op jit(solution)/shard_map/add | solution.py:1109
  169.4 11.2 %all-to-all-done.1 = bf16[8,176,512]{2,1,0:T(8,128)(2,1)S(1)} async-done(((bf16[8,176,512]{2,1,0:T(8,128)(2,1)}), bf16[8,176,512]{2,1,0:T(8,128)(2,1)S(1)}, u32[]{:S(2)}, u32[]{:S(2)}) %all-to-all-start.1) | async-done | bytes 1441824 | tf_op jit(solution)/shard_map/all_to_all | solution.py:1058
  181.7 1.7 collective-permute-start.36
  (179 shorter events, 50.7 us)
Async XLA Ops:
  5.4 13.2 %collective-permute-start.3 = (bf16[256,512]{1,0:T(8,128)(2,1)}, bf16[256,512]{1,0:T(8,128)(2,1)S(1)}, u32[]{:S(2)}, u32[]{:S(2)}) collective-permute-start(bf16[256,512]{1,0:T(8,128)(2,1)} %get-tuple-element.101.refs_4_), channel_id=1, source_target_pairs={{0,8},{8,16},{16,24},{24,28},{28,20},{20,12},{12,4},{4,0},{1,9},{9... | collective-permute-start | bytes 786440 | tf_op jit(solution)/shard_map/ppermute | solution.py:709
  8.5 10.1 %collective-permute-start.4 = (bf16[256,512]{1,0:T(8,128)(2,1)}, bf16[256,512]{1,0:T(8,128)(2,1)S(1)}, u32[]{:S(2)}, u32[]{:S(2)}) collective-permute-start(bf16[256,512]{1,0:T(8,128)(2,1)} %get-tuple-element.101.refs_4_), channel_id=1, source_target_pairs={{0,4},{8,0},{16,8},{24,16},{28,24},{20,28},{12,20},{4,12},{1,5},{9... | collective-permute-start | bytes 786440 | tf_op jit(solution)/shard_map/ppermute | solution.py:709
  18.6 8.0 %collective-permute-start.8 = (bf16[208,512]{1,0:T(8,128)(2,1)}, bf16[208,512]{1,0:T(8,128)(2,1)S(1)}, u32[]{:S(2)}, u32[]{:S(2)}) collective-permute-start(bf16[208,512]{1,0:T(8,128)(2,1)} %shard_map.273.refs_4_), channel_id=1, source_target_pairs={{0,8},{8,16},{16,24},{24,28},{28,20},{20,12},{12,4},{4,0},{1,9},{9... | collective-permute-start | bytes 638984 | tf_op jit(solution)/shard_map/ppermute | solution.py:709
  20.3 14.8 %collective-permute-start.1 = (bf16[256,1024]{1,0:T(8,128)(2,1)S(1)}, bf16[256,1024]{1,0:T(8,128)(2,1)S(1)}, u32[]{:S(2)}, u32[]{:S(2)}) collective-permute-start(bf16[256,1024]{1,0:T(8,128)(2,1)S(1)} %constant_dynamic-update-slice_fusion.refs_0_), channel_id=1, source_target_pairs={{0,2},{1,3},{2,0},{3,1},{4,6},{5,7},{6,4},{7,5},{8,10},{9,11},{10,... | collective-permute-start | bytes 1572872 | tf_op jit(solution)/shard_map/ppermute | solution.py:758
  21.8 6.6 %collective-permute-start.9 = (bf16[208,512]{1,0:T(8,128)(2,1)}, bf16[208,512]{1,0:T(8,128)(2,1)S(1)}, u32[]{:S(2)}, u32[]{:S(2)}) collective-permute-start(bf16[208,512]{1,0:T(8,128)(2,1)} %shard_map.273.refs_4_), channel_id=1, source_target_pairs={{0,4},{8,0},{16,8},{24,16},{28,24},{20,28},{12,20},{4,12},{1,5},{9... | collective-permute-start | bytes 638984 | tf_op jit(solution)/shard_map/ppermute | solution.py:709
  26.6 6.9 %collective-permute-start.10 = (bf16[208,512]{1,0:T(8,128)(2,1)S(1)}, bf16[208,512]{1,0:T(8,128)(2,1)S(1)}, u32[]{:S(2)}, u32[]{:S(2)}) collective-permute-start(bf16[208,512]{1,0:T(8,128)(2,1)S(1)} %collective-permute-done.8.refs_5_), channel_id=1, source_target_pairs={{0,8},{8,16},{16,24},{24,28},{28,20},{20,12},{12,4},{4,0},{1,9},{9... | collective-permute-start | bytes 638984 | tf_op jit(solution)/shard_map/ppermute | solution.py:709
  28.4 7.2 %collective-permute-start.11 = (bf16[208,512]{1,0:T(8,128)(2,1)S(1)}, bf16[208,512]{1,0:T(8,128)(2,1)S(1)}, u32[]{:S(2)}, u32[]{:S(2)}) collective-permute-start(bf16[208,512]{1,0:T(8,128)(2,1)S(1)} %collective-permute-done.9.refs_6_), channel_id=1, source_target_pairs={{0,4},{8,0},{16,8},{24,16},{28,24},{20,28},{12,20},{4,12},{1,5},{9... | collective-permute-start | bytes 638984 | tf_op jit(solution)/shard_map/ppermute | solution.py:709
  33.5 6.0 %collective-permute-start.12 = (bf16[208,512]{1,0:T(8,128)(2,1)S(1)}, bf16[208,512]{1,0:T(8,128)(2,1)S(1)}, u32[]{:S(2)}, u32[]{:S(2)}) collective-permute-start(bf16[208,512]{1,0:T(8,128)(2,1)S(1)} %collective-permute-done.10.refs_7_), channel_id=1, source_target_pairs={{0,8},{8,16},{16,24},{24,28},{28,20},{20,12},{12,4},{4,0},{1,9},{9... | collective-permute-start | bytes 638984 | tf_op jit(solution)/shard_map/ppermute | solution.py:709
  35.1 20.1 %collective-permute-start = (bf16[256,1024]{1,0:T(8,128)(2,1)S(1)}, bf16[256,1024]{1,0:T(8,128)(2,1)S(1)}, u32[]{:S(2)}, u32[]{:S(2)}) collective-permute-start(bf16[256,1024]{1,0:T(8,128)(2,1)S(1)} %constant_dynamic-update-slice_fusion.refs_0_), channel_id=1, source_target_pairs={{0,1},{1,0},{2,3},{3,2},{4,5},{5,4},{6,7},{7,6},{8,9},{9,8},{10,11... | collective-permute-start | bytes 1572872 | tf_op jit(solution)/shard_map/ppermute | solution.py:758
  35.1 20.1 %collective-permute-start.2 = (bf16[256,1024]{1,0:T(8,128)(2,1)S(1)}, bf16[256,1024]{1,0:T(8,128)(2,1)S(1)}, u32[]{:S(2)}, u32[]{:S(2)}) collective-permute-start(bf16[256,1024]{1,0:T(8,128)(2,1)S(1)} %collective-permute-done.1.refs_2_), channel_id=1, source_target_pairs={{0,1},{1,0},{2,3},{3,2},{4,5},{5,4},{6,7},{7,6},{8,9},{9,8},{10,11... | collective-permute-start | bytes 1572872 | tf_op jit(solution)/shard_map/ppermute | solution.py:758
  35.6 7.2 %collective-permute-start.13 = (bf16[208,512]{1,0:T(8,128)(2,1)S(1)}, bf16[208,512]{1,0:T(8,128)(2,1)S(1)}, u32[]{:S(2)}, u32[]{:S(2)}) collective-permute-start(bf16[208,512]{1,0:T(8,128)(2,1)S(1)} %collective-permute-done.11.refs_8_), channel_id=1, source_target_pairs={{0,4},{8,0},{16,8},{24,16},{28,24},{20,28},{12,20},{4,12},{1,5},{9... | collective-permute-start | bytes 638984 | tf_op jit(solution)/shard_map/ppermute | solution.py:709
  39.6 5.8 %collective-permute-start.14 = (bf16[208,512]{1,0:T(8,128)(2,1)S(1)}, bf16[208,512]{1,0:T(8,128)(2,1)S(1)}, u32[]{:S(2)}, u32[]{:S(2)}) collective-permute-start(bf16[208,512]{1,0:T(8,128)(2,1)S(1)} %collective-permute-done.12.refs_9_), channel_id=1, source_target_pairs={{0,8},{8,16},{16,24},{24,28},{28,20},{20,12},{12,4},{4,0},{1,9},{9... | collective-permute-start | bytes 638984 | tf_op jit(solution)/shard_map/ppermute | solution.py:709
  46.1 7.5 %collective-permute-start.15 = (bf16[256,512]{1,0:T(8,128)(2,1)S(1)}, bf16[256,512]{1,0:T(8,128)(2,1)S(1)}, u32[]{:S(2)}, u32[]{:S(2)}) collective-permute-start(bf16[256,512]{1,0:T(8,128)(2,1)S(1)} %collective-permute-done.3.refs_5_), channel_id=1, source_target_pairs={{0,8},{8,16},{16,24},{24,28},{28,20},{20,12},{12,4},{4,0},{1,9},{9... | collective-permute-start | bytes 786440 | tf_op jit(solution)/shard_map/ppermute | solution.py:709
  48.3 17.4 %collective-permute-start.16 = (bf16[256,512]{1,0:T(8,128)(2,1)S(1)}, bf16[256,512]{1,0:T(8,128)(2,1)S(1)}, u32[]{:S(2)}, u32[]{:S(2)}) collective-permute-start(bf16[256,512]{1,0:T(8,128)(2,1)S(1)} %collective-permute-done.4.refs_6_), channel_id=1, source_target_pairs={{0,4},{8,0},{16,8},{24,16},{28,24},{20,28},{12,20},{4,12},{1,5},{9... | collective-permute-start | bytes 786440 | tf_op jit(solution)/shard_map/ppermute | solution.py:709
  53.6 12.7 %collective-permute-start.17 = (bf16[256,512]{1,0:T(8,128)(2,1)S(1)}, bf16[256,512]{1,0:T(8,128)(2,1)S(1)}, u32[]{:S(2)}, u32[]{:S(2)}) collective-permute-start(bf16[256,512]{1,0:T(8,128)(2,1)S(1)} %collective-permute-done.15.refs_7_), channel_id=1, source_target_pairs={{0,8},{8,16},{16,24},{24,28},{28,20},{20,12},{12,4},{4,0},{1,9},{9... | collective-permute-start | bytes 786440 | tf_op jit(solution)/shard_map/ppermute | solution.py:709
  65.7 7.6 %collective-permute-start.18 = (bf16[256,512]{1,0:T(8,128)(2,1)S(1)}, bf16[256,512]{1,0:T(8,128)(2,1)S(1)}, u32[]{:S(2)}, u32[]{:S(2)}) collective-permute-start(bf16[256,512]{1,0:T(8,128)(2,1)S(1)} %collective-permute-done.16.refs_8_), channel_id=1, source_target_pairs={{0,4},{8,0},{16,8},{24,16},{28,24},{20,28},{12,20},{4,12},{1,5},{9... | collective-permute-start | bytes 786440 | tf_op jit(solution)/shard_map/ppermute | solution.py:709
  66.3 7.1 %collective-permute-start.19 = (bf16[256,512]{1,0:T(8,128)(2,1)S(1)}, bf16[256,512]{1,0:T(8,128)(2,1)S(1)}, u32[]{:S(2)}, u32[]{:S(2)}) collective-permute-start(bf16[256,512]{1,0:T(8,128)(2,1)S(1)} %collective-permute-done.17.refs_9_), channel_id=1, source_target_pairs={{0,8},{8,16},{16,24},{24,28},{28,20},{20,12},{12,4},{4,0},{1,9},{9... | collective-permute-start | bytes 786440 | tf_op jit(solution)/shard_map/ppermute | solution.py:709
  94.6 12.2 %collective-permute-start.24 = (bf16[256,512]{1,0:T(8,128)(2,1)}, bf16[256,512]{1,0:T(8,128)(2,1)S(1)}, u32[]{:S(2)}, u32[]{:S(2)}) collective-permute-start(bf16[256,512]{1,0:T(8,128)(2,1)} %get-tuple-element.139), channel_id=1, source_target_pairs={{0,4},{8,0},{16,8},{24,16},{28,24},{20,28},{12,20},{4,12},{1,5},{9... | collective-permute-start | bytes 786440 | tf_op jit(solution)/shard_map/ppermute | solution.py:709
  96.2 10.7 %collective-permute-start.23 = (bf16[256,512]{1,0:T(8,128)(2,1)}, bf16[256,512]{1,0:T(8,128)(2,1)S(1)}, u32[]{:S(2)}, u32[]{:S(2)}) collective-permute-start(bf16[256,512]{1,0:T(8,128)(2,1)} %get-tuple-element.137), channel_id=1, source_target_pairs={{0,8},{8,16},{16,24},{24,28},{28,20},{20,12},{12,4},{4,0},{1,9},{9... | collective-permute-start | bytes 786440 | tf_op jit(solution)/shard_map/ppermute | solution.py:709
  103.2 30.2 %all-to-all-start = ((bf16[4,128,1024]{2,1,0:T(8,128)(2,1)}), bf16[4,128,1024]{2,1,0:T(8,128)(2,1)S(1)}, u32[]{:S(2)}, u32[]{:S(2)}) async-start(bf16[4,128,1024]{2,1,0:T(8,128)(2,1)} %bitcast.19), calls=%async_computation | async-start | bytes 2097152 | tf_op jit(solution)/shard_map/all_to_all | solution.py:753
  107.0 8.7 %collective-permute-start.26 = (bf16[256,512]{1,0:T(8,128)(2,1)S(1)}, bf16[256,512]{1,0:T(8,128)(2,1)S(1)}, u32[]{:S(2)}, u32[]{:S(2)}) collective-permute-start(bf16[256,512]{1,0:T(8,128)(2,1)S(1)} %add_convert_fusion.4), channel_id=1, source_target_pairs={{0,4},{8,0},{16,8},{24,16},{28,24},{20,28},{12,20},{4,12},{1,5},{9... | collective-permute-start | bytes 786440 | tf_op jit(solution)/shard_map/ppermute | solution.py:709
  108.6 8.4 %collective-permute-start.25 = (bf16[256,512]{1,0:T(8,128)(2,1)S(1)}, bf16[256,512]{1,0:T(8,128)(2,1)S(1)}, u32[]{:S(2)}, u32[]{:S(2)}) collective-permute-start(bf16[256,512]{1,0:T(8,128)(2,1)S(1)} %add_convert_fusion.5), channel_id=1, source_target_pairs={{0,8},{8,16},{16,24},{24,28},{28,20},{20,12},{12,4},{4,0},{1,9},{9... | collective-permute-start | bytes 786440 | tf_op jit(solution)/shard_map/ppermute | solution.py:709
  117.1 9.6 %collective-permute-start.27 = (bf16[256,512]{1,0:T(8,128)(2,1)S(1)}, bf16[256,512]{1,0:T(8,128)(2,1)S(1)}, u32[]{:S(2)}, u32[]{:S(2)}) collective-permute-start(bf16[256,512]{1,0:T(8,128)(2,1)S(1)} %add_convert_fusion.3), channel_id=1, source_target_pairs={{0,8},{8,16},{16,24},{24,28},{28,20},{20,12},{12,4},{4,0},{1,9},{9... | collective-permute-start | bytes 786440 | tf_op jit(solution)/shard_map/ppermute | solution.py:709
  117.7 9.1 %collective-permute-start.28 = (bf16[256,512]{1,0:T(8,128)(2,1)S(1)}, bf16[256,512]{1,0:T(8,128)(2,1)S(1)}, u32[]{:S(2)}, u32[]{:S(2)}) collective-permute-start(bf16[256,512]{1,0:T(8,128)(2,1)S(1)} %add_convert_fusion.2), channel_id=1, source_target_pairs={{0,4},{8,0},{16,8},{24,16},{28,24},{20,28},{12,20},{4,12},{1,5},{9... | collective-permute-start | bytes 786440 | tf_op jit(solution)/shard_map/ppermute | solution.py:709
  124.9 10.9 %collective-permute-start.30 = (bf16[272,256]{1,0:T(8,128)(2,1)}, bf16[272,256]{1,0:T(8,128)(2,1)S(1)}, u32[]{:S(2)}, u32[]{:S(2)}) collective-permute-start(bf16[272,256]{1,0:T(8,128)(2,1)} %get-tuple-element.174), channel_id=1, source_target_pairs={{0,1},{1,0},{2,3},{3,2},{4,5},{5,4},{6,7},{7,6},{8,9},{9,8},{10,11... | collective-permute-start | bytes 417800 | tf_op jit(solution)/shard_map/ppermute | solution.py:758
  124.9 10.9 %collective-permute-start.31 = (bf16[272,256]{1,0:T(8,128)(2,1)}, bf16[272,256]{1,0:T(8,128)(2,1)}, u32[]{:S(2)}, u32[]{:S(2)}) collective-permute-start(bf16[272,256]{1,0:T(8,128)(2,1)} %get-tuple-element.175), channel_id=1, source_target_pairs={{0,2},{1,3},{2,0},{3,1},{4,6},{5,7},{6,4},{7,5},{8,10},{9,11},{10,... | collective-permute-start | bytes 417800 | tf_op jit(solution)/shard_map/ppermute | solution.py:758
  126.6 9.2 %collective-permute-start.32 = (bf16[272,256]{1,0:T(8,128)(2,1)}, bf16[272,256]{1,0:T(8,128)(2,1)}, u32[]{:S(2)}, u32[]{:S(2)}) collective-permute-start(bf16[272,256]{1,0:T(8,128)(2,1)} %get-tuple-element.176), channel_id=1, source_target_pairs={{0,3},{1,2},{2,1},{3,0},{4,7},{5,6},{6,5},{7,4},{8,11},{9,10},{10,... | collective-permute-start | bytes 417800 | tf_op jit(solution)/shard_map/ppermute | solution.py:758
  126.8 8.8 %collective-permute-start.29 = (bf16[256,512]{1,0:T(8,128)(2,1)S(1)}, bf16[256,512]{1,0:T(8,128)(2,1)S(1)}, u32[]{:S(2)}, u32[]{:S(2)}) collective-permute-start(bf16[256,512]{1,0:T(8,128)(2,1)S(1)} %add_convert_fusion.1), channel_id=1, source_target_pairs={{0,8},{8,16},{16,24},{24,28},{28,20},{20,12},{12,4},{4,0},{1,9},{9... | collective-permute-start | bytes 786440 | tf_op jit(solution)/shard_map/ppermute | solution.py:709
  141.4 39.2 %all-to-all-start.1 = ((bf16[8,176,512]{2,1,0:T(8,128)(2,1)}), bf16[8,176,512]{2,1,0:T(8,128)(2,1)S(1)}, u32[]{:S(2)}, u32[]{:S(2)}) async-start(bf16[8,176,512]{2,1,0:T(8,128)(2,1)} %shard_map.282), calls=%async_computation.1 | async-start | bytes 2883584 | tf_op jit(solution)/shard_map/all_to_all | solution.py:1058
  157.4 8.6 %collective-permute-start.34 = (bf16[128,1024]{1,0:T(8,128)(2,1)}, bf16[128,1024]{1,0:T(8,128)(2,1)S(1)}, u32[]{:S(2)}, u32[]{:S(2)}) collective-permute-start(bf16[128,1024]{1,0:T(8,128)(2,1)} %fusion.6), channel_id=1, source_target_pairs={{0,2},{1,3},{2,0},{3,1},{4,6},{5,7},{6,4},{7,5},{8,10},{9,11},{10,... | collective-permute-start | bytes 786440 | tf_op jit(solution)/shard_map/ppermute | solution.py:758
  181.6 6.9 %collective-permute-start.35 = (f32[128]{0:T(128)S(1)}, f32[128]{0:T(128)S(1)}, u32[]{:S(2)}, u32[]{:S(2)}) collective-permute-start(f32[128]{0:T(128)S(1)} %add.187), channel_id=1, source_target_pairs={{0,1},{1,0},{2,3},{3,2},{4,5},{5,4},{6,7},{7,6},{8,9},{9,8},{10,11... | collective-permute-start | bytes 1544 | tf_op jit(solution)/shard_map/ppermute | solution.py:758
  181.7 6.9 %collective-permute-start.36 = (f32[128]{0:T(128)S(1)}, f32[128]{0:T(128)S(1)}, u32[]{:S(2)}, u32[]{:S(2)}) collective-permute-start(f32[128]{0:T(128)S(1)} %add.187), channel_id=1, source_target_pairs={{0,2},{1,3},{2,0},{3,1},{4,6},{5,7},{6,4},{7,5},{8,10},{9,11},{10,... | collective-permute-start | bytes 1544 | tf_op jit(solution)/shard_map/ppermute | solution.py:758
  (47 other events, 387.3 us)

commit v5 on v4

--- a/solution.py
+++ b/solution.py
@@ -15,7 +15,7 @@
 pad = 8
 head_rows = 16
 head_width = 64
-vmem_bytes = 54 * 1024 * 1024
+vmem_bytes = 61 * 1024 * 1024
 
 
 def mm(a, b, over=(1, 0)):
@@ -144,10 +144,10 @@
     n_msg = 8 if fast else 4
     n_rows = 4 if fast else 1
     row_refs, msg_refs, refs = refs[:n_rows], refs[n_rows : n_rows + n_msg], refs[n_rows + n_msg :]
-    taps_ref, bias_ref = refs[:2]
+    (taps_ref, bias_ref, step_bias_ref, step_bias_col_ref, log_ref, log_col_ref, skip_ref) = refs[:7]
     (
-        rows_ref,
         normed_ref,
+        turned_ref,
         weight_ref,
         state_weight_ref,
         step_weight_ref,
@@ -158,10 +158,10 @@
         step_row_ref,
         act_ref,
         state_ref,
-    ) = refs[2:14]
-    mask_ref, state_taps_ref, state_bias_ref = refs[14:]
-    total = rows_ref.shape[0]
-    channels = act_ref.shape[1]
+        mixed_ref,
+    ) = refs[7:20]
+    mask_ref, state_taps_ref, state_bias_ref = refs[20:]
+    total, channels = act_ref.shape
     ends = ends_of(lengths_ref)
 
     if fast:
@@ -196,11 +196,11 @@
     tall = total // n_rows
     for member in range(n_rows):
         at = pl.multiple_of(place_ref[8 + member] * tall, tall) if fast else 0
-        own = row_refs[member][:tall, :]
-        rows_ref[pl.ds(at, tall), :] = own
-        value = own.astype(f32)
+        value = row_refs[member][:tall, :].astype(f32)
         scale = lax.rsqrt(jnp.mean(value * value, axis=1, keepdims=True) + epsilon)
-        normed_ref[pl.ds(at, tall), :] = (value * scale * gain).astype(bf16)
+        normed = (value * scale * gain).astype(bf16)
+        normed_ref[pl.ds(at, tall), :] = normed
+        turned_ref[:, pl.ds(at, tall)] = normed.astype(f32).T.astype(bf16)
 
     raw_ref[:pad, :] = jnp.zeros((pad, channels), f32)
     state_raw_ref[:pad, :] = jnp.zeros((pad, state_raw_ref.shape[1]), f32)
@@ -227,12 +227,6 @@
     activate(raw_ref, act_ref, taps_ref, bias_ref)
     activate(state_raw_ref, state_ref, state_taps_ref, state_bias_ref)
 
-
-def scan_kernel(lengths_ref, *refs):
-    act_ref, state_ref, step_col_ref, step_row_ref = refs[:4]
-    step_bias_ref, step_bias_col_ref, log_ref, log_col_ref, skip_ref, mixed_ref = refs[4:]
-    total, channels = act_ref.shape
-    ends = ends_of(lengths_ref)
     steps = step_sizes(
         step_col_ref[...],
         step_row_ref[...],
@@ -305,7 +299,7 @@
 def norm_kernel(inner_total, place_ref, lengths_ref, *refs):
     n_sums = len(refs) - 21
     sums_refs, refs = refs[:n_sums], refs[n_sums:]
-    gate_ref, mixed_ref, grad_ref, norm_ref, weight_ref, rows_ref, normed_ref = refs[:7]
+    gate_ref, mixed_ref, grad_ref, norm_ref, weight_ref, rows_ref, turned_ref = refs[:7]
     chunk_refs = refs[7:15]
     partial_ref, grad_gate_ref, grad_mixed_ref, norm_grad_ref = refs[15:19]
     wide_ref, out_rows_ref = refs[19:]
@@ -336,14 +330,18 @@
         grad_mixed_ref[rows, :] = grad_gated * gate_act
         grad_gate = grad_gated * mixed * sig * (1.0 + gate * (1.0 - sig))
         grad_gate_ref[rows, :] = grad_gate.astype(bf16)
-        partial_ref[rows, :] = mm(out_rows_ref[rows, :], weight_ref[...], (1, 1)).astype(bf16)
 
     row_loop(total, 128, part)
 
+    def back(at):
+        cols = pl.ds(at, 256)
+        partial_ref[:, cols] = mm(out_rows_ref[...], weight_ref[cols, :], (1, 1)).astype(bf16)
+
+    row_loop(weight_ref.shape[0], 256, back)
     tall = chunk_refs[0].shape[0] // 2
     for slot, chunk_ref in enumerate(chunk_refs):
         cols = pl.ds(pl.multiple_of(place_ref[slot] * tall, tall), tall)
-        chunk_ref[:tall, :] = mm(normed_ref[:, cols], grad_gate_ref[...], (0, 0)).astype(bf16)
+        chunk_ref[:tall, :] = mm(turned_ref[cols, :], grad_gate_ref[...]).astype(bf16)
         chunk_ref[tall:, :] = mm(rows_ref[:, cols], out_rows_ref[...], (0, 0)).astype(bf16)
 
 
@@ -483,7 +481,7 @@
 
 def state_back_kernel(fast, place_ref, lengths_ref, *refs):
     state_refs, step_refs, refs = refs[0:2], refs[2:4], refs[4:]
-    state_raw_ref, normed_ref, small_ref, grad_state_low_ref, step_low_ref = refs[:5]
+    state_raw_ref, turned_ref, small_ref, grad_state_low_ref, step_low_ref = refs[:5]
     n_out = 4 if fast else 2
     out_refs, refs = refs[5 : 5 + n_out], refs[5 + n_out :]
     mask_ref, taps_ref, bias_ref, grad_state_ref, pre_ref, part_ref, sums_ref = refs
@@ -506,10 +504,10 @@
     )
 
     def chunk(at):
-        part = normed_ref[:, pl.ds(at, 256)]
-        part_ref[pl.ds(at, 256), :] = mm(part, grad_state_low_ref[...], (0, 0)).astype(bf16)
-
-    depth = normed_ref.shape[1]
+        part = turned_ref[pl.ds(at, 256), :]
+        part_ref[pl.ds(at, 256), :] = mm(part, grad_state_low_ref[...]).astype(bf16)
+
+    depth = turned_ref.shape[0]
     row_loop(depth, 256, chunk)
     if fast:
         share = depth // 32
@@ -532,10 +530,12 @@
     grad_act_ref[:, :half] = act_refs[0][...]
     grad_act_ref[:, half:] = act_refs[1][...]
     sums_ref[...] = jnp.zeros(sums_ref.shape, f32)
-    sums_ref[6:7, :] = norm_grad_ref[...]
-    sums_ref[7:9, :half] = head_refs[0][:2, :] + head_refs[1][:2, :]
-    sums_ref[9:10, :half] = head_refs[0][2:3, :]
-    sums_ref[9:10, half:] = head_refs[1][2:3, :]
+    heads = head_refs[0][:2, :128] + head_refs[1][:2, :128]
+    sums_ref[5:6, :] = norm_grad_ref[...]
+    sums_ref[6:7, :half] = head_refs[0][2:3, :]
+    sums_ref[6:7, half:] = head_refs[1][2:3, :]
+    sums_ref[9:10, half : half + 128] = heads[0:1, :]
+    sums_ref[9:10, half + 128 :] = heads[1:2, :]
     conv_back(
         raw_ref,
         mask_ref,
@@ -548,63 +548,89 @@
     )
 
 
-def message_kernel(fast, *refs):
-    grad_inner_ref, step_low_ref, normed_ref = refs[:3]
-    msg_ref = refs[-1]
+def message_kernel(grad_inner_ref, step_low_ref, turned_ref, msg_ref):
     chunks = msg_ref.shape[0]
-    tall = normed_ref.shape[1] // chunks
+    tall = turned_ref.shape[0] // chunks
     step_low = step_low_ref[...]
-    tail = tall + head_rows
 
     def chunk(c, carry):
-        part = normed_ref[:, pl.ds(pl.multiple_of(c * tall, tall), tall)]
-        msg_ref[c, :tall, :] = mm(part, grad_inner_ref[...], (0, 0)).astype(bf16)
-        msg_ref[c, tall:tail, :tall] = mm(step_low, part).astype(bf16)
-        msg_ref[c, tall:tail, tall:] = jnp.zeros((head_rows, msg_ref.shape[2] - tall), bf16)
+        part = turned_ref[pl.ds(pl.multiple_of(c * tall, tall), tall), :]
+        msg_ref[c, :tall, :] = mm(part, grad_inner_ref[...]).astype(bf16)
+        msg_ref[c, tall:, :tall] = mm(step_low, part, (1, 1)).astype(bf16)
+        msg_ref[c, tall:, tall:] = jnp.zeros((head_rows, msg_ref.shape[2] - tall), bf16)
         return carry
 
     lax.fori_loop(0, chunks, chunk, 0)
-    if fast:
-        sums_ref, state_refs = refs[3], refs[4:8]
-
-        def state_rows(low, high):
-            return sum(ref[low:high, :].astype(f32) for ref in state_refs)
-
-        states = state_refs[0].shape[1]
-        share = (state_refs[0].shape[0] - 16) // chunks
-        shared = state_rows(share * chunks, share * chunks + 5)
-        shared = jnp.concatenate([shared, jnp.zeros((5, states), f32)], axis=1)
-        sums = jnp.concatenate([sums_ref[:10, :], shared, jnp.zeros((1, 2 * states), f32)], axis=0)
-        sums = sums.astype(bf16)
-        for c in range(chunks):
-            low = share * c
-            part = jnp.concatenate(
-                [state_rows(low, low + 16), state_rows(low + 16, low + 32)], axis=1
-            )
-            msg_ref[c, tail : tail + 16, :] = part.astype(bf16)
-            msg_ref[c, tail + 16 :, :] = sums
+
+
+def chunk_kernel(slots, n_got, place_ref, *refs):
+    grad_inner_ref, step_low_ref, sums_ref = refs[:3]
+    state_refs, turned_refs, got_refs = refs[3:7], refs[7:9], refs[9 : 9 + n_got]
+    out_refs = refs[9 + n_got :]
+    states = state_refs[0].shape[1]
+    share = (state_refs[0].shape[0] - 16) // 8
+
+    def state_rows(low, tall):
+        return sum(ref[pl.ds(low, tall), :].astype(f32) for ref in state_refs)
+
+    shared = state_rows(8 * share, 16)
+    sums = [
+        sums_ref[:7, :],
+        jnp.concatenate([shared[0:1, :], shared[1:2, :]], axis=1),
+        jnp.concatenate([shared[2:3, :], shared[3:4, :]], axis=1),
+        jnp.concatenate([shared[4:5, :], sums_ref[9:10, states:]], axis=1),
+    ]
+    for n, (slot, out_ref) in enumerate(zip(slots, out_refs)):
+        index = place_ref[slot]
+        part = turned_refs[n][...]
+        step = mm(step_low_ref[...], part, (1, 1))
+        step = [
+            jnp.concatenate([step[4 * k + i : 4 * k + i + 1, :] for i in range(4)], axis=1)
+            for k in range(2)
+        ]
+        state = state_rows(pl.multiple_of(index * share, share), share)
+        value = jnp.concatenate(
+            [
+                mm(part, grad_inner_ref[...]),
+                jnp.concatenate([state[:16, :], state[16:, :]], axis=1),
+                *sums,
+                *step,
+                jnp.zeros((4, 2 * states), f32),
+            ],
+            axis=0,
+        )
+        tail = value.shape[0] - 16
+        main, sums_here = value[:tail, :], value[tail:, :]
+        if n < n_got:
+            got = got_refs[n]
+            main = main + got[:tail, :].astype(f32)
+            sums_here = sums_here + got[tail : tail + 16, :].astype(f32)
+            sums_here = sums_here + got[tail + 16 :, :].astype(f32)
+        out_ref[:tail, :] = main.astype(out_ref.dtype)
+        high = sums_here.astype(bf16)
+        out_ref[tail : tail + 16, :] = high.astype(out_ref.dtype)
+        out_ref[tail + 16 :, :] = (sums_here - high.astype(f32)).astype(out_ref.dtype)
 
 
 def project_back_kernel(fast, place_ref, *refs):
-    (
-        grad_gate_ref,
-        grad_inner_ref,
-        grad_state_low_ref,
-        step_low_ref,
-        gate_weight_ref,
-        weight_ref,
-        state_weight_ref,
-        step_weight_ref,
-    ) = refs[:8]
-    out_refs = refs[8:]
-    for member in range(4):
+    grad_refs, step_low_ref, weight_refs, step_weight_ref = refs[:3], refs[3], refs[4:7], refs[7]
+    out_refs, held_refs, step_ref = refs[8:10], refs[10:13], refs[13]
+    for n, member in enumerate((0, 2, 1, 3)):
         at = pl.multiple_of(place_ref[8 + member] * 128, 128) if fast else 128 * member
-        rows = pl.ds(at, 128)
-        grad = mm(grad_gate_ref[rows, :], gate_weight_ref[...], (1, 1))
-        grad = grad + mm(grad_inner_ref[rows, :], weight_ref[...], (1, 1))
-        grad = grad + mm(grad_state_low_ref[rows, :], state_weight_ref[...], (1, 1))
-        grad = grad + mm(step_low_ref[:, rows], step_weight_ref[...], (0, 0))
-        out_refs[member % 2][member // 2] = grad.astype(bf16)
+        for held_ref, grad_ref in zip(held_refs, grad_refs):
+            held_ref[128 * n : 128 * (n + 1), :] = grad_ref[pl.ds(at, 128), :]
+        step_ref[:, 128 * n : 128 * (n + 1)] = step_low_ref[:, pl.ds(at, 128)]
+
+    def back(at):
+        cols = pl.ds(at, 256)
+        grad = mm(step_ref[...], step_weight_ref[:, cols], (0, 0))
+        for held_ref, weight_ref in zip(held_refs, weight_refs):
+            grad = grad + mm(held_ref[...], weight_ref[cols, :], (1, 1))
+        grad = grad.astype(bf16)
+        for n in range(4):
+            out_refs[n // 2][n % 2, :, cols] = grad[128 * n : 128 * (n + 1), :]
+
+    row_loop(step_weight_ref.shape[1], 256, back)
 
 
 def prepare_kernel(place_ref, gain_ref, taps_ref, bias_ref, state_ref, shared_ref):
@@ -628,12 +654,15 @@
     shared_ref[share:, :] = small.astype(bf16)
 
 
-def prepare_late_kernel(*refs):
-    input_ref, out_ref, taps_ref, bias_ref, step_bias_ref, log_ref, skip_ref, norm_ref = refs[:8]
-    late_ref, outs = refs[8], refs[9:]
+def prepare_late_kernel(input_ref, out_ref, late_ref):
     depth_part = input_ref.shape[0]
     late_ref[:depth_part, :] = input_ref[:, 0, :]
     late_ref[depth_part:, :] = out_ref[...].astype(f32).T.astype(bf16)
+
+
+def params_kernel(*refs):
+    taps_ref, bias_ref, step_bias_ref, log_ref, skip_ref, norm_ref = refs[:6]
+    outs = refs[6:]
     heads = step_bias_ref.shape[1]
     pick = jnp.where(iota((heads, head_rows), 0) == iota((heads, head_rows), 1), 1.0, 0.0)
     square = iota((head_rows, head_rows), 0) == iota((head_rows, head_rows), 1)
@@ -800,13 +829,20 @@
         [],
     )
     step_rows = jnp.pad(step_weight.T, ((0, head_rows - heads), (0, 0)))
-    late, *params = call(
+    shared, out_shard = ordered(shared, output_weight)
+    (late,) = call(
         prepare_late_kernel,
         2,
         [],
+        [input_weight, out_shard],
+        [((input_weight.shape[0] + output_weight.shape[1], channels), bf16)],
+        [],
+    )
+    params = call(
+        params_kernel,
+        1,
+        [],
         [
-            input_weight,
-            output_weight,
             conv_inner,
             conv_inner_bias[None, :],
             step_bias[None, :],
@@ -815,7 +851,6 @@
             norm_gain[None, :],
         ],
         [
-            ((input_weight.shape[0] + output_weight.shape[1], channels), bf16),
             ((taps, channels), f32),
             ((1, channels), f32),
             ((1, head_rows), f32),
@@ -827,6 +862,7 @@
         ],
         [],
     )
+    params = list(params)
     conv_params, head_params, norm_row = params[:2], params[2:7], params[7]
     if fast:
         shared = tensor_direct(shared)
@@ -841,11 +877,12 @@
         )
         late_one, msg = ordered(late_one, msg)
         msg = ring_gather(msg)
-        weight_pieces, late_one = ordered([piece for piece, _ in msg], late_one)
+        weight_pieces = [piece for piece, _ in msg]
         late_two = ring_step(late_one)
         late_three = ring_step(late_two)
         late_pieces = [late, *late_one, *late_two, *late_three, ring_send(late_three[0], True)]
-        row_pieces = tensor_gather(jnp.concatenate([tokens, cotangent], axis=0))
+        own_rows_both = jnp.concatenate([tokens, cotangent], axis=0)
+        row_pieces = tensor_gather(ordered(shared, own_rows_both)[1])
         grad_pieces = row_pieces
         place = jnp.stack([index for _, index in msg] + [me, me ^ 1, me ^ 2, me ^ 3])
     else:
@@ -868,8 +905,8 @@
     masks = ((taps - 1, total + pad, 128), f32)
     state_taps = [((taps, states), f32), ((1, states), f32)]
     (
-        rows,
         normed,
+        turned,
         inner_full,
         state_full,
         step_full,
@@ -880,14 +917,15 @@
         step_row,
         act,
         state_act,
+        mixed,
     ) = call(
         functools.partial(forward_kernel, fast),
-        6,
+        11,
         [place, lengths],
-        row_pieces + weight_pieces + conv_params,
+        row_pieces + weight_pieces + conv_params + head_params,
         [
             ((total, depth), bf16),
-            ((total, depth), bf16),
+            ((depth, total), bf16),
             ((depth, channels), bf16),
             ((depth, states), bf16),
             ((head_rows, depth), bf16),
@@ -898,19 +936,9 @@
             ((head_rows, total), f32),
             ((total, channels), f32),
             ((total, states), f32),
+            ((total, channels), f32),
         ],
         [masks] + state_taps,
-    )
-    if fast:
-        late_two, act = ordered(late_two, act)
-        late_pieces[3:5] = late_two
-    (mixed,) = call(
-        scan_kernel,
-        5,
-        [lengths],
-        [act, state_act, step_col, step_row] + head_params,
-        [((total, channels), f32)],
-        [],
     )
     grad_rows, gate_full, output_full, gate, grad_normalized, sums = call(
         functools.partial(grad_in_kernel, fast),
@@ -937,7 +965,7 @@
         functools.partial(norm_kernel, inner_total),
         9,
         [place, lengths],
-        [*sums, gate, mixed, grad_normalized, norm_row, output_full, grad_rows, normed],
+        [*sums, gate, mixed, grad_normalized, norm_row, output_full, grad_rows, turned],
         [((2 * tall, channels), bf16)] * chunks
         + [
             ((total, depth), bf16),
@@ -983,7 +1011,7 @@
         functools.partial(state_back_kernel, fast),
         4,
         [place, lengths],
-        [first[1], second[1], first[2], second[2], state_raw, normed, small_full],
+        [first[1], second[1], first[2], second[2], state_raw, turned, small_full],
         [((total, states), bf16), ((head_rows, total), bf16)]
         + (
             [((share_rows, states), bf16)] * 4
@@ -1018,34 +1046,75 @@
     if fast:
         mixed_rows = tensor_sum(partial_out, depth)
         (gate_out, mixed_rows), grad_inner = ordered((gate_out, mixed_rows), grad_inner)
-    msg_rows = tall + head_rows + (32 if fast else 0)
-    (inner_msg,) = call(
-        functools.partial(message_kernel, fast),
-        5,
-        [],
-        [grad_inner, step_low, normed] + ([sums, *state_parts] if fast else []),
-        [((chunks, msg_rows, channels), bf16)],
-        [],
-    )
-    if fast:
-        inner_msg, grad_inner = ordered(inner_msg, grad_inner)
-    keep_rows, give_rows = call(
-        functools.partial(project_back_kernel, fast),
-        6,
-        [place],
-        [
-            grad_gate,
-            grad_inner,
-            grad_state_low,
-            step_low,
-            gate_full,
-            inner_full,
-            state_full,
-            step_full,
-        ],
-        [((2, 128, depth), bf16)] * 2,
-        [],
-    )
+
+    def project_back():
+        return call(
+            functools.partial(project_back_kernel, fast),
+            6,
+            [place],
+            [
+                grad_gate,
+                grad_inner,
+                grad_state_low,
+                step_low,
+                gate_full,
+                inner_full,
+                state_full,
+                step_full,
+            ],
+            [((2, 128, depth), bf16)] * 2,
+            [
+                ((total, channels), bf16),
+                ((total, channels), bf16),
+                ((total, states), bf16),
+                ((head_rows, total), bf16),
+            ],
+        )
+
+    def chunk_pair(slots, got, after=None, last=bf16):
+        grad = grad_inner if after is None else ordered(after, grad_inner)[1]
+        arrays = [grad, step_low, sums, *state_parts, turned, turned, *got]
+
+        def whole(array):
+            return pl.BlockSpec(array.shape, lambda i, place: (0, 0))
+
+        def block(slot):
+            return pl.BlockSpec((tall, total), lambda i, place: (place[slot], 0))
+
+        specs = [whole(array) for array in arrays]
+        specs[7:9] = [block(slot) for slot in slots]
+        out = pl.BlockSpec((tall + 48, channels), lambda i, place: (0, 0))
+        return pl.pallas_call(
+            functools.partial(chunk_kernel, slots, len(got)),
+            grid_spec=pltpu.PrefetchScalarGridSpec(
+                num_scalar_prefetch=1, grid=(1,), in_specs=specs, out_specs=[out, out]
+            ),
+            out_shape=[
+                jax.ShapeDtypeStruct((tall + 48, channels), kind) for kind in (bf16, last)
+            ],
+            compiler_params=pltpu.CompilerParams(vmem_limit_bytes=vmem_bytes),
+            cost_estimate=pl.CostEstimate(
+                flops=2_000_000_000, bytes_accessed=1 << 20, transcendentals=0
+            ),
+        )(place, *arrays)
+
+    if fast:
+        got = ring_step(chunk_pair((7, 5), ()))
+        keep_rows, give_rows = project_back()
+        got = ring_step(chunk_pair((6, 3), got, give_rows))
+        got = ring_step(chunk_pair((4, 1), got))
+        held, inner_own = chunk_pair((2, 0), got, last=f32)
+        inner_out = inner_own + ring_send(held, True).astype(f32)
+    else:
+        (inner_msg,) = call(
+            message_kernel,
+            5,
+            [],
+            [grad_inner, step_low, turned],
+            [((chunks, tall + head_rows, channels), bf16)],
+            [],
+        )
+        keep_rows, give_rows = project_back()
 
     token_float = tokens.astype(f32)
     gain_full = small_full[: depth // states].reshape(1, depth)
@@ -1055,18 +1124,16 @@
         far = tensor_swap(add_low(keep_rows[1], got[1]), 2)
         grad_local = keep_rows[0].astype(f32) + got[0].astype(f32) + far.astype(f32)
         gate_grad, output_grad = gate_out[:tall], gate_out[tall:].T
-        inner_out = lax.all_to_all(inner_msg, "dp", 0, 0, tiled=True)
-        inner_out = jnp.sum(inner_out.astype(f32), axis=0)
-        tail = tall + head_rows
-        state_grad = inner_out[tail : tail + 16]
+        inner_grad = inner_out[:tall]
+        state_grad = inner_out[tall : tall + 16]
         state_grad = jnp.concatenate([state_grad[:, :states], state_grad[:, states:]], axis=0)
-        sums = inner_out[tail + 16 :]
+        sums = inner_out[tall + 16 : tall + 32] + inner_out[tall + 32 :]
+        step_grad = sums[10:12].reshape(heads, tall).T
         width = states // owners
         conv_state_sum = lax.dynamic_slice(
-            sums, (10, owner * width), (taps + 1, width)
+            sums[7:10].reshape(6, states), (0, owner * width), (taps + 1, width)
         )
         conv_state_grad, conv_state_bias_grad = conv_state_sum[:taps], conv_state_sum[taps]
-        inner_grad, step_grad = inner_out[:tall], inner_out[tall : tall + heads, :tall].T
     else:
         state_part, state_sums = state_parts
         state_grad = lax.psum_scatter(
@@ -1110,7 +1177,7 @@
         - token_float * (scale * scale * scale * along)
         + cotangent.astype(f32)
     )
-    skip_grad = sums[9].reshape(heads, -1).sum(axis=1)
+    skip_grad = sums[6].reshape(heads, -1).sum(axis=1)
     return (
         block_out,
         tokens_grad,
@@ -1122,10 +1189,10 @@
         sums[taps],
         conv_state_grad,
         conv_state_bias_grad,
-        sums[7, :heads],
-        sums[8, :heads],
+        sums[9, states : states + heads],
+        sums[9, states + 128 : states + 128 + heads],
         skip_grad,
-        sums[6],
+        sums[5],
         output_grad,
     )
 

time: 190 us -> 181 us (0.953)
  waiting for transfers between devices: 47.8 us -> 35.2 us
  Pallas kernels: 72.3 us -> 76.2 us
  starting transfers between devices: 43.6 us -> 46.7 us
    pallas_call x0 -> x4, Pallas kernels: none -> 12.8 us  [chunk_pair(): pl.pallas_call(functools.partial(chunk_kernel, slots, len(got)), grid_spe...]
    all_to_all x1 -> x0, waiting for transfers between devices: 11.2 us -> none  [body(): inner_out = lax.all_to_all(inner_msg, 'dp', 0, 0, tiled=True)]
    pallas_call x13 -> x12, Pallas kernels: 72.3 us -> 63.4 us  [call(): pl.pallas_call(kernel, out_shape=[jax.ShapeDtypeStruct(shape, kind) for s...]
    ppermute x17, waiting for transfers between devices: 10.8 us -> 3.09 us  [tensor_swap(): return lax.ppermute(value, 'tensor', [(i, i ^ bit) for i in range(4)])]
    ppermute x21 -> x28, starting transfers between devices: 23.2 us -> 30.4 us  [ring_send(): return lax.ppermute(value, 'dp', pairs)]
    ppermute x21 -> x28, waiting for transfers between devices: 25.7 us -> 32.1 us  [ring_send(): return lax.ppermute(value, 'dp', pairs)]
    all_to_all x1 -> x0, starting transfers between devices: 5.32 us -> none  [body(): inner_out = lax.all_to_all(inner_msg, 'dp', 0, 0, tiled=True)]
    unnamed x83 -> x86, local copies, waits for them, and re-layouts: 8 us -> 7.62 us
  transfers between devices with their start and end apart: 40 -> 46, of which waited for: 16 -> 17; matrix products, arithmetic and copies ran while one was open for 8% -> 8% of each run, Pallas kernels for 26% -> 29%
where the time goes in v5:
time: 181 us; the launch traced here: 180 us
  Pallas kernels  76.2 us (42%)
  starting transfers between devices  46.7 us (26%)
  waiting for transfers between devices  35.2 us (19%)
  local copies, waits for them, and re-layouts  13.3 us (7%)
  other arithmetic  7.59 us (4%)
    pallas_call x12, Pallas kernels, call(): pl.pallas_call(kernel, out_shape=[jax.ShapeDtypeStruct(shape, kind) for s...  63.4 us
    ppermute x28, waiting for transfers between devices, ring_send(): return lax.ppermute(value, 'dp', pairs)  32.1 us
    ppermute x28, starting transfers between devices, ring_send(): return lax.ppermute(value, 'dp', pairs)  30.4 us
    pallas_call x4, Pallas kernels, chunk_pair(): pl.pallas_call(functools.partial(chunk_kernel, slots, len(got)), grid_spe...  12.8 us
    ppermute x17, starting transfers between devices, tensor_swap(): return lax.ppermute(value, 'tensor', [(i, i ^ bit) for i in range(4)])  12.6 us
    unnamed x86, local copies, waits for them, and re-layouts  7.62 us
    all_to_all x1, starting transfers between devices, tensor_sum(): parts = lax.all_to_all(parts, 'tensor', 0, 0, tiled=True)  3.7 us
  transfers between devices with their start and end apart: 46, of which 17 were waited for; matrix products, arithmetic and copies ran while one was open for 8% of the time, Pallas kernels for 29%

profile of v5, /device:TPU:0, one launch (start us, length us, event | category | flops | bytes accessed | tf_op | source)
XLA Modules:
  0.0 180.1 jit_solution(4086242403243294191)
XLA Ops:
  3.3 2.6 %collective-permute-start.1 = (bf16[48,256]{1,0:T(8,128)(2,1)}, bf16[48,256]{1,0:T(8,128)(2,1)S(1)}, u32[]{:S(2)}, u32[]{:S(2)}) collective-permute-start(bf16[48,256]{1,0:T(8,128)(2,1)} %shard_map.271.refs_0_), channel_id=1, source_target_pairs={{0,2},{1,3},{2,0},{3,1},{4,6},{5,7},{6,4},{7,5},{8,10},{9,11},{10,... | collective-permute-start | bytes 73736 | tf_op jit(solution)/shard_map/ppermute | solution.py:787
  5.9 2.0 %shard_map.272.refs_4_ = bf16[256,512]{1,0:T(8,128)(2,1)} custom-call(bf16[128,2,512]{2,1,0:T(2,128)(2,1)} %input_ref.3, bf16[512,128]{1,0:T(8,128)(2,1)} %out_ref), custom_call_target="tpu_custom_call" | custom-call | flops 2200000000 | bytes 1048576 | tf_op jit(solution)/shard_map/pallas_call | solution.py:703
  8.0 1.8 %collective-permute-start.6 = (bf16[256,512]{1,0:T(8,128)(2,1)}, bf16[256,512]{1,0:T(8,128)(2,1)S(1)}, u32[]{:S(2)}, u32[]{:S(2)}) collective-permute-start(bf16[256,512]{1,0:T(8,128)(2,1)} %shard_map.272.refs_4_), channel_id=1, source_target_pairs={{0,8},{8,16},{16,24},{24,28},{28,20},{20,12},{12,4},{4,0},{1,9},{9... | collective-permute-start | bytes 786440 | tf_op jit(solution)/shard_map/ppermute | solution.py:738
  10.1 1.8 collective-permute-start.4
  12.5 2.0 %shard_map.273.refs_4_ = bf16[208,512]{1,0:T(8,128)(2,1)} custom-call(bf16[128,2,512]{2,1,0:T(2,128)(2,1)} %input_ref.3, bf16[16,128]{1,0:T(8,128)(2,1)} %pad.4.step_ref, bf16[48,256]{1,0:T(8,128)(2,1)} %shard_map.271.refs_0_, bf16[48,256]{1,0:T(8,128)(2,1)} %copy-done.35, bf16[48,256]{1,0:T(8,128)(2,1)} %copy-done.36, bf16[48,256]{1,0:T(8,128)(2,1)} %copy-done.37), custom_call_target="tpu_custom_call" | custom-call | flops 1100000000 | bytes 1048576 | tf_op jit(solution)/shard_map/pallas_call | solution.py:703
  14.5 2.2 %collective-permute-done.6.refs_5_ = bf16[256,512]{1,0:T(8,128)(2,1)S(1)} collective-permute-done((bf16[256,512]{1,0:T(8,128)(2,1)}, bf16[256,512]{1,0:T(8,128)(2,1)S(1)}, u32[]{:S(2)}, u32[]{:S(2)}) %collective-permute-start.6) | collective-permute-done | bytes 262176 | tf_op jit(solution)/shard_map/ppermute | solution.py:738
  21.9 4.8 %collective-permute-done.13.refs_5_ = bf16[208,512]{1,0:T(8,128)(2,1)S(1)} collective-permute-done((bf16[208,512]{1,0:T(8,128)(2,1)}, bf16[208,512]{1,0:T(8,128)(2,1)S(1)}, u32[]{:S(2)}, u32[]{:S(2)}) %collective-permute-start.13) | collective-permute-done | bytes 213024 | tf_op jit(solution)/shard_map/ppermute | solution.py:738
  29.0 3.4 %collective-permute-done.8.refs_7_ = bf16[256,512]{1,0:T(8,128)(2,1)} collective-permute-done((bf16[256,512]{1,0:T(8,128)(2,1)S(1)}, bf16[256,512]{1,0:T(8,128)(2,1)}, u32[]{:S(2)}, u32[]{:S(2)}) %collective-permute-start.8) | collective-permute-done | bytes 262176 | tf_op jit(solution)/shard_map/ppermute | solution.py:738
  32.7 2.3 %collective-permute-done.15.refs_7_ = bf16[208,512]{1,0:T(8,128)(2,1)S(1)} collective-permute-done((bf16[208,512]{1,0:T(8,128)(2,1)S(1)}, bf16[208,512]{1,0:T(8,128)(2,1)S(1)}, u32[]{:S(2)}, u32[]{:S(2)}) %collective-permute-start.15) | collective-permute-done | bytes 213024 | tf_op jit(solution)/shard_map/ppermute | solution.py:738
  39.7 1.9 %collective-permute-done.16.refs_8_ = bf16[208,512]{1,0:T(8,128)(2,1)} collective-permute-done((bf16[208,512]{1,0:T(8,128)(2,1)S(1)}, bf16[208,512]{1,0:T(8,128)(2,1)}, u32[]{:S(2)}, u32[]{:S(2)}) %collective-permute-start.16) | collective-permute-done | bytes 213024 | tf_op jit(solution)/shard_map/ppermute | solution.py:738
  49.3 3.0 %collective-permute-done.19.refs_11_ = bf16[208,512]{1,0:T(8,128)(2,1)} collective-permute-done((bf16[208,512]{1,0:T(8,128)(2,1)}, bf16[208,512]{1,0:T(8,128)(2,1)}, u32[]{:S(2)}, u32[]{:S(2)}) %collective-permute-start.19) | collective-permute-done | bytes 213024 | tf_op jit(solution)/shard_map/ppermute | solution.py:738
  52.3 11.1 %shard_map.275 = (bf16[512,1024]{1,0:T(8,128)(2,1)}, bf16[1024,512]{1,0:T(8,128)(2,1)}, bf16[1024,512]{1,0:T(8,128)(2,1)}, bf16[1024,256]{1,0:T(8,128)(2,1)}, bf...) custom-call(s32[12]{0:T(128)} %stack.66.place_ref, ...), custom_call_target="tpu_custom_call" | custom-call | flops 12099999744 | bytes 1048576 | tf_op jit(solution)/shard_map/pallas_call | solution.py:703
  64.2 7.3 %shard_map.276 = (bf16[512,1024]{1,0:T(8,128)(2,1)}, bf16[1024,512]{1,0:T(8,128)(2,1)}, bf16[1024,512]{1,0:T(8,128)(2,1)}, f32[512,512]{1,0:T(8,128)}, f32[512,512]{1,0:T(8,128)}, /*index=5*/f32[8,512]{1,0:T(8,128)}) custom-call(s32[12]{0:T(128)} %stack.66.place_ref, s32[1,4]{1,0:T(1,128)} %lengths_ref.13, bf16[256,1024]{1,0:T(8,128)(2,1)} %copy-done.4, ...), custom_call_target="tpu_custom_call" | custom-call | flops 5500000256 | bytes 1048576 | tf_op jit(solution)/shard_map/pallas_call | solution.py:703
  73.4 2.1 %collective-permute-done.21.refs_2_ = f32[8,512]{1,0:T(8,128)S(1)} collective-permute-done((f32[8,512]{1,0:T(8,128)}, f32[8,512]{1,0:T(8,128)S(1)}, u32[]{:S(2)}, u32[]{:S(2)}) %collective-permute-start.21) | collective-permute-done | bytes 16416 | tf_op jit(solution)/shard_map/ppermute | solution.py:787
  77.1 8.2 %shard_map.277 = (bf16[256,512]{1,0:T(8,128)(2,1)}, bf16[256,512]{1,0:T(8,128)(2,1)}, bf16[256,512]{1,0:T(8,128)(2,1)}, bf16[256,512]{1,0:T(8,128)(2,1)}, bf16[2...) custom-call(s32[12]{0:T(128)} %stack.66.place_ref, ...), custom_call_target="tpu_custom_call" | custom-call | flops 9900000256 | bytes 1048576 | tf_op jit(solution)/shard_map/pallas_call | solution.py:703
  87.3 3.7 %all-to-all-start = ((bf16[4,128,1024]{2,1,0:T(8,128)(2,1)}), bf16[4,128,1024]{2,1,0:T(8,128)(2,1)S(1)}, u32[]{:S(2)}, u32[]{:S(2)}) async-start(bf16[4,128,1024]{2,1,0:T(8,128)(2,1)} %bitcast.49), calls=%async_computation | async-start | bytes 2097152 | tf_op jit(solution)/shard_map/all_to_all | solution.py:782
  91.1 6.5 %shard_map.278 = (f32[512,256]{1,0:T(8,128)}, f32[512,256]{1,0:T(8,128)}, f32[16,512]{1,0:T(8,128)}, f32[8,256]{1,0:T(8,128)}) custom-call(s32[1,4]{1,0:T(1,128)} %lengths_ref.13, f32[512,512]{1,0:T(8,128)} %get-tuple-element.144.refs_0_, f32[512,512]{1,0:T(8,128)} %get-tuple-element.139.refs_1_, f32[512,256]{1,0:T(8,128)} %get-tuple-element.140.refs_2_, ...), custom_call_target="tpu_custom_call" | custom-call | flops 6600000000 | bytes 1048576 | tf_op jit(solution)/shard_map/pallas_call | solution.py:703
  99.9 6.5 %shard_map.279 = (f32[512,256]{1,0:T(8,128)}, f32[512,256]{1,0:T(8,128)}, f32[16,512]{1,0:T(8,128)}, f32[8,256]{1,0:T(8,128)}) custom-call(s32[1,4]{1,0:T(1,128)} %lengths_ref.13, f32[512,512]{1,0:T(8,128)} %get-tuple-element.144.refs_0_, f32[512,512]{1,0:T(8,128)} %get-tuple-element.139.refs_1_, f32[512,256]{1,0:T(8,128)} %get-tuple-element.140.refs_2_, ...), custom_call_target="tpu_custom_call" | custom-call | flops 6600000000 | bytes 1048576 | tf_op jit(solution)/shard_map/pallas_call | solution.py:703
  109.5 5.4 %shard_map.281 = (bf16[512,256]{1,0:T(8,128)(2,1)}, bf16[16,512]{1,0:T(8,128)(2,1)}, bf16[272,256]{1,0:T(8,128)(2,1)}, bf16[272,256]{1,0:T(8,128)(2,1)}, bf16[27...) custom-call(s32[12]{0:T(128)} %stack.66.place_ref, s32[1,4]{1,0:T(1,128)} %lengths_ref.13, ...), custom_call_target="tpu_custom_call" | custom-call | flops 4400000000 | bytes 1048576 | tf_op jit(solution)/shard_map/pallas_call | solution.py:703
  117.9 5.6 %shard_map.280 = (bf16[512,512]{1,0:T(8,128)(2,1)}, f32[16,512]{1,0:T(8,128)}) custom-call(s32[1,4]{1,0:T(1,128)} %lengths_ref.13, f32[512,256]{1,0:T(8,128)} %get-tuple-element.143.refs_0_, f32[512,256]{1,0:T(8,128)} %get-tuple-element.145.refs_1_, f32[8,256]{1,0:T(8,128)} %get-tuple-element.146.refs_2_, f32[8,256]{1,0:T(8,128)} %get-tuple-element.147.refs_3_, ...), custom_call_target="tpu_custom_call" | custom-call | flops 6600000000 | bytes 1048576 | tf_op jit(solution)/shard_map/pallas_call | solution.py:703
  123.7 2.0 %collective-permute-done.29 = bf16[256,512]{1,0:T(8,128)(2,1)S(1)} collective-permute-done((bf16[256,512]{1,0:T(8,128)(2,1)S(1)}, bf16[256,512]{1,0:T(8,128)(2,1)S(1)}, u32[]{:S(2)}, u32[]{:S(2)}) %collective-permute-start.29) | collective-permute-done | bytes 262176 | tf_op jit(solution)/shard_map/ppermute | solution.py:738
  125.8 3.1 %shard_map.283 = (bf16[176,512]{1,0:T(8,128)(2,1)}, bf16[176,512]{1,0:T(8,128)(2,1)}) custom-call(s32[12]{0:T(128)} %stack.66.place_ref, bf16[512,512]{1,0:T(8,128)(2,1)} %get-tuple-element.174.refs_1_.refs_0_, bf16[16,512]{1,0:T(8,128)(2,1)} %get-tuple-element.161.refs_3_.refs_1_, f32[16,512]{1,0:T(8,128)} %get-tuple-element.169.refs_2_, ...), custom_call_target="tpu_custom_call" | custom-call | flops 2000000000 | bytes 1048576 | tf_op jit(solution)/shard_map/pallas_call | solution.py:1087
  130.9 5.6 %shard_map.282 = (bf16[2,128,1024]{2,1,0:T(8,128)(2,1)}, bf16[2,128,1024]{2,1,0:T(8,128)(2,1)}) custom-call(s32[12]{0:T(128)} %stack.66.place_ref, bf16[512,512]{1,0:T(8,128)(2,1)} %get-tuple-element.152.refs_0_, bf16[512,512]{1,0:T(8,128)(2,1)} %get-tuple-element.174.refs_1_.refs_0_, bf16[512,256]{1,0:T(8,128)(2,1)} %get-tuple-element.160.refs_2_, ...), custom_call_target="tpu_custom_call" | custom-call | flops 6600000000 | bytes 1048576 | tf_op jit(solution)/shard_map/pallas_call | solution.py:703
  137.9 3.2 %shard_map.284 = (bf16[176,512]{1,0:T(8,128)(2,1)}, bf16[176,512]{1,0:T(8,128)(2,1)}) custom-call(s32[12]{0:T(128)} %stack.66.place_ref, bf16[512,512]{1,0:T(8,128)(2,1)} %get-tuple-element.174.refs_1_.refs_0_, bf16[16,512]{1,0:T(8,128)(2,1)} %get-tuple-element.161.refs_3_.refs_1_, f32[16,512]{1,0:T(8,128)} %get-tuple-element.169.refs_2_, ...), custom_call_target="tpu_custom_call" | custom-call | flops 2000000000 | bytes 1048576 | tf_op jit(solution)/shard_map/pallas_call | solution.py:1087
  143.8 3.0 %collective-permute-done.37.refs_9_ = bf16[176,512]{1,0:T(8,128)(2,1)S(1)} collective-permute-done((bf16[176,512]{1,0:T(8,128)(2,1)}, bf16[176,512]{1,0:T(8,128)(2,1)S(1)}, u32[]{:S(2)}, u32[]{:S(2)}) %collective-permute-start.37) | collective-permute-done | bytes 180256 | tf_op jit(solution)/shard_map/ppermute | solution.py:738
  148.4 3.2 %shard_map.285 = (bf16[176,512]{1,0:T(8,128)(2,1)}, bf16[176,512]{1,0:T(8,128)(2,1)}) custom-call(s32[12]{0:T(128)} %stack.66.place_ref, bf16[512,512]{1,0:T(8,128)(2,1)} %get-tuple-element.174.refs_1_.refs_0_, bf16[16,512]{1,0:T(8,128)(2,1)} %get-tuple-element.161.refs_3_.refs_1_, f32[16,512]{1,0:T(8,128)} %get-tuple-element.169.refs_2_, ...), custom_call_target="tpu_custom_call" | custom-call | flops 2000000000 | bytes 1048576 | tf_op jit(solution)/shard_map/pallas_call | solution.py:1087
  151.6 1.8 collective-permute-start.39
  155.2 2.1 %collective-permute-done.39.refs_9_ = bf16[176,512]{1,0:T(8,128)(2,1)S(1)} collective-permute-done((bf16[176,512]{1,0:T(8,128)(2,1)}, bf16[176,512]{1,0:T(8,128)(2,1)S(1)}, u32[]{:S(2)}, u32[]{:S(2)}) %collective-permute-start.39) | collective-permute-done | bytes 180256 | tf_op jit(solution)/shard_map/ppermute | solution.py:738
  157.3 1.8 collective-permute-done.40.refs_10_
  159.8 3.3 %shard_map.286 = (bf16[176,512]{1,0:T(8,128)(2,1)}, f32[176,512]{1,0:T(8,128)}) custom-call(s32[12]{0:T(128)} %stack.66.place_ref, bf16[512,512]{1,0:T(8,128)(2,1)} %get-tuple-element.174.refs_1_.refs_0_, bf16[16,512]{1,0:T(8,128)(2,1)} %get-tuple-element.161.refs_3_.refs_1_, f32[16,512]{1,0:T(8,128)} %get-tuple-element.169.refs_2_, ...), custom_call_target="tpu_custom_call" | custom-call | flops 2000000000 | bytes 1048576 | tf_op jit(solution)/shard_map/pallas_call | solution.py:1087
  163.0 1.8 collective-permute-start.41
  171.2 1.8 collective-permute-start.43
  (201 shorter events, 62.0 us)
Async XLA Ops:
  2.8 7.3 %collective-permute-start = (bf16[48,256]{1,0:T(8,128)(2,1)}, bf16[48,256]{1,0:T(8,128)(2,1)S(1)}, u32[]{:S(2)}, u32[]{:S(2)}) collective-permute-start(bf16[48,256]{1,0:T(8,128)(2,1)} %shard_map.271.refs_0_), channel_id=1, source_target_pairs={{0,1},{1,0},{2,3},{3,2},{4,5},{5,4},{6,7},{7,6},{8,9},{9,8},{10,11... | collective-permute-start | bytes 73736 | tf_op jit(solution)/shard_map/ppermute | solution.py:787
  8.0 8.8 %collective-permute-start.6 = (bf16[256,512]{1,0:T(8,128)(2,1)}, bf16[256,512]{1,0:T(8,128)(2,1)S(1)}, u32[]{:S(2)}, u32[]{:S(2)}) collective-permute-start(bf16[256,512]{1,0:T(8,128)(2,1)} %shard_map.272.refs_4_), channel_id=1, source_target_pairs={{0,8},{8,16},{16,24},{24,28},{28,20},{20,12},{12,4},{4,0},{1,9},{9... | collective-permute-start | bytes 786440 | tf_op jit(solution)/shard_map/ppermute | solution.py:738
  9.8 8.5 %collective-permute-start.7 = (bf16[256,512]{1,0:T(8,128)(2,1)}, bf16[256,512]{1,0:T(8,128)(2,1)S(1)}, u32[]{:S(2)}, u32[]{:S(2)}) collective-permute-start(bf16[256,512]{1,0:T(8,128)(2,1)} %shard_map.272.refs_4_), channel_id=1, source_target_pairs={{0,4},{8,0},{16,8},{24,16},{28,24},{20,28},{12,20},{4,12},{1,5},{9... | collective-permute-start | bytes 786440 | tf_op jit(solution)/shard_map/ppermute | solution.py:738
  10.1 18.7 %collective-permute-start.4 = (bf16[256,1024]{1,0:T(8,128)(2,1)S(1)}, bf16[256,1024]{1,0:T(8,128)(2,1)S(1)}, u32[]{:S(2)}, u32[]{:S(2)}) collective-permute-start(bf16[256,1024]{1,0:T(8,128)(2,1)S(1)} %pad_maximum_fusion.refs_0_), channel_id=1, source_target_pairs={{0,2},{1,3},{2,0},{3,1},{4,6},{5,7},{6,4},{7,5},{8,10},{9,11},{10,... | collective-permute-start | bytes 1572872 | tf_op jit(solution)/shard_map/ppermute | solution.py:787
  18.3 8.4 %collective-permute-start.13 = (bf16[208,512]{1,0:T(8,128)(2,1)}, bf16[208,512]{1,0:T(8,128)(2,1)S(1)}, u32[]{:S(2)}, u32[]{:S(2)}) collective-permute-start(bf16[208,512]{1,0:T(8,128)(2,1)} %shard_map.273.refs_4_), channel_id=1, source_target_pairs={{0,8},{8,16},{16,24},{24,28},{28,20},{20,12},{12,4},{4,0},{1,9},{9... | collective-permute-start | bytes 638984 | tf_op jit(solution)/shard_map/ppermute | solution.py:738
  19.9 8.4 %collective-permute-start.14 = (bf16[208,512]{1,0:T(8,128)(2,1)}, bf16[208,512]{1,0:T(8,128)(2,1)S(1)}, u32[]{:S(2)}, u32[]{:S(2)}) collective-permute-start(bf16[208,512]{1,0:T(8,128)(2,1)} %shard_map.273.refs_4_), channel_id=1, source_target_pairs={{0,4},{8,0},{16,8},{24,16},{28,24},{20,28},{12,20},{4,12},{1,5},{9... | collective-permute-start | bytes 638984 | tf_op jit(solution)/shard_map/ppermute | solution.py:738
  20.3 12.1 %collective-permute-start.8 = (bf16[256,512]{1,0:T(8,128)(2,1)S(1)}, bf16[256,512]{1,0:T(8,128)(2,1)}, u32[]{:S(2)}, u32[]{:S(2)}) collective-permute-start(bf16[256,512]{1,0:T(8,128)(2,1)S(1)} %collective-permute-done.6.refs_5_), channel_id=1, source_target_pairs={{0,8},{8,16},{16,24},{24,28},{28,20},{20,12},{12,4},{4,0},{1,9},{9... | collective-permute-start | bytes 786440 | tf_op jit(solution)/shard_map/ppermute | solution.py:738
  26.7 8.4 %collective-permute-start.15 = (bf16[208,512]{1,0:T(8,128)(2,1)S(1)}, bf16[208,512]{1,0:T(8,128)(2,1)S(1)}, u32[]{:S(2)}, u32[]{:S(2)}) collective-permute-start(bf16[208,512]{1,0:T(8,128)(2,1)S(1)} %collective-permute-done.13.refs_5_), channel_id=1, source_target_pairs={{0,8},{8,16},{16,24},{24,28},{28,20},{20,12},{12,4},{4,0},{1,9},{9... | collective-permute-start | bytes 638984 | tf_op jit(solution)/shard_map/ppermute | solution.py:738
  28.3 18.9 %collective-permute-start.3 = (bf16[256,1024]{1,0:T(8,128)(2,1)S(1)}, bf16[256,1024]{1,0:T(8,128)(2,1)S(1)}, u32[]{:S(2)}, u32[]{:S(2)}) collective-permute-start(bf16[256,1024]{1,0:T(8,128)(2,1)S(1)} %pad_maximum_fusion.refs_0_), channel_id=1, source_target_pairs={{0,1},{1,0},{2,3},{3,2},{4,5},{5,4},{6,7},{7,6},{8,9},{9,8},{10,11... | collective-permute-start | bytes 1572872 | tf_op jit(solution)/shard_map/ppermute | solution.py:787
  28.3 9.2 %collective-permute-start.9 = (bf16[256,512]{1,0:T(8,128)(2,1)S(1)}, bf16[256,512]{1,0:T(8,128)(2,1)S(1)}, u32[]{:S(2)}, u32[]{:S(2)}) collective-permute-start(bf16[256,512]{1,0:T(8,128)(2,1)S(1)} %collective-permute-done.7.refs_6_), channel_id=1, source_target_pairs={{0,4},{8,0},{16,8},{24,16},{28,24},{20,28},{12,20},{4,12},{1,5},{9... | collective-permute-start | bytes 786440 | tf_op jit(solution)/shard_map/ppermute | solution.py:738
  28.8 20.5 %collective-permute-start.5 = (bf16[256,1024]{1,0:T(8,128)(2,1)S(1)}, bf16[256,1024]{1,0:T(8,128)(2,1)S(1)}, u32[]{:S(2)}, u32[]{:S(2)}) collective-permute-start(bf16[256,1024]{1,0:T(8,128)(2,1)S(1)} %collective-permute-done.4.refs_2_), channel_id=1, source_target_pairs={{0,1},{1,0},{2,3},{3,2},{4,5},{5,4},{6,7},{7,6},{8,9},{9,8},{10,11... | collective-permute-start | bytes 1572872 | tf_op jit(solution)/shard_map/ppermute | solution.py:787
  32.4 9.3 %collective-permute-start.16 = (bf16[208,512]{1,0:T(8,128)(2,1)S(1)}, bf16[208,512]{1,0:T(8,128)(2,1)}, u32[]{:S(2)}, u32[]{:S(2)}) collective-permute-start(bf16[208,512]{1,0:T(8,128)(2,1)S(1)} %collective-permute-done.14.refs_6_), channel_id=1, source_target_pairs={{0,4},{8,0},{16,8},{24,16},{28,24},{20,28},{12,20},{4,12},{1,5},{9... | collective-permute-start | bytes 638984 | tf_op jit(solution)/shard_map/ppermute | solution.py:738
  35.0 7.1 %collective-permute-start.17 = (bf16[208,512]{1,0:T(8,128)(2,1)S(1)}, bf16[208,512]{1,0:T(8,128)(2,1)}, u32[]{:S(2)}, u32[]{:S(2)}) collective-permute-start(bf16[208,512]{1,0:T(8,128)(2,1)S(1)} %collective-permute-done.15.refs_7_), channel_id=1, source_target_pairs={{0,8},{8,16},{16,24},{24,28},{28,20},{20,12},{12,4},{4,0},{1,9},{9... | collective-permute-start | bytes 638984 | tf_op jit(solution)/shard_map/ppermute | solution.py:738
  38.1 9.6 %collective-permute-start.10 = (bf16[256,512]{1,0:T(8,128)(2,1)}, bf16[256,512]{1,0:T(8,128)(2,1)}, u32[]{:S(2)}, u32[]{:S(2)}) collective-permute-start(bf16[256,512]{1,0:T(8,128)(2,1)} %collective-permute-done.8.refs_7_), channel_id=1, source_target_pairs={{0,8},{8,16},{16,24},{24,28},{28,20},{20,12},{12,4},{4,0},{1,9},{9... | collective-permute-start | bytes 786440 | tf_op jit(solution)/shard_map/ppermute | solution.py:738
  41.7 7.6 %collective-permute-start.18 = (bf16[208,512]{1,0:T(8,128)(2,1)}, bf16[208,512]{1,0:T(8,128)(2,1)}, u32[]{:S(2)}, u32[]{:S(2)}) collective-permute-start(bf16[208,512]{1,0:T(8,128)(2,1)} %collective-permute-done.16.refs_8_), channel_id=1, source_target_pairs={{0,4},{8,0},{16,8},{24,16},{28,24},{20,28},{12,20},{4,12},{1,5},{9... | collective-permute-start | bytes 638984 | tf_op jit(solution)/shard_map/ppermute | solution.py:738
  42.1 10.1 %collective-permute-start.19 = (bf16[208,512]{1,0:T(8,128)(2,1)}, bf16[208,512]{1,0:T(8,128)(2,1)}, u32[]{:S(2)}, u32[]{:S(2)}) collective-permute-start(bf16[208,512]{1,0:T(8,128)(2,1)} %collective-permute-done.17.refs_9_), channel_id=1, source_target_pairs={{0,8},{8,16},{16,24},{24,28},{28,20},{20,12},{12,4},{4,0},{1,9},{9... | collective-permute-start | bytes 638984 | tf_op jit(solution)/shard_map/ppermute | solution.py:738
  47.2 16.2 %collective-permute-start.11 = (bf16[256,512]{1,0:T(8,128)(2,1)}, bf16[256,512]{1,0:T(8,128)(2,1)S(1)}, u32[]{:S(2)}, u32[]{:S(2)}) collective-permute-start(bf16[256,512]{1,0:T(8,128)(2,1)} %copy-done.23), channel_id=1, source_target_pairs={{0,4},{8,0},{16,8},{24,16},{28,24},{20,28},{12,20},{4,12},{1,5},{9... | collective-permute-start | bytes 786440 | tf_op jit(solution)/shard_map/ppermute | solution.py:738
  47.7 15.7 %collective-permute-start.12 = (bf16[256,512]{1,0:T(8,128)(2,1)}, bf16[256,512]{1,0:T(8,128)(2,1)S(1)}, u32[]{:S(2)}, u32[]{:S(2)}) collective-permute-start(bf16[256,512]{1,0:T(8,128)(2,1)} %collective-permute-done.10.refs_9_), channel_id=1, source_target_pairs={{0,8},{8,16},{16,24},{24,28},{28,20},{20,12},{12,4},{4,0},{1,9},{9... | collective-permute-start | bytes 786440 | tf_op jit(solution)/shard_map/ppermute | solution.py:738
  85.2 12.3 %collective-permute-start.24 = (bf16[256,512]{1,0:T(8,128)(2,1)}, bf16[256,512]{1,0:T(8,128)(2,1)S(1)}, u32[]{:S(2)}, u32[]{:S(2)}) collective-permute-start(bf16[256,512]{1,0:T(8,128)(2,1)} %get-tuple-element.124), channel_id=1, source_target_pairs={{0,4},{8,0},{16,8},{24,16},{28,24},{20,28},{12,20},{4,12},{1,5},{9... | collective-permute-start | bytes 786440 | tf_op jit(solution)/shard_map/ppermute | solution.py:738
  85.8 11.9 %collective-permute-start.23 = (bf16[256,512]{1,0:T(8,128)(2,1)}, bf16[256,512]{1,0:T(8,128)(2,1)S(1)}, u32[]{:S(2)}, u32[]{:S(2)}) collective-permute-start(bf16[256,512]{1,0:T(8,128)(2,1)} %get-tuple-element.122), channel_id=1, source_target_pairs={{0,8},{8,16},{16,24},{24,28},{28,20},{20,12},{12,4},{4,0},{1,9},{9... | collective-permute-start | bytes 786440 | tf_op jit(solution)/shard_map/ppermute | solution.py:738
  87.3 36.2 %all-to-all-start = ((bf16[4,128,1024]{2,1,0:T(8,128)(2,1)}), bf16[4,128,1024]{2,1,0:T(8,128)(2,1)S(1)}, u32[]{:S(2)}, u32[]{:S(2)}) async-start(bf16[4,128,1024]{2,1,0:T(8,128)(2,1)} %bitcast.49), calls=%async_computation | async-start | bytes 2097152 | tf_op jit(solution)/shard_map/all_to_all | solution.py:782
  97.8 8.6 %collective-permute-start.26 = (bf16[256,512]{1,0:T(8,128)(2,1)S(1)}, bf16[256,512]{1,0:T(8,128)(2,1)S(1)}, u32[]{:S(2)}, u32[]{:S(2)}) collective-permute-start(bf16[256,512]{1,0:T(8,128)(2,1)S(1)} %add_convert_fusion.4), channel_id=1, source_target_pairs={{0,4},{8,0},{16,8},{24,16},{28,24},{20,28},{12,20},{4,12},{1,5},{9... | collective-permute-start | bytes 786440 | tf_op jit(solution)/shard_map/ppermute | solution.py:738
  98.8 8.5 %collective-permute-start.25 = (bf16[256,512]{1,0:T(8,128)(2,1)S(1)}, bf16[256,512]{1,0:T(8,128)(2,1)S(1)}, u32[]{:S(2)}, u32[]{:S(2)}) collective-permute-start(bf16[256,512]{1,0:T(8,128)(2,1)S(1)} %add_convert_fusion.5), channel_id=1, source_target_pairs={{0,8},{8,16},{16,24},{24,28},{28,20},{20,12},{12,4},{4,0},{1,9},{9... | collective-permute-start | bytes 786440 | tf_op jit(solution)/shard_map/ppermute | solution.py:738
  107.4 9.4 %collective-permute-start.27 = (bf16[256,512]{1,0:T(8,128)(2,1)S(1)}, bf16[256,512]{1,0:T(8,128)(2,1)S(1)}, u32[]{:S(2)}, u32[]{:S(2)}) collective-permute-start(bf16[256,512]{1,0:T(8,128)(2,1)S(1)} %add_convert_fusion.3), channel_id=1, source_target_pairs={{0,8},{8,16},{16,24},{24,28},{28,20},{20,12},{12,4},{4,0},{1,9},{9... | collective-permute-start | bytes 786440 | tf_op jit(solution)/shard_map/ppermute | solution.py:738
  108.2 8.7 %collective-permute-start.28 = (bf16[256,512]{1,0:T(8,128)(2,1)S(1)}, bf16[256,512]{1,0:T(8,128)(2,1)S(1)}, u32[]{:S(2)}, u32[]{:S(2)}) collective-permute-start(bf16[256,512]{1,0:T(8,128)(2,1)S(1)} %add_convert_fusion.2), channel_id=1, source_target_pairs={{0,4},{8,0},{16,8},{24,16},{28,24},{20,28},{12,20},{4,12},{1,5},{9... | collective-permute-start | bytes 786440 | tf_op jit(solution)/shard_map/ppermute | solution.py:738
  114.9 10.9 %collective-permute-start.32 = (bf16[272,256]{1,0:T(8,128)(2,1)}, bf16[272,256]{1,0:T(8,128)(2,1)}, u32[]{:S(2)}, u32[]{:S(2)}) collective-permute-start(bf16[272,256]{1,0:T(8,128)(2,1)} %get-tuple-element.171), channel_id=1, source_target_pairs={{0,1},{1,0},{2,3},{3,2},{4,5},{5,4},{6,7},{7,6},{8,9},{9,8},{10,11... | collective-permute-start | bytes 417800 | tf_op jit(solution)/shard_map/ppermute | solution.py:787
  114.9 10.9 %collective-permute-start.33 = (bf16[272,256]{1,0:T(8,128)(2,1)}, bf16[272,256]{1,0:T(8,128)(2,1)}, u32[]{:S(2)}, u32[]{:S(2)}) collective-permute-start(bf16[272,256]{1,0:T(8,128)(2,1)} %get-tuple-element.172), channel_id=1, source_target_pairs={{0,2},{1,3},{2,0},{3,1},{4,6},{5,7},{6,4},{7,5},{8,10},{9,11},{10,... | collective-permute-start | bytes 417800 | tf_op jit(solution)/shard_map/ppermute | solution.py:787
  116.6 9.2 %collective-permute-start.34 = (bf16[272,256]{1,0:T(8,128)(2,1)}, bf16[272,256]{1,0:T(8,128)(2,1)}, u32[]{:S(2)}, u32[]{:S(2)}) collective-permute-start(bf16[272,256]{1,0:T(8,128)(2,1)} %get-tuple-element.173), channel_id=1, source_target_pairs={{0,3},{1,2},{2,1},{3,0},{4,7},{5,6},{6,5},{7,4},{8,11},{9,10},{10,... | collective-permute-start | bytes 417800 | tf_op jit(solution)/shard_map/ppermute | solution.py:787
  116.8 8.8 %collective-permute-start.29 = (bf16[256,512]{1,0:T(8,128)(2,1)S(1)}, bf16[256,512]{1,0:T(8,128)(2,1)S(1)}, u32[]{:S(2)}, u32[]{:S(2)}) collective-permute-start(bf16[256,512]{1,0:T(8,128)(2,1)S(1)} %add_convert_fusion.1), channel_id=1, source_target_pairs={{0,8},{8,16},{16,24},{24,28},{28,20},{20,12},{12,4},{4,0},{1,9},{9... | collective-permute-start | bytes 786440 | tf_op jit(solution)/shard_map/ppermute | solution.py:738
  128.9 7.6 %collective-permute-start.35 = (bf16[176,512]{1,0:T(8,128)(2,1)}, bf16[176,512]{1,0:T(8,128)(2,1)S(1)}, u32[]{:S(2)}, u32[]{:S(2)}) collective-permute-start(bf16[176,512]{1,0:T(8,128)(2,1)} %get-tuple-element.175), channel_id=1, source_target_pairs={{0,8},{8,16},{16,24},{24,28},{28,20},{20,12},{12,4},{4,0},{1,9},{9... | collective-permute-start | bytes 540680 | tf_op jit(solution)/shard_map/ppermute | solution.py:738
  143.8 21.0 %collective-permute-start.30 = (bf16[2,128,1024]{2,1,0:T(8,128)(2,1)S(1)}, bf16[2,128,1024]{2,1,0:T(8,128)(2,1)S(1)}, u32[]{:S(2)}, u32[]{:S(2)}) collective-permute-start(bf16[2,128,1024]{2,1,0:T(8,128)(2,1)S(1)} %copy-done.20), channel_id=1, source_target_pairs={{0,1},{1,0},{2,3},{3,2},{4,5},{5,4},{6,7},{7,6},{8,9},{9,8},{10,11... | collective-permute-start | bytes 1572872 | tf_op jit(solution)/shard_map/ppermute | solution.py:787
  165.6 13.1 %collective-permute-start.31 = (bf16[128,1024]{1,0:T(8,128)(2,1)}, bf16[128,1024]{1,0:T(8,128)(2,1)S(1)}, u32[]{:S(2)}, u32[]{:S(2)}) collective-permute-start(bf16[128,1024]{1,0:T(8,128)(2,1)} %fusion.6), channel_id=1, source_target_pairs={{0,2},{1,3},{2,0},{3,1},{4,6},{5,7},{6,4},{7,5},{8,10},{9,11},{10,... | collective-permute-start | bytes 786440 | tf_op jit(solution)/shard_map/ppermute | solution.py:787
  (55 other events, 398.4 us)

commit v6 on v5

--- a/solution.py
+++ b/solution.py
@@ -15,7 +15,7 @@
 pad = 8
 head_rows = 16
 head_width = 64
-vmem_bytes = 61 * 1024 * 1024
+vmem_bytes = 63 * 1024 * 1024
 
 
 def mm(a, b, over=(1, 0)):
@@ -580,9 +580,12 @@
         jnp.concatenate([shared[2:3, :], shared[3:4, :]], axis=1),
         jnp.concatenate([shared[4:5, :], sums_ref[9:10, states:]], axis=1),
     ]
+    tall = turned_refs[0].shape[0]
+    parts = jnp.concatenate([ref[...] for ref in turned_refs], axis=0)
+    products = mm(parts, grad_inner_ref[...])
     for n, (slot, out_ref) in enumerate(zip(slots, out_refs)):
         index = place_ref[slot]
-        part = turned_refs[n][...]
+        part = parts[tall * n : tall * (n + 1), :]
         step = mm(step_low_ref[...], part, (1, 1))
         step = [
             jnp.concatenate([step[4 * k + i : 4 * k + i + 1, :] for i in range(4)], axis=1)
@@ -591,7 +594,7 @@
         state = state_rows(pl.multiple_of(index * share, share), share)
         value = jnp.concatenate(
             [
-                mm(part, grad_inner_ref[...]),
+                products[tall * n : tall * (n + 1), :],
                 jnp.concatenate([state[:16, :], state[16:, :]], axis=1),
                 *sums,
                 *step,
@@ -612,6 +615,35 @@
         out_ref[tail + 16 :, :] = (sums_here - high.astype(f32)).astype(out_ref.dtype)
 
 
+def finish_kernel(*refs):
+    own_ref, got_ref, gate_ref, input_ref, step_rows_ref, state_ref = refs[:6]
+    input_grad_ref, step_grad_ref, state_grad_ref, sums_ref, gain_ref, state_gain_ref = refs[6:]
+    tall = input_ref.shape[0]
+    states = state_ref.shape[1]
+    heads = step_grad_ref.shape[1]
+    inner = own_ref[:tall, :] + got_ref[:tall, :].astype(f32)
+    gate = gate_ref[...]
+    input_grad_ref[:, 0, :] = gate
+    input_grad_ref[:, 1, :] = inner
+    state = own_ref[tall : tall + 16, :] + got_ref[tall : tall + 16, :].astype(f32)
+    state = jnp.concatenate([state[:, :states], state[:, states:]], axis=0)
+    state_grad_ref[...] = state
+    sums = own_ref[tall + 16 : tall + 32, :] + own_ref[tall + 32 :, :]
+    sums = sums + got_ref[tall + 16 : tall + 32, :].astype(f32)
+    sums = sums + got_ref[tall + 32 :, :].astype(f32)
+    sums_ref[...] = sums
+    step = [sums[10 + h // 4 : 11 + h // 4, 128 * (h % 4) : 128 * (h % 4 + 1)] for h in range(heads)]
+    step = jnp.concatenate(step, axis=0)
+    along = input_ref[:, 0, :].astype(f32) * gate + input_ref[:, 1, :].astype(f32) * inner
+    gain = mm_exact(jnp.ones((8, along.shape[1]), f32), along, (1, 1))
+    over = jnp.sum(step_rows_ref[:heads, :].astype(f32) * step, axis=0, keepdims=True)
+    gain_ref[...] = gain + over
+    along = state_ref[...].astype(f32) * state
+    state_gain_ref[...] = mm_exact(jnp.ones((8, states), f32), along, (1, 1))
+    step = jnp.concatenate([step, jnp.zeros((128 - heads, 128), f32)], axis=0).T
+    step_grad_ref[...] = step[:, :heads]
+
+
 def project_back_kernel(fast, place_ref, *refs):
     grad_refs, step_low_ref, weight_refs, step_weight_ref = refs[:3], refs[3], refs[4:7], refs[7]
     out_refs, held_refs, step_ref = refs[8:10], refs[10:13], refs[13]
@@ -633,7 +665,9 @@
     row_loop(step_weight_ref.shape[1], 256, back)
 
 
-def prepare_kernel(place_ref, gain_ref, taps_ref, bias_ref, state_ref, shared_ref):
+def prepare_kernel(place_ref, *refs):
+    gain_ref, taps_ref, bias_ref, state_ref, step_ref, input_ref, out_ref = refs[:7]
+    shared_ref, step_rows_ref, late_ref = refs[7:]
     owner = place_ref[0]
     share, states = state_ref.shape
     shared_ref[:share, :] = state_ref[...]
@@ -652,10 +686,10 @@
         axis=0,
     )
     shared_ref[share:, :] = small.astype(bf16)
-
-
-def prepare_late_kernel(input_ref, out_ref, late_ref):
-    depth_part = input_ref.shape[0]
+    depth_part, heads = step_ref.shape
+    step = step_ref[...].astype(f32)
+    step = jnp.concatenate([step, jnp.zeros((depth_part, 128 - heads), f32)], axis=1).T
+    step_rows_ref[...] = step[:head_rows, :].astype(bf16)
     late_ref[:depth_part, :] = input_ref[:, 0, :]
     late_ref[depth_part:, :] = out_ref[...].astype(f32).T.astype(bf16)
 
@@ -820,22 +854,24 @@
     inner_total = channels * n_tensor
 
     owner_place = jnp.stack([owner, owners]).astype(jnp.int32)
-    (shared,) = call(
+    shared, step_rows, late = call(
         prepare_kernel,
-        1,
+        3,
         [owner_place],
-        [pre_gain[None, :], conv_state, conv_state_bias[None, :], state_weight],
-        [((share + 16, states), bf16)],
-        [],
-    )
-    step_rows = jnp.pad(step_weight.T, ((0, head_rows - heads), (0, 0)))
-    shared, out_shard = ordered(shared, output_weight)
-    (late,) = call(
-        prepare_late_kernel,
-        2,
-        [],
-        [input_weight, out_shard],
-        [((input_weight.shape[0] + output_weight.shape[1], channels), bf16)],
+        [
+            pre_gain[None, :],
+            conv_state,
+            conv_state_bias[None, :],
+            state_weight,
+            step_weight,
+            input_weight,
+            output_weight,
+        ],
+        [
+            ((share + 16, states), bf16),
+            ((head_rows, step_weight.shape[0]), bf16),
+            ((input_weight.shape[0] + output_weight.shape[1], channels), bf16),
+        ],
         [],
     )
     params = call(
@@ -875,7 +911,6 @@
             [((input_weight.shape[0] + 2 * share + 16, channels), bf16)],
             [],
         )
-        late_one, msg = ordered(late_one, msg)
         msg = ring_gather(msg)
         weight_pieces = [piece for piece, _ in msg]
         late_two = ring_step(late_one)
@@ -1104,7 +1139,7 @@
         got = ring_step(chunk_pair((6, 3), got, give_rows))
         got = ring_step(chunk_pair((4, 1), got))
         held, inner_own = chunk_pair((2, 0), got, last=f32)
-        inner_out = inner_own + ring_send(held, True).astype(f32)
+        inner_got = ring_send(held, True)
     else:
         (inner_msg,) = call(
             message_kernel,
@@ -1124,11 +1159,23 @@
         far = tensor_swap(add_low(keep_rows[1], got[1]), 2)
         grad_local = keep_rows[0].astype(f32) + got[0].astype(f32) + far.astype(f32)
         gate_grad, output_grad = gate_out[:tall], gate_out[tall:].T
-        inner_grad = inner_out[:tall]
-        state_grad = inner_out[tall : tall + 16]
-        state_grad = jnp.concatenate([state_grad[:, :states], state_grad[:, states:]], axis=0)
-        sums = inner_out[tall + 16 : tall + 32] + inner_out[tall + 32 :]
-        step_grad = sums[10:12].reshape(heads, tall).T
+        input_grad, step_grad, state_grad, sums, own_gain, state_gain = call(
+            finish_kernel,
+            2,
+            [],
+            [inner_own, inner_got, gate_grad, input_weight, step_rows, state_weight],
+            [
+                (input_weight.shape, f32),
+                (step_weight.shape, f32),
+                (state_weight.shape, f32),
+                ((16, channels), f32),
+                ((8, tall), f32),
+                ((8, share), f32),
+            ],
+            [],
+        )
+        own_gain, state_gain = sum(tensor_direct(own_gain))[0], state_gain[0]
+        own_gain = lax.dynamic_slice(own_gain, (me * share,), (share,))
         width = states // owners
         conv_state_sum = lax.dynamic_slice(
             sums[7:10].reshape(6, states), (0, owner * width), (taps + 1, width)
@@ -1158,15 +1205,11 @@
         step_part = step_part.reshape(depth, heads)
         step_grad = lax.psum_scatter(step_part, "dp", scatter_dimension=0, tiled=True)
         sums = lax.psum(sums, "dp")
-    input_grad = jnp.stack([gate_grad, inner_grad], axis=1)
-    own_gain = jnp.sum(input_weight.astype(f32) * input_grad, axis=(1, 2))
-    own_gain = own_gain + jnp.sum(step_weight.astype(f32) * step_grad, axis=1)
-    state_gain = jnp.sum(state_weight.astype(f32) * state_grad, axis=1)
-    if fast:
-        own_gain = sum(tensor_direct(own_gain))
-        own_gain = lax.dynamic_slice(own_gain, (me * share,), (share,))
-    else:
+        input_grad = jnp.stack([gate_grad, inner_grad], axis=1)
+        own_gain = jnp.sum(input_weight.astype(f32) * input_grad, axis=(1, 2))
+        own_gain = own_gain + jnp.sum(step_weight.astype(f32) * step_grad, axis=1)
         own_gain = lax.psum_scatter(own_gain, "tensor", scatter_dimension=0, tiled=True)
+        state_gain = jnp.sum(state_weight.astype(f32) * state_grad, axis=1)
     pre_gain_grad = (own_gain + state_gain) / pre_gain.astype(f32)
     block_out = (token_float + mixed_rows).astype(bf16)
     scale = lax.rsqrt(jnp.mean(token_float * token_float, axis=1, keepdims=True) + epsilon)

time: 181 us -> 198 us (1.094)
  other arithmetic: 7.59 us -> 21.3 us
  local copies, waits for them, and re-layouts: 13.3 us -> 16.4 us
    convert_element_type x6, other arithmetic: 1.1 us -> 10.4 us  [add_low(): return (got.astype(f32) + own.astype(f32)).astype(bf16)]
    ppermute x28, waiting for transfers between devices: 32.1 us -> 28.8 us  [ring_send(): return lax.ppermute(value, 'dp', pairs)]
    ppermute x17, waiting for transfers between devices: 3.09 us -> 5.26 us  [tensor_swap(): return lax.ppermute(value, 'tensor', [(i, i ^ bit) for i in range(4)])]
    unnamed x86 -> x71, local copies, waits for them, and re-layouts: 7.62 us -> 7.42 us
  transfers between devices with their start and end apart: 46 -> 46, of which waited for: 17 -> 20; matrix products, arithmetic and copies ran while one was open for 8% -> 15% of each run, Pallas kernels for 29% -> 27%
where the time goes in v6:
time: 198 us; the launch traced here: 197 us
  Pallas kernels  77.5 us (39%)
  starting transfers between devices  46.7 us (24%)
  waiting for transfers between devices  34.1 us (17%)
  other arithmetic  21.3 us (11%)
  local copies, waits for them, and re-layouts  16.4 us (8%)
    pallas_call x12, Pallas kernels, call(): pl.pallas_call(kernel, out_shape=[jax.ShapeDtypeStruct(shape, kind) for s...  64.6 us
    ppermute x28, starting transfers between devices, ring_send(): return lax.ppermute(value, 'dp', pairs)  31 us
    ppermute x28, waiting for transfers between devices, ring_send(): return lax.ppermute(value, 'dp', pairs)  28.8 us
    pallas_call x4, Pallas kernels, chunk_pair(): pl.pallas_call(functools.partial(chunk_kernel, slots, len(got)), grid_spe...  13 us
    ppermute x17, starting transfers between devices, tensor_swap(): return lax.ppermute(value, 'tensor', [(i, i ^ bit) for i in range(4)])  11.3 us
    convert_element_type x6, other arithmetic, add_low(): return (got.astype(f32) + own.astype(f32)).astype(bf16)  10.4 us
    unnamed x71, local copies, waits for them, and re-layouts  7.42 us
    ppermute x17, waiting for transfers between devices, tensor_swap(): return lax.ppermute(value, 'tensor', [(i, i ^ bit) for i in range(4)])  5.26 us
  transfers between devices with their start and end apart: 46, of which 20 were waited for; matrix products, arithmetic and copies ran while one was open for 15% of the time, Pallas kernels for 27%

profile of v6, /device:TPU:0, one launch (start us, length us, event | category | flops | bytes accessed | tf_op | source)
XLA Modules:
  0.0 197.0 jit_solution(12190145552122682866)
XLA Ops:
  2.6 2.2 %shard_map.271 = (bf16[48,256]{1,0:T(8,128)(2,1)}, bf16[16,128]{1,0:T(8,128)(2,1)}, bf16[256,512]{1,0:T(8,128)(2,1)}) custom-call(s32[2]{0:T(128)} %pad_add_fusion.place_ref, bf16[1,32]{1,0:T(2,128)(2,1)} %bitcast.49, bf16[4,8]{1,0:T(4,128)(2,1)} %refs_1_.1, bf16[1,8]{1,0:T(2,128)(2,1)} %bitcast.50, bf16[32,256]{1,0:T(8,128)(2,1)} %refs_5_.3, ...), custom_call_target="tpu_custom_call" | custom-call | flops 3300000000 | bytes 1048576 | tf_op jit(solution)/shard_map/pallas_call | solution.py:737
  5.3 2.5 %collective-permute-start.1 = (bf16[48,256]{1,0:T(8,128)(2,1)}, bf16[48,256]{1,0:T(8,128)(2,1)S(1)}, u32[]{:S(2)}, u32[]{:S(2)}) collective-permute-start(bf16[48,256]{1,0:T(8,128)(2,1)} %get-tuple-element.103.refs_0_), channel_id=1, source_target_pairs={{0,2},{1,3},{2,0},{3,1},{4,6},{5,7},{6,4},{7,5},{8,10},{9,11},{10,... | collective-permute-start | bytes 73736 | tf_op jit(solution)/shard_map/ppermute | solution.py:821
  12.0 2.0 %shard_map.272.refs_4_ = bf16[208,512]{1,0:T(8,128)(2,1)} custom-call(bf16[128,2,512]{2,1,0:T(2,128)(2,1)} %refs_3_.3, bf16[16,128]{1,0:T(8,128)(2,1)} %get-tuple-element.106.step_ref.refs_4_, bf16[48,256]{1,0:T(8,128)(2,1)} %get-tuple-element.103.refs_0_, bf16[48,256]{1,0:T(8,128)(2,1)} %copy-done.27, bf16[48,256]{1,0:T(8,128)(2,1)} %copy-done.28, ...), custom_call_target="tpu_custom_call" | custom-call | flops 1100000000 | bytes 1048576 | tf_op jit(solution)/shard_map/pallas_call | solution.py:737
  18.0 4.3 %collective-permute-done.13.refs_5_ = bf16[208,512]{1,0:T(8,128)(2,1)S(1)} collective-permute-done((bf16[208,512]{1,0:T(8,128)(2,1)}, bf16[208,512]{1,0:T(8,128)(2,1)S(1)}, u32[]{:S(2)}, u32[]{:S(2)}) %collective-permute-start.13) | collective-permute-done | bytes 213024 | tf_op jit(solution)/shard_map/ppermute | solution.py:772
  22.3 1.7 collective-permute-start.15
  24.4 3.5 %collective-permute-done.6.refs_5_ = bf16[256,512]{1,0:T(8,128)(2,1)S(1)} collective-permute-done((bf16[256,512]{1,0:T(8,128)(2,1)}, bf16[256,512]{1,0:T(8,128)(2,1)S(1)}, u32[]{:S(2)}, u32[]{:S(2)}) %collective-permute-start.6) | collective-permute-done | bytes 262176 | tf_op jit(solution)/shard_map/ppermute | solution.py:772
  27.9 1.8 collective-permute-done.7.refs_6_
  34.6 4.4 %collective-permute-done.8.refs_7_ = bf16[256,512]{1,0:T(8,128)(2,1)} collective-permute-done((bf16[256,512]{1,0:T(8,128)(2,1)S(1)}, bf16[256,512]{1,0:T(8,128)(2,1)}, u32[]{:S(2)}, u32[]{:S(2)}) %collective-permute-start.8) | collective-permute-done | bytes 262176 | tf_op jit(solution)/shard_map/ppermute | solution.py:772
  41.8 1.8 collective-permute-done.17.refs_9_
  50.8 3.0 %collective-permute-done.19.refs_11_ = bf16[208,512]{1,0:T(8,128)(2,1)} collective-permute-done((bf16[208,512]{1,0:T(8,128)(2,1)}, bf16[208,512]{1,0:T(8,128)(2,1)}, u32[]{:S(2)}, u32[]{:S(2)}) %collective-permute-start.19) | collective-permute-done | bytes 213024 | tf_op jit(solution)/shard_map/ppermute | solution.py:772
  53.8 11.2 %shard_map.274 = (bf16[512,1024]{1,0:T(8,128)(2,1)}, bf16[1024,512]{1,0:T(8,128)(2,1)}, bf16[1024,512]{1,0:T(8,128)(2,1)}, bf16[1024,256]{1,0:T(8,128)(2,1)}, bf...) custom-call(s32[12]{0:T(128)} %stack.57.place_ref, ...), custom_call_target="tpu_custom_call" | custom-call | flops 12099999744 | bytes 1048576 | tf_op jit(solution)/shard_map/pallas_call | solution.py:737
  65.0 7.3 %shard_map.275 = (bf16[512,1024]{1,0:T(8,128)(2,1)}, bf16[1024,512]{1,0:T(8,128)(2,1)}, bf16[1024,512]{1,0:T(8,128)(2,1)}, f32[512,512]{1,0:T(8,128)}, f32[512,512]{1,0:T(8,128)}, /*index=5*/f32[8,512]{1,0:T(8,128)}) custom-call(s32[12]{0:T(128)} %stack.57.place_ref, s32[1,4]{1,0:T(1,128)} %lengths_ref.13, bf16[256,1024]{1,0:T(8,128)(2,1)} %pad_maximum_fusion.refs_0_, ...), custom_call_target="tpu_custom_call" | custom-call | flops 5500000256 | bytes 1048576 | tf_op jit(solution)/shard_map/pallas_call | solution.py:737
  74.3 2.1 %collective-permute-done.21.refs_2_ = f32[8,512]{1,0:T(8,128)S(1)} collective-permute-done((f32[8,512]{1,0:T(8,128)}, f32[8,512]{1,0:T(8,128)S(1)}, u32[]{:S(2)}, u32[]{:S(2)}) %collective-permute-start.21) | collective-permute-done | bytes 16416 | tf_op jit(solution)/shard_map/ppermute | solution.py:821
  77.6 8.1 %shard_map.276 = (bf16[256,512]{1,0:T(8,128)(2,1)}, bf16[256,512]{1,0:T(8,128)(2,1)}, bf16[256,512]{1,0:T(8,128)(2,1)}, bf16[256,512]{1,0:T(8,128)(2,1)}, bf16[2...) custom-call(s32[12]{0:T(128)} %stack.57.place_ref, ...), custom_call_target="tpu_custom_call" | custom-call | flops 9900000256 | bytes 1048576 | tf_op jit(solution)/shard_map/pallas_call | solution.py:737
  87.8 4.4 %all-to-all-start = ((bf16[4,128,1024]{2,1,0:T(8,128)(2,1)}), bf16[4,128,1024]{2,1,0:T(8,128)(2,1)}, u32[]{:S(2)}, u32[]{:S(2)}) async-start(bf16[4,128,1024]{2,1,0:T(8,128)(2,1)} %bitcast.44), calls=%async_computation | async-start | bytes 2097152 | tf_op jit(solution)/shard_map/all_to_all | solution.py:816
  92.2 6.5 %shard_map.277 = (f32[512,256]{1,0:T(8,128)}, f32[512,256]{1,0:T(8,128)}, f32[16,512]{1,0:T(8,128)}, f32[8,256]{1,0:T(8,128)}) custom-call(s32[1,4]{1,0:T(1,128)} %lengths_ref.13, f32[512,512]{1,0:T(8,128)} %get-tuple-element.146.refs_0_, f32[512,512]{1,0:T(8,128)} %get-tuple-element.141.refs_1_, f32[512,256]{1,0:T(8,128)} %get-tuple-element.142.refs_2_, ...), custom_call_target="tpu_custom_call" | custom-call | flops 6600000000 | bytes 1048576 | tf_op jit(solution)/shard_map/pallas_call | solution.py:737
  104.2 6.5 %shard_map.278 = (f32[512,256]{1,0:T(8,128)}, f32[512,256]{1,0:T(8,128)}, f32[16,512]{1,0:T(8,128)}, f32[8,256]{1,0:T(8,128)}) custom-call(s32[1,4]{1,0:T(1,128)} %lengths_ref.13, f32[512,512]{1,0:T(8,128)} %get-tuple-element.146.refs_0_, f32[512,512]{1,0:T(8,128)} %get-tuple-element.141.refs_1_, f32[512,256]{1,0:T(8,128)} %get-tuple-element.142.refs_2_, ...), custom_call_target="tpu_custom_call" | custom-call | flops 6600000000 | bytes 1048576 | tf_op jit(solution)/shard_map/pallas_call | solution.py:737
  116.5 5.4 %shard_map.280 = (bf16[512,256]{1,0:T(8,128)(2,1)}, bf16[16,512]{1,0:T(8,128)(2,1)}, bf16[272,256]{1,0:T(8,128)(2,1)}, bf16[272,256]{1,0:T(8,128)(2,1)}, bf16[27...) custom-call(s32[12]{0:T(128)} %stack.57.place_ref, s32[1,4]{1,0:T(1,128)} %lengths_ref.13, ...), custom_call_target="tpu_custom_call" | custom-call | flops 4400000000 | bytes 1048576 | tf_op jit(solution)/shard_map/pallas_call | solution.py:737
  121.9 1.7 collective-permute-start.33
  127.1 5.6 %shard_map.279 = (bf16[512,512]{1,0:T(8,128)(2,1)}, f32[16,512]{1,0:T(8,128)}) custom-call(s32[1,4]{1,0:T(1,128)} %lengths_ref.13, f32[512,256]{1,0:T(8,128)} %get-tuple-element.145.refs_0_, f32[512,256]{1,0:T(8,128)} %get-tuple-element.147.refs_1_, f32[8,256]{1,0:T(8,128)} %get-tuple-element.148.refs_2_, f32[8,256]{1,0:T(8,128)} %get-tuple-element.149.refs_3_, ...), custom_call_target="tpu_custom_call" | custom-call | flops 6600000000 | bytes 1048576 | tf_op jit(solution)/shard_map/pallas_call | solution.py:737
  134.4 1.9 convert_add_fusion.1
  136.9 3.1 %shard_map.282 = (bf16[176,512]{1,0:T(8,128)(2,1)}, bf16[176,512]{1,0:T(8,128)(2,1)}) custom-call(s32[12]{0:T(128)} %stack.57.place_ref, bf16[512,512]{1,0:T(8,128)(2,1)} %get-tuple-element.175.refs_1_.refs_0_, bf16[16,512]{1,0:T(8,128)(2,1)} %get-tuple-element.163.refs_3_.refs_1_, f32[16,512]{1,0:T(8,128)} %get-tuple-element.170.refs_2_, ...), custom_call_target="tpu_custom_call" | custom-call | flops 2000000000 | bytes 1048576 | tf_op jit(solution)/shard_map/pallas_call | solution.py:1122
  142.1 5.6 %shard_map.281 = (bf16[2,128,1024]{2,1,0:T(8,128)(2,1)}, bf16[2,128,1024]{2,1,0:T(8,128)(2,1)}) custom-call(s32[12]{0:T(128)} %stack.57.place_ref, bf16[512,512]{1,0:T(8,128)(2,1)} %get-tuple-element.154.refs_0_, bf16[512,512]{1,0:T(8,128)(2,1)} %get-tuple-element.175.refs_1_.refs_0_, bf16[512,256]{1,0:T(8,128)(2,1)} %get-tuple-element.162.refs_2_, ...), custom_call_target="tpu_custom_call" | custom-call | flops 6600000000 | bytes 1048576 | tf_op jit(solution)/shard_map/pallas_call | solution.py:737
  148.4 3.3 %shard_map.283 = (bf16[176,512]{1,0:T(8,128)(2,1)}, bf16[176,512]{1,0:T(8,128)(2,1)}) custom-call(s32[12]{0:T(128)} %stack.57.place_ref, bf16[512,512]{1,0:T(8,128)(2,1)} %get-tuple-element.175.refs_1_.refs_0_, bf16[16,512]{1,0:T(8,128)(2,1)} %get-tuple-element.163.refs_3_.refs_1_, f32[16,512]{1,0:T(8,128)} %get-tuple-element.170.refs_2_, ...), custom_call_target="tpu_custom_call" | custom-call | flops 2000000000 | bytes 1048576 | tf_op jit(solution)/shard_map/pallas_call | solution.py:1122
  154.4 3.3 %collective-permute-done.37.refs_9_ = bf16[176,512]{1,0:T(8,128)(2,1)S(1)} collective-permute-done((bf16[176,512]{1,0:T(8,128)(2,1)}, bf16[176,512]{1,0:T(8,128)(2,1)S(1)}, u32[]{:S(2)}, u32[]{:S(2)}) %collective-permute-start.37) | collective-permute-done | bytes 180256 | tf_op jit(solution)/shard_map/ppermute | solution.py:772
  159.1 3.3 %shard_map.284 = (bf16[176,512]{1,0:T(8,128)(2,1)}, bf16[176,512]{1,0:T(8,128)(2,1)}) custom-call(s32[12]{0:T(128)} %stack.57.place_ref, bf16[512,512]{1,0:T(8,128)(2,1)} %get-tuple-element.175.refs_1_.refs_0_, bf16[16,512]{1,0:T(8,128)(2,1)} %get-tuple-element.163.refs_3_.refs_1_, f32[16,512]{1,0:T(8,128)} %get-tuple-element.170.refs_2_, ...), custom_call_target="tpu_custom_call" | custom-call | flops 2000000000 | bytes 1048576 | tf_op jit(solution)/shard_map/pallas_call | solution.py:1122
  164.4 1.8 slice_bitcast_fusion
  169.7 3.3 %shard_map.285 = (bf16[176,512]{1,0:T(8,128)(2,1)}, f32[176,512]{1,0:T(8,128)}) custom-call(s32[12]{0:T(128)} %stack.57.place_ref, bf16[512,512]{1,0:T(8,128)(2,1)} %get-tuple-element.175.refs_1_.refs_0_, bf16[16,512]{1,0:T(8,128)(2,1)} %get-tuple-element.163.refs_3_.refs_1_, f32[16,512]{1,0:T(8,128)} %get-tuple-element.170.refs_2_, ...), custom_call_target="tpu_custom_call" | custom-call | flops 2000000000 | bytes 1048576 | tf_op jit(solution)/shard_map/pallas_call | solution.py:1122
  174.5 1.8 fusion.6
  179.4 2.5 %shard_map.286 = (f32[128,2,512]{2,1,0:T(2,128)}, f32[128,8]{1,0:T(8,128)}, f32[32,256]{1,0:T(8,128)}, f32[16,512]{1,0:T(8,128)}, f32[8,128]{1,0:T(8,128)}, /*index=5*/f32[8,32]{1,0:T(8,128)}) custom-call(f32[176,512]{1,0:T(8,128)} %get-tuple-element.182.refs_0_, bf16[176,512]{1,0:T(8,128)(2,1)} %copy-done.24, f32[128,512]{1,0:T(8,128)} %get-tuple-element.209.refs_2_, ...), custom_call_target="tpu_custom_call" | custom-call | flops 2200000000 | bytes 1048576 | tf_op jit(solution)/shard_map/pallas_call | solution.py:737
  182.0 1.7 collective-permute-start.43
  194.8 2.2 %fusion.4 = (f32[128,1024]{1,0:T(8,128)}, bf16[128,1024]{1,0:T(8,128)(2,1)}) fusion(bf16[128,1024]{1,0:T(8,128)(2,1)S(1)} %copy-done, bf16[128,1024]{1,0:T(8,128)(2,1)S(1)} %copy-done.3, bf16[128,1024]{1,0:T(8,128)(2,1)} %collective-permute-done.31, f32[128]{0:T(128)S(1)} %get-tuple-element.218, f32[1024]{0:T(1024)S(1)} %bitcast.46, ...), kind=kLoop, calls=%fused_computation.9 | loop fusion | flops 1835008 | bytes 2626560 | tf_op jit(solution)/shard_map/add | solution.py:1219
  (176 shorter events, 76.1 us)
Async XLA Ops:
  11.3 20.0 %collective-permute-start.4 = (bf16[256,1024]{1,0:T(8,128)(2,1)}, bf16[256,1024]{1,0:T(8,128)(2,1)S(1)}, u32[]{:S(2)}, u32[]{:S(2)}) collective-permute-start(bf16[256,1024]{1,0:T(8,128)(2,1)} %pad_maximum_fusion.refs_0_), channel_id=1, source_target_pairs={{0,2},{1,3},{2,0},{3,1},{4,6},{5,7},{6,4},{7,5},{8,10},{9,11},{10,... | collective-permute-start | bytes 1572872 | tf_op jit(solution)/shard_map/ppermute | solution.py:821
  14.0 8.3 %collective-permute-start.13 = (bf16[208,512]{1,0:T(8,128)(2,1)}, bf16[208,512]{1,0:T(8,128)(2,1)S(1)}, u32[]{:S(2)}, u32[]{:S(2)}) collective-permute-start(bf16[208,512]{1,0:T(8,128)(2,1)} %shard_map.272.refs_4_), channel_id=1, source_target_pairs={{0,8},{8,16},{16,24},{24,28},{28,20},{20,12},{12,4},{4,0},{1,9},{9... | collective-permute-start | bytes 638984 | tf_op jit(solution)/shard_map/ppermute | solution.py:772
  15.7 8.4 %collective-permute-start.14 = (bf16[208,512]{1,0:T(8,128)(2,1)}, bf16[208,512]{1,0:T(8,128)(2,1)S(1)}, u32[]{:S(2)}, u32[]{:S(2)}) collective-permute-start(bf16[208,512]{1,0:T(8,128)(2,1)} %shard_map.272.refs_4_), channel_id=1, source_target_pairs={{0,4},{8,0},{16,8},{24,16},{28,24},{20,28},{12,20},{4,12},{1,5},{9... | collective-permute-start | bytes 638984 | tf_op jit(solution)/shard_map/ppermute | solution.py:772
  16.0 11.9 %collective-permute-start.6 = (bf16[256,512]{1,0:T(8,128)(2,1)}, bf16[256,512]{1,0:T(8,128)(2,1)S(1)}, u32[]{:S(2)}, u32[]{:S(2)}) collective-permute-start(bf16[256,512]{1,0:T(8,128)(2,1)} %get-tuple-element.105.refs_4_), channel_id=1, source_target_pairs={{0,8},{8,16},{16,24},{24,28},{28,20},{20,12},{12,4},{4,0},{1,9},{9... | collective-permute-start | bytes 786440 | tf_op jit(solution)/shard_map/ppermute | solution.py:772
  17.7 12.0 %collective-permute-start.7 = (bf16[256,512]{1,0:T(8,128)(2,1)}, bf16[256,512]{1,0:T(8,128)(2,1)S(1)}, u32[]{:S(2)}, u32[]{:S(2)}) collective-permute-start(bf16[256,512]{1,0:T(8,128)(2,1)} %get-tuple-element.105.refs_4_), channel_id=1, source_target_pairs={{0,4},{8,0},{16,8},{24,16},{28,24},{20,28},{12,20},{4,12},{1,5},{9... | collective-permute-start | bytes 786440 | tf_op jit(solution)/shard_map/ppermute | solution.py:772
  22.3 9.9 %collective-permute-start.15 = (bf16[208,512]{1,0:T(8,128)(2,1)S(1)}, bf16[208,512]{1,0:T(8,128)(2,1)S(1)}, u32[]{:S(2)}, u32[]{:S(2)}) collective-permute-start(bf16[208,512]{1,0:T(8,128)(2,1)S(1)} %collective-permute-done.13.refs_5_), channel_id=1, source_target_pairs={{0,8},{8,16},{16,24},{24,28},{28,20},{20,12},{12,4},{4,0},{1,9},{9... | collective-permute-start | bytes 638984 | tf_op jit(solution)/shard_map/ppermute | solution.py:772
  24.1 9.4 %collective-permute-start.16 = (bf16[208,512]{1,0:T(8,128)(2,1)S(1)}, bf16[208,512]{1,0:T(8,128)(2,1)}, u32[]{:S(2)}, u32[]{:S(2)}) collective-permute-start(bf16[208,512]{1,0:T(8,128)(2,1)S(1)} %collective-permute-done.14.refs_6_), channel_id=1, source_target_pairs={{0,4},{8,0},{16,8},{24,16},{28,24},{20,28},{12,20},{4,12},{1,5},{9... | collective-permute-start | bytes 638984 | tf_op jit(solution)/shard_map/ppermute | solution.py:772
  27.9 20.7 %collective-permute-start.3 = (bf16[256,1024]{1,0:T(8,128)(2,1)}, bf16[256,1024]{1,0:T(8,128)(2,1)}, u32[]{:S(2)}, u32[]{:S(2)}) collective-permute-start(bf16[256,1024]{1,0:T(8,128)(2,1)} %pad_maximum_fusion.refs_0_), channel_id=1, source_target_pairs={{0,1},{1,0},{2,3},{3,2},{4,5},{5,4},{6,7},{7,6},{8,9},{9,8},{10,11... | collective-permute-start | bytes 1572872 | tf_op jit(solution)/shard_map/ppermute | solution.py:821
  29.7 9.3 %collective-permute-start.8 = (bf16[256,512]{1,0:T(8,128)(2,1)S(1)}, bf16[256,512]{1,0:T(8,128)(2,1)}, u32[]{:S(2)}, u32[]{:S(2)}) collective-permute-start(bf16[256,512]{1,0:T(8,128)(2,1)S(1)} %collective-permute-done.6.refs_5_), channel_id=1, source_target_pairs={{0,8},{8,16},{16,24},{24,28},{28,20},{20,12},{12,4},{4,0},{1,9},{9... | collective-permute-start | bytes 786440 | tf_op jit(solution)/shard_map/ppermute | solution.py:772
  31.3 22.5 %collective-permute-start.5 = (bf16[256,1024]{1,0:T(8,128)(2,1)S(1)}, bf16[256,1024]{1,0:T(8,128)(2,1)}, u32[]{:S(2)}, u32[]{:S(2)}) collective-permute-start(bf16[256,1024]{1,0:T(8,128)(2,1)S(1)} %collective-permute-done.4.refs_2_), channel_id=1, source_target_pairs={{0,1},{1,0},{2,3},{3,2},{4,5},{5,4},{6,7},{7,6},{8,9},{9,8},{10,11... | collective-permute-start | bytes 1572872 | tf_op jit(solution)/shard_map/ppermute | solution.py:821
  32.2 8.4 %collective-permute-start.9 = (bf16[256,512]{1,0:T(8,128)(2,1)S(1)}, bf16[256,512]{1,0:T(8,128)(2,1)S(1)}, u32[]{:S(2)}, u32[]{:S(2)}) collective-permute-start(bf16[256,512]{1,0:T(8,128)(2,1)S(1)} %collective-permute-done.7.refs_6_), channel_id=1, source_target_pairs={{0,4},{8,0},{16,8},{24,16},{28,24},{20,28},{12,20},{4,12},{1,5},{9... | collective-permute-start | bytes 786440 | tf_op jit(solution)/shard_map/ppermute | solution.py:772
  33.5 10.1 %collective-permute-start.17 = (bf16[208,512]{1,0:T(8,128)(2,1)S(1)}, bf16[208,512]{1,0:T(8,128)(2,1)}, u32[]{:S(2)}, u32[]{:S(2)}) collective-permute-start(bf16[208,512]{1,0:T(8,128)(2,1)S(1)} %collective-permute-done.15.refs_7_), channel_id=1, source_target_pairs={{0,8},{8,16},{16,24},{24,28},{28,20},{20,12},{12,4},{4,0},{1,9},{9... | collective-permute-start | bytes 638984 | tf_op jit(solution)/shard_map/ppermute | solution.py:772
  39.1 10.2 %collective-permute-start.10 = (bf16[256,512]{1,0:T(8,128)(2,1)}, bf16[256,512]{1,0:T(8,128)(2,1)}, u32[]{:S(2)}, u32[]{:S(2)}) collective-permute-start(bf16[256,512]{1,0:T(8,128)(2,1)} %collective-permute-done.8.refs_7_), channel_id=1, source_target_pairs={{0,8},{8,16},{16,24},{24,28},{28,20},{20,12},{12,4},{4,0},{1,9},{9... | collective-permute-start | bytes 786440 | tf_op jit(solution)/shard_map/ppermute | solution.py:772
  41.3 9.5 %collective-permute-start.18 = (bf16[208,512]{1,0:T(8,128)(2,1)}, bf16[208,512]{1,0:T(8,128)(2,1)}, u32[]{:S(2)}, u32[]{:S(2)}) collective-permute-start(bf16[208,512]{1,0:T(8,128)(2,1)} %collective-permute-done.16.refs_8_), channel_id=1, source_target_pairs={{0,4},{8,0},{16,8},{24,16},{28,24},{20,28},{12,20},{4,12},{1,5},{9... | collective-permute-start | bytes 638984 | tf_op jit(solution)/shard_map/ppermute | solution.py:772
  43.6 10.2 %collective-permute-start.19 = (bf16[208,512]{1,0:T(8,128)(2,1)}, bf16[208,512]{1,0:T(8,128)(2,1)}, u32[]{:S(2)}, u32[]{:S(2)}) collective-permute-start(bf16[208,512]{1,0:T(8,128)(2,1)} %collective-permute-done.17.refs_9_), channel_id=1, source_target_pairs={{0,8},{8,16},{16,24},{24,28},{28,20},{20,12},{12,4},{4,0},{1,9},{9... | collective-permute-start | bytes 638984 | tf_op jit(solution)/shard_map/ppermute | solution.py:772
  48.6 16.4 %collective-permute-start.11 = (bf16[256,512]{1,0:T(8,128)(2,1)}, bf16[256,512]{1,0:T(8,128)(2,1)}, u32[]{:S(2)}, u32[]{:S(2)}) collective-permute-start(bf16[256,512]{1,0:T(8,128)(2,1)} %copy-done.18), channel_id=1, source_target_pairs={{0,4},{8,0},{16,8},{24,16},{28,24},{20,28},{12,20},{4,12},{1,5},{9... | collective-permute-start | bytes 786440 | tf_op jit(solution)/shard_map/ppermute | solution.py:772
  49.2 15.8 %collective-permute-start.12 = (bf16[256,512]{1,0:T(8,128)(2,1)}, bf16[256,512]{1,0:T(8,128)(2,1)}, u32[]{:S(2)}, u32[]{:S(2)}) collective-permute-start(bf16[256,512]{1,0:T(8,128)(2,1)} %collective-permute-done.10.refs_9_), channel_id=1, source_target_pairs={{0,8},{8,16},{16,24},{24,28},{28,20},{20,12},{12,4},{4,0},{1,9},{9... | collective-permute-start | bytes 786440 | tf_op jit(solution)/shard_map/ppermute | solution.py:772
  85.7 13.1 %collective-permute-start.24 = (bf16[256,512]{1,0:T(8,128)(2,1)}, bf16[256,512]{1,0:T(8,128)(2,1)}, u32[]{:S(2)}, u32[]{:S(2)}) collective-permute-start(bf16[256,512]{1,0:T(8,128)(2,1)} %get-tuple-element.126), channel_id=1, source_target_pairs={{0,4},{8,0},{16,8},{24,16},{28,24},{20,28},{12,20},{4,12},{1,5},{9... | collective-permute-start | bytes 786440 | tf_op jit(solution)/shard_map/ppermute | solution.py:772
  86.1 14.4 %collective-permute-start.23 = (bf16[256,512]{1,0:T(8,128)(2,1)}, bf16[256,512]{1,0:T(8,128)(2,1)}, u32[]{:S(2)}, u32[]{:S(2)}) collective-permute-start(bf16[256,512]{1,0:T(8,128)(2,1)} %get-tuple-element.124), channel_id=1, source_target_pairs={{0,8},{8,16},{16,24},{24,28},{28,20},{20,12},{12,4},{4,0},{1,9},{9... | collective-permute-start | bytes 786440 | tf_op jit(solution)/shard_map/ppermute | solution.py:772
  87.8 44.9 %all-to-all-start = ((bf16[4,128,1024]{2,1,0:T(8,128)(2,1)}), bf16[4,128,1024]{2,1,0:T(8,128)(2,1)}, u32[]{:S(2)}, u32[]{:S(2)}) async-start(bf16[4,128,1024]{2,1,0:T(8,128)(2,1)} %bitcast.44), calls=%async_computation | async-start | bytes 2097152 | tf_op jit(solution)/shard_map/all_to_all | solution.py:816
  102.2 8.8 %collective-permute-start.26 = (bf16[256,512]{1,0:T(8,128)(2,1)}, bf16[256,512]{1,0:T(8,128)(2,1)}, u32[]{:S(2)}, u32[]{:S(2)}) collective-permute-start(bf16[256,512]{1,0:T(8,128)(2,1)} %add_convert_fusion.4), channel_id=1, source_target_pairs={{0,4},{8,0},{16,8},{24,16},{28,24},{20,28},{12,20},{4,12},{1,5},{9... | collective-permute-start | bytes 786440 | tf_op jit(solution)/shard_map/ppermute | solution.py:772
  102.6 10.1 %collective-permute-start.25 = (bf16[256,512]{1,0:T(8,128)(2,1)}, bf16[256,512]{1,0:T(8,128)(2,1)}, u32[]{:S(2)}, u32[]{:S(2)}) collective-permute-start(bf16[256,512]{1,0:T(8,128)(2,1)} %add_convert_fusion.5), channel_id=1, source_target_pairs={{0,8},{8,16},{16,24},{24,28},{28,20},{20,12},{12,4},{4,0},{1,9},{9... | collective-permute-start | bytes 786440 | tf_op jit(solution)/shard_map/ppermute | solution.py:772
  114.5 9.3 %collective-permute-start.27 = (bf16[256,512]{1,0:T(8,128)(2,1)}, bf16[256,512]{1,0:T(8,128)(2,1)}, u32[]{:S(2)}, u32[]{:S(2)}) collective-permute-start(bf16[256,512]{1,0:T(8,128)(2,1)} %add_convert_fusion.3), channel_id=1, source_target_pairs={{0,8},{8,16},{16,24},{24,28},{28,20},{20,12},{12,4},{4,0},{1,9},{9... | collective-permute-start | bytes 786440 | tf_op jit(solution)/shard_map/ppermute | solution.py:772
  116.0 9.5 %collective-permute-start.28 = (bf16[256,512]{1,0:T(8,128)(2,1)}, bf16[256,512]{1,0:T(8,128)(2,1)S(1)}, u32[]{:S(2)}, u32[]{:S(2)}) collective-permute-start(bf16[256,512]{1,0:T(8,128)(2,1)} %add_convert_fusion.2), channel_id=1, source_target_pairs={{0,4},{8,0},{16,8},{24,16},{28,24},{20,28},{12,20},{4,12},{1,5},{9... | collective-permute-start | bytes 786440 | tf_op jit(solution)/shard_map/ppermute | solution.py:772
  121.9 14.3 %collective-permute-start.32 = (bf16[272,256]{1,0:T(8,128)(2,1)}, bf16[272,256]{1,0:T(8,128)(2,1)S(1)}, u32[]{:S(2)}, u32[]{:S(2)}) collective-permute-start(bf16[272,256]{1,0:T(8,128)(2,1)} %get-tuple-element.172), channel_id=1, source_target_pairs={{0,1},{1,0},{2,3},{3,2},{4,5},{5,4},{6,7},{7,6},{8,9},{9,8},{10,11... | collective-permute-start | bytes 417800 | tf_op jit(solution)/shard_map/ppermute | solution.py:821
  121.9 14.3 %collective-permute-start.33 = (bf16[272,256]{1,0:T(8,128)(2,1)}, bf16[272,256]{1,0:T(8,128)(2,1)}, u32[]{:S(2)}, u32[]{:S(2)}) collective-permute-start(bf16[272,256]{1,0:T(8,128)(2,1)} %get-tuple-element.173), channel_id=1, source_target_pairs={{0,2},{1,3},{2,0},{3,1},{4,6},{5,7},{6,4},{7,5},{8,10},{9,11},{10,... | collective-permute-start | bytes 417800 | tf_op jit(solution)/shard_map/ppermute | solution.py:821
  123.7 12.6 %collective-permute-start.34 = (bf16[272,256]{1,0:T(8,128)(2,1)}, bf16[272,256]{1,0:T(8,128)(2,1)}, u32[]{:S(2)}, u32[]{:S(2)}) collective-permute-start(bf16[272,256]{1,0:T(8,128)(2,1)} %get-tuple-element.174), channel_id=1, source_target_pairs={{0,3},{1,2},{2,1},{3,0},{4,7},{5,6},{6,5},{7,4},{8,11},{9,10},{10,... | collective-permute-start | bytes 417800 | tf_op jit(solution)/shard_map/ppermute | solution.py:821
  125.5 8.9 %collective-permute-start.29 = (bf16[256,512]{1,0:T(8,128)(2,1)}, bf16[256,512]{1,0:T(8,128)(2,1)}, u32[]{:S(2)}, u32[]{:S(2)}) collective-permute-start(bf16[256,512]{1,0:T(8,128)(2,1)} %add_convert_fusion.1), channel_id=1, source_target_pairs={{0,8},{8,16},{16,24},{24,28},{28,20},{20,12},{12,4},{4,0},{1,9},{9... | collective-permute-start | bytes 786440 | tf_op jit(solution)/shard_map/ppermute | solution.py:772
  154.4 20.2 %collective-permute-start.30 = (bf16[2,128,1024]{2,1,0:T(8,128)(2,1)}, bf16[2,128,1024]{2,1,0:T(8,128)(2,1)}, u32[]{:S(2)}, u32[]{:S(2)}) collective-permute-start(bf16[2,128,1024]{2,1,0:T(8,128)(2,1)} %get-tuple-element.169), channel_id=1, source_target_pairs={{0,1},{1,0},{2,3},{3,2},{4,5},{5,4},{6,7},{7,6},{8,9},{9,8},{10,11... | collective-permute-start | bytes 1572872 | tf_op jit(solution)/shard_map/ppermute | solution.py:821
  176.3 17.1 %collective-permute-start.31 = (bf16[128,1024]{1,0:T(8,128)(2,1)}, bf16[128,1024]{1,0:T(8,128)(2,1)}, u32[]{:S(2)}, u32[]{:S(2)}) collective-permute-start(bf16[128,1024]{1,0:T(8,128)(2,1)} %fusion.6), channel_id=1, source_target_pairs={{0,2},{1,3},{2,0},{3,1},{4,6},{5,7},{6,4},{7,5},{8,10},{9,11},{10,... | collective-permute-start | bytes 786440 | tf_op jit(solution)/shard_map/ppermute | solution.py:821
  181.9 9.5 %collective-permute-start.42 = (f32[8,128]{1,0:T(8,128)}, f32[8,128]{1,0:T(8,128)S(1)}, u32[]{:S(2)}, u32[]{:S(2)}) collective-permute-start(f32[8,128]{1,0:T(8,128)} %get-tuple-element.185), channel_id=1, source_target_pairs={{0,1},{1,0},{2,3},{3,2},{4,5},{5,4},{6,7},{7,6},{8,9},{9,8},{10,11... | collective-permute-start | bytes 12296 | tf_op jit(solution)/shard_map/ppermute | solution.py:821
  182.0 9.4 %collective-permute-start.43 = (f32[8,128]{1,0:T(8,128)}, f32[8,128]{1,0:T(8,128)S(1)}, u32[]{:S(2)}, u32[]{:S(2)}) collective-permute-start(f32[8,128]{1,0:T(8,128)} %get-tuple-element.185), channel_id=1, source_target_pairs={{0,2},{1,3},{2,0},{3,1},{4,6},{5,7},{6,4},{7,5},{8,10},{9,11},{10,... | collective-permute-start | bytes 12296 | tf_op jit(solution)/shard_map/ppermute | solution.py:821
  (47 other events, 324.3 us)

commit v7 on v6

--- a/solution.py
+++ b/solution.py
@@ -15,7 +15,7 @@
 pad = 8
 head_rows = 16
 head_width = 64
-vmem_bytes = 63 * 1024 * 1024
+vmem_bytes = 61 * 1024 * 1024
 
 
 def mm(a, b, over=(1, 0)):
@@ -113,9 +113,17 @@
         self.mask = jnp.where(segment == segment_row, lower, 0.0)
         self.contact = mm(self.outputs, self.inputs, (1, 1)) * self.mask
 
-    def decay(self, h):
-        gap = self.cum[:, h : h + 1] - self.cum_row[h : h + 1, :]
-        return jnp.exp(jnp.minimum(gap, 0.0))
+    def decay(self, h, at):
+        end = at + span // 2
+        gap = self.cum[at:end, h : h + 1] - self.cum_row[h : h + 1, :end]
+        return jnp.exp(jnp.minimum(gap, 0.0)), self.contact[at:end, :end]
+
+    def mix(self, h, x_step):
+        parts = []
+        for at in (0, span // 2):
+            decay, contact = self.decay(h, at)
+            parts.append(mm((decay * contact).astype(bf16), x_step[: at + span // 2]))
+        return jnp.concatenate(parts, axis=0)
 
     def from_edge(self, h):
         return jnp.exp(self.cum[:, h : h + 1]) * self.near_edge
@@ -144,7 +152,7 @@
     n_msg = 8 if fast else 4
     n_rows = 4 if fast else 1
     row_refs, msg_refs, refs = refs[:n_rows], refs[n_rows : n_rows + n_msg], refs[n_rows + n_msg :]
-    (taps_ref, bias_ref, step_bias_ref, step_bias_col_ref, log_ref, log_col_ref, skip_ref) = refs[:7]
+    taps_ref, bias_ref = refs[:2]
     (
         normed_ref,
         turned_ref,
@@ -158,9 +166,8 @@
         step_row_ref,
         act_ref,
         state_ref,
-        mixed_ref,
-    ) = refs[7:20]
-    mask_ref, state_taps_ref, state_bias_ref = refs[20:]
+    ) = refs[2:14]
+    mask_ref, state_taps_ref, state_bias_ref = refs[14:]
     total, channels = act_ref.shape
     ends = ends_of(lengths_ref)
 
@@ -227,6 +234,12 @@
     activate(raw_ref, act_ref, taps_ref, bias_ref)
     activate(state_raw_ref, state_ref, state_taps_ref, state_bias_ref)
 
+
+def scan_kernel(lengths_ref, *refs):
+    act_ref, state_ref, step_col_ref, step_row_ref = refs[:4]
+    step_bias_ref, step_bias_col_ref, log_ref, log_col_ref, skip_ref, mixed_ref = refs[4:]
+    total, channels = act_ref.shape
+    ends = ends_of(lengths_ref)
     steps = step_sizes(
         step_col_ref[...],
         step_row_ref[...],
@@ -245,7 +258,7 @@
             x = act_ref[block.rows, cols]
             step_wide = wide(low_half, *(block.step[:, h : h + 1] for h in pair))
             x_step = (x * step_wide).astype(bf16)
-            y = [mm((block.decay(h) * block.contact).astype(bf16), x_step) for h in pair]
+            y = [block.mix(h, x_step) for h in pair]
             y = wide(low_half, *y) + skip_ref[:, cols] * x
             if b == 0:
                 reach = wide(low_half, *(block.to_edge(h) for h in pair))
@@ -389,15 +402,24 @@
             step_wide = wide(low_half, *(block.step[:, h : h + 1] for h in pair))
             grads = []
             for h, half in zip(pair, halves):
-                decay = block.decay(h)
-                spread = mm(half, x_low, (1, 1)) * decay
-                stepped = spread * block.step_row[h : h + 1, :]
-                acc_ref[...] += stepped
-                row_here = jnp.sum(stepped * block.contact, axis=1, keepdims=True)
-                row_sum = jnp.where(lane == h, row_here, row_sum)
-                step_here = jnp.sum(spread * block.contact, axis=0, keepdims=True)
+                strips = []
+                for at in (0, span // 2):
+                    end = at + span // 2
+                    decay, contact = block.decay(h, at)
+                    spread = mm(half[at:end], x_low[:end], (1, 1)) * decay
+                    stepped = spread * block.step_row[h : h + 1, :end]
+                    acc_ref[at:end, :end] += stepped
+                    row_here = jnp.sum(stepped * contact, axis=1, keepdims=True)
+                    step_here = jnp.sum(spread * contact, axis=0, keepdims=True)
+                    back = mm((decay * contact).astype(bf16), grad_low[at:end], (0, 0))
+                    strips.append((row_here, step_here, back))
+                (row_a, step_a, back_a), (row_b, step_b, back_b) = strips
+                mid = span // 2
+                row_sum = jnp.where(lane == h, jnp.concatenate([row_a, row_b], axis=0), row_sum)
+                step_here = [step_a + step_b[:, :mid], step_b[:, mid:]]
+                step_here = jnp.concatenate(step_here, axis=1)
                 step_grad = jnp.where(head_row == h, step_here, step_grad)
-                grads.append(mm((decay * block.contact).astype(bf16), grad_low, (0, 0)))
+                grads.append(jnp.concatenate([back_a + back_b[:mid], back_b[mid:]], axis=0))
             grad_act = wide(low_half, *grads) * step_wide + skip_ref[:, cols] * grad
             sums_ref[2:3, own_cols] += jnp.sum(grad * x, axis=0, keepdims=True)
             picks = jnp.where(lane_head + 2 * i == head_of, 1.0, 0.0)
@@ -915,7 +937,7 @@
         weight_pieces = [piece for piece, _ in msg]
         late_two = ring_step(late_one)
         late_three = ring_step(late_two)
-        late_pieces = [late, *late_one, *late_two, *late_three, ring_send(late_three[0], True)]
+        late_pieces = [late, *late_one, *late_two, *late_three]
         own_rows_both = jnp.concatenate([tokens, cotangent], axis=0)
         row_pieces = tensor_gather(ordered(shared, own_rows_both)[1])
         grad_pieces = row_pieces
@@ -952,12 +974,11 @@
         step_row,
         act,
         state_act,
-        mixed,
     ) = call(
         functools.partial(forward_kernel, fast),
-        11,
+        6,
         [place, lengths],
-        row_pieces + weight_pieces + conv_params + head_params,
+        row_pieces + weight_pieces + conv_params,
         [
             ((total, depth), bf16),
             ((depth, total), bf16),
@@ -971,9 +992,20 @@
             ((head_rows, total), f32),
             ((total, channels), f32),
             ((total, states), f32),
-            ((total, channels), f32),
         ],
         [masks] + state_taps,
+    )
+    if fast:
+        late_three, act = ordered(late_three, act)
+        late_pieces[5:7] = late_three
+        late_pieces.append(ring_send(late_three[0], True))
+    (mixed,) = call(
+        scan_kernel,
+        5,
+        [lengths],
+        [act, state_act, step_col, step_row] + head_params,
+        [((total, channels), f32)],
+        [],
     )
     grad_rows, gate_full, output_full, gate, grad_normalized, sums = call(
         functools.partial(grad_in_kernel, fast),

time: 198 us -> 193 us (0.975)
  other arithmetic: 21.3 us -> 6.91 us
  Pallas kernels: 77.5 us -> 81.9 us
  local copies, waits for them, and re-layouts: 16.4 us -> 19.6 us
  waiting for transfers between devices: 34.1 us -> 36.9 us
    convert_element_type x6, other arithmetic: 10.4 us -> 2.04 us  [add_low(): return (got.astype(f32) + own.astype(f32)).astype(bf16)]
    pallas_call x12 -> x13, Pallas kernels: 64.6 us -> 68.8 us  [call(): pl.pallas_call(kernel, out_shape=[jax.ShapeDtypeStruct(shape, kind) for s...]
    unnamed x71 -> x81, local copies, waits for them, and re-layouts: 7.42 us -> 11.6 us
    ppermute x28, waiting for transfers between devices: 28.8 us -> 30.9 us  [ring_send(): return lax.ppermute(value, 'dp', pairs)]
  transfers between devices with their start and end apart: 46 -> 46, of which waited for: 20 -> 16; matrix products, arithmetic and copies ran while one was open for 15% -> 8% of each run, Pallas kernels for 27% -> 30%
where the time goes in v7:
time: 193 us; the launch traced here: 192 us
  Pallas kernels  81.9 us (42%)
  starting transfers between devices  45.9 us (24%)
  waiting for transfers between devices  36.9 us (19%)
  local copies, waits for them, and re-layouts  19.6 us (10%)
  other arithmetic  6.91 us (4%)
    pallas_call x13, Pallas kernels, call(): pl.pallas_call(kernel, out_shape=[jax.ShapeDtypeStruct(shape, kind) for s...  68.8 us
    ppermute x28, waiting for transfers between devices, ring_send(): return lax.ppermute(value, 'dp', pairs)  30.9 us
    ppermute x28, starting transfers between devices, ring_send(): return lax.ppermute(value, 'dp', pairs)  30.5 us
    pallas_call x4, Pallas kernels, chunk_pair(): pl.pallas_call(functools.partial(chunk_kernel, slots, len(got)), grid_spe...  13 us
    ppermute x17, starting transfers between devices, tensor_swap(): return lax.ppermute(value, 'tensor', [(i, i ^ bit) for i in range(4)])  11.7 us
    unnamed x81, local copies, waits for them, and re-layouts  11.6 us
    ppermute x17, waiting for transfers between devices, tensor_swap(): return lax.ppermute(value, 'tensor', [(i, i ^ bit) for i in range(4)])  6 us
  transfers between devices with their start and end apart: 46, of which 16 were waited for; matrix products, arithmetic and copies ran while one was open for 8% of the time, Pallas kernels for 30%

profile of v7, /device:TPU:0, one launch (start us, length us, event | category | flops | bytes accessed | tf_op | source)
XLA Modules:
  0.0 192.2 jit_solution(9013870736107407141)
XLA Ops:
  2.6 2.2 %shard_map.271 = (bf16[48,256]{1,0:T(8,128)(2,1)}, bf16[16,128]{1,0:T(8,128)(2,1)}, bf16[256,512]{1,0:T(8,128)(2,1)}) custom-call(s32[2]{0:T(128)} %pad_add_fusion.place_ref, bf16[1,32]{1,0:T(2,128)(2,1)} %bitcast.48, bf16[4,8]{1,0:T(4,128)(2,1)} %refs_1_.1, bf16[1,8]{1,0:T(2,128)(2,1)} %bitcast.49, bf16[32,256]{1,0:T(8,128)(2,1)} %refs_5_.3, ...), custom_call_target="tpu_custom_call" | custom-call | flops 3300000000 | bytes 1048576 | tf_op jit(solution)/shard_map/pallas_call | solution.py:759
  5.3 2.5 %collective-permute-start.1 = (bf16[48,256]{1,0:T(8,128)(2,1)}, bf16[48,256]{1,0:T(8,128)(2,1)S(1)}, u32[]{:S(2)}, u32[]{:S(2)}) collective-permute-start(bf16[48,256]{1,0:T(8,128)(2,1)} %get-tuple-element.105.refs_0_), channel_id=1, source_target_pairs={{0,2},{1,3},{2,0},{3,1},{4,6},{5,7},{6,4},{7,5},{8,10},{9,11},{10,... | collective-permute-start | bytes 73736 | tf_op jit(solution)/shard_map/ppermute | solution.py:843
  8.0 1.9 collective-permute-done.1.refs_2_
  12.0 2.0 %shard_map.272.refs_4_ = bf16[208,512]{1,0:T(8,128)(2,1)} custom-call(bf16[128,2,512]{2,1,0:T(2,128)(2,1)} %refs_3_.3, bf16[16,128]{1,0:T(8,128)(2,1)} %get-tuple-element.108.step_ref.refs_4_, bf16[48,256]{1,0:T(8,128)(2,1)} %get-tuple-element.105.refs_0_, bf16[48,256]{1,0:T(8,128)(2,1)} %copy-done.32, bf16[48,256]{1,0:T(8,128)(2,1)} %copy-done.33, ...), custom_call_target="tpu_custom_call" | custom-call | flops 1100000000 | bytes 1048576 | tf_op jit(solution)/shard_map/pallas_call | solution.py:759
  18.0 4.3 %collective-permute-done.12.refs_5_ = bf16[208,512]{1,0:T(8,128)(2,1)S(1)} collective-permute-done((bf16[208,512]{1,0:T(8,128)(2,1)}, bf16[208,512]{1,0:T(8,128)(2,1)S(1)}, u32[]{:S(2)}, u32[]{:S(2)}) %collective-permute-start.12) | collective-permute-done | bytes 213024 | tf_op jit(solution)/shard_map/ppermute | solution.py:794
  24.1 5.6 %collective-permute-done.13.refs_6_ = bf16[208,512]{1,0:T(8,128)(2,1)S(1)} collective-permute-done((bf16[208,512]{1,0:T(8,128)(2,1)}, bf16[208,512]{1,0:T(8,128)(2,1)S(1)}, u32[]{:S(2)}, u32[]{:S(2)}) %collective-permute-start.13) | collective-permute-done | bytes 213024 | tf_op jit(solution)/shard_map/ppermute | solution.py:794
  34.0 3.5 %collective-permute-done.15.refs_8_ = bf16[208,512]{1,0:T(8,128)(2,1)} collective-permute-done((bf16[208,512]{1,0:T(8,128)(2,1)S(1)}, bf16[208,512]{1,0:T(8,128)(2,1)}, u32[]{:S(2)}, u32[]{:S(2)}) %collective-permute-start.15) | collective-permute-done | bytes 213024 | tf_op jit(solution)/shard_map/ppermute | solution.py:794
  38.0 2.1 %collective-permute-done.8.refs_7_ = bf16[256,512]{1,0:T(8,128)(2,1)S(1)} collective-permute-done((bf16[256,512]{1,0:T(8,128)(2,1)S(1)}, bf16[256,512]{1,0:T(8,128)(2,1)S(1)}, u32[]{:S(2)}, u32[]{:S(2)}) %collective-permute-start.8) | collective-permute-done | bytes 262176 | tf_op jit(solution)/shard_map/ppermute | solution.py:794
  41.2 2.7 %collective-permute-done.16.refs_9_ = bf16[208,512]{1,0:T(8,128)(2,1)} collective-permute-done((bf16[208,512]{1,0:T(8,128)(2,1)S(1)}, bf16[208,512]{1,0:T(8,128)(2,1)}, u32[]{:S(2)}, u32[]{:S(2)}) %collective-permute-start.16) | collective-permute-done | bytes 213024 | tf_op jit(solution)/shard_map/ppermute | solution.py:794
  52.0 9.8 %shard_map.274 = (bf16[512,1024]{1,0:T(8,128)(2,1)}, bf16[1024,512]{1,0:T(8,128)(2,1)}, bf16[1024,512]{1,0:T(8,128)(2,1)}, bf16[1024,256]{1,0:T(8,128)(2,1)}, bf...) custom-call(s32[12]{0:T(128)} %stack.57.place_ref, ...), custom_call_target="tpu_custom_call" | custom-call | flops 6600000000 | bytes 1048576 | tf_op jit(solution)/shard_map/pallas_call | solution.py:759
  63.4 5.5 %shard_map.275.refs_13_.refs_5_ = f32[512,512]{1,0:T(8,128)} custom-call(s32[1,4]{1,0:T(1,128)} %lengths_ref.15, f32[512,512]{1,0:T(8,128)} %get-tuple-element.115.refs_0_.refs_1_, f32[512,256]{1,0:T(8,128)} %get-tuple-element.116.refs_1_.refs_2_, f32[512,16]{1,0:T(8,128)} %get-tuple-element.117.refs_2_.refs_3_, ...), custom_call_target="tpu_custom_call" | custom-call | flops 5500000256 | bytes 1048576 | tf_op jit(solution)/shard_map/pallas_call | solution.py:759
  69.6 7.3 %shard_map.276 = (bf16[512,1024]{1,0:T(8,128)(2,1)}, bf16[1024,512]{1,0:T(8,128)(2,1)}, bf16[1024,512]{1,0:T(8,128)(2,1)}, f32[512,512]{1,0:T(8,128)}, f32[512,512]{1,0:T(8,128)}, /*index=5*/f32[8,512]{1,0:T(8,128)}) custom-call(s32[12]{0:T(128)} %stack.57.place_ref, s32[1,4]{1,0:T(1,128)} %lengths_ref.15, bf16[256,1024]{1,0:T(8,128)(2,1)} %copy-done.3, ...), custom_call_target="tpu_custom_call" | custom-call | flops 5500000256 | bytes 1048576 | tf_op jit(solution)/shard_map/pallas_call | solution.py:759
  78.8 2.1 %collective-permute-done.21.refs_2_ = f32[8,512]{1,0:T(8,128)S(1)} collective-permute-done((f32[8,512]{1,0:T(8,128)}, f32[8,512]{1,0:T(8,128)S(1)}, u32[]{:S(2)}, u32[]{:S(2)}) %collective-permute-start.21) | collective-permute-done | bytes 16416 | tf_op jit(solution)/shard_map/ppermute | solution.py:843
  82.1 8.1 %shard_map.277 = (bf16[256,512]{1,0:T(8,128)(2,1)}, bf16[256,512]{1,0:T(8,128)(2,1)}, bf16[256,512]{1,0:T(8,128)(2,1)}, bf16[256,512]{1,0:T(8,128)(2,1)}, bf16[2...) custom-call(s32[12]{0:T(128)} %stack.57.place_ref, ...), custom_call_target="tpu_custom_call" | custom-call | flops 9900000256 | bytes 1048576 | tf_op jit(solution)/shard_map/pallas_call | solution.py:759
  90.8 1.8 collective-permute-start.23
  92.6 6.8 %shard_map.278 = (f32[512,256]{1,0:T(8,128)}, f32[512,256]{1,0:T(8,128)}, f32[16,512]{1,0:T(8,128)}, f32[8,256]{1,0:T(8,128)}) custom-call(s32[1,4]{1,0:T(1,128)} %lengths_ref.15, f32[512,512]{1,0:T(8,128)} %get-tuple-element.150.refs_0_, f32[512,512]{1,0:T(8,128)} %get-tuple-element.115.refs_0_.refs_1_, f32[512,256]{1,0:T(8,128)} %get-tuple-element.116.refs_1_.refs_2_, ...), custom_call_target="tpu_custom_call" | custom-call | flops 6600000000 | bytes 1048576 | tf_op jit(solution)/shard_map/pallas_call | solution.py:759
  99.4 3.7 %all-to-all-start = ((bf16[4,128,1024]{2,1,0:T(8,128)(2,1)}), bf16[4,128,1024]{2,1,0:T(8,128)(2,1)S(1)}, u32[]{:S(2)}, u32[]{:S(2)}) async-start(bf16[4,128,1024]{2,1,0:T(8,128)(2,1)} %bitcast.18), calls=%async_computation | async-start | bytes 2097152 | tf_op jit(solution)/shard_map/all_to_all | solution.py:838
  103.5 1.8 collective-permute-start.25
  105.4 6.4 %shard_map.279 = (f32[512,256]{1,0:T(8,128)}, f32[512,256]{1,0:T(8,128)}, f32[16,512]{1,0:T(8,128)}, f32[8,256]{1,0:T(8,128)}) custom-call(s32[1,4]{1,0:T(1,128)} %lengths_ref.15, f32[512,512]{1,0:T(8,128)} %get-tuple-element.150.refs_0_, f32[512,512]{1,0:T(8,128)} %get-tuple-element.115.refs_0_.refs_1_, f32[512,256]{1,0:T(8,128)} %get-tuple-element.116.refs_1_.refs_2_, ...), custom_call_target="tpu_custom_call" | custom-call | flops 6600000000 | bytes 1048576 | tf_op jit(solution)/shard_map/pallas_call | solution.py:759
  113.3 1.8 collective-permute-start.27
  115.4 5.4 %shard_map.281 = (bf16[512,256]{1,0:T(8,128)(2,1)}, bf16[16,512]{1,0:T(8,128)(2,1)}, bf16[272,256]{1,0:T(8,128)(2,1)}, bf16[272,256]{1,0:T(8,128)(2,1)}, bf16[27...) custom-call(s32[12]{0:T(128)} %stack.57.place_ref, s32[1,4]{1,0:T(1,128)} %lengths_ref.15, ...), custom_call_target="tpu_custom_call" | custom-call | flops 4400000000 | bytes 1048576 | tf_op jit(solution)/shard_map/pallas_call | solution.py:759
  123.4 1.7 collective-permute-start.29
  125.2 5.6 %shard_map.280 = (bf16[512,512]{1,0:T(8,128)(2,1)}, f32[16,512]{1,0:T(8,128)}) custom-call(s32[1,4]{1,0:T(1,128)} %lengths_ref.15, f32[512,256]{1,0:T(8,128)} %get-tuple-element.149.refs_0_, f32[512,256]{1,0:T(8,128)} %get-tuple-element.151.refs_1_, f32[8,256]{1,0:T(8,128)} %get-tuple-element.152.refs_2_, f32[8,256]{1,0:T(8,128)} %get-tuple-element.153.refs_3_, ...), custom_call_target="tpu_custom_call" | custom-call | flops 6600000000 | bytes 1048576 | tf_op jit(solution)/shard_map/pallas_call | solution.py:759
  132.9 3.1 %shard_map.283 = (bf16[176,512]{1,0:T(8,128)(2,1)}, bf16[176,512]{1,0:T(8,128)(2,1)}) custom-call(s32[12]{0:T(128)} %stack.57.place_ref, bf16[512,512]{1,0:T(8,128)(2,1)} %get-tuple-element.179.refs_1_.refs_0_, bf16[16,512]{1,0:T(8,128)(2,1)} %get-tuple-element.167.refs_3_.refs_1_, f32[16,512]{1,0:T(8,128)} %get-tuple-element.174.refs_2_, ...), custom_call_target="tpu_custom_call" | custom-call | flops 2000000000 | bytes 1048576 | tf_op jit(solution)/shard_map/pallas_call | solution.py:1154
  138.1 5.6 %shard_map.282 = (bf16[2,128,1024]{2,1,0:T(8,128)(2,1)}, bf16[2,128,1024]{2,1,0:T(8,128)(2,1)}) custom-call(s32[12]{0:T(128)} %stack.57.place_ref, bf16[512,512]{1,0:T(8,128)(2,1)} %get-tuple-element.158.refs_0_, bf16[512,512]{1,0:T(8,128)(2,1)} %get-tuple-element.179.refs_1_.refs_0_, bf16[512,256]{1,0:T(8,128)(2,1)} %get-tuple-element.166.refs_2_, ...), custom_call_target="tpu_custom_call" | custom-call | flops 6600000000 | bytes 1048576 | tf_op jit(solution)/shard_map/pallas_call | solution.py:759
  145.1 3.3 %shard_map.284 = (bf16[176,512]{1,0:T(8,128)(2,1)}, bf16[176,512]{1,0:T(8,128)(2,1)}) custom-call(s32[12]{0:T(128)} %stack.57.place_ref, bf16[512,512]{1,0:T(8,128)(2,1)} %get-tuple-element.179.refs_1_.refs_0_, bf16[16,512]{1,0:T(8,128)(2,1)} %get-tuple-element.167.refs_3_.refs_1_, f32[16,512]{1,0:T(8,128)} %get-tuple-element.174.refs_2_, ...), custom_call_target="tpu_custom_call" | custom-call | flops 2000000000 | bytes 1048576 | tf_op jit(solution)/shard_map/pallas_call | solution.py:1154
  151.1 3.0 %collective-permute-done.37.refs_9_ = bf16[176,512]{1,0:T(8,128)(2,1)S(1)} collective-permute-done((bf16[176,512]{1,0:T(8,128)(2,1)}, bf16[176,512]{1,0:T(8,128)(2,1)S(1)}, u32[]{:S(2)}, u32[]{:S(2)}) %collective-permute-start.37) | collective-permute-done | bytes 180256 | tf_op jit(solution)/shard_map/ppermute | solution.py:794
  156.5 3.3 %shard_map.285 = (bf16[176,512]{1,0:T(8,128)(2,1)}, bf16[176,512]{1,0:T(8,128)(2,1)}) custom-call(s32[12]{0:T(128)} %stack.57.place_ref, bf16[512,512]{1,0:T(8,128)(2,1)} %get-tuple-element.179.refs_1_.refs_0_, bf16[16,512]{1,0:T(8,128)(2,1)} %get-tuple-element.167.refs_3_.refs_1_, f32[16,512]{1,0:T(8,128)} %get-tuple-element.174.refs_2_, ...), custom_call_target="tpu_custom_call" | custom-call | flops 2000000000 | bytes 1048576 | tf_op jit(solution)/shard_map/pallas_call | solution.py:1154
  163.3 2.1 %collective-permute-done.39.refs_9_ = bf16[176,512]{1,0:T(8,128)(2,1)S(1)} collective-permute-done((bf16[176,512]{1,0:T(8,128)(2,1)}, bf16[176,512]{1,0:T(8,128)(2,1)S(1)}, u32[]{:S(2)}, u32[]{:S(2)}) %collective-permute-start.39) | collective-permute-done | bytes 180256 | tf_op jit(solution)/shard_map/ppermute | solution.py:794
  167.1 3.4 %shard_map.286 = (bf16[176,512]{1,0:T(8,128)(2,1)}, f32[176,512]{1,0:T(8,128)}) custom-call(s32[12]{0:T(128)} %stack.57.place_ref, bf16[512,512]{1,0:T(8,128)(2,1)} %get-tuple-element.179.refs_1_.refs_0_, bf16[16,512]{1,0:T(8,128)(2,1)} %get-tuple-element.167.refs_3_.refs_1_, f32[16,512]{1,0:T(8,128)} %get-tuple-element.174.refs_2_, ...), custom_call_target="tpu_custom_call" | custom-call | flops 2000000000 | bytes 1048576 | tf_op jit(solution)/shard_map/pallas_call | solution.py:1154
  173.0 3.2 %collective-permute-done.41.refs_1_ = bf16[176,512]{1,0:T(8,128)(2,1)S(1)} collective-permute-done((bf16[176,512]{1,0:T(8,128)(2,1)}, bf16[176,512]{1,0:T(8,128)(2,1)S(1)}, u32[]{:S(2)}, u32[]{:S(2)}) %collective-permute-start.41) | collective-permute-done | bytes 180256 | tf_op jit(solution)/shard_map/ppermute | solution.py:794
  176.9 2.5 %shard_map.287 = (f32[128,2,512]{2,1,0:T(2,128)}, f32[128,8]{1,0:T(8,128)}, f32[32,256]{1,0:T(8,128)}, f32[16,512]{1,0:T(8,128)}, f32[8,128]{1,0:T(8,128)}, /*index=5*/f32[8,32]{1,0:T(8,128)}) custom-call(f32[176,512]{1,0:T(8,128)} %get-tuple-element.186.refs_0_, bf16[176,512]{1,0:T(8,128)(2,1)} %copy-done.27, f32[128,512]{1,0:T(8,128)} %get-tuple-element.213.refs_2_, ...), custom_call_target="tpu_custom_call" | custom-call | flops 2200000000 | bytes 1048576 | tf_op jit(solution)/shard_map/pallas_call | solution.py:759
  (187 shorter events, 67.0 us)
Async XLA Ops:
  11.3 18.4 %collective-permute-start.4 = (bf16[256,1024]{1,0:T(8,128)(2,1)S(1)}, bf16[256,1024]{1,0:T(8,128)(2,1)S(1)}, u32[]{:S(2)}, u32[]{:S(2)}) collective-permute-start(bf16[256,1024]{1,0:T(8,128)(2,1)S(1)} %pad_maximum_fusion.refs_0_), channel_id=1, source_target_pairs={{0,2},{1,3},{2,0},{3,1},{4,6},{5,7},{6,4},{7,5},{8,10},{9,11},{10,... | collective-permute-start | bytes 1572872 | tf_op jit(solution)/shard_map/ppermute | solution.py:843
  14.0 8.3 %collective-permute-start.12 = (bf16[208,512]{1,0:T(8,128)(2,1)}, bf16[208,512]{1,0:T(8,128)(2,1)S(1)}, u32[]{:S(2)}, u32[]{:S(2)}) collective-permute-start(bf16[208,512]{1,0:T(8,128)(2,1)} %shard_map.272.refs_4_), channel_id=1, source_target_pairs={{0,8},{8,16},{16,24},{24,28},{28,20},{20,12},{12,4},{4,0},{1,9},{9... | collective-permute-start | bytes 638984 | tf_op jit(solution)/shard_map/ppermute | solution.py:794
  15.7 14.5 %collective-permute-start.6 = (bf16[256,512]{1,0:T(8,128)(2,1)}, bf16[256,512]{1,0:T(8,128)(2,1)S(1)}, u32[]{:S(2)}, u32[]{:S(2)}) collective-permute-start(bf16[256,512]{1,0:T(8,128)(2,1)} %get-tuple-element.107.refs_4_), channel_id=1, source_target_pairs={{0,8},{8,16},{16,24},{24,28},{28,20},{20,12},{12,4},{4,0},{1,9},{9... | collective-permute-start | bytes 786440 | tf_op jit(solution)/shard_map/ppermute | solution.py:794
  17.3 13.4 %collective-permute-start.7 = (bf16[256,512]{1,0:T(8,128)(2,1)}, bf16[256,512]{1,0:T(8,128)(2,1)}, u32[]{:S(2)}, u32[]{:S(2)}) collective-permute-start(bf16[256,512]{1,0:T(8,128)(2,1)} %get-tuple-element.107.refs_4_), channel_id=1, source_target_pairs={{0,4},{8,0},{16,8},{24,16},{28,24},{20,28},{12,20},{4,12},{1,5},{9... | collective-permute-start | bytes 786440 | tf_op jit(solution)/shard_map/ppermute | solution.py:794
  17.7 11.9 %collective-permute-start.13 = (bf16[208,512]{1,0:T(8,128)(2,1)}, bf16[208,512]{1,0:T(8,128)(2,1)S(1)}, u32[]{:S(2)}, u32[]{:S(2)}) collective-permute-start(bf16[208,512]{1,0:T(8,128)(2,1)} %shard_map.272.refs_4_), channel_id=1, source_target_pairs={{0,4},{8,0},{16,8},{24,16},{28,24},{20,28},{12,20},{4,12},{1,5},{9... | collective-permute-start | bytes 638984 | tf_op jit(solution)/shard_map/ppermute | solution.py:794
  22.3 10.2 %collective-permute-start.14 = (bf16[208,512]{1,0:T(8,128)(2,1)S(1)}, bf16[208,512]{1,0:T(8,128)(2,1)S(1)}, u32[]{:S(2)}, u32[]{:S(2)}) collective-permute-start(bf16[208,512]{1,0:T(8,128)(2,1)S(1)} %collective-permute-done.12.refs_5_), channel_id=1, source_target_pairs={{0,8},{8,16},{16,24},{24,28},{28,20},{20,12},{12,4},{4,0},{1,9},{9... | collective-permute-start | bytes 638984 | tf_op jit(solution)/shard_map/ppermute | solution.py:794
  29.7 20.9 %collective-permute-start.3 = (bf16[256,1024]{1,0:T(8,128)(2,1)S(1)}, bf16[256,1024]{1,0:T(8,128)(2,1)S(1)}, u32[]{:S(2)}, u32[]{:S(2)}) collective-permute-start(bf16[256,1024]{1,0:T(8,128)(2,1)S(1)} %pad_maximum_fusion.refs_0_), channel_id=1, source_target_pairs={{0,1},{1,0},{2,3},{3,2},{4,5},{5,4},{6,7},{7,6},{8,9},{9,8},{10,11... | collective-permute-start | bytes 1572872 | tf_op jit(solution)/shard_map/ppermute | solution.py:843
  29.7 21.4 %collective-permute-start.5 = (bf16[256,1024]{1,0:T(8,128)(2,1)S(1)}, bf16[256,1024]{1,0:T(8,128)(2,1)S(1)}, u32[]{:S(2)}, u32[]{:S(2)}) collective-permute-start(bf16[256,1024]{1,0:T(8,128)(2,1)S(1)} %collective-permute-done.4.refs_2_), channel_id=1, source_target_pairs={{0,1},{1,0},{2,3},{3,2},{4,5},{5,4},{6,7},{7,6},{8,9},{9,8},{10,11... | collective-permute-start | bytes 1572872 | tf_op jit(solution)/shard_map/ppermute | solution.py:843
  30.2 7.3 %collective-permute-start.15 = (bf16[208,512]{1,0:T(8,128)(2,1)S(1)}, bf16[208,512]{1,0:T(8,128)(2,1)}, u32[]{:S(2)}, u32[]{:S(2)}) collective-permute-start(bf16[208,512]{1,0:T(8,128)(2,1)S(1)} %collective-permute-done.13.refs_6_), channel_id=1, source_target_pairs={{0,4},{8,0},{16,8},{24,16},{28,24},{20,28},{12,20},{4,12},{1,5},{9... | collective-permute-start | bytes 638984 | tf_op jit(solution)/shard_map/ppermute | solution.py:794
  30.9 9.2 %collective-permute-start.8 = (bf16[256,512]{1,0:T(8,128)(2,1)S(1)}, bf16[256,512]{1,0:T(8,128)(2,1)S(1)}, u32[]{:S(2)}, u32[]{:S(2)}) collective-permute-start(bf16[256,512]{1,0:T(8,128)(2,1)S(1)} %collective-permute-done.6.refs_5_), channel_id=1, source_target_pairs={{0,8},{8,16},{16,24},{24,28},{28,20},{20,12},{12,4},{4,0},{1,9},{9... | collective-permute-start | bytes 786440 | tf_op jit(solution)/shard_map/ppermute | solution.py:794
  32.5 11.5 %collective-permute-start.16 = (bf16[208,512]{1,0:T(8,128)(2,1)S(1)}, bf16[208,512]{1,0:T(8,128)(2,1)}, u32[]{:S(2)}, u32[]{:S(2)}) collective-permute-start(bf16[208,512]{1,0:T(8,128)(2,1)S(1)} %collective-permute-done.14.refs_7_), channel_id=1, source_target_pairs={{0,8},{8,16},{16,24},{24,28},{28,20},{20,12},{12,4},{4,0},{1,9},{9... | collective-permute-start | bytes 638984 | tf_op jit(solution)/shard_map/ppermute | solution.py:794
  37.5 11.5 %collective-permute-start.9 = (bf16[256,512]{1,0:T(8,128)(2,1)}, bf16[256,512]{1,0:T(8,128)(2,1)}, u32[]{:S(2)}, u32[]{:S(2)}) collective-permute-start(bf16[256,512]{1,0:T(8,128)(2,1)} %collective-permute-done.7.refs_6_), channel_id=1, source_target_pairs={{0,4},{8,0},{16,8},{24,16},{28,24},{20,28},{12,20},{4,12},{1,5},{9... | collective-permute-start | bytes 786440 | tf_op jit(solution)/shard_map/ppermute | solution.py:794
  40.8 10.3 %collective-permute-start.17 = (bf16[208,512]{1,0:T(8,128)(2,1)}, bf16[208,512]{1,0:T(8,128)(2,1)}, u32[]{:S(2)}, u32[]{:S(2)}) collective-permute-start(bf16[208,512]{1,0:T(8,128)(2,1)} %collective-permute-done.15.refs_8_), channel_id=1, source_target_pairs={{0,4},{8,0},{16,8},{24,16},{28,24},{20,28},{12,20},{4,12},{1,5},{9... | collective-permute-start | bytes 638984 | tf_op jit(solution)/shard_map/ppermute | solution.py:794
  49.0 12.7 %collective-permute-start.10 = (bf16[256,512]{1,0:T(8,128)(2,1)S(1)}, bf16[256,512]{1,0:T(8,128)(2,1)}, u32[]{:S(2)}, u32[]{:S(2)}) collective-permute-start(bf16[256,512]{1,0:T(8,128)(2,1)S(1)} %copy-done.18), channel_id=1, source_target_pairs={{0,8},{8,16},{16,24},{24,28},{28,20},{20,12},{12,4},{4,0},{1,9},{9... | collective-permute-start | bytes 786440 | tf_op jit(solution)/shard_map/ppermute | solution.py:794
  50.6 11.2 %collective-permute-start.11 = (bf16[256,512]{1,0:T(8,128)(2,1)}, bf16[256,512]{1,0:T(8,128)(2,1)S(1)}, u32[]{:S(2)}, u32[]{:S(2)}) collective-permute-start(bf16[256,512]{1,0:T(8,128)(2,1)} %collective-permute-done.9.refs_8_), channel_id=1, source_target_pairs={{0,4},{8,0},{16,8},{24,16},{28,24},{20,28},{12,20},{4,12},{1,5},{9... | collective-permute-start | bytes 786440 | tf_op jit(solution)/shard_map/ppermute | solution.py:794
  90.2 12.9 %collective-permute-start.24 = (bf16[256,512]{1,0:T(8,128)(2,1)}, bf16[256,512]{1,0:T(8,128)(2,1)S(1)}, u32[]{:S(2)}, u32[]{:S(2)}) collective-permute-start(bf16[256,512]{1,0:T(8,128)(2,1)} %get-tuple-element.134), channel_id=1, source_target_pairs={{0,4},{8,0},{16,8},{24,16},{28,24},{20,28},{12,20},{4,12},{1,5},{9... | collective-permute-start | bytes 786440 | tf_op jit(solution)/shard_map/ppermute | solution.py:794
  90.8 12.4 %collective-permute-start.23 = (bf16[256,512]{1,0:T(8,128)(2,1)}, bf16[256,512]{1,0:T(8,128)(2,1)S(1)}, u32[]{:S(2)}, u32[]{:S(2)}) collective-permute-start(bf16[256,512]{1,0:T(8,128)(2,1)} %get-tuple-element.132), channel_id=1, source_target_pairs={{0,8},{8,16},{16,24},{24,28},{28,20},{20,12},{12,4},{4,0},{1,9},{9... | collective-permute-start | bytes 786440 | tf_op jit(solution)/shard_map/ppermute | solution.py:794
  99.4 31.4 %all-to-all-start = ((bf16[4,128,1024]{2,1,0:T(8,128)(2,1)}), bf16[4,128,1024]{2,1,0:T(8,128)(2,1)S(1)}, u32[]{:S(2)}, u32[]{:S(2)}) async-start(bf16[4,128,1024]{2,1,0:T(8,128)(2,1)} %bitcast.18), calls=%async_computation | async-start | bytes 2097152 | tf_op jit(solution)/shard_map/all_to_all | solution.py:838
  103.3 8.9 %collective-permute-start.26 = (bf16[256,512]{1,0:T(8,128)(2,1)S(1)}, bf16[256,512]{1,0:T(8,128)(2,1)}, u32[]{:S(2)}, u32[]{:S(2)}) collective-permute-start(bf16[256,512]{1,0:T(8,128)(2,1)S(1)} %add_convert_fusion.4), channel_id=1, source_target_pairs={{0,4},{8,0},{16,8},{24,16},{28,24},{20,28},{12,20},{4,12},{1,5},{9... | collective-permute-start | bytes 786440 | tf_op jit(solution)/shard_map/ppermute | solution.py:794
  103.5 9.6 %collective-permute-start.25 = (bf16[256,512]{1,0:T(8,128)(2,1)S(1)}, bf16[256,512]{1,0:T(8,128)(2,1)S(1)}, u32[]{:S(2)}, u32[]{:S(2)}) collective-permute-start(bf16[256,512]{1,0:T(8,128)(2,1)S(1)} %add_convert_fusion.5), channel_id=1, source_target_pairs={{0,8},{8,16},{16,24},{24,28},{28,20},{20,12},{12,4},{4,0},{1,9},{9... | collective-permute-start | bytes 786440 | tf_op jit(solution)/shard_map/ppermute | solution.py:794
  113.3 9.4 %collective-permute-start.27 = (bf16[256,512]{1,0:T(8,128)(2,1)S(1)}, bf16[256,512]{1,0:T(8,128)(2,1)S(1)}, u32[]{:S(2)}, u32[]{:S(2)}) collective-permute-start(bf16[256,512]{1,0:T(8,128)(2,1)S(1)} %add_convert_fusion.3), channel_id=1, source_target_pairs={{0,8},{8,16},{16,24},{24,28},{28,20},{20,12},{12,4},{4,0},{1,9},{9... | collective-permute-start | bytes 786440 | tf_op jit(solution)/shard_map/ppermute | solution.py:794
  115.1 8.3 %collective-permute-start.28 = (bf16[256,512]{1,0:T(8,128)(2,1)S(1)}, bf16[256,512]{1,0:T(8,128)(2,1)S(1)}, u32[]{:S(2)}, u32[]{:S(2)}) collective-permute-start(bf16[256,512]{1,0:T(8,128)(2,1)S(1)} %add_convert_fusion.2), channel_id=1, source_target_pairs={{0,4},{8,0},{16,8},{24,16},{28,24},{20,28},{12,20},{4,12},{1,5},{9... | collective-permute-start | bytes 786440 | tf_op jit(solution)/shard_map/ppermute | solution.py:794
  120.8 11.5 %collective-permute-start.32 = (bf16[272,256]{1,0:T(8,128)(2,1)}, bf16[272,256]{1,0:T(8,128)(2,1)S(1)}, u32[]{:S(2)}, u32[]{:S(2)}) collective-permute-start(bf16[272,256]{1,0:T(8,128)(2,1)} %get-tuple-element.176), channel_id=1, source_target_pairs={{0,1},{1,0},{2,3},{3,2},{4,5},{5,4},{6,7},{7,6},{8,9},{9,8},{10,11... | collective-permute-start | bytes 417800 | tf_op jit(solution)/shard_map/ppermute | solution.py:843
  120.8 11.5 %collective-permute-start.33 = (bf16[272,256]{1,0:T(8,128)(2,1)}, bf16[272,256]{1,0:T(8,128)(2,1)}, u32[]{:S(2)}, u32[]{:S(2)}) collective-permute-start(bf16[272,256]{1,0:T(8,128)(2,1)} %get-tuple-element.177), channel_id=1, source_target_pairs={{0,2},{1,3},{2,0},{3,1},{4,6},{5,7},{6,4},{7,5},{8,10},{9,11},{10,... | collective-permute-start | bytes 417800 | tf_op jit(solution)/shard_map/ppermute | solution.py:843
  122.5 9.8 %collective-permute-start.34 = (bf16[272,256]{1,0:T(8,128)(2,1)}, bf16[272,256]{1,0:T(8,128)(2,1)}, u32[]{:S(2)}, u32[]{:S(2)}) collective-permute-start(bf16[272,256]{1,0:T(8,128)(2,1)} %get-tuple-element.178), channel_id=1, source_target_pairs={{0,3},{1,2},{2,1},{3,0},{4,7},{5,6},{6,5},{7,4},{8,11},{9,10},{10,... | collective-permute-start | bytes 417800 | tf_op jit(solution)/shard_map/ppermute | solution.py:843
  123.4 8.8 %collective-permute-start.29 = (bf16[256,512]{1,0:T(8,128)(2,1)}, bf16[256,512]{1,0:T(8,128)(2,1)S(1)}, u32[]{:S(2)}, u32[]{:S(2)}) collective-permute-start(bf16[256,512]{1,0:T(8,128)(2,1)} %add_convert_fusion.1), channel_id=1, source_target_pairs={{0,8},{8,16},{16,24},{24,28},{28,20},{20,12},{12,4},{4,0},{1,9},{9... | collective-permute-start | bytes 786440 | tf_op jit(solution)/shard_map/ppermute | solution.py:794
  136.1 7.6 %collective-permute-start.35 = (bf16[176,512]{1,0:T(8,128)(2,1)}, bf16[176,512]{1,0:T(8,128)(2,1)S(1)}, u32[]{:S(2)}, u32[]{:S(2)}) collective-permute-start(bf16[176,512]{1,0:T(8,128)(2,1)} %get-tuple-element.180), channel_id=1, source_target_pairs={{0,8},{8,16},{16,24},{24,28},{28,20},{20,12},{12,4},{4,0},{1,9},{9... | collective-permute-start | bytes 540680 | tf_op jit(solution)/shard_map/ppermute | solution.py:794
  151.1 20.1 %collective-permute-start.30 = (bf16[2,128,1024]{2,1,0:T(8,128)(2,1)}, bf16[2,128,1024]{2,1,0:T(8,128)(2,1)S(1)}, u32[]{:S(2)}, u32[]{:S(2)}) collective-permute-start(bf16[2,128,1024]{2,1,0:T(8,128)(2,1)} %get-tuple-element.173), channel_id=1, source_target_pairs={{0,1},{1,0},{2,3},{3,2},{4,5},{5,4},{6,7},{7,6},{8,9},{9,8},{10,11... | collective-permute-start | bytes 1572872 | tf_op jit(solution)/shard_map/ppermute | solution.py:843
  171.2 19.5 %collective-permute-start.31 = (bf16[128,1024]{1,0:T(8,128)(2,1)S(1)}, bf16[128,1024]{1,0:T(8,128)(2,1)S(1)}, u32[]{:S(2)}, u32[]{:S(2)}) collective-permute-start(bf16[128,1024]{1,0:T(8,128)(2,1)S(1)} %fusion.6), channel_id=1, source_target_pairs={{0,2},{1,3},{2,0},{3,1},{4,6},{5,7},{6,4},{7,5},{8,10},{9,11},{10,... | collective-permute-start | bytes 786440 | tf_op jit(solution)/shard_map/ppermute | solution.py:843
  179.4 9.4 %collective-permute-start.42 = (f32[8,128]{1,0:T(8,128)}, f32[8,128]{1,0:T(8,128)S(1)}, u32[]{:S(2)}, u32[]{:S(2)}) collective-permute-start(f32[8,128]{1,0:T(8,128)} %get-tuple-element.189), channel_id=1, source_target_pairs={{0,1},{1,0},{2,3},{3,2},{4,5},{5,4},{6,7},{7,6},{8,9},{9,8},{10,11... | collective-permute-start | bytes 12296 | tf_op jit(solution)/shard_map/ppermute | solution.py:843
  179.4 9.4 %collective-permute-start.43 = (f32[8,128]{1,0:T(8,128)}, f32[8,128]{1,0:T(8,128)S(1)}, u32[]{:S(2)}, u32[]{:S(2)}) collective-permute-start(f32[8,128]{1,0:T(8,128)} %get-tuple-element.189), channel_id=1, source_target_pairs={{0,2},{1,3},{2,0},{3,1},{4,6},{5,7},{6,4},{7,5},{8,10},{9,11},{10,... | collective-permute-start | bytes 12296 | tf_op jit(solution)/shard_map/ppermute | solution.py:843
  181.1 7.7 %collective-permute-start.44 = (f32[8,128]{1,0:T(8,128)}, f32[8,128]{1,0:T(8,128)S(1)}, u32[]{:S(2)}, u32[]{:S(2)}) collective-permute-start(f32[8,128]{1,0:T(8,128)} %get-tuple-element.189), channel_id=1, source_target_pairs={{0,3},{1,2},{2,1},{3,0},{4,7},{5,6},{6,5},{7,4},{8,11},{9,10},{10,... | collective-permute-start | bytes 12296 | tf_op jit(solution)/shard_map/ppermute | solution.py:843
  (52 other events, 322.1 us)

commit v8 on v5

--- a/solution.py
+++ b/solution.py
@@ -1043,9 +1043,6 @@
         [((total, channels), bf16), ((16, channels), f32)],
         [masks, ((total, channels), f32), ((total + pad, channels), f32)],
     )
-    if fast:
-        mixed_rows = tensor_sum(partial_out, depth)
-        (gate_out, mixed_rows), grad_inner = ordered((gate_out, mixed_rows), grad_inner)
 
     def project_back():
         return call(
@@ -1099,11 +1096,17 @@
         )(place, *arrays)
 
     if fast:
-        got = ring_step(chunk_pair((7, 5), ()))
+        held = chunk_pair((7, 5), ())
+        got = ring_step(held)
         keep_rows, give_rows = project_back()
-        got = ring_step(chunk_pair((6, 3), got, give_rows))
+        held = chunk_pair((6, 3), got, give_rows)
+        partial_out = ordered(held, partial_out)[1]
+        got = ring_step(held)
+        mixed_rows = tensor_sum(partial_out, depth)
+        near = tensor_swap(give_rows, 1)
+        far_half = add_low(keep_rows[1], near[1])
         got = ring_step(chunk_pair((4, 1), got))
-        held, inner_own = chunk_pair((2, 0), got, last=f32)
+        held, inner_own = chunk_pair((2, 0), got, (mixed_rows, far_half), last=f32)
         inner_out = inner_own + ring_send(held, True).astype(f32)
     else:
         (inner_msg,) = call(
@@ -1120,9 +1123,8 @@
     gain_full = small_full[: depth // states].reshape(1, depth)
 
     if fast:
-        got = tensor_swap(give_rows, 1)
-        far = tensor_swap(add_low(keep_rows[1], got[1]), 2)
-        grad_local = keep_rows[0].astype(f32) + got[0].astype(f32) + far.astype(f32)
+        far = tensor_swap(far_half, 2)
+        grad_local = keep_rows[0].astype(f32) + near[0].astype(f32) + far.astype(f32)
         gate_grad, output_grad = gate_out[:tall], gate_out[tall:].T
         inner_grad = inner_out[:tall]
         state_grad = inner_out[tall : tall + 16]

time: 181 us -> 183 us (1.011)
  waiting for transfers between devices: 35.2 us -> 38.1 us
    ppermute x17, waiting for transfers between devices: 3.09 us -> 13 us  [tensor_swap(): return lax.ppermute(value, 'tensor', [(i, i ^ bit) for i in range(4)])]
    ppermute x28, waiting for transfers between devices: 32.1 us -> 25.1 us  [ring_send(): return lax.ppermute(value, 'dp', pairs)]
    unnamed x86 -> x92, local copies, waits for them, and re-layouts: 7.62 us -> 7.98 us
  transfers between devices with their start and end apart: 46 -> 46, of which waited for: 17 -> 15; matrix products, arithmetic and copies ran while one was open for 8% -> 7% of each run, Pallas kernels for 29% -> 29%
where the time goes in v8:
time: 183 us; the launch traced here: 182 us
  Pallas kernels  76.2 us (42%)
  starting transfers between devices  46.8 us (26%)
  waiting for transfers between devices  38.1 us (21%)
  local copies, waits for them, and re-layouts  13.6 us (7%)
  other arithmetic  6.58 us (4%)
    pallas_call x12, Pallas kernels, call(): pl.pallas_call(kernel, out_shape=[jax.ShapeDtypeStruct(shape, kind) for s...  63.4 us
    ppermute x28, starting transfers between devices, ring_send(): return lax.ppermute(value, 'dp', pairs)  30.5 us
    ppermute x28, waiting for transfers between devices, ring_send(): return lax.ppermute(value, 'dp', pairs)  25.1 us
    ppermute x17, waiting for transfers between devices, tensor_swap(): return lax.ppermute(value, 'tensor', [(i, i ^ bit) for i in range(4)])  13 us
    pallas_call x4, Pallas kernels, chunk_pair(): pl.pallas_call(functools.partial(chunk_kernel, slots, len(got)), grid_spe...  12.8 us
    ppermute x17, starting transfers between devices, tensor_swap(): return lax.ppermute(value, 'tensor', [(i, i ^ bit) for i in range(4)])  12.8 us
    unnamed x92, local copies, waits for them, and re-layouts  7.98 us
  transfers between devices with their start and end apart: 46, of which 15 were waited for; matrix products, arithmetic and copies ran while one was open for 7% of the time, Pallas kernels for 29%

profile of v8, /device:TPU:0, one launch (start us, length us, event | category | flops | bytes accessed | tf_op | source)
XLA Modules:
  0.0 182.5 jit_solution(6490812588612337370)
XLA Ops:
  3.3 2.6 %collective-permute-start.1 = (bf16[48,256]{1,0:T(8,128)(2,1)}, bf16[48,256]{1,0:T(8,128)(2,1)S(1)}, u32[]{:S(2)}, u32[]{:S(2)}) collective-permute-start(bf16[48,256]{1,0:T(8,128)(2,1)} %shard_map.271.refs_0_), channel_id=1, source_target_pairs={{0,2},{1,3},{2,0},{3,1},{4,6},{5,7},{6,4},{7,5},{8,10},{9,11},{10,... | collective-permute-start | bytes 73736 | tf_op jit(solution)/shard_map/ppermute | solution.py:787
  5.9 2.0 %shard_map.272.refs_4_ = bf16[256,512]{1,0:T(8,128)(2,1)} custom-call(bf16[128,2,512]{2,1,0:T(2,128)(2,1)} %input_ref.3, bf16[512,128]{1,0:T(8,128)(2,1)} %out_ref), custom_call_target="tpu_custom_call" | custom-call | flops 2200000000 | bytes 1048576 | tf_op jit(solution)/shard_map/pallas_call | solution.py:703
  8.0 1.8 collective-permute-start.6
  10.1 1.8 collective-permute-start.4
  12.5 2.0 %shard_map.273.refs_4_ = bf16[208,512]{1,0:T(8,128)(2,1)} custom-call(bf16[128,2,512]{2,1,0:T(2,128)(2,1)} %input_ref.3, bf16[16,128]{1,0:T(8,128)(2,1)} %pad.4.step_ref, bf16[48,256]{1,0:T(8,128)(2,1)} %shard_map.271.refs_0_, bf16[48,256]{1,0:T(8,128)(2,1)} %copy-done.38, bf16[48,256]{1,0:T(8,128)(2,1)} %copy-done.39, bf16[48,256]{1,0:T(8,128)(2,1)} %copy-done.40), custom_call_target="tpu_custom_call" | custom-call | flops 1100000000 | bytes 1048576 | tf_op jit(solution)/shard_map/pallas_call | solution.py:703
  14.5 2.2 %collective-permute-done.6.refs_5_ = bf16[256,512]{1,0:T(8,128)(2,1)S(1)} collective-permute-done((bf16[256,512]{1,0:T(8,128)(2,1)}, bf16[256,512]{1,0:T(8,128)(2,1)S(1)}, u32[]{:S(2)}, u32[]{:S(2)}) %collective-permute-start.6) | collective-permute-done | bytes 262176 | tf_op jit(solution)/shard_map/ppermute | solution.py:738
  22.0 4.8 %collective-permute-done.13.refs_5_ = bf16[208,512]{1,0:T(8,128)(2,1)S(1)} collective-permute-done((bf16[208,512]{1,0:T(8,128)(2,1)}, bf16[208,512]{1,0:T(8,128)(2,1)S(1)}, u32[]{:S(2)}, u32[]{:S(2)}) %collective-permute-start.13) | collective-permute-done | bytes 213024 | tf_op jit(solution)/shard_map/ppermute | solution.py:738
  29.1 3.4 %collective-permute-done.8.refs_7_ = bf16[256,512]{1,0:T(8,128)(2,1)} collective-permute-done((bf16[256,512]{1,0:T(8,128)(2,1)S(1)}, bf16[256,512]{1,0:T(8,128)(2,1)}, u32[]{:S(2)}, u32[]{:S(2)}) %collective-permute-start.8) | collective-permute-done | bytes 262176 | tf_op jit(solution)/shard_map/ppermute | solution.py:738
  32.8 2.3 %collective-permute-done.15.refs_7_ = bf16[208,512]{1,0:T(8,128)(2,1)S(1)} collective-permute-done((bf16[208,512]{1,0:T(8,128)(2,1)S(1)}, bf16[208,512]{1,0:T(8,128)(2,1)S(1)}, u32[]{:S(2)}, u32[]{:S(2)}) %collective-permute-start.15) | collective-permute-done | bytes 213024 | tf_op jit(solution)/shard_map/ppermute | solution.py:738
  39.4 2.5 %collective-permute-done.16.refs_8_ = bf16[208,512]{1,0:T(8,128)(2,1)} collective-permute-done((bf16[208,512]{1,0:T(8,128)(2,1)S(1)}, bf16[208,512]{1,0:T(8,128)(2,1)}, u32[]{:S(2)}, u32[]{:S(2)}) %collective-permute-start.16) | collective-permute-done | bytes 213024 | tf_op jit(solution)/shard_map/ppermute | solution.py:738
  49.5 2.9 %collective-permute-done.19.refs_11_ = bf16[208,512]{1,0:T(8,128)(2,1)} collective-permute-done((bf16[208,512]{1,0:T(8,128)(2,1)}, bf16[208,512]{1,0:T(8,128)(2,1)}, u32[]{:S(2)}, u32[]{:S(2)}) %collective-permute-start.19) | collective-permute-done | bytes 213024 | tf_op jit(solution)/shard_map/ppermute | solution.py:738
  52.4 11.2 %shard_map.275 = (bf16[512,1024]{1,0:T(8,128)(2,1)}, bf16[1024,512]{1,0:T(8,128)(2,1)}, bf16[1024,512]{1,0:T(8,128)(2,1)}, bf16[1024,256]{1,0:T(8,128)(2,1)}, bf...) custom-call(s32[12]{0:T(128)} %stack.66.place_ref, ...), custom_call_target="tpu_custom_call" | custom-call | flops 12099999744 | bytes 1048576 | tf_op jit(solution)/shard_map/pallas_call | solution.py:703
  64.4 7.3 %shard_map.276 = (bf16[512,1024]{1,0:T(8,128)(2,1)}, bf16[1024,512]{1,0:T(8,128)(2,1)}, bf16[1024,512]{1,0:T(8,128)(2,1)}, f32[512,512]{1,0:T(8,128)}, f32[512,512]{1,0:T(8,128)}, /*index=5*/f32[8,512]{1,0:T(8,128)}) custom-call(s32[12]{0:T(128)} %stack.66.place_ref, s32[1,4]{1,0:T(1,128)} %lengths_ref.13, bf16[256,1024]{1,0:T(8,128)(2,1)} %copy-done.7, ...), custom_call_target="tpu_custom_call" | custom-call | flops 5500000256 | bytes 1048576 | tf_op jit(solution)/shard_map/pallas_call | solution.py:703
  73.6 2.1 %collective-permute-done.21.refs_2_ = f32[8,512]{1,0:T(8,128)S(1)} collective-permute-done((f32[8,512]{1,0:T(8,128)}, f32[8,512]{1,0:T(8,128)S(1)}, u32[]{:S(2)}, u32[]{:S(2)}) %collective-permute-start.21) | collective-permute-done | bytes 16416 | tf_op jit(solution)/shard_map/ppermute | solution.py:787
  77.3 8.1 %shard_map.277 = (bf16[256,512]{1,0:T(8,128)(2,1)}, bf16[256,512]{1,0:T(8,128)(2,1)}, bf16[256,512]{1,0:T(8,128)(2,1)}, bf16[256,512]{1,0:T(8,128)(2,1)}, bf16[2...) custom-call(s32[12]{0:T(128)} %stack.66.place_ref, ...), custom_call_target="tpu_custom_call" | custom-call | flops 9900000256 | bytes 1048576 | tf_op jit(solution)/shard_map/pallas_call | solution.py:703
  87.5 6.5 %shard_map.278 = (f32[512,256]{1,0:T(8,128)}, f32[512,256]{1,0:T(8,128)}, f32[16,512]{1,0:T(8,128)}, f32[8,256]{1,0:T(8,128)}) custom-call(s32[1,4]{1,0:T(1,128)} %lengths_ref.13, f32[512,512]{1,0:T(8,128)} %get-tuple-element.131.refs_0_, f32[512,512]{1,0:T(8,128)} %get-tuple-element.122.refs_1_, f32[512,256]{1,0:T(8,128)} %get-tuple-element.123.refs_2_, ...), custom_call_target="tpu_custom_call" | custom-call | flops 6600000000 | bytes 1048576 | tf_op jit(solution)/shard_map/pallas_call | solution.py:703
  94.7 1.8 collective-permute-start.26
  96.8 6.5 %shard_map.279 = (f32[512,256]{1,0:T(8,128)}, f32[512,256]{1,0:T(8,128)}, f32[16,512]{1,0:T(8,128)}, f32[8,256]{1,0:T(8,128)}) custom-call(s32[1,4]{1,0:T(1,128)} %lengths_ref.13, f32[512,512]{1,0:T(8,128)} %get-tuple-element.131.refs_0_, f32[512,512]{1,0:T(8,128)} %get-tuple-element.122.refs_1_, f32[512,256]{1,0:T(8,128)} %get-tuple-element.123.refs_2_, ...), custom_call_target="tpu_custom_call" | custom-call | flops 6600000000 | bytes 1048576 | tf_op jit(solution)/shard_map/pallas_call | solution.py:703
  105.6 5.4 %shard_map.281 = (bf16[512,256]{1,0:T(8,128)(2,1)}, bf16[16,512]{1,0:T(8,128)(2,1)}, bf16[272,256]{1,0:T(8,128)(2,1)}, bf16[272,256]{1,0:T(8,128)(2,1)}, bf16[27...) custom-call(s32[12]{0:T(128)} %stack.66.place_ref, s32[1,4]{1,0:T(1,128)} %lengths_ref.13, ...), custom_call_target="tpu_custom_call" | custom-call | flops 4400000000 | bytes 1048576 | tf_op jit(solution)/shard_map/pallas_call | solution.py:703
  113.0 5.6 %shard_map.280 = (bf16[512,512]{1,0:T(8,128)(2,1)}, f32[16,512]{1,0:T(8,128)}) custom-call(s32[1,4]{1,0:T(1,128)} %lengths_ref.13, f32[512,256]{1,0:T(8,128)} %get-tuple-element.126.refs_0_, f32[512,256]{1,0:T(8,128)} %get-tuple-element.132.refs_1_, f32[8,256]{1,0:T(8,128)} %get-tuple-element.133.refs_2_, f32[8,256]{1,0:T(8,128)} %get-tuple-element.134.refs_3_, ...), custom_call_target="tpu_custom_call" | custom-call | flops 6600000000 | bytes 1048576 | tf_op jit(solution)/shard_map/pallas_call | solution.py:703
  120.5 3.1 %shard_map.283 = (bf16[176,512]{1,0:T(8,128)(2,1)}, bf16[176,512]{1,0:T(8,128)(2,1)}) custom-call(s32[12]{0:T(128)} %stack.66.place_ref, bf16[512,512]{1,0:T(8,128)(2,1)} %get-tuple-element.176.refs_1_.refs_0_, bf16[16,512]{1,0:T(8,128)(2,1)} %get-tuple-element.154.refs_3_.refs_1_, f32[16,512]{1,0:T(8,128)} %get-tuple-element.161.refs_2_, ...), custom_call_target="tpu_custom_call" | custom-call | flops 2000000000 | bytes 1048576 | tf_op jit(solution)/shard_map/pallas_call | solution.py:1084
  125.7 5.6 %shard_map.282 = (bf16[2,128,1024]{2,1,0:T(8,128)(2,1)}, bf16[2,128,1024]{2,1,0:T(8,128)(2,1)}) custom-call(s32[12]{0:T(128)} %stack.66.place_ref, bf16[512,512]{1,0:T(8,128)(2,1)} %get-tuple-element.120.refs_0_, bf16[512,512]{1,0:T(8,128)(2,1)} %get-tuple-element.176.refs_1_.refs_0_, bf16[512,256]{1,0:T(8,128)(2,1)} %get-tuple-element.153.refs_2_, ...), custom_call_target="tpu_custom_call" | custom-call | flops 6600000000 | bytes 1048576 | tf_op jit(solution)/shard_map/pallas_call | solution.py:703
  134.5 3.2 %shard_map.284 = (bf16[176,512]{1,0:T(8,128)(2,1)}, bf16[176,512]{1,0:T(8,128)(2,1)}) custom-call(s32[12]{0:T(128)} %stack.66.place_ref, bf16[512,512]{1,0:T(8,128)(2,1)} %get-tuple-element.176.refs_1_.refs_0_, bf16[16,512]{1,0:T(8,128)(2,1)} %get-tuple-element.154.refs_3_.refs_1_, f32[16,512]{1,0:T(8,128)} %get-tuple-element.161.refs_2_, ...), custom_call_target="tpu_custom_call" | custom-call | flops 2000000000 | bytes 1048576 | tf_op jit(solution)/shard_map/pallas_call | solution.py:1084
  137.7 1.7 collective-permute-start.37
  139.8 3.5 %all-to-all-start = ((bf16[4,128,1024]{2,1,0:T(8,128)(2,1)}), bf16[4,128,1024]{2,1,0:T(8,128)(2,1)S(1)}, u32[]{:S(2)}, u32[]{:S(2)}) async-start(bf16[4,128,1024]{2,1,0:T(8,128)(2,1)} %bitcast.19), calls=%async_computation | async-start | bytes 2097152 | tf_op jit(solution)/shard_map/all_to_all | solution.py:782
  145.2 2.0 %collective-permute-start.35 = (bf16[128,1024]{1,0:T(8,128)(2,1)}, bf16[128,1024]{1,0:T(8,128)(2,1)S(1)}, u32[]{:S(2)}, u32[]{:S(2)}) collective-permute-start(bf16[128,1024]{1,0:T(8,128)(2,1)} %fusion.6), channel_id=1, source_target_pairs={{0,2},{1,3},{2,0},{3,1},{4,6},{5,7},{6,4},{7,5},{8,10},{9,11},{10,... | collective-permute-start | bytes 786440 | tf_op jit(solution)/shard_map/ppermute | solution.py:787
  149.4 3.2 %shard_map.285 = (bf16[176,512]{1,0:T(8,128)(2,1)}, bf16[176,512]{1,0:T(8,128)(2,1)}) custom-call(s32[12]{0:T(128)} %stack.66.place_ref, bf16[512,512]{1,0:T(8,128)(2,1)} %get-tuple-element.176.refs_1_.refs_0_, bf16[16,512]{1,0:T(8,128)(2,1)} %get-tuple-element.154.refs_3_.refs_1_, f32[16,512]{1,0:T(8,128)} %get-tuple-element.161.refs_2_, ...), custom_call_target="tpu_custom_call" | custom-call | flops 2000000000 | bytes 1048576 | tf_op jit(solution)/shard_map/pallas_call | solution.py:1084
  152.7 1.7 collective-permute-start.39
  154.7 8.7 %collective-permute-done.35 = bf16[128,1024]{1,0:T(8,128)(2,1)S(1)} collective-permute-done((bf16[128,1024]{1,0:T(8,128)(2,1)}, bf16[128,1024]{1,0:T(8,128)(2,1)S(1)}, u32[]{:S(2)}, u32[]{:S(2)}) %collective-permute-start.35) | collective-permute-done | bytes 262176 | tf_op jit(solution)/shard_map/ppermute | solution.py:787
  164.9 3.3 %shard_map.286 = (bf16[176,512]{1,0:T(8,128)(2,1)}, f32[176,512]{1,0:T(8,128)}) custom-call(s32[12]{0:T(128)} %stack.66.place_ref, bf16[512,512]{1,0:T(8,128)(2,1)} %get-tuple-element.176.refs_1_.refs_0_, bf16[16,512]{1,0:T(8,128)(2,1)} %get-tuple-element.154.refs_3_.refs_1_, f32[16,512]{1,0:T(8,128)} %get-tuple-element.161.refs_2_, ...), custom_call_target="tpu_custom_call" | custom-call | flops 2000000000 | bytes 1048576 | tf_op jit(solution)/shard_map/pallas_call | solution.py:1084
  168.2 1.7 collective-permute-start.41
  171.1 3.5 %collective-permute-done.41 = bf16[176,512]{1,0:T(8,128)(2,1)S(1)} collective-permute-done((bf16[176,512]{1,0:T(8,128)(2,1)}, bf16[176,512]{1,0:T(8,128)(2,1)S(1)}, u32[]{:S(2)}, u32[]{:S(2)}) %collective-permute-start.41) | collective-permute-done | bytes 180256 | tf_op jit(solution)/shard_map/ppermute | solution.py:738
  (207 shorter events, 57.2 us)
Async XLA Ops:
  8.0 8.8 %collective-permute-start.6 = (bf16[256,512]{1,0:T(8,128)(2,1)}, bf16[256,512]{1,0:T(8,128)(2,1)S(1)}, u32[]{:S(2)}, u32[]{:S(2)}) collective-permute-start(bf16[256,512]{1,0:T(8,128)(2,1)} %shard_map.272.refs_4_), channel_id=1, source_target_pairs={{0,8},{8,16},{16,24},{24,28},{28,20},{20,12},{12,4},{4,0},{1,9},{9... | collective-permute-start | bytes 786440 | tf_op jit(solution)/shard_map/ppermute | solution.py:738
  9.8 8.6 %collective-permute-start.7 = (bf16[256,512]{1,0:T(8,128)(2,1)}, bf16[256,512]{1,0:T(8,128)(2,1)}, u32[]{:S(2)}, u32[]{:S(2)}) collective-permute-start(bf16[256,512]{1,0:T(8,128)(2,1)} %shard_map.272.refs_4_), channel_id=1, source_target_pairs={{0,4},{8,0},{16,8},{24,16},{28,24},{20,28},{12,20},{4,12},{1,5},{9... | collective-permute-start | bytes 786440 | tf_op jit(solution)/shard_map/ppermute | solution.py:738
  10.1 18.8 %collective-permute-start.4 = (bf16[256,1024]{1,0:T(8,128)(2,1)S(1)}, bf16[256,1024]{1,0:T(8,128)(2,1)S(1)}, u32[]{:S(2)}, u32[]{:S(2)}) collective-permute-start(bf16[256,1024]{1,0:T(8,128)(2,1)S(1)} %pad_maximum_fusion.refs_0_), channel_id=1, source_target_pairs={{0,2},{1,3},{2,0},{3,1},{4,6},{5,7},{6,4},{7,5},{8,10},{9,11},{10,... | collective-permute-start | bytes 1572872 | tf_op jit(solution)/shard_map/ppermute | solution.py:787
  18.4 8.4 %collective-permute-start.13 = (bf16[208,512]{1,0:T(8,128)(2,1)}, bf16[208,512]{1,0:T(8,128)(2,1)S(1)}, u32[]{:S(2)}, u32[]{:S(2)}) collective-permute-start(bf16[208,512]{1,0:T(8,128)(2,1)} %shard_map.273.refs_4_), channel_id=1, source_target_pairs={{0,8},{8,16},{16,24},{24,28},{28,20},{20,12},{12,4},{4,0},{1,9},{9... | collective-permute-start | bytes 638984 | tf_op jit(solution)/shard_map/ppermute | solution.py:738
  20.0 8.4 %collective-permute-start.14 = (bf16[208,512]{1,0:T(8,128)(2,1)}, bf16[208,512]{1,0:T(8,128)(2,1)S(1)}, u32[]{:S(2)}, u32[]{:S(2)}) collective-permute-start(bf16[208,512]{1,0:T(8,128)(2,1)} %shard_map.273.refs_4_), channel_id=1, source_target_pairs={{0,4},{8,0},{16,8},{24,16},{28,24},{20,28},{12,20},{4,12},{1,5},{9... | collective-permute-start | bytes 638984 | tf_op jit(solution)/shard_map/ppermute | solution.py:738
  20.4 12.1 %collective-permute-start.8 = (bf16[256,512]{1,0:T(8,128)(2,1)S(1)}, bf16[256,512]{1,0:T(8,128)(2,1)}, u32[]{:S(2)}, u32[]{:S(2)}) collective-permute-start(bf16[256,512]{1,0:T(8,128)(2,1)S(1)} %collective-permute-done.6.refs_5_), channel_id=1, source_target_pairs={{0,8},{8,16},{16,24},{24,28},{28,20},{20,12},{12,4},{4,0},{1,9},{9... | collective-permute-start | bytes 786440 | tf_op jit(solution)/shard_map/ppermute | solution.py:738
  26.8 8.4 %collective-permute-start.15 = (bf16[208,512]{1,0:T(8,128)(2,1)S(1)}, bf16[208,512]{1,0:T(8,128)(2,1)S(1)}, u32[]{:S(2)}, u32[]{:S(2)}) collective-permute-start(bf16[208,512]{1,0:T(8,128)(2,1)S(1)} %collective-permute-done.13.refs_5_), channel_id=1, source_target_pairs={{0,8},{8,16},{16,24},{24,28},{28,20},{20,12},{12,4},{4,0},{1,9},{9... | collective-permute-start | bytes 638984 | tf_op jit(solution)/shard_map/ppermute | solution.py:738
  28.4 19.0 %collective-permute-start.3 = (bf16[256,1024]{1,0:T(8,128)(2,1)S(1)}, bf16[256,1024]{1,0:T(8,128)(2,1)S(1)}, u32[]{:S(2)}, u32[]{:S(2)}) collective-permute-start(bf16[256,1024]{1,0:T(8,128)(2,1)S(1)} %pad_maximum_fusion.refs_0_), channel_id=1, source_target_pairs={{0,1},{1,0},{2,3},{3,2},{4,5},{5,4},{6,7},{7,6},{8,9},{9,8},{10,11... | collective-permute-start | bytes 1572872 | tf_op jit(solution)/shard_map/ppermute | solution.py:787
  28.4 9.5 %collective-permute-start.9 = (bf16[256,512]{1,0:T(8,128)(2,1)}, bf16[256,512]{1,0:T(8,128)(2,1)}, u32[]{:S(2)}, u32[]{:S(2)}) collective-permute-start(bf16[256,512]{1,0:T(8,128)(2,1)} %collective-permute-done.7.refs_6_), channel_id=1, source_target_pairs={{0,4},{8,0},{16,8},{24,16},{28,24},{20,28},{12,20},{4,12},{1,5},{9... | collective-permute-start | bytes 786440 | tf_op jit(solution)/shard_map/ppermute | solution.py:738
  28.9 20.6 %collective-permute-start.5 = (bf16[256,1024]{1,0:T(8,128)(2,1)S(1)}, bf16[256,1024]{1,0:T(8,128)(2,1)S(1)}, u32[]{:S(2)}, u32[]{:S(2)}) collective-permute-start(bf16[256,1024]{1,0:T(8,128)(2,1)S(1)} %collective-permute-done.4.refs_2_), channel_id=1, source_target_pairs={{0,1},{1,0},{2,3},{3,2},{4,5},{5,4},{6,7},{7,6},{8,9},{9,8},{10,11... | collective-permute-start | bytes 1572872 | tf_op jit(solution)/shard_map/ppermute | solution.py:787
  32.5 9.5 %collective-permute-start.16 = (bf16[208,512]{1,0:T(8,128)(2,1)S(1)}, bf16[208,512]{1,0:T(8,128)(2,1)}, u32[]{:S(2)}, u32[]{:S(2)}) collective-permute-start(bf16[208,512]{1,0:T(8,128)(2,1)S(1)} %collective-permute-done.14.refs_6_), channel_id=1, source_target_pairs={{0,4},{8,0},{16,8},{24,16},{28,24},{20,28},{12,20},{4,12},{1,5},{9... | collective-permute-start | bytes 638984 | tf_op jit(solution)/shard_map/ppermute | solution.py:738
  37.9 10.1 %collective-permute-start.10 = (bf16[256,512]{1,0:T(8,128)(2,1)}, bf16[256,512]{1,0:T(8,128)(2,1)}, u32[]{:S(2)}, u32[]{:S(2)}) collective-permute-start(bf16[256,512]{1,0:T(8,128)(2,1)} %collective-permute-done.8.refs_7_), channel_id=1, source_target_pairs={{0,8},{8,16},{16,24},{24,28},{28,20},{20,12},{12,4},{4,0},{1,9},{9... | collective-permute-start | bytes 786440 | tf_op jit(solution)/shard_map/ppermute | solution.py:738
  42.4 10.0 %collective-permute-start.19 = (bf16[208,512]{1,0:T(8,128)(2,1)}, bf16[208,512]{1,0:T(8,128)(2,1)}, u32[]{:S(2)}, u32[]{:S(2)}) collective-permute-start(bf16[208,512]{1,0:T(8,128)(2,1)} %collective-permute-done.17.refs_9_), channel_id=1, source_target_pairs={{0,8},{8,16},{16,24},{24,28},{28,20},{20,12},{12,4},{4,0},{1,9},{9... | collective-permute-start | bytes 638984 | tf_op jit(solution)/shard_map/ppermute | solution.py:738
  47.4 16.2 %collective-permute-start.11 = (bf16[256,512]{1,0:T(8,128)(2,1)}, bf16[256,512]{1,0:T(8,128)(2,1)S(1)}, u32[]{:S(2)}, u32[]{:S(2)}) collective-permute-start(bf16[256,512]{1,0:T(8,128)(2,1)} %collective-permute-done.9.refs_8_), channel_id=1, source_target_pairs={{0,4},{8,0},{16,8},{24,16},{28,24},{20,28},{12,20},{4,12},{1,5},{9... | collective-permute-start | bytes 786440 | tf_op jit(solution)/shard_map/ppermute | solution.py:738
  47.9 15.7 %collective-permute-start.12 = (bf16[256,512]{1,0:T(8,128)(2,1)}, bf16[256,512]{1,0:T(8,128)(2,1)S(1)}, u32[]{:S(2)}, u32[]{:S(2)}) collective-permute-start(bf16[256,512]{1,0:T(8,128)(2,1)} %collective-permute-done.10.refs_9_), channel_id=1, source_target_pairs={{0,8},{8,16},{16,24},{24,28},{28,20},{20,12},{12,4},{4,0},{1,9},{9... | collective-permute-start | bytes 786440 | tf_op jit(solution)/shard_map/ppermute | solution.py:738
  85.4 8.7 %collective-permute-start.24 = (bf16[256,512]{1,0:T(8,128)(2,1)}, bf16[256,512]{1,0:T(8,128)(2,1)S(1)}, u32[]{:S(2)}, u32[]{:S(2)}) collective-permute-start(bf16[256,512]{1,0:T(8,128)(2,1)} %get-tuple-element.129), channel_id=1, source_target_pairs={{0,4},{8,0},{16,8},{24,16},{28,24},{20,28},{12,20},{4,12},{1,5},{9... | collective-permute-start | bytes 786440 | tf_op jit(solution)/shard_map/ppermute | solution.py:738
  86.1 8.5 %collective-permute-start.23 = (bf16[256,512]{1,0:T(8,128)(2,1)}, bf16[256,512]{1,0:T(8,128)(2,1)S(1)}, u32[]{:S(2)}, u32[]{:S(2)}) collective-permute-start(bf16[256,512]{1,0:T(8,128)(2,1)} %get-tuple-element.127), channel_id=1, source_target_pairs={{0,8},{8,16},{16,24},{24,28},{28,20},{20,12},{12,4},{4,0},{1,9},{9... | collective-permute-start | bytes 786440 | tf_op jit(solution)/shard_map/ppermute | solution.py:738
  94.7 8.6 %collective-permute-start.26 = (bf16[256,512]{1,0:T(8,128)(2,1)S(1)}, bf16[256,512]{1,0:T(8,128)(2,1)S(1)}, u32[]{:S(2)}, u32[]{:S(2)}) collective-permute-start(bf16[256,512]{1,0:T(8,128)(2,1)S(1)} %add_convert_fusion.4), channel_id=1, source_target_pairs={{0,4},{8,0},{16,8},{24,16},{28,24},{20,28},{12,20},{4,12},{1,5},{9... | collective-permute-start | bytes 786440 | tf_op jit(solution)/shard_map/ppermute | solution.py:738
  103.5 9.4 %collective-permute-start.27 = (bf16[256,512]{1,0:T(8,128)(2,1)S(1)}, bf16[256,512]{1,0:T(8,128)(2,1)S(1)}, u32[]{:S(2)}, u32[]{:S(2)}) collective-permute-start(bf16[256,512]{1,0:T(8,128)(2,1)S(1)} %add_convert_fusion.3), channel_id=1, source_target_pairs={{0,8},{8,16},{16,24},{24,28},{28,20},{20,12},{12,4},{4,0},{1,9},{9... | collective-permute-start | bytes 786440 | tf_op jit(solution)/shard_map/ppermute | solution.py:738
  104.8 8.2 %collective-permute-start.28 = (bf16[256,512]{1,0:T(8,128)(2,1)S(1)}, bf16[256,512]{1,0:T(8,128)(2,1)S(1)}, u32[]{:S(2)}, u32[]{:S(2)}) collective-permute-start(bf16[256,512]{1,0:T(8,128)(2,1)S(1)} %add_convert_fusion.2), channel_id=1, source_target_pairs={{0,4},{8,0},{16,8},{24,16},{28,24},{20,28},{12,20},{4,12},{1,5},{9... | collective-permute-start | bytes 786440 | tf_op jit(solution)/shard_map/ppermute | solution.py:738
  111.1 7.6 %collective-permute-start.30 = (bf16[272,256]{1,0:T(8,128)(2,1)}, bf16[272,256]{1,0:T(8,128)(2,1)S(1)}, u32[]{:S(2)}, u32[]{:S(2)}) collective-permute-start(bf16[272,256]{1,0:T(8,128)(2,1)} %get-tuple-element.164), channel_id=1, source_target_pairs={{0,2},{1,3},{2,0},{3,1},{4,6},{5,7},{6,4},{7,5},{8,10},{9,11},{10,... | collective-permute-start | bytes 417800 | tf_op jit(solution)/shard_map/ppermute | solution.py:787
  111.6 8.3 %collective-permute-start.31 = (bf16[272,256]{1,0:T(8,128)(2,1)}, bf16[272,256]{1,0:T(8,128)(2,1)S(1)}, u32[]{:S(2)}, u32[]{:S(2)}) collective-permute-start(bf16[272,256]{1,0:T(8,128)(2,1)} %get-tuple-element.165), channel_id=1, source_target_pairs={{0,3},{1,2},{2,1},{3,0},{4,7},{5,6},{6,5},{7,4},{8,11},{9,10},{10,... | collective-permute-start | bytes 417800 | tf_op jit(solution)/shard_map/ppermute | solution.py:787
  123.6 9.6 %collective-permute-start.32 = (bf16[176,512]{1,0:T(8,128)(2,1)}, bf16[176,512]{1,0:T(8,128)(2,1)S(1)}, u32[]{:S(2)}, u32[]{:S(2)}) collective-permute-start(bf16[176,512]{1,0:T(8,128)(2,1)} %get-tuple-element.166), channel_id=1, source_target_pairs={{0,8},{8,16},{16,24},{24,28},{28,20},{20,12},{12,4},{4,0},{1,9},{9... | collective-permute-start | bytes 540680 | tf_op jit(solution)/shard_map/ppermute | solution.py:738
  124.8 8.4 %collective-permute-start.33 = (bf16[176,512]{1,0:T(8,128)(2,1)}, bf16[176,512]{1,0:T(8,128)(2,1)S(1)}, u32[]{:S(2)}, u32[]{:S(2)}) collective-permute-start(bf16[176,512]{1,0:T(8,128)(2,1)} %get-tuple-element.167), channel_id=1, source_target_pairs={{0,4},{8,0},{16,8},{24,16},{28,24},{20,28},{12,20},{4,12},{1,5},{9... | collective-permute-start | bytes 540680 | tf_op jit(solution)/shard_map/ppermute | solution.py:738
  131.3 13.2 %collective-permute-start.34 = (bf16[2,128,1024]{2,1,0:T(8,128)(2,1)}, bf16[2,128,1024]{2,1,0:T(8,128)(2,1)S(1)}, u32[]{:S(2)}, u32[]{:S(2)}) collective-permute-start(bf16[2,128,1024]{2,1,0:T(8,128)(2,1)} %get-tuple-element.159), channel_id=1, source_target_pairs={{0,1},{1,0},{2,3},{3,2},{4,5},{5,4},{6,7},{7,6},{8,9},{9,8},{10,11... | collective-permute-start | bytes 1572872 | tf_op jit(solution)/shard_map/ppermute | solution.py:787
  131.3 12.0 %collective-permute-start.36 = (bf16[256,512]{1,0:T(8,128)(2,1)S(1)}, bf16[256,512]{1,0:T(8,128)(2,1)}, u32[]{:S(2)}, u32[]{:S(2)}) collective-permute-start(bf16[256,512]{1,0:T(8,128)(2,1)S(1)} %add_convert_fusion.1), channel_id=1, source_target_pairs={{0,8},{8,16},{16,24},{24,28},{28,20},{20,12},{12,4},{4,0},{1,9},{9... | collective-permute-start | bytes 786440 | tf_op jit(solution)/shard_map/ppermute | solution.py:738
  137.7 11.0 %collective-permute-start.37 = (bf16[176,512]{1,0:T(8,128)(2,1)}, bf16[176,512]{1,0:T(8,128)(2,1)S(1)}, u32[]{:S(2)}, u32[]{:S(2)}) collective-permute-start(bf16[176,512]{1,0:T(8,128)(2,1)} %get-tuple-element.168), channel_id=1, source_target_pairs={{0,8},{8,16},{16,24},{24,28},{28,20},{20,12},{12,4},{4,0},{1,9},{9... | collective-permute-start | bytes 540680 | tf_op jit(solution)/shard_map/ppermute | solution.py:738
  139.4 9.3 %collective-permute-start.38 = (bf16[176,512]{1,0:T(8,128)(2,1)}, bf16[176,512]{1,0:T(8,128)(2,1)}, u32[]{:S(2)}, u32[]{:S(2)}) collective-permute-start(bf16[176,512]{1,0:T(8,128)(2,1)} %get-tuple-element.169), channel_id=1, source_target_pairs={{0,4},{8,0},{16,8},{24,16},{28,24},{20,28},{12,20},{4,12},{1,5},{9... | collective-permute-start | bytes 540680 | tf_op jit(solution)/shard_map/ppermute | solution.py:738
  139.8 24.3 %all-to-all-start = ((bf16[4,128,1024]{2,1,0:T(8,128)(2,1)}), bf16[4,128,1024]{2,1,0:T(8,128)(2,1)S(1)}, u32[]{:S(2)}, u32[]{:S(2)}) async-start(bf16[4,128,1024]{2,1,0:T(8,128)(2,1)} %bitcast.19), calls=%async_computation | async-start | bytes 2097152 | tf_op jit(solution)/shard_map/all_to_all | solution.py:782
  145.2 18.1 %collective-permute-start.35 = (bf16[128,1024]{1,0:T(8,128)(2,1)}, bf16[128,1024]{1,0:T(8,128)(2,1)S(1)}, u32[]{:S(2)}, u32[]{:S(2)}) collective-permute-start(bf16[128,1024]{1,0:T(8,128)(2,1)} %fusion.6), channel_id=1, source_target_pairs={{0,2},{1,3},{2,0},{3,1},{4,6},{5,7},{6,4},{7,5},{8,10},{9,11},{10,... | collective-permute-start | bytes 786440 | tf_op jit(solution)/shard_map/ppermute | solution.py:787
  152.7 11.6 %collective-permute-start.39 = (bf16[176,512]{1,0:T(8,128)(2,1)}, bf16[176,512]{1,0:T(8,128)(2,1)S(1)}, u32[]{:S(2)}, u32[]{:S(2)}) collective-permute-start(bf16[176,512]{1,0:T(8,128)(2,1)} %get-tuple-element.177), channel_id=1, source_target_pairs={{0,8},{8,16},{16,24},{24,28},{28,20},{20,12},{12,4},{4,0},{1,9},{9... | collective-permute-start | bytes 540680 | tf_op jit(solution)/shard_map/ppermute | solution.py:738
  154.3 9.9 %collective-permute-start.40 = (bf16[176,512]{1,0:T(8,128)(2,1)}, bf16[176,512]{1,0:T(8,128)(2,1)}, u32[]{:S(2)}, u32[]{:S(2)}) collective-permute-start(bf16[176,512]{1,0:T(8,128)(2,1)} %get-tuple-element.178), channel_id=1, source_target_pairs={{0,4},{8,0},{16,8},{24,16},{28,24},{20,28},{12,20},{4,12},{1,5},{9... | collective-permute-start | bytes 540680 | tf_op jit(solution)/shard_map/ppermute | solution.py:738
  (58 other events, 384.8 us)

commit v9 on v8

--- a/solution.py
+++ b/solution.py
@@ -1123,7 +1123,7 @@
     gain_full = small_full[: depth // states].reshape(1, depth)
 
     if fast:
-        far = tensor_swap(far_half, 2)
+        far = ordered(inner_out, tensor_swap(far_half, 2))[1]
         grad_local = keep_rows[0].astype(f32) + near[0].astype(f32) + far.astype(f32)
         gate_grad, output_grad = gate_out[:tall], gate_out[tall:].T
         inner_grad = inner_out[:tall]

time: 183 us -> 181 us (0.989)
    ppermute x17, waiting for transfers between devices: 13 us -> 4.32 us  [tensor_swap(): return lax.ppermute(value, 'tensor', [(i, i ^ bit) for i in range(4)])]
    ppermute x28, waiting for transfers between devices: 25.1 us -> 33.3 us  [ring_send(): return lax.ppermute(value, 'dp', pairs)]
    unnamed x92 -> x88, local copies, waits for them, and re-layouts: 7.98 us -> 6.26 us
  transfers between devices with their start and end apart: 46 -> 46, of which waited for: 15 -> 20; matrix products, arithmetic and copies ran while one was open for 7% -> 8% of each run, Pallas kernels for 29% -> 29%
where the time goes in v9:
time: 181 us; the launch traced here: 180 us
  Pallas kernels  76.2 us (42%)
  starting transfers between devices  46.5 us (26%)
  waiting for transfers between devices  37.6 us (21%)
  local copies, waits for them, and re-layouts  11.9 us (7%)
  other arithmetic  6.75 us (4%)
    pallas_call x12, Pallas kernels, call(): pl.pallas_call(kernel, out_shape=[jax.ShapeDtypeStruct(shape, kind) for s...  63.4 us
    ppermute x28, waiting for transfers between devices, ring_send(): return lax.ppermute(value, 'dp', pairs)  33.3 us
    ppermute x28, starting transfers between devices, ring_send(): return lax.ppermute(value, 'dp', pairs)  30.3 us
    pallas_call x4, Pallas kernels, chunk_pair(): pl.pallas_call(functools.partial(chunk_kernel, slots, len(got)), grid_spe...  12.8 us
    ppermute x17, starting transfers between devices, tensor_swap(): return lax.ppermute(value, 'tensor', [(i, i ^ bit) for i in range(4)])  12.5 us
    unnamed x88, local copies, waits for them, and re-layouts  6.26 us
    ppermute x17, waiting for transfers between devices, tensor_swap(): return lax.ppermute(value, 'tensor', [(i, i ^ bit) for i in range(4)])  4.32 us
    all_to_all x1, starting transfers between devices, tensor_sum(): parts = lax.all_to_all(parts, 'tensor', 0, 0, tiled=True)  3.65 us
  transfers between devices with their start and end apart: 46, of which 20 were waited for; matrix products, arithmetic and copies ran while one was open for 8% of the time, Pallas kernels for 29%

profile of v9, /device:TPU:0, one launch (start us, length us, event | category | flops | bytes accessed | tf_op | source)
XLA Modules:
  0.0 180.0 jit_solution(5355690461255148640)
XLA Ops:
  3.3 2.6 %collective-permute-start.1 = (bf16[48,256]{1,0:T(8,128)(2,1)}, bf16[48,256]{1,0:T(8,128)(2,1)S(1)}, u32[]{:S(2)}, u32[]{:S(2)}) collective-permute-start(bf16[48,256]{1,0:T(8,128)(2,1)} %shard_map.271.refs_0_), channel_id=1, source_target_pairs={{0,2},{1,3},{2,0},{3,1},{4,6},{5,7},{6,4},{7,5},{8,10},{9,11},{10,... | collective-permute-start | bytes 73736 | tf_op jit(solution)/shard_map/ppermute | solution.py:787
  5.9 2.0 %shard_map.272.refs_4_ = bf16[256,512]{1,0:T(8,128)(2,1)} custom-call(bf16[128,2,512]{2,1,0:T(2,128)(2,1)} %input_ref.3, bf16[512,128]{1,0:T(8,128)(2,1)} %out_ref), custom_call_target="tpu_custom_call" | custom-call | flops 2200000000 | bytes 1048576 | tf_op jit(solution)/shard_map/pallas_call | solution.py:703
  8.0 1.8 %collective-permute-start.6 = (bf16[256,512]{1,0:T(8,128)(2,1)}, bf16[256,512]{1,0:T(8,128)(2,1)S(1)}, u32[]{:S(2)}, u32[]{:S(2)}) collective-permute-start(bf16[256,512]{1,0:T(8,128)(2,1)} %shard_map.272.refs_4_), channel_id=1, source_target_pairs={{0,8},{8,16},{16,24},{24,28},{28,20},{20,12},{12,4},{4,0},{1,9},{9... | collective-permute-start | bytes 786440 | tf_op jit(solution)/shard_map/ppermute | solution.py:738
  10.1 1.8 collective-permute-start.4
  12.5 2.0 %shard_map.273.refs_4_ = bf16[208,512]{1,0:T(8,128)(2,1)} custom-call(bf16[128,2,512]{2,1,0:T(2,128)(2,1)} %input_ref.3, bf16[16,128]{1,0:T(8,128)(2,1)} %pad.4.step_ref, bf16[48,256]{1,0:T(8,128)(2,1)} %shard_map.271.refs_0_, bf16[48,256]{1,0:T(8,128)(2,1)} %copy-done.36, bf16[48,256]{1,0:T(8,128)(2,1)} %copy-done.37, bf16[48,256]{1,0:T(8,128)(2,1)} %copy-done.38), custom_call_target="tpu_custom_call" | custom-call | flops 1100000000 | bytes 1048576 | tf_op jit(solution)/shard_map/pallas_call | solution.py:703
  14.5 2.2 %collective-permute-done.6.refs_5_ = bf16[256,512]{1,0:T(8,128)(2,1)S(1)} collective-permute-done((bf16[256,512]{1,0:T(8,128)(2,1)}, bf16[256,512]{1,0:T(8,128)(2,1)S(1)}, u32[]{:S(2)}, u32[]{:S(2)}) %collective-permute-start.6) | collective-permute-done | bytes 262176 | tf_op jit(solution)/shard_map/ppermute | solution.py:738
  21.9 4.8 %collective-permute-done.13.refs_5_ = bf16[208,512]{1,0:T(8,128)(2,1)S(1)} collective-permute-done((bf16[208,512]{1,0:T(8,128)(2,1)}, bf16[208,512]{1,0:T(8,128)(2,1)S(1)}, u32[]{:S(2)}, u32[]{:S(2)}) %collective-permute-start.13) | collective-permute-done | bytes 213024 | tf_op jit(solution)/shard_map/ppermute | solution.py:738
  29.0 3.4 %collective-permute-done.8.refs_7_ = bf16[256,512]{1,0:T(8,128)(2,1)} collective-permute-done((bf16[256,512]{1,0:T(8,128)(2,1)S(1)}, bf16[256,512]{1,0:T(8,128)(2,1)}, u32[]{:S(2)}, u32[]{:S(2)}) %collective-permute-start.8) | collective-permute-done | bytes 262176 | tf_op jit(solution)/shard_map/ppermute | solution.py:738
  32.7 2.3 %collective-permute-done.15.refs_7_ = bf16[208,512]{1,0:T(8,128)(2,1)S(1)} collective-permute-done((bf16[208,512]{1,0:T(8,128)(2,1)S(1)}, bf16[208,512]{1,0:T(8,128)(2,1)S(1)}, u32[]{:S(2)}, u32[]{:S(2)}) %collective-permute-start.15) | collective-permute-done | bytes 213024 | tf_op jit(solution)/shard_map/ppermute | solution.py:738
  39.1 2.5 %collective-permute-done.16.refs_8_ = bf16[208,512]{1,0:T(8,128)(2,1)} collective-permute-done((bf16[208,512]{1,0:T(8,128)(2,1)S(1)}, bf16[208,512]{1,0:T(8,128)(2,1)}, u32[]{:S(2)}, u32[]{:S(2)}) %collective-permute-start.16) | collective-permute-done | bytes 213024 | tf_op jit(solution)/shard_map/ppermute | solution.py:738
  45.7 1.6 shard_map.274
  49.6 3.0 %collective-permute-done.19.refs_11_ = bf16[208,512]{1,0:T(8,128)(2,1)} collective-permute-done((bf16[208,512]{1,0:T(8,128)(2,1)}, bf16[208,512]{1,0:T(8,128)(2,1)}, u32[]{:S(2)}, u32[]{:S(2)}) %collective-permute-start.19) | collective-permute-done | bytes 213024 | tf_op jit(solution)/shard_map/ppermute | solution.py:738
  52.5 11.2 %shard_map.275 = (bf16[512,1024]{1,0:T(8,128)(2,1)}, bf16[1024,512]{1,0:T(8,128)(2,1)}, bf16[1024,512]{1,0:T(8,128)(2,1)}, bf16[1024,256]{1,0:T(8,128)(2,1)}, bf...) custom-call(s32[12]{0:T(128)} %stack.66.place_ref, ...), custom_call_target="tpu_custom_call" | custom-call | flops 12099999744 | bytes 1048576 | tf_op jit(solution)/shard_map/pallas_call | solution.py:703
  64.5 7.3 %shard_map.276 = (bf16[512,1024]{1,0:T(8,128)(2,1)}, bf16[1024,512]{1,0:T(8,128)(2,1)}, bf16[1024,512]{1,0:T(8,128)(2,1)}, f32[512,512]{1,0:T(8,128)}, f32[512,512]{1,0:T(8,128)}, /*index=5*/f32[8,512]{1,0:T(8,128)}) custom-call(s32[12]{0:T(128)} %stack.66.place_ref, s32[1,4]{1,0:T(1,128)} %lengths_ref.13, bf16[256,1024]{1,0:T(8,128)(2,1)} %copy-done.6, ...), custom_call_target="tpu_custom_call" | custom-call | flops 5500000256 | bytes 1048576 | tf_op jit(solution)/shard_map/pallas_call | solution.py:703
  73.7 2.1 %collective-permute-done.21.refs_2_ = f32[8,512]{1,0:T(8,128)S(1)} collective-permute-done((f32[8,512]{1,0:T(8,128)}, f32[8,512]{1,0:T(8,128)S(1)}, u32[]{:S(2)}, u32[]{:S(2)}) %collective-permute-start.21) | collective-permute-done | bytes 16416 | tf_op jit(solution)/shard_map/ppermute | solution.py:787
  77.4 8.1 %shard_map.277 = (bf16[256,512]{1,0:T(8,128)(2,1)}, bf16[256,512]{1,0:T(8,128)(2,1)}, bf16[256,512]{1,0:T(8,128)(2,1)}, bf16[256,512]{1,0:T(8,128)(2,1)}, bf16[2...) custom-call(s32[12]{0:T(128)} %stack.66.place_ref, ...), custom_call_target="tpu_custom_call" | custom-call | flops 9900000256 | bytes 1048576 | tf_op jit(solution)/shard_map/pallas_call | solution.py:703
  87.6 6.5 %shard_map.278 = (f32[512,256]{1,0:T(8,128)}, f32[512,256]{1,0:T(8,128)}, f32[16,512]{1,0:T(8,128)}, f32[8,256]{1,0:T(8,128)}) custom-call(s32[1,4]{1,0:T(1,128)} %lengths_ref.13, f32[512,512]{1,0:T(8,128)} %get-tuple-element.132.refs_0_, f32[512,512]{1,0:T(8,128)} %get-tuple-element.123.refs_1_, f32[512,256]{1,0:T(8,128)} %get-tuple-element.124.refs_2_, ...), custom_call_target="tpu_custom_call" | custom-call | flops 6600000000 | bytes 1048576 | tf_op jit(solution)/shard_map/pallas_call | solution.py:703
  94.8 1.8 collective-permute-start.26
  96.9 6.5 %shard_map.279 = (f32[512,256]{1,0:T(8,128)}, f32[512,256]{1,0:T(8,128)}, f32[16,512]{1,0:T(8,128)}, f32[8,256]{1,0:T(8,128)}) custom-call(s32[1,4]{1,0:T(1,128)} %lengths_ref.13, f32[512,512]{1,0:T(8,128)} %get-tuple-element.132.refs_0_, f32[512,512]{1,0:T(8,128)} %get-tuple-element.123.refs_1_, f32[512,256]{1,0:T(8,128)} %get-tuple-element.124.refs_2_, ...), custom_call_target="tpu_custom_call" | custom-call | flops 6600000000 | bytes 1048576 | tf_op jit(solution)/shard_map/pallas_call | solution.py:703
  105.7 5.4 %shard_map.281 = (bf16[512,256]{1,0:T(8,128)(2,1)}, bf16[16,512]{1,0:T(8,128)(2,1)}, bf16[272,256]{1,0:T(8,128)(2,1)}, bf16[272,256]{1,0:T(8,128)(2,1)}, bf16[27...) custom-call(s32[12]{0:T(128)} %stack.66.place_ref, s32[1,4]{1,0:T(1,128)} %lengths_ref.13, ...), custom_call_target="tpu_custom_call" | custom-call | flops 4400000000 | bytes 1048576 | tf_op jit(solution)/shard_map/pallas_call | solution.py:703
  113.1 5.6 %shard_map.280 = (bf16[512,512]{1,0:T(8,128)(2,1)}, f32[16,512]{1,0:T(8,128)}) custom-call(s32[1,4]{1,0:T(1,128)} %lengths_ref.13, f32[512,256]{1,0:T(8,128)} %get-tuple-element.127.refs_0_, f32[512,256]{1,0:T(8,128)} %get-tuple-element.133.refs_1_, f32[8,256]{1,0:T(8,128)} %get-tuple-element.134.refs_2_, f32[8,256]{1,0:T(8,128)} %get-tuple-element.135.refs_3_, ...), custom_call_target="tpu_custom_call" | custom-call | flops 6600000000 | bytes 1048576 | tf_op jit(solution)/shard_map/pallas_call | solution.py:703
  120.7 3.1 %shard_map.283 = (bf16[176,512]{1,0:T(8,128)(2,1)}, bf16[176,512]{1,0:T(8,128)(2,1)}) custom-call(s32[12]{0:T(128)} %stack.66.place_ref, bf16[512,512]{1,0:T(8,128)(2,1)} %get-tuple-element.174.refs_1_.refs_0_, bf16[16,512]{1,0:T(8,128)(2,1)} %get-tuple-element.155.refs_3_.refs_1_, f32[16,512]{1,0:T(8,128)} %get-tuple-element.162.refs_2_, ...), custom_call_target="tpu_custom_call" | custom-call | flops 2000000000 | bytes 1048576 | tf_op jit(solution)/shard_map/pallas_call | solution.py:1084
  125.8 5.6 %shard_map.282 = (bf16[2,128,1024]{2,1,0:T(8,128)(2,1)}, bf16[2,128,1024]{2,1,0:T(8,128)(2,1)}) custom-call(s32[12]{0:T(128)} %stack.66.place_ref, bf16[512,512]{1,0:T(8,128)(2,1)} %get-tuple-element.121.refs_0_, bf16[512,512]{1,0:T(8,128)(2,1)} %get-tuple-element.174.refs_1_.refs_0_, bf16[512,256]{1,0:T(8,128)(2,1)} %get-tuple-element.154.refs_2_, ...), custom_call_target="tpu_custom_call" | custom-call | flops 6600000000 | bytes 1048576 | tf_op jit(solution)/shard_map/pallas_call | solution.py:703
  134.0 3.2 %shard_map.284 = (bf16[176,512]{1,0:T(8,128)(2,1)}, bf16[176,512]{1,0:T(8,128)(2,1)}) custom-call(s32[12]{0:T(128)} %stack.66.place_ref, bf16[512,512]{1,0:T(8,128)(2,1)} %get-tuple-element.174.refs_1_.refs_0_, bf16[16,512]{1,0:T(8,128)(2,1)} %get-tuple-element.155.refs_3_.refs_1_, f32[16,512]{1,0:T(8,128)} %get-tuple-element.162.refs_2_, ...), custom_call_target="tpu_custom_call" | custom-call | flops 2000000000 | bytes 1048576 | tf_op jit(solution)/shard_map/pallas_call | solution.py:1084
  137.2 3.7 %all-to-all-start = ((bf16[4,128,1024]{2,1,0:T(8,128)(2,1)}), bf16[4,128,1024]{2,1,0:T(8,128)(2,1)S(1)}, u32[]{:S(2)}, u32[]{:S(2)}) async-start(bf16[4,128,1024]{2,1,0:T(8,128)(2,1)} %bitcast.19), calls=%async_computation | async-start | bytes 2097152 | tf_op jit(solution)/shard_map/all_to_all | solution.py:782
  141.6 1.6 collective-permute-start.35
  143.7 5.1 %collective-permute-done.35.refs_9_ = bf16[176,512]{1,0:T(8,128)(2,1)} collective-permute-done((bf16[176,512]{1,0:T(8,128)(2,1)}, bf16[176,512]{1,0:T(8,128)(2,1)}, u32[]{:S(2)}, u32[]{:S(2)}) %collective-permute-start.35) | collective-permute-done | bytes 180256 | tf_op jit(solution)/shard_map/ppermute | solution.py:738
  149.9 3.2 %shard_map.285 = (bf16[176,512]{1,0:T(8,128)(2,1)}, bf16[176,512]{1,0:T(8,128)(2,1)}) custom-call(s32[12]{0:T(128)} %stack.66.place_ref, bf16[512,512]{1,0:T(8,128)(2,1)} %get-tuple-element.174.refs_1_.refs_0_, bf16[16,512]{1,0:T(8,128)(2,1)} %get-tuple-element.155.refs_3_.refs_1_, f32[16,512]{1,0:T(8,128)} %get-tuple-element.162.refs_2_, ...), custom_call_target="tpu_custom_call" | custom-call | flops 2000000000 | bytes 1048576 | tf_op jit(solution)/shard_map/pallas_call | solution.py:1084
  156.3 3.0 %collective-permute-done.37.refs_9_ = bf16[176,512]{1,0:T(8,128)(2,1)} collective-permute-done((bf16[176,512]{1,0:T(8,128)(2,1)}, bf16[176,512]{1,0:T(8,128)(2,1)}, u32[]{:S(2)}, u32[]{:S(2)}) %collective-permute-start.37) | collective-permute-done | bytes 180256 | tf_op jit(solution)/shard_map/ppermute | solution.py:738
  160.6 3.3 %shard_map.286 = (bf16[176,512]{1,0:T(8,128)(2,1)}, f32[176,512]{1,0:T(8,128)}) custom-call(s32[12]{0:T(128)} %stack.66.place_ref, bf16[512,512]{1,0:T(8,128)(2,1)} %get-tuple-element.174.refs_1_.refs_0_, bf16[16,512]{1,0:T(8,128)(2,1)} %get-tuple-element.155.refs_3_.refs_1_, f32[16,512]{1,0:T(8,128)} %get-tuple-element.162.refs_2_, ...), custom_call_target="tpu_custom_call" | custom-call | flops 2000000000 | bytes 1048576 | tf_op jit(solution)/shard_map/pallas_call | solution.py:1084
  166.9 1.6 collective-permute-start.40
  171.0 1.7 collective-permute-start.43
  (203 shorter events, 59.1 us)
Async XLA Ops:
  8.0 8.8 %collective-permute-start.6 = (bf16[256,512]{1,0:T(8,128)(2,1)}, bf16[256,512]{1,0:T(8,128)(2,1)S(1)}, u32[]{:S(2)}, u32[]{:S(2)}) collective-permute-start(bf16[256,512]{1,0:T(8,128)(2,1)} %shard_map.272.refs_4_), channel_id=1, source_target_pairs={{0,8},{8,16},{16,24},{24,28},{28,20},{20,12},{12,4},{4,0},{1,9},{9... | collective-permute-start | bytes 786440 | tf_op jit(solution)/shard_map/ppermute | solution.py:738
  9.8 8.5 %collective-permute-start.7 = (bf16[256,512]{1,0:T(8,128)(2,1)}, bf16[256,512]{1,0:T(8,128)(2,1)S(1)}, u32[]{:S(2)}, u32[]{:S(2)}) collective-permute-start(bf16[256,512]{1,0:T(8,128)(2,1)} %shard_map.272.refs_4_), channel_id=1, source_target_pairs={{0,4},{8,0},{16,8},{24,16},{28,24},{20,28},{12,20},{4,12},{1,5},{9... | collective-permute-start | bytes 786440 | tf_op jit(solution)/shard_map/ppermute | solution.py:738
  10.1 18.7 %collective-permute-start.4 = (bf16[256,1024]{1,0:T(8,128)(2,1)S(1)}, bf16[256,1024]{1,0:T(8,128)(2,1)S(1)}, u32[]{:S(2)}, u32[]{:S(2)}) collective-permute-start(bf16[256,1024]{1,0:T(8,128)(2,1)S(1)} %pad_maximum_fusion.refs_0_), channel_id=1, source_target_pairs={{0,2},{1,3},{2,0},{3,1},{4,6},{5,7},{6,4},{7,5},{8,10},{9,11},{10,... | collective-permute-start | bytes 1572872 | tf_op jit(solution)/shard_map/ppermute | solution.py:787
  18.3 8.4 %collective-permute-start.13 = (bf16[208,512]{1,0:T(8,128)(2,1)}, bf16[208,512]{1,0:T(8,128)(2,1)S(1)}, u32[]{:S(2)}, u32[]{:S(2)}) collective-permute-start(bf16[208,512]{1,0:T(8,128)(2,1)} %shard_map.273.refs_4_), channel_id=1, source_target_pairs={{0,8},{8,16},{16,24},{24,28},{28,20},{20,12},{12,4},{4,0},{1,9},{9... | collective-permute-start | bytes 638984 | tf_op jit(solution)/shard_map/ppermute | solution.py:738
  19.9 8.4 %collective-permute-start.14 = (bf16[208,512]{1,0:T(8,128)(2,1)}, bf16[208,512]{1,0:T(8,128)(2,1)S(1)}, u32[]{:S(2)}, u32[]{:S(2)}) collective-permute-start(bf16[208,512]{1,0:T(8,128)(2,1)} %shard_map.273.refs_4_), channel_id=1, source_target_pairs={{0,4},{8,0},{16,8},{24,16},{28,24},{20,28},{12,20},{4,12},{1,5},{9... | collective-permute-start | bytes 638984 | tf_op jit(solution)/shard_map/ppermute | solution.py:738
  20.3 12.1 %collective-permute-start.8 = (bf16[256,512]{1,0:T(8,128)(2,1)S(1)}, bf16[256,512]{1,0:T(8,128)(2,1)}, u32[]{:S(2)}, u32[]{:S(2)}) collective-permute-start(bf16[256,512]{1,0:T(8,128)(2,1)S(1)} %collective-permute-done.6.refs_5_), channel_id=1, source_target_pairs={{0,8},{8,16},{16,24},{24,28},{28,20},{20,12},{12,4},{4,0},{1,9},{9... | collective-permute-start | bytes 786440 | tf_op jit(solution)/shard_map/ppermute | solution.py:738
  26.7 8.4 %collective-permute-start.15 = (bf16[208,512]{1,0:T(8,128)(2,1)S(1)}, bf16[208,512]{1,0:T(8,128)(2,1)S(1)}, u32[]{:S(2)}, u32[]{:S(2)}) collective-permute-start(bf16[208,512]{1,0:T(8,128)(2,1)S(1)} %collective-permute-done.13.refs_5_), channel_id=1, source_target_pairs={{0,8},{8,16},{16,24},{24,28},{28,20},{20,12},{12,4},{4,0},{1,9},{9... | collective-permute-start | bytes 638984 | tf_op jit(solution)/shard_map/ppermute | solution.py:738
  28.3 19.1 %collective-permute-start.3 = (bf16[256,1024]{1,0:T(8,128)(2,1)S(1)}, bf16[256,1024]{1,0:T(8,128)(2,1)S(1)}, u32[]{:S(2)}, u32[]{:S(2)}) collective-permute-start(bf16[256,1024]{1,0:T(8,128)(2,1)S(1)} %pad_maximum_fusion.refs_0_), channel_id=1, source_target_pairs={{0,1},{1,0},{2,3},{3,2},{4,5},{5,4},{6,7},{7,6},{8,9},{9,8},{10,11... | collective-permute-start | bytes 1572872 | tf_op jit(solution)/shard_map/ppermute | solution.py:787
  28.3 9.3 %collective-permute-start.9 = (bf16[256,512]{1,0:T(8,128)(2,1)S(1)}, bf16[256,512]{1,0:T(8,128)(2,1)}, u32[]{:S(2)}, u32[]{:S(2)}) collective-permute-start(bf16[256,512]{1,0:T(8,128)(2,1)S(1)} %collective-permute-done.7.refs_6_), channel_id=1, source_target_pairs={{0,4},{8,0},{16,8},{24,16},{28,24},{20,28},{12,20},{4,12},{1,5},{9... | collective-permute-start | bytes 786440 | tf_op jit(solution)/shard_map/ppermute | solution.py:738
  28.8 20.8 %collective-permute-start.5 = (bf16[256,1024]{1,0:T(8,128)(2,1)S(1)}, bf16[256,1024]{1,0:T(8,128)(2,1)S(1)}, u32[]{:S(2)}, u32[]{:S(2)}) collective-permute-start(bf16[256,1024]{1,0:T(8,128)(2,1)S(1)} %collective-permute-done.4.refs_2_), channel_id=1, source_target_pairs={{0,1},{1,0},{2,3},{3,2},{4,5},{5,4},{6,7},{7,6},{8,9},{9,8},{10,11... | collective-permute-start | bytes 1572872 | tf_op jit(solution)/shard_map/ppermute | solution.py:787
  32.4 9.3 %collective-permute-start.16 = (bf16[208,512]{1,0:T(8,128)(2,1)S(1)}, bf16[208,512]{1,0:T(8,128)(2,1)}, u32[]{:S(2)}, u32[]{:S(2)}) collective-permute-start(bf16[208,512]{1,0:T(8,128)(2,1)S(1)} %collective-permute-done.14.refs_6_), channel_id=1, source_target_pairs={{0,4},{8,0},{16,8},{24,16},{28,24},{20,28},{12,20},{4,12},{1,5},{9... | collective-permute-start | bytes 638984 | tf_op jit(solution)/shard_map/ppermute | solution.py:738
  35.0 7.3 %collective-permute-start.17 = (bf16[208,512]{1,0:T(8,128)(2,1)S(1)}, bf16[208,512]{1,0:T(8,128)(2,1)}, u32[]{:S(2)}, u32[]{:S(2)}) collective-permute-start(bf16[208,512]{1,0:T(8,128)(2,1)S(1)} %collective-permute-done.15.refs_7_), channel_id=1, source_target_pairs={{0,8},{8,16},{16,24},{24,28},{28,20},{20,12},{12,4},{4,0},{1,9},{9... | collective-permute-start | bytes 638984 | tf_op jit(solution)/shard_map/ppermute | solution.py:738
  37.5 10.4 %collective-permute-start.10 = (bf16[256,512]{1,0:T(8,128)(2,1)}, bf16[256,512]{1,0:T(8,128)(2,1)}, u32[]{:S(2)}, u32[]{:S(2)}) collective-permute-start(bf16[256,512]{1,0:T(8,128)(2,1)} %collective-permute-done.8.refs_7_), channel_id=1, source_target_pairs={{0,8},{8,16},{16,24},{24,28},{28,20},{20,12},{12,4},{4,0},{1,9},{9... | collective-permute-start | bytes 786440 | tf_op jit(solution)/shard_map/ppermute | solution.py:738
  41.7 7.9 %collective-permute-start.18 = (bf16[208,512]{1,0:T(8,128)(2,1)}, bf16[208,512]{1,0:T(8,128)(2,1)}, u32[]{:S(2)}, u32[]{:S(2)}) collective-permute-start(bf16[208,512]{1,0:T(8,128)(2,1)} %collective-permute-done.16.refs_8_), channel_id=1, source_target_pairs={{0,4},{8,0},{16,8},{24,16},{28,24},{20,28},{12,20},{4,12},{1,5},{9... | collective-permute-start | bytes 638984 | tf_op jit(solution)/shard_map/ppermute | solution.py:738
  42.3 10.2 %collective-permute-start.19 = (bf16[208,512]{1,0:T(8,128)(2,1)}, bf16[208,512]{1,0:T(8,128)(2,1)}, u32[]{:S(2)}, u32[]{:S(2)}) collective-permute-start(bf16[208,512]{1,0:T(8,128)(2,1)} %collective-permute-done.17.refs_9_), channel_id=1, source_target_pairs={{0,8},{8,16},{16,24},{24,28},{28,20},{20,12},{12,4},{4,0},{1,9},{9... | collective-permute-start | bytes 638984 | tf_op jit(solution)/shard_map/ppermute | solution.py:738
  47.4 16.3 %collective-permute-start.11 = (bf16[256,512]{1,0:T(8,128)(2,1)}, bf16[256,512]{1,0:T(8,128)(2,1)S(1)}, u32[]{:S(2)}, u32[]{:S(2)}) collective-permute-start(bf16[256,512]{1,0:T(8,128)(2,1)} %collective-permute-done.9.refs_8_), channel_id=1, source_target_pairs={{0,4},{8,0},{16,8},{24,16},{28,24},{20,28},{12,20},{4,12},{1,5},{9... | collective-permute-start | bytes 786440 | tf_op jit(solution)/shard_map/ppermute | solution.py:738
  48.0 15.8 %collective-permute-start.12 = (bf16[256,512]{1,0:T(8,128)(2,1)}, bf16[256,512]{1,0:T(8,128)(2,1)S(1)}, u32[]{:S(2)}, u32[]{:S(2)}) collective-permute-start(bf16[256,512]{1,0:T(8,128)(2,1)} %collective-permute-done.10.refs_9_), channel_id=1, source_target_pairs={{0,8},{8,16},{16,24},{24,28},{28,20},{20,12},{12,4},{4,0},{1,9},{9... | collective-permute-start | bytes 786440 | tf_op jit(solution)/shard_map/ppermute | solution.py:738
  85.5 8.6 %collective-permute-start.24 = (bf16[256,512]{1,0:T(8,128)(2,1)}, bf16[256,512]{1,0:T(8,128)(2,1)S(1)}, u32[]{:S(2)}, u32[]{:S(2)}) collective-permute-start(bf16[256,512]{1,0:T(8,128)(2,1)} %get-tuple-element.130), channel_id=1, source_target_pairs={{0,4},{8,0},{16,8},{24,16},{28,24},{20,28},{12,20},{4,12},{1,5},{9... | collective-permute-start | bytes 786440 | tf_op jit(solution)/shard_map/ppermute | solution.py:738
  86.3 8.4 %collective-permute-start.23 = (bf16[256,512]{1,0:T(8,128)(2,1)}, bf16[256,512]{1,0:T(8,128)(2,1)S(1)}, u32[]{:S(2)}, u32[]{:S(2)}) collective-permute-start(bf16[256,512]{1,0:T(8,128)(2,1)} %get-tuple-element.128), channel_id=1, source_target_pairs={{0,8},{8,16},{16,24},{24,28},{28,20},{20,12},{12,4},{4,0},{1,9},{9... | collective-permute-start | bytes 786440 | tf_op jit(solution)/shard_map/ppermute | solution.py:738
  94.8 8.6 %collective-permute-start.26 = (bf16[256,512]{1,0:T(8,128)(2,1)S(1)}, bf16[256,512]{1,0:T(8,128)(2,1)S(1)}, u32[]{:S(2)}, u32[]{:S(2)}) collective-permute-start(bf16[256,512]{1,0:T(8,128)(2,1)S(1)} %add_convert_fusion.4), channel_id=1, source_target_pairs={{0,4},{8,0},{16,8},{24,16},{28,24},{20,28},{12,20},{4,12},{1,5},{9... | collective-permute-start | bytes 786440 | tf_op jit(solution)/shard_map/ppermute | solution.py:738
  103.7 9.4 %collective-permute-start.27 = (bf16[256,512]{1,0:T(8,128)(2,1)S(1)}, bf16[256,512]{1,0:T(8,128)(2,1)S(1)}, u32[]{:S(2)}, u32[]{:S(2)}) collective-permute-start(bf16[256,512]{1,0:T(8,128)(2,1)S(1)} %add_convert_fusion.3), channel_id=1, source_target_pairs={{0,8},{8,16},{16,24},{24,28},{28,20},{20,12},{12,4},{4,0},{1,9},{9... | collective-permute-start | bytes 786440 | tf_op jit(solution)/shard_map/ppermute | solution.py:738
  104.9 8.2 %collective-permute-start.28 = (bf16[256,512]{1,0:T(8,128)(2,1)S(1)}, bf16[256,512]{1,0:T(8,128)(2,1)S(1)}, u32[]{:S(2)}, u32[]{:S(2)}) collective-permute-start(bf16[256,512]{1,0:T(8,128)(2,1)S(1)} %add_convert_fusion.2), channel_id=1, source_target_pairs={{0,4},{8,0},{16,8},{24,16},{28,24},{20,28},{12,20},{4,12},{1,5},{9... | collective-permute-start | bytes 786440 | tf_op jit(solution)/shard_map/ppermute | solution.py:738
  111.2 7.6 %collective-permute-start.29 = (bf16[272,256]{1,0:T(8,128)(2,1)}, bf16[272,256]{1,0:T(8,128)(2,1)S(1)}, u32[]{:S(2)}, u32[]{:S(2)}) collective-permute-start(bf16[272,256]{1,0:T(8,128)(2,1)} %get-tuple-element.164), channel_id=1, source_target_pairs={{0,1},{1,0},{2,3},{3,2},{4,5},{5,4},{6,7},{7,6},{8,9},{9,8},{10,11... | collective-permute-start | bytes 417800 | tf_op jit(solution)/shard_map/ppermute | solution.py:787
  111.2 7.6 %collective-permute-start.30 = (bf16[272,256]{1,0:T(8,128)(2,1)}, bf16[272,256]{1,0:T(8,128)(2,1)S(1)}, u32[]{:S(2)}, u32[]{:S(2)}) collective-permute-start(bf16[272,256]{1,0:T(8,128)(2,1)} %get-tuple-element.165), channel_id=1, source_target_pairs={{0,2},{1,3},{2,0},{3,1},{4,6},{5,7},{6,4},{7,5},{8,10},{9,11},{10,... | collective-permute-start | bytes 417800 | tf_op jit(solution)/shard_map/ppermute | solution.py:787
  111.9 8.2 %collective-permute-start.31 = (bf16[272,256]{1,0:T(8,128)(2,1)}, bf16[272,256]{1,0:T(8,128)(2,1)S(1)}, u32[]{:S(2)}, u32[]{:S(2)}) collective-permute-start(bf16[272,256]{1,0:T(8,128)(2,1)} %get-tuple-element.166), channel_id=1, source_target_pairs={{0,3},{1,2},{2,1},{3,0},{4,7},{5,6},{6,5},{7,4},{8,11},{9,10},{10,... | collective-permute-start | bytes 417800 | tf_op jit(solution)/shard_map/ppermute | solution.py:787
  123.8 8.9 %collective-permute-start.32 = (bf16[176,512]{1,0:T(8,128)(2,1)}, bf16[176,512]{1,0:T(8,128)(2,1)S(1)}, u32[]{:S(2)}, u32[]{:S(2)}) collective-permute-start(bf16[176,512]{1,0:T(8,128)(2,1)} %get-tuple-element.167), channel_id=1, source_target_pairs={{0,8},{8,16},{16,24},{24,28},{28,20},{20,12},{12,4},{4,0},{1,9},{9... | collective-permute-start | bytes 540680 | tf_op jit(solution)/shard_map/ppermute | solution.py:738
  124.9 7.7 %collective-permute-start.33 = (bf16[176,512]{1,0:T(8,128)(2,1)}, bf16[176,512]{1,0:T(8,128)(2,1)S(1)}, u32[]{:S(2)}, u32[]{:S(2)}) collective-permute-start(bf16[176,512]{1,0:T(8,128)(2,1)} %get-tuple-element.168), channel_id=1, source_target_pairs={{0,4},{8,0},{16,8},{24,16},{28,24},{20,28},{12,20},{4,12},{1,5},{9... | collective-permute-start | bytes 540680 | tf_op jit(solution)/shard_map/ppermute | solution.py:738
  131.4 23.8 %collective-permute-start.34 = (bf16[2,128,1024]{2,1,0:T(8,128)(2,1)}, bf16[2,128,1024]{2,1,0:T(8,128)(2,1)S(1)}, u32[]{:S(2)}, u32[]{:S(2)}) collective-permute-start(bf16[2,128,1024]{2,1,0:T(8,128)(2,1)} %get-tuple-element.160), channel_id=1, source_target_pairs={{0,1},{1,0},{2,3},{3,2},{4,5},{5,4},{6,7},{7,6},{8,9},{9,8},{10,11... | collective-permute-start | bytes 1572872 | tf_op jit(solution)/shard_map/ppermute | solution.py:787
  131.4 12.2 %collective-permute-start.41 = (bf16[256,512]{1,0:T(8,128)(2,1)S(1)}, bf16[256,512]{1,0:T(8,128)(2,1)S(1)}, u32[]{:S(2)}, u32[]{:S(2)}) collective-permute-start(bf16[256,512]{1,0:T(8,128)(2,1)S(1)} %add_convert_fusion.1), channel_id=1, source_target_pairs={{0,8},{8,16},{16,24},{24,28},{28,20},{20,12},{12,4},{4,0},{1,9},{9... | collective-permute-start | bytes 786440 | tf_op jit(solution)/shard_map/ppermute | solution.py:738
  137.2 18.9 %all-to-all-start = ((bf16[4,128,1024]{2,1,0:T(8,128)(2,1)}), bf16[4,128,1024]{2,1,0:T(8,128)(2,1)S(1)}, u32[]{:S(2)}, u32[]{:S(2)}) async-start(bf16[4,128,1024]{2,1,0:T(8,128)(2,1)} %bitcast.19), calls=%async_computation | async-start | bytes 2097152 | tf_op jit(solution)/shard_map/all_to_all | solution.py:782
  171.0 8.4 %collective-permute-start.42 = (f32[128]{0:T(128)S(1)}, f32[128]{0:T(128)S(1)}, u32[]{:S(2)}, u32[]{:S(2)}) collective-permute-start(f32[128]{0:T(128)S(1)} %add.195), channel_id=1, source_target_pairs={{0,1},{1,0},{2,3},{3,2},{4,5},{5,4},{6,7},{7,6},{8,9},{9,8},{10,11... | collective-permute-start | bytes 1544 | tf_op jit(solution)/shard_map/ppermute | solution.py:787
  171.0 8.3 %collective-permute-start.43 = (f32[128]{0:T(128)S(1)}, f32[128]{0:T(128)S(1)}, u32[]{:S(2)}, u32[]{:S(2)}) collective-permute-start(f32[128]{0:T(128)S(1)} %add.195), channel_id=1, source_target_pairs={{0,2},{1,3},{2,0},{3,1},{4,6},{5,7},{6,4},{7,5},{8,10},{9,11},{10,... | collective-permute-start | bytes 1544 | tf_op jit(solution)/shard_map/ppermute | solution.py:787
  (56 other events, 407.0 us)

commit v10 on v9

--- a/solution.py
+++ b/solution.py
@@ -1099,14 +1099,13 @@
         held = chunk_pair((7, 5), ())
         got = ring_step(held)
         keep_rows, give_rows = project_back()
-        held = chunk_pair((6, 3), got, give_rows)
-        partial_out = ordered(held, partial_out)[1]
-        got = ring_step(held)
-        mixed_rows = tensor_sum(partial_out, depth)
+        got = ring_step(chunk_pair((6, 3), got, give_rows))
         near = tensor_swap(give_rows, 1)
         far_half = add_low(keep_rows[1], near[1])
-        got = ring_step(chunk_pair((4, 1), got))
-        held, inner_own = chunk_pair((2, 0), got, (mixed_rows, far_half), last=f32)
+        held = chunk_pair((4, 1), got, far_half)
+        mixed_rows = tensor_sum(ordered(held, partial_out)[1], depth)
+        got = ring_step(held)
+        held, inner_own = chunk_pair((2, 0), got, last=f32)
         inner_out = inner_own + ring_send(held, True).astype(f32)
     else:
         (inner_msg,) = call(
@@ -1123,7 +1122,7 @@
     gain_full = small_full[: depth // states].reshape(1, depth)
 
     if fast:
-        far = ordered(inner_out, tensor_swap(far_half, 2))[1]
+        far, mixed_rows = ordered(inner_out, (tensor_swap(far_half, 2), mixed_rows))[1]
         grad_local = keep_rows[0].astype(f32) + near[0].astype(f32) + far.astype(f32)
         gate_grad, output_grad = gate_out[:tall], gate_out[tall:].T
         inner_grad = inner_out[:tall]

time: 181 us -> 188 us (1.039)
  local copies, waits for them, and re-layouts: 11.9 us -> 15.1 us
  waiting for transfers between devices: 37.6 us -> 40.6 us
  other arithmetic: 6.75 us -> 8.98 us
    unnamed x88, local copies, waits for them, and re-layouts: 6.26 us -> 8.8 us
  transfers between devices with their start and end apart: 46 -> 46, of which waited for: 20 -> 19; matrix products, arithmetic and copies ran while one was open for 8% -> 8% of each run, Pallas kernels for 29% -> 30%
where the time goes in v10:
time: 188 us
  Pallas kernels  76.2 us (41%)
  starting transfers between devices  45.6 us (24%)
  waiting for transfers between devices  40.6 us (22%)
  local copies, waits for them, and re-layouts  15.1 us (8%)
  other arithmetic  8.98 us (5%)
    pallas_call x12, Pallas kernels, call(): pl.pallas_call(kernel, out_shape=[jax.ShapeDtypeStruct(shape, kind) for s...  63.4 us
    ppermute x28, waiting for transfers between devices, ring_send(): return lax.ppermute(value, 'dp', pairs)  34.8 us
    ppermute x28, starting transfers between devices, ring_send(): return lax.ppermute(value, 'dp', pairs)  30.1 us
    pallas_call x4, Pallas kernels, chunk_pair(): pl.pallas_call(functools.partial(chunk_kernel, slots, len(got)), grid_spe...  12.8 us
    ppermute x17, starting transfers between devices, tensor_swap(): return lax.ppermute(value, 'tensor', [(i, i ^ bit) for i in range(4)])  12 us
    unnamed x88, local copies, waits for them, and re-layouts  8.8 us
    ppermute x17, waiting for transfers between devices, tensor_swap(): return lax.ppermute(value, 'tensor', [(i, i ^ bit) for i in range(4)])  5.88 us
  transfers between devices with their start and end apart: 46, of which 19 were waited for; matrix products, arithmetic and copies ran while one was open for 8% of the time, Pallas kernels for 30%

profile of v10, /device:TPU:0, one launch (start us, length us, event | category | flops | bytes accessed | tf_op | source)
XLA Modules:
  0.0 187.7 jit_solution(627415932278309920)
XLA Ops:
  3.3 2.6 %collective-permute-start.1 = (bf16[48,256]{1,0:T(8,128)(2,1)}, bf16[48,256]{1,0:T(8,128)(2,1)S(1)}, u32[]{:S(2)}, u32[]{:S(2)}) collective-permute-start(bf16[48,256]{1,0:T(8,128)(2,1)} %shard_map.271.refs_0_), channel_id=1, source_target_pairs={{0,2},{1,3},{2,0},{3,1},{4,6},{5,7},{6,4},{7,5},{8,10},{9,11},{10,... | collective-permute-start | bytes 73736 | tf_op jit(solution)/shard_map/ppermute | solution.py:787
  5.9 2.0 %shard_map.272.refs_4_ = bf16[256,512]{1,0:T(8,128)(2,1)} custom-call(bf16[128,2,512]{2,1,0:T(2,128)(2,1)} %input_ref.3, bf16[512,128]{1,0:T(8,128)(2,1)} %out_ref), custom_call_target="tpu_custom_call" | custom-call | flops 2200000000 | bytes 1048576 | tf_op jit(solution)/shard_map/pallas_call | solution.py:703
  8.0 1.8 collective-permute-start.6
  10.1 1.8 collective-permute-start.4
  12.5 2.0 %shard_map.273.refs_4_ = bf16[208,512]{1,0:T(8,128)(2,1)} custom-call(bf16[128,2,512]{2,1,0:T(2,128)(2,1)} %input_ref.3, bf16[16,128]{1,0:T(8,128)(2,1)} %pad.4.step_ref, bf16[48,256]{1,0:T(8,128)(2,1)} %shard_map.271.refs_0_, bf16[48,256]{1,0:T(8,128)(2,1)} %copy-done.36, bf16[48,256]{1,0:T(8,128)(2,1)} %copy-done.37, bf16[48,256]{1,0:T(8,128)(2,1)} %copy-done.38), custom_call_target="tpu_custom_call" | custom-call | flops 1100000000 | bytes 1048576 | tf_op jit(solution)/shard_map/pallas_call | solution.py:703
  14.5 2.2 %collective-permute-done.6.refs_5_ = bf16[256,512]{1,0:T(8,128)(2,1)S(1)} collective-permute-done((bf16[256,512]{1,0:T(8,128)(2,1)}, bf16[256,512]{1,0:T(8,128)(2,1)S(1)}, u32[]{:S(2)}, u32[]{:S(2)}) %collective-permute-start.6) | collective-permute-done | bytes 262176 | tf_op jit(solution)/shard_map/ppermute | solution.py:738
  21.9 4.8 %collective-permute-done.13.refs_5_ = bf16[208,512]{1,0:T(8,128)(2,1)S(1)} collective-permute-done((bf16[208,512]{1,0:T(8,128)(2,1)}, bf16[208,512]{1,0:T(8,128)(2,1)S(1)}, u32[]{:S(2)}, u32[]{:S(2)}) %collective-permute-start.13) | collective-permute-done | bytes 213024 | tf_op jit(solution)/shard_map/ppermute | solution.py:738
  29.0 3.4 %collective-permute-done.8.refs_7_ = bf16[256,512]{1,0:T(8,128)(2,1)} collective-permute-done((bf16[256,512]{1,0:T(8,128)(2,1)S(1)}, bf16[256,512]{1,0:T(8,128)(2,1)}, u32[]{:S(2)}, u32[]{:S(2)}) %collective-permute-start.8) | collective-permute-done | bytes 262176 | tf_op jit(solution)/shard_map/ppermute | solution.py:738
  32.7 2.3 %collective-permute-done.15.refs_7_ = bf16[208,512]{1,0:T(8,128)(2,1)S(1)} collective-permute-done((bf16[208,512]{1,0:T(8,128)(2,1)S(1)}, bf16[208,512]{1,0:T(8,128)(2,1)S(1)}, u32[]{:S(2)}, u32[]{:S(2)}) %collective-permute-start.15) | collective-permute-done | bytes 213024 | tf_op jit(solution)/shard_map/ppermute | solution.py:738
  39.7 2.0 %collective-permute-done.16.refs_8_ = bf16[208,512]{1,0:T(8,128)(2,1)} collective-permute-done((bf16[208,512]{1,0:T(8,128)(2,1)S(1)}, bf16[208,512]{1,0:T(8,128)(2,1)}, u32[]{:S(2)}, u32[]{:S(2)}) %collective-permute-start.16) | collective-permute-done | bytes 213024 | tf_op jit(solution)/shard_map/ppermute | solution.py:738
  49.3 3.0 %collective-permute-done.19.refs_11_ = bf16[208,512]{1,0:T(8,128)(2,1)} collective-permute-done((bf16[208,512]{1,0:T(8,128)(2,1)}, bf16[208,512]{1,0:T(8,128)(2,1)}, u32[]{:S(2)}, u32[]{:S(2)}) %collective-permute-start.19) | collective-permute-done | bytes 213024 | tf_op jit(solution)/shard_map/ppermute | solution.py:738
  52.3 11.2 %shard_map.275 = (bf16[512,1024]{1,0:T(8,128)(2,1)}, bf16[1024,512]{1,0:T(8,128)(2,1)}, bf16[1024,512]{1,0:T(8,128)(2,1)}, bf16[1024,256]{1,0:T(8,128)(2,1)}, bf...) custom-call(s32[12]{0:T(128)} %stack.66.place_ref, ...), custom_call_target="tpu_custom_call" | custom-call | flops 12099999744 | bytes 1048576 | tf_op jit(solution)/shard_map/pallas_call | solution.py:703
  64.2 7.3 %shard_map.276 = (bf16[512,1024]{1,0:T(8,128)(2,1)}, bf16[1024,512]{1,0:T(8,128)(2,1)}, bf16[1024,512]{1,0:T(8,128)(2,1)}, f32[512,512]{1,0:T(8,128)}, f32[512,512]{1,0:T(8,128)}, /*index=5*/f32[8,512]{1,0:T(8,128)}) custom-call(s32[12]{0:T(128)} %stack.66.place_ref, s32[1,4]{1,0:T(1,128)} %lengths_ref.13, bf16[256,1024]{1,0:T(8,128)(2,1)} %copy-done.4, ...), custom_call_target="tpu_custom_call" | custom-call | flops 5500000256 | bytes 1048576 | tf_op jit(solution)/shard_map/pallas_call | solution.py:703
  73.5 2.1 %collective-permute-done.21.refs_2_ = f32[8,512]{1,0:T(8,128)S(1)} collective-permute-done((f32[8,512]{1,0:T(8,128)}, f32[8,512]{1,0:T(8,128)S(1)}, u32[]{:S(2)}, u32[]{:S(2)}) %collective-permute-start.21) | collective-permute-done | bytes 16416 | tf_op jit(solution)/shard_map/ppermute | solution.py:787
  77.2 8.1 %shard_map.277 = (bf16[256,512]{1,0:T(8,128)(2,1)}, bf16[256,512]{1,0:T(8,128)(2,1)}, bf16[256,512]{1,0:T(8,128)(2,1)}, bf16[256,512]{1,0:T(8,128)(2,1)}, bf16[2...) custom-call(s32[12]{0:T(128)} %stack.66.place_ref, ...), custom_call_target="tpu_custom_call" | custom-call | flops 9900000256 | bytes 1048576 | tf_op jit(solution)/shard_map/pallas_call | solution.py:703
  87.4 6.5 %shard_map.278 = (f32[512,256]{1,0:T(8,128)}, f32[512,256]{1,0:T(8,128)}, f32[16,512]{1,0:T(8,128)}, f32[8,256]{1,0:T(8,128)}) custom-call(s32[1,4]{1,0:T(1,128)} %lengths_ref.13, f32[512,512]{1,0:T(8,128)} %get-tuple-element.132.refs_0_, f32[512,512]{1,0:T(8,128)} %get-tuple-element.123.refs_1_, f32[512,256]{1,0:T(8,128)} %get-tuple-element.124.refs_2_, ...), custom_call_target="tpu_custom_call" | custom-call | flops 6600000000 | bytes 1048576 | tf_op jit(solution)/shard_map/pallas_call | solution.py:703
  95.0 1.8 collective-permute-start.26
  97.1 6.5 %shard_map.279 = (f32[512,256]{1,0:T(8,128)}, f32[512,256]{1,0:T(8,128)}, f32[16,512]{1,0:T(8,128)}, f32[8,256]{1,0:T(8,128)}) custom-call(s32[1,4]{1,0:T(1,128)} %lengths_ref.13, f32[512,512]{1,0:T(8,128)} %get-tuple-element.132.refs_0_, f32[512,512]{1,0:T(8,128)} %get-tuple-element.123.refs_1_, f32[512,256]{1,0:T(8,128)} %get-tuple-element.124.refs_2_, ...), custom_call_target="tpu_custom_call" | custom-call | flops 6600000000 | bytes 1048576 | tf_op jit(solution)/shard_map/pallas_call | solution.py:703
  105.9 5.4 %shard_map.281 = (bf16[512,256]{1,0:T(8,128)(2,1)}, bf16[16,512]{1,0:T(8,128)(2,1)}, bf16[272,256]{1,0:T(8,128)(2,1)}, bf16[272,256]{1,0:T(8,128)(2,1)}, bf16[27...) custom-call(s32[12]{0:T(128)} %stack.66.place_ref, s32[1,4]{1,0:T(1,128)} %lengths_ref.13, ...), custom_call_target="tpu_custom_call" | custom-call | flops 4400000000 | bytes 1048576 | tf_op jit(solution)/shard_map/pallas_call | solution.py:703
  113.3 5.6 %shard_map.280 = (bf16[512,512]{1,0:T(8,128)(2,1)}, f32[16,512]{1,0:T(8,128)}) custom-call(s32[1,4]{1,0:T(1,128)} %lengths_ref.13, f32[512,256]{1,0:T(8,128)} %get-tuple-element.127.refs_0_, f32[512,256]{1,0:T(8,128)} %get-tuple-element.133.refs_1_, f32[8,256]{1,0:T(8,128)} %get-tuple-element.134.refs_2_, f32[8,256]{1,0:T(8,128)} %get-tuple-element.135.refs_3_, ...), custom_call_target="tpu_custom_call" | custom-call | flops 6600000000 | bytes 1048576 | tf_op jit(solution)/shard_map/pallas_call | solution.py:703
  118.9 5.6 %shard_map.282 = (bf16[2,128,1024]{2,1,0:T(8,128)(2,1)}, bf16[2,128,1024]{2,1,0:T(8,128)(2,1)}) custom-call(s32[12]{0:T(128)} %stack.66.place_ref, bf16[512,512]{1,0:T(8,128)(2,1)} %get-tuple-element.160.refs_0_, bf16[512,512]{1,0:T(8,128)(2,1)} %get-tuple-element.169.refs_1_.refs_0_, bf16[512,256]{1,0:T(8,128)(2,1)} %get-tuple-element.161.refs_2_, ...), custom_call_target="tpu_custom_call" | custom-call | flops 6600000000 | bytes 1048576 | tf_op jit(solution)/shard_map/pallas_call | solution.py:703
  125.7 3.1 %shard_map.283 = (bf16[176,512]{1,0:T(8,128)(2,1)}, bf16[176,512]{1,0:T(8,128)(2,1)}) custom-call(s32[12]{0:T(128)} %stack.66.place_ref, bf16[512,512]{1,0:T(8,128)(2,1)} %get-tuple-element.169.refs_1_.refs_0_, bf16[16,512]{1,0:T(8,128)(2,1)} %get-tuple-element.154.refs_3_.refs_1_, f32[16,512]{1,0:T(8,128)} %get-tuple-element.155.refs_2_, ...), custom_call_target="tpu_custom_call" | custom-call | flops 2000000000 | bytes 1048576 | tf_op jit(solution)/shard_map/pallas_call | solution.py:1084
  132.2 4.1 %collective-permute-done.33.refs_9_ = bf16[176,512]{1,0:T(8,128)(2,1)S(1)} collective-permute-done((bf16[176,512]{1,0:T(8,128)(2,1)}, bf16[176,512]{1,0:T(8,128)(2,1)S(1)}, u32[]{:S(2)}, u32[]{:S(2)}) %collective-permute-start.33) | collective-permute-done | bytes 180256 | tf_op jit(solution)/shard_map/ppermute | solution.py:738
  137.7 3.2 %shard_map.284 = (bf16[176,512]{1,0:T(8,128)(2,1)}, bf16[176,512]{1,0:T(8,128)(2,1)}) custom-call(s32[12]{0:T(128)} %stack.66.place_ref, bf16[512,512]{1,0:T(8,128)(2,1)} %get-tuple-element.169.refs_1_.refs_0_, bf16[16,512]{1,0:T(8,128)(2,1)} %get-tuple-element.154.refs_3_.refs_1_, f32[16,512]{1,0:T(8,128)} %get-tuple-element.155.refs_2_, ...), custom_call_target="tpu_custom_call" | custom-call | flops 2000000000 | bytes 1048576 | tf_op jit(solution)/shard_map/pallas_call | solution.py:1084
  143.8 2.9 %collective-permute-done.35.refs_9_ = bf16[176,512]{1,0:T(8,128)(2,1)S(1)} collective-permute-done((bf16[176,512]{1,0:T(8,128)(2,1)}, bf16[176,512]{1,0:T(8,128)(2,1)S(1)}, u32[]{:S(2)}, u32[]{:S(2)}) %collective-permute-start.35) | collective-permute-done | bytes 180256 | tf_op jit(solution)/shard_map/ppermute | solution.py:738
  148.4 3.2 %shard_map.285 = (bf16[176,512]{1,0:T(8,128)(2,1)}, bf16[176,512]{1,0:T(8,128)(2,1)}) custom-call(s32[12]{0:T(128)} %stack.66.place_ref, bf16[512,512]{1,0:T(8,128)(2,1)} %get-tuple-element.169.refs_1_.refs_0_, bf16[16,512]{1,0:T(8,128)(2,1)} %get-tuple-element.154.refs_3_.refs_1_, f32[16,512]{1,0:T(8,128)} %get-tuple-element.155.refs_2_, ...), custom_call_target="tpu_custom_call" | custom-call | flops 2000000000 | bytes 1048576 | tf_op jit(solution)/shard_map/pallas_call | solution.py:1084
  151.6 1.7 collective-permute-start.37
  153.8 3.7 %collective-permute-done.37.refs_9_ = bf16[176,512]{1,0:T(8,128)(2,1)} collective-permute-done((bf16[176,512]{1,0:T(8,128)(2,1)}, bf16[176,512]{1,0:T(8,128)(2,1)}, u32[]{:S(2)}, u32[]{:S(2)}) %collective-permute-start.37) | collective-permute-done | bytes 180256 | tf_op jit(solution)/shard_map/ppermute | solution.py:738
  157.4 1.7 collective-permute-done.38.refs_10_
  159.2 3.3 %shard_map.286 = (bf16[176,512]{1,0:T(8,128)(2,1)}, f32[176,512]{1,0:T(8,128)}) custom-call(s32[12]{0:T(128)} %stack.66.place_ref, bf16[512,512]{1,0:T(8,128)(2,1)} %get-tuple-element.169.refs_1_.refs_0_, bf16[16,512]{1,0:T(8,128)(2,1)} %get-tuple-element.154.refs_3_.refs_1_, f32[16,512]{1,0:T(8,128)} %get-tuple-element.155.refs_2_, ...), custom_call_target="tpu_custom_call" | custom-call | flops 2000000000 | bytes 1048576 | tf_op jit(solution)/shard_map/pallas_call | solution.py:1084
  166.3 3.5 %all-to-all-start = ((bf16[4,128,1024]{2,1,0:T(8,128)(2,1)}), bf16[4,128,1024]{2,1,0:T(8,128)(2,1)S(1)}, u32[]{:S(2)}, u32[]{:S(2)}) async-start(bf16[4,128,1024]{2,1,0:T(8,128)(2,1)} %bitcast.49), calls=%async_computation | async-start | bytes 2097152 | tf_op jit(solution)/shard_map/all_to_all | solution.py:782
  181.5 2.8 %collective-permute-done.43 = f32[128]{0:T(128)} collective-permute-done((f32[128]{0:T(128)S(1)}, f32[128]{0:T(128)}, u32[]{:S(2)}, u32[]{:S(2)}) %collective-permute-start.43) | collective-permute-done | bytes 544 | tf_op jit(solution)/shard_map/ppermute | solution.py:787
  (203 shorter events, 65.2 us)
Async XLA Ops:
  8.0 8.8 %collective-permute-start.6 = (bf16[256,512]{1,0:T(8,128)(2,1)}, bf16[256,512]{1,0:T(8,128)(2,1)S(1)}, u32[]{:S(2)}, u32[]{:S(2)}) collective-permute-start(bf16[256,512]{1,0:T(8,128)(2,1)} %shard_map.272.refs_4_), channel_id=1, source_target_pairs={{0,8},{8,16},{16,24},{24,28},{28,20},{20,12},{12,4},{4,0},{1,9},{9... | collective-permute-start | bytes 786440 | tf_op jit(solution)/shard_map/ppermute | solution.py:738
  9.8 8.5 %collective-permute-start.7 = (bf16[256,512]{1,0:T(8,128)(2,1)}, bf16[256,512]{1,0:T(8,128)(2,1)S(1)}, u32[]{:S(2)}, u32[]{:S(2)}) collective-permute-start(bf16[256,512]{1,0:T(8,128)(2,1)} %shard_map.272.refs_4_), channel_id=1, source_target_pairs={{0,4},{8,0},{16,8},{24,16},{28,24},{20,28},{12,20},{4,12},{1,5},{9... | collective-permute-start | bytes 786440 | tf_op jit(solution)/shard_map/ppermute | solution.py:738
  10.1 18.7 %collective-permute-start.4 = (bf16[256,1024]{1,0:T(8,128)(2,1)S(1)}, bf16[256,1024]{1,0:T(8,128)(2,1)S(1)}, u32[]{:S(2)}, u32[]{:S(2)}) collective-permute-start(bf16[256,1024]{1,0:T(8,128)(2,1)S(1)} %pad_maximum_fusion.refs_0_), channel_id=1, source_target_pairs={{0,2},{1,3},{2,0},{3,1},{4,6},{5,7},{6,4},{7,5},{8,10},{9,11},{10,... | collective-permute-start | bytes 1572872 | tf_op jit(solution)/shard_map/ppermute | solution.py:787
  18.3 8.4 %collective-permute-start.13 = (bf16[208,512]{1,0:T(8,128)(2,1)}, bf16[208,512]{1,0:T(8,128)(2,1)S(1)}, u32[]{:S(2)}, u32[]{:S(2)}) collective-permute-start(bf16[208,512]{1,0:T(8,128)(2,1)} %shard_map.273.refs_4_), channel_id=1, source_target_pairs={{0,8},{8,16},{16,24},{24,28},{28,20},{20,12},{12,4},{4,0},{1,9},{9... | collective-permute-start | bytes 638984 | tf_op jit(solution)/shard_map/ppermute | solution.py:738
  19.9 8.4 %collective-permute-start.14 = (bf16[208,512]{1,0:T(8,128)(2,1)}, bf16[208,512]{1,0:T(8,128)(2,1)S(1)}, u32[]{:S(2)}, u32[]{:S(2)}) collective-permute-start(bf16[208,512]{1,0:T(8,128)(2,1)} %shard_map.273.refs_4_), channel_id=1, source_target_pairs={{0,4},{8,0},{16,8},{24,16},{28,24},{20,28},{12,20},{4,12},{1,5},{9... | collective-permute-start | bytes 638984 | tf_op jit(solution)/shard_map/ppermute | solution.py:738
  20.3 12.1 %collective-permute-start.8 = (bf16[256,512]{1,0:T(8,128)(2,1)S(1)}, bf16[256,512]{1,0:T(8,128)(2,1)}, u32[]{:S(2)}, u32[]{:S(2)}) collective-permute-start(bf16[256,512]{1,0:T(8,128)(2,1)S(1)} %collective-permute-done.6.refs_5_), channel_id=1, source_target_pairs={{0,8},{8,16},{16,24},{24,28},{28,20},{20,12},{12,4},{4,0},{1,9},{9... | collective-permute-start | bytes 786440 | tf_op jit(solution)/shard_map/ppermute | solution.py:738
  26.7 8.4 %collective-permute-start.15 = (bf16[208,512]{1,0:T(8,128)(2,1)S(1)}, bf16[208,512]{1,0:T(8,128)(2,1)S(1)}, u32[]{:S(2)}, u32[]{:S(2)}) collective-permute-start(bf16[208,512]{1,0:T(8,128)(2,1)S(1)} %collective-permute-done.13.refs_5_), channel_id=1, source_target_pairs={{0,8},{8,16},{16,24},{24,28},{28,20},{20,12},{12,4},{4,0},{1,9},{9... | collective-permute-start | bytes 638984 | tf_op jit(solution)/shard_map/ppermute | solution.py:738
  28.3 18.8 %collective-permute-start.3 = (bf16[256,1024]{1,0:T(8,128)(2,1)S(1)}, bf16[256,1024]{1,0:T(8,128)(2,1)S(1)}, u32[]{:S(2)}, u32[]{:S(2)}) collective-permute-start(bf16[256,1024]{1,0:T(8,128)(2,1)S(1)} %pad_maximum_fusion.refs_0_), channel_id=1, source_target_pairs={{0,1},{1,0},{2,3},{3,2},{4,5},{5,4},{6,7},{7,6},{8,9},{9,8},{10,11... | collective-permute-start | bytes 1572872 | tf_op jit(solution)/shard_map/ppermute | solution.py:787
  28.3 9.2 %collective-permute-start.9 = (bf16[256,512]{1,0:T(8,128)(2,1)S(1)}, bf16[256,512]{1,0:T(8,128)(2,1)S(1)}, u32[]{:S(2)}, u32[]{:S(2)}) collective-permute-start(bf16[256,512]{1,0:T(8,128)(2,1)S(1)} %collective-permute-done.7.refs_6_), channel_id=1, source_target_pairs={{0,4},{8,0},{16,8},{24,16},{28,24},{20,28},{12,20},{4,12},{1,5},{9... | collective-permute-start | bytes 786440 | tf_op jit(solution)/shard_map/ppermute | solution.py:738
  28.8 20.5 %collective-permute-start.5 = (bf16[256,1024]{1,0:T(8,128)(2,1)S(1)}, bf16[256,1024]{1,0:T(8,128)(2,1)S(1)}, u32[]{:S(2)}, u32[]{:S(2)}) collective-permute-start(bf16[256,1024]{1,0:T(8,128)(2,1)S(1)} %collective-permute-done.4.refs_2_), channel_id=1, source_target_pairs={{0,1},{1,0},{2,3},{3,2},{4,5},{5,4},{6,7},{7,6},{8,9},{9,8},{10,11... | collective-permute-start | bytes 1572872 | tf_op jit(solution)/shard_map/ppermute | solution.py:787
  32.4 9.3 %collective-permute-start.16 = (bf16[208,512]{1,0:T(8,128)(2,1)S(1)}, bf16[208,512]{1,0:T(8,128)(2,1)}, u32[]{:S(2)}, u32[]{:S(2)}) collective-permute-start(bf16[208,512]{1,0:T(8,128)(2,1)S(1)} %collective-permute-done.14.refs_6_), channel_id=1, source_target_pairs={{0,4},{8,0},{16,8},{24,16},{28,24},{20,28},{12,20},{4,12},{1,5},{9... | collective-permute-start | bytes 638984 | tf_op jit(solution)/shard_map/ppermute | solution.py:738
  38.1 9.6 %collective-permute-start.10 = (bf16[256,512]{1,0:T(8,128)(2,1)}, bf16[256,512]{1,0:T(8,128)(2,1)}, u32[]{:S(2)}, u32[]{:S(2)}) collective-permute-start(bf16[256,512]{1,0:T(8,128)(2,1)} %collective-permute-done.8.refs_7_), channel_id=1, source_target_pairs={{0,8},{8,16},{16,24},{24,28},{28,20},{20,12},{12,4},{4,0},{1,9},{9... | collective-permute-start | bytes 786440 | tf_op jit(solution)/shard_map/ppermute | solution.py:738
  41.7 7.6 %collective-permute-start.18 = (bf16[208,512]{1,0:T(8,128)(2,1)}, bf16[208,512]{1,0:T(8,128)(2,1)}, u32[]{:S(2)}, u32[]{:S(2)}) collective-permute-start(bf16[208,512]{1,0:T(8,128)(2,1)} %collective-permute-done.16.refs_8_), channel_id=1, source_target_pairs={{0,4},{8,0},{16,8},{24,16},{28,24},{20,28},{12,20},{4,12},{1,5},{9... | collective-permute-start | bytes 638984 | tf_op jit(solution)/shard_map/ppermute | solution.py:738
  42.1 10.1 %collective-permute-start.19 = (bf16[208,512]{1,0:T(8,128)(2,1)}, bf16[208,512]{1,0:T(8,128)(2,1)}, u32[]{:S(2)}, u32[]{:S(2)}) collective-permute-start(bf16[208,512]{1,0:T(8,128)(2,1)} %collective-permute-done.17.refs_9_), channel_id=1, source_target_pairs={{0,8},{8,16},{16,24},{24,28},{28,20},{20,12},{12,4},{4,0},{1,9},{9... | collective-permute-start | bytes 638984 | tf_op jit(solution)/shard_map/ppermute | solution.py:738
  47.1 16.3 %collective-permute-start.11 = (bf16[256,512]{1,0:T(8,128)(2,1)}, bf16[256,512]{1,0:T(8,128)(2,1)S(1)}, u32[]{:S(2)}, u32[]{:S(2)}) collective-permute-start(bf16[256,512]{1,0:T(8,128)(2,1)} %copy-done.23), channel_id=1, source_target_pairs={{0,4},{8,0},{16,8},{24,16},{28,24},{20,28},{12,20},{4,12},{1,5},{9... | collective-permute-start | bytes 786440 | tf_op jit(solution)/shard_map/ppermute | solution.py:738
  47.7 15.8 %collective-permute-start.12 = (bf16[256,512]{1,0:T(8,128)(2,1)}, bf16[256,512]{1,0:T(8,128)(2,1)S(1)}, u32[]{:S(2)}, u32[]{:S(2)}) collective-permute-start(bf16[256,512]{1,0:T(8,128)(2,1)} %collective-permute-done.10.refs_9_), channel_id=1, source_target_pairs={{0,8},{8,16},{16,24},{24,28},{28,20},{20,12},{12,4},{4,0},{1,9},{9... | collective-permute-start | bytes 786440 | tf_op jit(solution)/shard_map/ppermute | solution.py:738
  85.3 8.6 %collective-permute-start.24 = (bf16[256,512]{1,0:T(8,128)(2,1)}, bf16[256,512]{1,0:T(8,128)(2,1)S(1)}, u32[]{:S(2)}, u32[]{:S(2)}) collective-permute-start(bf16[256,512]{1,0:T(8,128)(2,1)} %get-tuple-element.130), channel_id=1, source_target_pairs={{0,4},{8,0},{16,8},{24,16},{28,24},{20,28},{12,20},{4,12},{1,5},{9... | collective-permute-start | bytes 786440 | tf_op jit(solution)/shard_map/ppermute | solution.py:738
  85.8 9.2 %collective-permute-start.23 = (bf16[256,512]{1,0:T(8,128)(2,1)}, bf16[256,512]{1,0:T(8,128)(2,1)S(1)}, u32[]{:S(2)}, u32[]{:S(2)}) collective-permute-start(bf16[256,512]{1,0:T(8,128)(2,1)} %get-tuple-element.128), channel_id=1, source_target_pairs={{0,8},{8,16},{16,24},{24,28},{28,20},{20,12},{12,4},{4,0},{1,9},{9... | collective-permute-start | bytes 786440 | tf_op jit(solution)/shard_map/ppermute | solution.py:738
  95.0 8.6 %collective-permute-start.26 = (bf16[256,512]{1,0:T(8,128)(2,1)S(1)}, bf16[256,512]{1,0:T(8,128)(2,1)S(1)}, u32[]{:S(2)}, u32[]{:S(2)}) collective-permute-start(bf16[256,512]{1,0:T(8,128)(2,1)S(1)} %add_convert_fusion.4), channel_id=1, source_target_pairs={{0,4},{8,0},{16,8},{24,16},{28,24},{20,28},{12,20},{4,12},{1,5},{9... | collective-permute-start | bytes 786440 | tf_op jit(solution)/shard_map/ppermute | solution.py:738
  103.9 9.4 %collective-permute-start.27 = (bf16[256,512]{1,0:T(8,128)(2,1)S(1)}, bf16[256,512]{1,0:T(8,128)(2,1)S(1)}, u32[]{:S(2)}, u32[]{:S(2)}) collective-permute-start(bf16[256,512]{1,0:T(8,128)(2,1)S(1)} %add_convert_fusion.3), channel_id=1, source_target_pairs={{0,8},{8,16},{16,24},{24,28},{28,20},{20,12},{12,4},{4,0},{1,9},{9... | collective-permute-start | bytes 786440 | tf_op jit(solution)/shard_map/ppermute | solution.py:738
  104.7 8.7 %collective-permute-start.28 = (bf16[256,512]{1,0:T(8,128)(2,1)S(1)}, bf16[256,512]{1,0:T(8,128)(2,1)S(1)}, u32[]{:S(2)}, u32[]{:S(2)}) collective-permute-start(bf16[256,512]{1,0:T(8,128)(2,1)S(1)} %add_convert_fusion.2), channel_id=1, source_target_pairs={{0,4},{8,0},{16,8},{24,16},{28,24},{20,28},{12,20},{4,12},{1,5},{9... | collective-permute-start | bytes 786440 | tf_op jit(solution)/shard_map/ppermute | solution.py:738
  111.4 13.5 %collective-permute-start.29 = (bf16[272,256]{1,0:T(8,128)(2,1)}, bf16[272,256]{1,0:T(8,128)(2,1)S(1)}, u32[]{:S(2)}, u32[]{:S(2)}) collective-permute-start(bf16[272,256]{1,0:T(8,128)(2,1)} %get-tuple-element.157), channel_id=1, source_target_pairs={{0,1},{1,0},{2,3},{3,2},{4,5},{5,4},{6,7},{7,6},{8,9},{9,8},{10,11... | collective-permute-start | bytes 417800 | tf_op jit(solution)/shard_map/ppermute | solution.py:787
  111.4 13.5 %collective-permute-start.30 = (bf16[272,256]{1,0:T(8,128)(2,1)}, bf16[272,256]{1,0:T(8,128)(2,1)S(1)}, u32[]{:S(2)}, u32[]{:S(2)}) collective-permute-start(bf16[272,256]{1,0:T(8,128)(2,1)} %get-tuple-element.158), channel_id=1, source_target_pairs={{0,2},{1,3},{2,0},{3,1},{4,6},{5,7},{6,4},{7,5},{8,10},{9,11},{10,... | collective-permute-start | bytes 417800 | tf_op jit(solution)/shard_map/ppermute | solution.py:787
  112.0 12.9 %collective-permute-start.31 = (bf16[272,256]{1,0:T(8,128)(2,1)}, bf16[272,256]{1,0:T(8,128)(2,1)S(1)}, u32[]{:S(2)}, u32[]{:S(2)}) collective-permute-start(bf16[272,256]{1,0:T(8,128)(2,1)} %get-tuple-element.159), channel_id=1, source_target_pairs={{0,3},{1,2},{2,1},{3,0},{4,7},{5,6},{6,5},{7,4},{8,11},{9,10},{10,... | collective-permute-start | bytes 417800 | tf_op jit(solution)/shard_map/ppermute | solution.py:787
  124.6 18.4 %collective-permute-start.32 = (bf16[2,128,1024]{2,1,0:T(8,128)(2,1)}, bf16[2,128,1024]{2,1,0:T(8,128)(2,1)S(1)}, u32[]{:S(2)}, u32[]{:S(2)}) collective-permute-start(bf16[2,128,1024]{2,1,0:T(8,128)(2,1)} %get-tuple-element.167), channel_id=1, source_target_pairs={{0,1},{1,0},{2,3},{3,2},{4,5},{5,4},{6,7},{7,6},{8,9},{9,8},{10,11... | collective-permute-start | bytes 1572872 | tf_op jit(solution)/shard_map/ppermute | solution.py:787
  128.8 7.6 %collective-permute-start.33 = (bf16[176,512]{1,0:T(8,128)(2,1)}, bf16[176,512]{1,0:T(8,128)(2,1)S(1)}, u32[]{:S(2)}, u32[]{:S(2)}) collective-permute-start(bf16[176,512]{1,0:T(8,128)(2,1)} %get-tuple-element.170), channel_id=1, source_target_pairs={{0,8},{8,16},{16,24},{24,28},{28,20},{20,12},{12,4},{4,0},{1,9},{9... | collective-permute-start | bytes 540680 | tf_op jit(solution)/shard_map/ppermute | solution.py:738
  131.5 22.2 %collective-permute-start.41 = (bf16[256,512]{1,0:T(8,128)(2,1)S(1)}, bf16[256,512]{1,0:T(8,128)(2,1)S(1)}, u32[]{:S(2)}, u32[]{:S(2)}) collective-permute-start(bf16[256,512]{1,0:T(8,128)(2,1)S(1)} %add_convert_fusion.1), channel_id=1, source_target_pairs={{0,8},{8,16},{16,24},{24,28},{28,20},{20,12},{12,4},{4,0},{1,9},{9... | collective-permute-start | bytes 786440 | tf_op jit(solution)/shard_map/ppermute | solution.py:738
  165.8 20.0 %collective-permute-start.40 = (bf16[128,1024]{1,0:T(8,128)(2,1)}, bf16[128,1024]{1,0:T(8,128)(2,1)S(1)}, u32[]{:S(2)}, u32[]{:S(2)}) collective-permute-start(bf16[128,1024]{1,0:T(8,128)(2,1)} %fusion.6), channel_id=1, source_target_pairs={{0,2},{1,3},{2,0},{3,1},{4,6},{5,7},{6,4},{7,5},{8,10},{9,11},{10,... | collective-permute-start | bytes 786440 | tf_op jit(solution)/shard_map/ppermute | solution.py:787
  166.3 19.2 %all-to-all-start = ((bf16[4,128,1024]{2,1,0:T(8,128)(2,1)}), bf16[4,128,1024]{2,1,0:T(8,128)(2,1)S(1)}, u32[]{:S(2)}, u32[]{:S(2)}) async-start(bf16[4,128,1024]{2,1,0:T(8,128)(2,1)} %bitcast.49), calls=%async_computation | async-start | bytes 2097152 | tf_op jit(solution)/shard_map/all_to_all | solution.py:782
  173.6 8.0 %collective-permute-start.42 = (f32[128]{0:T(128)S(1)}, f32[128]{0:T(128)}, u32[]{:S(2)}, u32[]{:S(2)}) collective-permute-start(f32[128]{0:T(128)S(1)} %add.195), channel_id=1, source_target_pairs={{0,1},{1,0},{2,3},{3,2},{4,5},{5,4},{6,7},{7,6},{8,9},{9,8},{10,11... | collective-permute-start | bytes 1544 | tf_op jit(solution)/shard_map/ppermute | solution.py:787
  174.1 10.2 %collective-permute-start.43 = (f32[128]{0:T(128)S(1)}, f32[128]{0:T(128)}, u32[]{:S(2)}, u32[]{:S(2)}) collective-permute-start(f32[128]{0:T(128)S(1)} %add.195), channel_id=1, source_target_pairs={{0,2},{1,3},{2,0},{3,1},{4,6},{5,7},{6,4},{7,5},{8,10},{9,11},{10,... | collective-permute-start | bytes 1544 | tf_op jit(solution)/shard_map/ppermute | solution.py:787
  175.8 8.5 %collective-permute-start.44 = (f32[128]{0:T(128)S(1)}, f32[128]{0:T(128)}, u32[]{:S(2)}, u32[]{:S(2)}) collective-permute-start(f32[128]{0:T(128)S(1)} %add.195), channel_id=1, source_target_pairs={{0,3},{1,2},{2,1},{3,0},{4,7},{5,6},{6,5},{7,4},{8,11},{9,10},{10,... | collective-permute-start | bytes 1544 | tf_op jit(solution)/shard_map/ppermute | solution.py:787
  (56 other events, 409.8 us)

commit v11 on v9

--- a/solution.py
+++ b/solution.py
@@ -15,7 +15,7 @@
 pad = 8
 head_rows = 16
 head_width = 64
-vmem_bytes = 61 * 1024 * 1024
+vmem_bytes = 57 * 1024 * 1024
 
 
 def mm(a, b, over=(1, 0)):

time: 181 us -> 183 us (1.011)
    unnamed x88 -> x90, local copies, waits for them, and re-layouts: 6.26 us -> 6.91 us
  transfers between devices with their start and end apart: 46 -> 46, of which waited for: 20 -> 19; matrix products, arithmetic and copies ran while one was open for 8% -> 8% of each run, Pallas kernels for 29% -> 29%
where the time goes in v11:
time: 183 us
  Pallas kernels  76.2 us (42%)
  starting transfers between devices  46 us (25%)
  waiting for transfers between devices  38.6 us (21%)
  local copies, waits for them, and re-layouts  12.6 us (7%)
  other arithmetic  8.16 us (4%)
    pallas_call x12, Pallas kernels, call(): pl.pallas_call(kernel, out_shape=[jax.ShapeDtypeStruct(shape, kind) for s...  63.4 us
    ppermute x28, waiting for transfers between devices, ring_send(): return lax.ppermute(value, 'dp', pairs)  34.2 us
    ppermute x28, starting transfers between devices, ring_send(): return lax.ppermute(value, 'dp', pairs)  30.2 us
    pallas_call x4, Pallas kernels, chunk_pair(): pl.pallas_call(functools.partial(chunk_kernel, slots, len(got)), grid_spe...  12.8 us
    ppermute x17, starting transfers between devices, tensor_swap(): return lax.ppermute(value, 'tensor', [(i, i ^ bit) for i in range(4)])  12.1 us
    unnamed x90, local copies, waits for them, and re-layouts  6.91 us
    ppermute x17, waiting for transfers between devices, tensor_swap(): return lax.ppermute(value, 'tensor', [(i, i ^ bit) for i in range(4)])  4.31 us
  transfers between devices with their start and end apart: 46, of which 19 were waited for; matrix products, arithmetic and copies ran while one was open for 8% of the time, Pallas kernels for 29%

profile of v11, /device:TPU:0, one launch (start us, length us, event | category | flops | bytes accessed | tf_op | source)
XLA Modules:
  0.0 182.7 jit_solution(15569745342748249264)
XLA Ops:
  3.3 2.6 %collective-permute-start.1 = (bf16[48,256]{1,0:T(8,128)(2,1)}, bf16[48,256]{1,0:T(8,128)(2,1)S(1)}, u32[]{:S(2)}, u32[]{:S(2)}) collective-permute-start(bf16[48,256]{1,0:T(8,128)(2,1)} %shard_map.271.refs_0_), channel_id=1, source_target_pairs={{0,2},{1,3},{2,0},{3,1},{4,6},{5,7},{6,4},{7,5},{8,10},{9,11},{10,... | collective-permute-start | bytes 73736 | tf_op jit(solution)/shard_map/ppermute | solution.py:787
  5.9 2.0 %shard_map.272.refs_4_ = bf16[256,512]{1,0:T(8,128)(2,1)} custom-call(bf16[128,2,512]{2,1,0:T(2,128)(2,1)} %input_ref.3, bf16[512,128]{1,0:T(8,128)(2,1)} %out_ref), custom_call_target="tpu_custom_call" | custom-call | flops 2200000000 | bytes 1048576 | tf_op jit(solution)/shard_map/pallas_call | solution.py:703
  8.0 1.8 collective-permute-start.6
  10.1 1.8 collective-permute-start.4
  12.5 2.0 %shard_map.273.refs_4_ = bf16[208,512]{1,0:T(8,128)(2,1)} custom-call(bf16[128,2,512]{2,1,0:T(2,128)(2,1)} %input_ref.3, bf16[16,128]{1,0:T(8,128)(2,1)} %pad.4.step_ref, bf16[48,256]{1,0:T(8,128)(2,1)} %shard_map.271.refs_0_, bf16[48,256]{1,0:T(8,128)(2,1)} %copy-done.37, bf16[48,256]{1,0:T(8,128)(2,1)} %copy-done.38, bf16[48,256]{1,0:T(8,128)(2,1)} %copy-done.39), custom_call_target="tpu_custom_call" | custom-call | flops 1100000000 | bytes 1048576 | tf_op jit(solution)/shard_map/pallas_call | solution.py:703
  14.5 2.2 %collective-permute-done.6.refs_5_ = bf16[256,512]{1,0:T(8,128)(2,1)S(1)} collective-permute-done((bf16[256,512]{1,0:T(8,128)(2,1)}, bf16[256,512]{1,0:T(8,128)(2,1)S(1)}, u32[]{:S(2)}, u32[]{:S(2)}) %collective-permute-start.6) | collective-permute-done | bytes 262176 | tf_op jit(solution)/shard_map/ppermute | solution.py:738
  21.9 4.8 %collective-permute-done.13.refs_5_ = bf16[208,512]{1,0:T(8,128)(2,1)S(1)} collective-permute-done((bf16[208,512]{1,0:T(8,128)(2,1)}, bf16[208,512]{1,0:T(8,128)(2,1)S(1)}, u32[]{:S(2)}, u32[]{:S(2)}) %collective-permute-start.13) | collective-permute-done | bytes 213024 | tf_op jit(solution)/shard_map/ppermute | solution.py:738
  29.0 3.3 %collective-permute-done.8.refs_7_ = bf16[256,512]{1,0:T(8,128)(2,1)S(1)} collective-permute-done((bf16[256,512]{1,0:T(8,128)(2,1)S(1)}, bf16[256,512]{1,0:T(8,128)(2,1)S(1)}, u32[]{:S(2)}, u32[]{:S(2)}) %collective-permute-start.8) | collective-permute-done | bytes 262176 | tf_op jit(solution)/shard_map/ppermute | solution.py:738
  32.6 2.4 %collective-permute-done.15.refs_7_ = bf16[208,512]{1,0:T(8,128)(2,1)S(1)} collective-permute-done((bf16[208,512]{1,0:T(8,128)(2,1)S(1)}, bf16[208,512]{1,0:T(8,128)(2,1)S(1)}, u32[]{:S(2)}, u32[]{:S(2)}) %collective-permute-start.15) | collective-permute-done | bytes 213024 | tf_op jit(solution)/shard_map/ppermute | solution.py:738
  37.4 1.6 collective-permute-start.10
  39.0 2.6 %collective-permute-done.16.refs_8_ = bf16[208,512]{1,0:T(8,128)(2,1)} collective-permute-done((bf16[208,512]{1,0:T(8,128)(2,1)S(1)}, bf16[208,512]{1,0:T(8,128)(2,1)}, u32[]{:S(2)}, u32[]{:S(2)}) %collective-permute-start.16) | collective-permute-done | bytes 213024 | tf_op jit(solution)/shard_map/ppermute | solution.py:738
  46.1 1.6 shard_map.274
  49.9 3.0 %collective-permute-done.19.refs_11_ = bf16[208,512]{1,0:T(8,128)(2,1)} collective-permute-done((bf16[208,512]{1,0:T(8,128)(2,1)}, bf16[208,512]{1,0:T(8,128)(2,1)}, u32[]{:S(2)}, u32[]{:S(2)}) %collective-permute-start.19) | collective-permute-done | bytes 213024 | tf_op jit(solution)/shard_map/ppermute | solution.py:738
  52.9 11.2 %shard_map.275 = (bf16[512,1024]{1,0:T(8,128)(2,1)}, bf16[1024,512]{1,0:T(8,128)(2,1)}, bf16[1024,512]{1,0:T(8,128)(2,1)}, bf16[1024,256]{1,0:T(8,128)(2,1)}, bf...) custom-call(s32[12]{0:T(128)} %stack.66.place_ref, ...), custom_call_target="tpu_custom_call" | custom-call | flops 12099999744 | bytes 1048576 | tf_op jit(solution)/shard_map/pallas_call | solution.py:703
  64.9 7.3 %shard_map.276 = (bf16[512,1024]{1,0:T(8,128)(2,1)}, bf16[1024,512]{1,0:T(8,128)(2,1)}, bf16[1024,512]{1,0:T(8,128)(2,1)}, f32[512,512]{1,0:T(8,128)}, f32[512,512]{1,0:T(8,128)}, /*index=5*/f32[8,512]{1,0:T(8,128)}) custom-call(s32[12]{0:T(128)} %stack.66.place_ref, s32[1,4]{1,0:T(1,128)} %lengths_ref.13, bf16[256,1024]{1,0:T(8,128)(2,1)} %copy-done.5, ...), custom_call_target="tpu_custom_call" | custom-call | flops 5500000256 | bytes 1048576 | tf_op jit(solution)/shard_map/pallas_call | solution.py:703
  74.1 2.1 %collective-permute-done.21.refs_2_ = f32[8,512]{1,0:T(8,128)S(1)} collective-permute-done((f32[8,512]{1,0:T(8,128)}, f32[8,512]{1,0:T(8,128)S(1)}, u32[]{:S(2)}, u32[]{:S(2)}) %collective-permute-start.21) | collective-permute-done | bytes 16416 | tf_op jit(solution)/shard_map/ppermute | solution.py:787
  77.8 8.1 %shard_map.277 = (bf16[256,512]{1,0:T(8,128)(2,1)}, bf16[256,512]{1,0:T(8,128)(2,1)}, bf16[256,512]{1,0:T(8,128)(2,1)}, bf16[256,512]{1,0:T(8,128)(2,1)}, bf16[2...) custom-call(s32[12]{0:T(128)} %stack.66.place_ref, ...), custom_call_target="tpu_custom_call" | custom-call | flops 9900000256 | bytes 1048576 | tf_op jit(solution)/shard_map/pallas_call | solution.py:703
  87.9 6.5 %shard_map.278 = (f32[512,256]{1,0:T(8,128)}, f32[512,256]{1,0:T(8,128)}, f32[16,512]{1,0:T(8,128)}, f32[8,256]{1,0:T(8,128)}) custom-call(s32[1,4]{1,0:T(1,128)} %lengths_ref.13, f32[512,512]{1,0:T(8,128)} %get-tuple-element.132.refs_0_, f32[512,512]{1,0:T(8,128)} %get-tuple-element.123.refs_1_, f32[512,256]{1,0:T(8,128)} %get-tuple-element.124.refs_2_, ...), custom_call_target="tpu_custom_call" | custom-call | flops 6600000000 | bytes 1048576 | tf_op jit(solution)/shard_map/pallas_call | solution.py:703
  97.2 6.5 %shard_map.279 = (f32[512,256]{1,0:T(8,128)}, f32[512,256]{1,0:T(8,128)}, f32[16,512]{1,0:T(8,128)}, f32[8,256]{1,0:T(8,128)}) custom-call(s32[1,4]{1,0:T(1,128)} %lengths_ref.13, f32[512,512]{1,0:T(8,128)} %get-tuple-element.132.refs_0_, f32[512,512]{1,0:T(8,128)} %get-tuple-element.123.refs_1_, f32[512,256]{1,0:T(8,128)} %get-tuple-element.124.refs_2_, ...), custom_call_target="tpu_custom_call" | custom-call | flops 6600000000 | bytes 1048576 | tf_op jit(solution)/shard_map/pallas_call | solution.py:703
  105.9 5.4 %shard_map.281 = (bf16[512,256]{1,0:T(8,128)(2,1)}, bf16[16,512]{1,0:T(8,128)(2,1)}, bf16[272,256]{1,0:T(8,128)(2,1)}, bf16[272,256]{1,0:T(8,128)(2,1)}, bf16[27...) custom-call(s32[12]{0:T(128)} %stack.66.place_ref, s32[1,4]{1,0:T(1,128)} %lengths_ref.13, ...), custom_call_target="tpu_custom_call" | custom-call | flops 4400000000 | bytes 1048576 | tf_op jit(solution)/shard_map/pallas_call | solution.py:703
  113.3 5.6 %shard_map.280 = (bf16[512,512]{1,0:T(8,128)(2,1)}, f32[16,512]{1,0:T(8,128)}) custom-call(s32[1,4]{1,0:T(1,128)} %lengths_ref.13, f32[512,256]{1,0:T(8,128)} %get-tuple-element.127.refs_0_, f32[512,256]{1,0:T(8,128)} %get-tuple-element.133.refs_1_, f32[8,256]{1,0:T(8,128)} %get-tuple-element.134.refs_2_, f32[8,256]{1,0:T(8,128)} %get-tuple-element.135.refs_3_, ...), custom_call_target="tpu_custom_call" | custom-call | flops 6600000000 | bytes 1048576 | tf_op jit(solution)/shard_map/pallas_call | solution.py:703
  120.8 3.1 %shard_map.283 = (bf16[176,512]{1,0:T(8,128)(2,1)}, bf16[176,512]{1,0:T(8,128)(2,1)}) custom-call(s32[12]{0:T(128)} %stack.66.place_ref, bf16[512,512]{1,0:T(8,128)(2,1)} %get-tuple-element.174.refs_1_.refs_0_, bf16[16,512]{1,0:T(8,128)(2,1)} %get-tuple-element.155.refs_3_.refs_1_, f32[16,512]{1,0:T(8,128)} %get-tuple-element.162.refs_2_, ...), custom_call_target="tpu_custom_call" | custom-call | flops 2000000000 | bytes 1048576 | tf_op jit(solution)/shard_map/pallas_call | solution.py:1084
  126.0 5.6 %shard_map.282 = (bf16[2,128,1024]{2,1,0:T(8,128)(2,1)}, bf16[2,128,1024]{2,1,0:T(8,128)(2,1)}) custom-call(s32[12]{0:T(128)} %stack.66.place_ref, bf16[512,512]{1,0:T(8,128)(2,1)} %get-tuple-element.121.refs_0_, bf16[512,512]{1,0:T(8,128)(2,1)} %get-tuple-element.174.refs_1_.refs_0_, bf16[512,256]{1,0:T(8,128)(2,1)} %get-tuple-element.154.refs_2_, ...), custom_call_target="tpu_custom_call" | custom-call | flops 6600000000 | bytes 1048576 | tf_op jit(solution)/shard_map/pallas_call | solution.py:703
  134.3 3.2 %shard_map.284 = (bf16[176,512]{1,0:T(8,128)(2,1)}, bf16[176,512]{1,0:T(8,128)(2,1)}) custom-call(s32[12]{0:T(128)} %stack.66.place_ref, bf16[512,512]{1,0:T(8,128)(2,1)} %get-tuple-element.174.refs_1_.refs_0_, bf16[16,512]{1,0:T(8,128)(2,1)} %get-tuple-element.155.refs_3_.refs_1_, f32[16,512]{1,0:T(8,128)} %get-tuple-element.162.refs_2_, ...), custom_call_target="tpu_custom_call" | custom-call | flops 2000000000 | bytes 1048576 | tf_op jit(solution)/shard_map/pallas_call | solution.py:1084
  137.5 3.6 %all-to-all-start = ((bf16[4,128,1024]{2,1,0:T(8,128)(2,1)}), bf16[4,128,1024]{2,1,0:T(8,128)(2,1)S(1)}, u32[]{:S(2)}, u32[]{:S(2)}) async-start(bf16[4,128,1024]{2,1,0:T(8,128)(2,1)} %bitcast.19), calls=%async_computation | async-start | bytes 2097152 | tf_op jit(solution)/shard_map/all_to_all | solution.py:782
  141.9 1.6 collective-permute-start.35
  144.1 5.0 %collective-permute-done.35.refs_9_ = bf16[176,512]{1,0:T(8,128)(2,1)S(1)} collective-permute-done((bf16[176,512]{1,0:T(8,128)(2,1)}, bf16[176,512]{1,0:T(8,128)(2,1)S(1)}, u32[]{:S(2)}, u32[]{:S(2)}) %collective-permute-start.35) | collective-permute-done | bytes 180256 | tf_op jit(solution)/shard_map/ppermute | solution.py:738
  151.0 3.2 %shard_map.285 = (bf16[176,512]{1,0:T(8,128)(2,1)}, bf16[176,512]{1,0:T(8,128)(2,1)}) custom-call(s32[12]{0:T(128)} %stack.66.place_ref, bf16[512,512]{1,0:T(8,128)(2,1)} %get-tuple-element.174.refs_1_.refs_0_, bf16[16,512]{1,0:T(8,128)(2,1)} %get-tuple-element.155.refs_3_.refs_1_, f32[16,512]{1,0:T(8,128)} %get-tuple-element.162.refs_2_, ...), custom_call_target="tpu_custom_call" | custom-call | flops 2000000000 | bytes 1048576 | tf_op jit(solution)/shard_map/pallas_call | solution.py:1084
  157.3 3.1 %collective-permute-done.37.refs_9_ = bf16[176,512]{1,0:T(8,128)(2,1)} collective-permute-done((bf16[176,512]{1,0:T(8,128)(2,1)}, bf16[176,512]{1,0:T(8,128)(2,1)}, u32[]{:S(2)}, u32[]{:S(2)}) %collective-permute-start.37) | collective-permute-done | bytes 180256 | tf_op jit(solution)/shard_map/ppermute | solution.py:738
  161.6 3.3 %shard_map.286 = (bf16[176,512]{1,0:T(8,128)(2,1)}, f32[176,512]{1,0:T(8,128)}) custom-call(s32[12]{0:T(128)} %stack.66.place_ref, bf16[512,512]{1,0:T(8,128)(2,1)} %get-tuple-element.174.refs_1_.refs_0_, bf16[16,512]{1,0:T(8,128)(2,1)} %get-tuple-element.155.refs_3_.refs_1_, f32[16,512]{1,0:T(8,128)} %get-tuple-element.162.refs_2_, ...), custom_call_target="tpu_custom_call" | custom-call | flops 2000000000 | bytes 1048576 | tf_op jit(solution)/shard_map/pallas_call | solution.py:1084
  169.0 1.7 collective-permute-done.39
  173.0 1.7 collective-permute-start.43
  (205 shorter events, 61.8 us)
Async XLA Ops:
  8.0 8.8 %collective-permute-start.6 = (bf16[256,512]{1,0:T(8,128)(2,1)}, bf16[256,512]{1,0:T(8,128)(2,1)S(1)}, u32[]{:S(2)}, u32[]{:S(2)}) collective-permute-start(bf16[256,512]{1,0:T(8,128)(2,1)} %shard_map.272.refs_4_), channel_id=1, source_target_pairs={{0,8},{8,16},{16,24},{24,28},{28,20},{20,12},{12,4},{4,0},{1,9},{9... | collective-permute-start | bytes 786440 | tf_op jit(solution)/shard_map/ppermute | solution.py:738
  9.8 8.5 %collective-permute-start.7 = (bf16[256,512]{1,0:T(8,128)(2,1)}, bf16[256,512]{1,0:T(8,128)(2,1)S(1)}, u32[]{:S(2)}, u32[]{:S(2)}) collective-permute-start(bf16[256,512]{1,0:T(8,128)(2,1)} %shard_map.272.refs_4_), channel_id=1, source_target_pairs={{0,4},{8,0},{16,8},{24,16},{28,24},{20,28},{12,20},{4,12},{1,5},{9... | collective-permute-start | bytes 786440 | tf_op jit(solution)/shard_map/ppermute | solution.py:738
  10.1 18.7 %collective-permute-start.4 = (bf16[256,1024]{1,0:T(8,128)(2,1)S(1)}, bf16[256,1024]{1,0:T(8,128)(2,1)S(1)}, u32[]{:S(2)}, u32[]{:S(2)}) collective-permute-start(bf16[256,1024]{1,0:T(8,128)(2,1)S(1)} %pad_maximum_fusion.refs_0_), channel_id=1, source_target_pairs={{0,2},{1,3},{2,0},{3,1},{4,6},{5,7},{6,4},{7,5},{8,10},{9,11},{10,... | collective-permute-start | bytes 1572872 | tf_op jit(solution)/shard_map/ppermute | solution.py:787
  18.3 8.4 %collective-permute-start.13 = (bf16[208,512]{1,0:T(8,128)(2,1)}, bf16[208,512]{1,0:T(8,128)(2,1)S(1)}, u32[]{:S(2)}, u32[]{:S(2)}) collective-permute-start(bf16[208,512]{1,0:T(8,128)(2,1)} %shard_map.273.refs_4_), channel_id=1, source_target_pairs={{0,8},{8,16},{16,24},{24,28},{28,20},{20,12},{12,4},{4,0},{1,9},{9... | collective-permute-start | bytes 638984 | tf_op jit(solution)/shard_map/ppermute | solution.py:738
  19.9 8.4 %collective-permute-start.14 = (bf16[208,512]{1,0:T(8,128)(2,1)}, bf16[208,512]{1,0:T(8,128)(2,1)S(1)}, u32[]{:S(2)}, u32[]{:S(2)}) collective-permute-start(bf16[208,512]{1,0:T(8,128)(2,1)} %shard_map.273.refs_4_), channel_id=1, source_target_pairs={{0,4},{8,0},{16,8},{24,16},{28,24},{20,28},{12,20},{4,12},{1,5},{9... | collective-permute-start | bytes 638984 | tf_op jit(solution)/shard_map/ppermute | solution.py:738
  20.3 12.0 %collective-permute-start.8 = (bf16[256,512]{1,0:T(8,128)(2,1)S(1)}, bf16[256,512]{1,0:T(8,128)(2,1)S(1)}, u32[]{:S(2)}, u32[]{:S(2)}) collective-permute-start(bf16[256,512]{1,0:T(8,128)(2,1)S(1)} %collective-permute-done.6.refs_5_), channel_id=1, source_target_pairs={{0,8},{8,16},{16,24},{24,28},{28,20},{20,12},{12,4},{4,0},{1,9},{9... | collective-permute-start | bytes 786440 | tf_op jit(solution)/shard_map/ppermute | solution.py:738
  26.7 8.4 %collective-permute-start.15 = (bf16[208,512]{1,0:T(8,128)(2,1)S(1)}, bf16[208,512]{1,0:T(8,128)(2,1)S(1)}, u32[]{:S(2)}, u32[]{:S(2)}) collective-permute-start(bf16[208,512]{1,0:T(8,128)(2,1)S(1)} %collective-permute-done.13.refs_5_), channel_id=1, source_target_pairs={{0,8},{8,16},{16,24},{24,28},{28,20},{20,12},{12,4},{4,0},{1,9},{9... | collective-permute-start | bytes 638984 | tf_op jit(solution)/shard_map/ppermute | solution.py:738
  28.3 19.5 %collective-permute-start.3 = (bf16[256,1024]{1,0:T(8,128)(2,1)S(1)}, bf16[256,1024]{1,0:T(8,128)(2,1)S(1)}, u32[]{:S(2)}, u32[]{:S(2)}) collective-permute-start(bf16[256,1024]{1,0:T(8,128)(2,1)S(1)} %pad_maximum_fusion.refs_0_), channel_id=1, source_target_pairs={{0,1},{1,0},{2,3},{3,2},{4,5},{5,4},{6,7},{7,6},{8,9},{9,8},{10,11... | collective-permute-start | bytes 1572872 | tf_op jit(solution)/shard_map/ppermute | solution.py:787
  28.3 9.2 %collective-permute-start.9 = (bf16[256,512]{1,0:T(8,128)(2,1)S(1)}, bf16[256,512]{1,0:T(8,128)(2,1)S(1)}, u32[]{:S(2)}, u32[]{:S(2)}) collective-permute-start(bf16[256,512]{1,0:T(8,128)(2,1)S(1)} %collective-permute-done.7.refs_6_), channel_id=1, source_target_pairs={{0,4},{8,0},{16,8},{24,16},{28,24},{20,28},{12,20},{4,12},{1,5},{9... | collective-permute-start | bytes 786440 | tf_op jit(solution)/shard_map/ppermute | solution.py:738
  28.8 21.1 %collective-permute-start.5 = (bf16[256,1024]{1,0:T(8,128)(2,1)S(1)}, bf16[256,1024]{1,0:T(8,128)(2,1)S(1)}, u32[]{:S(2)}, u32[]{:S(2)}) collective-permute-start(bf16[256,1024]{1,0:T(8,128)(2,1)S(1)} %collective-permute-done.4.refs_2_), channel_id=1, source_target_pairs={{0,1},{1,0},{2,3},{3,2},{4,5},{5,4},{6,7},{7,6},{8,9},{9,8},{10,11... | collective-permute-start | bytes 1572872 | tf_op jit(solution)/shard_map/ppermute | solution.py:787
  32.3 9.4 %collective-permute-start.16 = (bf16[208,512]{1,0:T(8,128)(2,1)S(1)}, bf16[208,512]{1,0:T(8,128)(2,1)}, u32[]{:S(2)}, u32[]{:S(2)}) collective-permute-start(bf16[208,512]{1,0:T(8,128)(2,1)S(1)} %collective-permute-done.14.refs_6_), channel_id=1, source_target_pairs={{0,4},{8,0},{16,8},{24,16},{28,24},{20,28},{12,20},{4,12},{1,5},{9... | collective-permute-start | bytes 638984 | tf_op jit(solution)/shard_map/ppermute | solution.py:738
  35.0 7.7 %collective-permute-start.17 = (bf16[208,512]{1,0:T(8,128)(2,1)S(1)}, bf16[208,512]{1,0:T(8,128)(2,1)}, u32[]{:S(2)}, u32[]{:S(2)}) collective-permute-start(bf16[208,512]{1,0:T(8,128)(2,1)S(1)} %collective-permute-done.15.refs_7_), channel_id=1, source_target_pairs={{0,8},{8,16},{16,24},{24,28},{28,20},{20,12},{12,4},{4,0},{1,9},{9... | collective-permute-start | bytes 638984 | tf_op jit(solution)/shard_map/ppermute | solution.py:738
  37.4 10.9 %collective-permute-start.10 = (bf16[256,512]{1,0:T(8,128)(2,1)S(1)}, bf16[256,512]{1,0:T(8,128)(2,1)}, u32[]{:S(2)}, u32[]{:S(2)}) collective-permute-start(bf16[256,512]{1,0:T(8,128)(2,1)S(1)} %collective-permute-done.8.refs_7_), channel_id=1, source_target_pairs={{0,8},{8,16},{16,24},{24,28},{28,20},{20,12},{12,4},{4,0},{1,9},{9... | collective-permute-start | bytes 786440 | tf_op jit(solution)/shard_map/ppermute | solution.py:738
  41.7 8.2 %collective-permute-start.18 = (bf16[208,512]{1,0:T(8,128)(2,1)}, bf16[208,512]{1,0:T(8,128)(2,1)}, u32[]{:S(2)}, u32[]{:S(2)}) collective-permute-start(bf16[208,512]{1,0:T(8,128)(2,1)} %collective-permute-done.16.refs_8_), channel_id=1, source_target_pairs={{0,4},{8,0},{16,8},{24,16},{28,24},{20,28},{12,20},{4,12},{1,5},{9... | collective-permute-start | bytes 638984 | tf_op jit(solution)/shard_map/ppermute | solution.py:738
  42.7 10.2 %collective-permute-start.19 = (bf16[208,512]{1,0:T(8,128)(2,1)}, bf16[208,512]{1,0:T(8,128)(2,1)}, u32[]{:S(2)}, u32[]{:S(2)}) collective-permute-start(bf16[208,512]{1,0:T(8,128)(2,1)} %collective-permute-done.17.refs_9_), channel_id=1, source_target_pairs={{0,8},{8,16},{16,24},{24,28},{28,20},{20,12},{12,4},{4,0},{1,9},{9... | collective-permute-start | bytes 638984 | tf_op jit(solution)/shard_map/ppermute | solution.py:738
  47.8 16.3 %collective-permute-start.11 = (bf16[256,512]{1,0:T(8,128)(2,1)S(1)}, bf16[256,512]{1,0:T(8,128)(2,1)S(1)}, u32[]{:S(2)}, u32[]{:S(2)}) collective-permute-start(bf16[256,512]{1,0:T(8,128)(2,1)S(1)} %collective-permute-done.9.refs_8_), channel_id=1, source_target_pairs={{0,4},{8,0},{16,8},{24,16},{28,24},{20,28},{12,20},{4,12},{1,5},{9... | collective-permute-start | bytes 786440 | tf_op jit(solution)/shard_map/ppermute | solution.py:738
  48.3 15.8 %collective-permute-start.12 = (bf16[256,512]{1,0:T(8,128)(2,1)}, bf16[256,512]{1,0:T(8,128)(2,1)S(1)}, u32[]{:S(2)}, u32[]{:S(2)}) collective-permute-start(bf16[256,512]{1,0:T(8,128)(2,1)} %collective-permute-done.10.refs_9_), channel_id=1, source_target_pairs={{0,8},{8,16},{16,24},{24,28},{28,20},{20,12},{12,4},{4,0},{1,9},{9... | collective-permute-start | bytes 786440 | tf_op jit(solution)/shard_map/ppermute | solution.py:738
  85.9 8.7 %collective-permute-start.24 = (bf16[256,512]{1,0:T(8,128)(2,1)}, bf16[256,512]{1,0:T(8,128)(2,1)S(1)}, u32[]{:S(2)}, u32[]{:S(2)}) collective-permute-start(bf16[256,512]{1,0:T(8,128)(2,1)} %get-tuple-element.130), channel_id=1, source_target_pairs={{0,4},{8,0},{16,8},{24,16},{28,24},{20,28},{12,20},{4,12},{1,5},{9... | collective-permute-start | bytes 786440 | tf_op jit(solution)/shard_map/ppermute | solution.py:738
  86.7 8.3 %collective-permute-start.23 = (bf16[256,512]{1,0:T(8,128)(2,1)}, bf16[256,512]{1,0:T(8,128)(2,1)S(1)}, u32[]{:S(2)}, u32[]{:S(2)}) collective-permute-start(bf16[256,512]{1,0:T(8,128)(2,1)} %get-tuple-element.128), channel_id=1, source_target_pairs={{0,8},{8,16},{16,24},{24,28},{28,20},{20,12},{12,4},{4,0},{1,9},{9... | collective-permute-start | bytes 786440 | tf_op jit(solution)/shard_map/ppermute | solution.py:738
  95.1 8.5 %collective-permute-start.26 = (bf16[256,512]{1,0:T(8,128)(2,1)S(1)}, bf16[256,512]{1,0:T(8,128)(2,1)S(1)}, u32[]{:S(2)}, u32[]{:S(2)}) collective-permute-start(bf16[256,512]{1,0:T(8,128)(2,1)S(1)} %add_convert_fusion.4), channel_id=1, source_target_pairs={{0,4},{8,0},{16,8},{24,16},{28,24},{20,28},{12,20},{4,12},{1,5},{9... | collective-permute-start | bytes 786440 | tf_op jit(solution)/shard_map/ppermute | solution.py:738
  103.9 9.4 %collective-permute-start.27 = (bf16[256,512]{1,0:T(8,128)(2,1)S(1)}, bf16[256,512]{1,0:T(8,128)(2,1)S(1)}, u32[]{:S(2)}, u32[]{:S(2)}) collective-permute-start(bf16[256,512]{1,0:T(8,128)(2,1)S(1)} %add_convert_fusion.3), channel_id=1, source_target_pairs={{0,8},{8,16},{16,24},{24,28},{28,20},{20,12},{12,4},{4,0},{1,9},{9... | collective-permute-start | bytes 786440 | tf_op jit(solution)/shard_map/ppermute | solution.py:738
  105.2 8.1 %collective-permute-start.28 = (bf16[256,512]{1,0:T(8,128)(2,1)S(1)}, bf16[256,512]{1,0:T(8,128)(2,1)S(1)}, u32[]{:S(2)}, u32[]{:S(2)}) collective-permute-start(bf16[256,512]{1,0:T(8,128)(2,1)S(1)} %add_convert_fusion.2), channel_id=1, source_target_pairs={{0,4},{8,0},{16,8},{24,16},{28,24},{20,28},{12,20},{4,12},{1,5},{9... | collective-permute-start | bytes 786440 | tf_op jit(solution)/shard_map/ppermute | solution.py:738
  111.4 7.6 %collective-permute-start.30 = (bf16[272,256]{1,0:T(8,128)(2,1)}, bf16[272,256]{1,0:T(8,128)(2,1)S(1)}, u32[]{:S(2)}, u32[]{:S(2)}) collective-permute-start(bf16[272,256]{1,0:T(8,128)(2,1)} %get-tuple-element.165), channel_id=1, source_target_pairs={{0,2},{1,3},{2,0},{3,1},{4,6},{5,7},{6,4},{7,5},{8,10},{9,11},{10,... | collective-permute-start | bytes 417800 | tf_op jit(solution)/shard_map/ppermute | solution.py:787
  112.1 8.1 %collective-permute-start.31 = (bf16[272,256]{1,0:T(8,128)(2,1)}, bf16[272,256]{1,0:T(8,128)(2,1)S(1)}, u32[]{:S(2)}, u32[]{:S(2)}) collective-permute-start(bf16[272,256]{1,0:T(8,128)(2,1)} %get-tuple-element.166), channel_id=1, source_target_pairs={{0,3},{1,2},{2,1},{3,0},{4,7},{5,6},{6,5},{7,4},{8,11},{9,10},{10,... | collective-permute-start | bytes 417800 | tf_op jit(solution)/shard_map/ppermute | solution.py:787
  123.9 9.0 %collective-permute-start.32 = (bf16[176,512]{1,0:T(8,128)(2,1)}, bf16[176,512]{1,0:T(8,128)(2,1)S(1)}, u32[]{:S(2)}, u32[]{:S(2)}) collective-permute-start(bf16[176,512]{1,0:T(8,128)(2,1)} %get-tuple-element.167), channel_id=1, source_target_pairs={{0,8},{8,16},{16,24},{24,28},{28,20},{20,12},{12,4},{4,0},{1,9},{9... | collective-permute-start | bytes 540680 | tf_op jit(solution)/shard_map/ppermute | solution.py:738
  125.3 7.7 %collective-permute-start.33 = (bf16[176,512]{1,0:T(8,128)(2,1)}, bf16[176,512]{1,0:T(8,128)(2,1)S(1)}, u32[]{:S(2)}, u32[]{:S(2)}) collective-permute-start(bf16[176,512]{1,0:T(8,128)(2,1)} %get-tuple-element.168), channel_id=1, source_target_pairs={{0,4},{8,0},{16,8},{24,16},{28,24},{20,28},{12,20},{4,12},{1,5},{9... | collective-permute-start | bytes 540680 | tf_op jit(solution)/shard_map/ppermute | solution.py:738
  131.6 24.7 %collective-permute-start.34 = (bf16[2,128,1024]{2,1,0:T(8,128)(2,1)}, bf16[2,128,1024]{2,1,0:T(8,128)(2,1)S(1)}, u32[]{:S(2)}, u32[]{:S(2)}) collective-permute-start(bf16[2,128,1024]{2,1,0:T(8,128)(2,1)} %get-tuple-element.160), channel_id=1, source_target_pairs={{0,1},{1,0},{2,3},{3,2},{4,5},{5,4},{6,7},{7,6},{8,9},{9,8},{10,11... | collective-permute-start | bytes 1572872 | tf_op jit(solution)/shard_map/ppermute | solution.py:787
  131.6 12.4 %collective-permute-start.41 = (bf16[256,512]{1,0:T(8,128)(2,1)S(1)}, bf16[256,512]{1,0:T(8,128)(2,1)S(1)}, u32[]{:S(2)}, u32[]{:S(2)}) collective-permute-start(bf16[256,512]{1,0:T(8,128)(2,1)S(1)} %add_convert_fusion.1), channel_id=1, source_target_pairs={{0,8},{8,16},{16,24},{24,28},{28,20},{20,12},{12,4},{4,0},{1,9},{9... | collective-permute-start | bytes 786440 | tf_op jit(solution)/shard_map/ppermute | solution.py:738
  137.5 19.5 %all-to-all-start = ((bf16[4,128,1024]{2,1,0:T(8,128)(2,1)}), bf16[4,128,1024]{2,1,0:T(8,128)(2,1)S(1)}, u32[]{:S(2)}, u32[]{:S(2)}) async-start(bf16[4,128,1024]{2,1,0:T(8,128)(2,1)} %bitcast.19), calls=%async_computation | async-start | bytes 2097152 | tf_op jit(solution)/shard_map/all_to_all | solution.py:782
  167.7 7.7 %collective-permute-start.40 = (bf16[128,1024]{1,0:T(8,128)(2,1)}, bf16[128,1024]{1,0:T(8,128)(2,1)S(1)}, u32[]{:S(2)}, u32[]{:S(2)}) collective-permute-start(bf16[128,1024]{1,0:T(8,128)(2,1)} %fusion.6), channel_id=1, source_target_pairs={{0,2},{1,3},{2,0},{3,1},{4,6},{5,7},{6,4},{7,5},{8,10},{9,11},{10,... | collective-permute-start | bytes 786440 | tf_op jit(solution)/shard_map/ppermute | solution.py:787
  172.9 9.1 %collective-permute-start.42 = (f32[128]{0:T(128)S(1)}, f32[128]{0:T(128)S(1)}, u32[]{:S(2)}, u32[]{:S(2)}) collective-permute-start(f32[128]{0:T(128)S(1)} %add.195), channel_id=1, source_target_pairs={{0,1},{1,0},{2,3},{3,2},{4,5},{5,4},{6,7},{7,6},{8,9},{9,8},{10,11... | collective-permute-start | bytes 1544 | tf_op jit(solution)/shard_map/ppermute | solution.py:787
  173.0 9.1 %collective-permute-start.43 = (f32[128]{0:T(128)S(1)}, f32[128]{0:T(128)S(1)}, u32[]{:S(2)}, u32[]{:S(2)}) collective-permute-start(f32[128]{0:T(128)S(1)} %add.195), channel_id=1, source_target_pairs={{0,2},{1,3},{2,0},{3,1},{4,6},{5,7},{6,4},{7,5},{8,10},{9,11},{10,... | collective-permute-start | bytes 1544 | tf_op jit(solution)/shard_map/ppermute | solution.py:787
  (57 other events, 429.8 us)
